TPU v7x, 32 devices: a whole 2x2x4 slice. The times are simulated.
32 devices in a mesh: groups: 2 (over x), row: 8 (over z, y), col: 2 (over core).
Axes of the slice: x: 2, y: 2, z: 4, core: 2. Of those that a mesh axis runs over, the one named last changes fastest.
Arguments:
- positions: float32 [32768, 384], P(('groups', 'row', 'col')), parts along dimension 0, may hold values from -1 to 1
- momenta: float32 [32768, 384], P(('groups', 'row', 'col')), parts along dimension 0, may hold values from -3 to 3
- tile_values: bfloat16 [3072, 128, 128], P(('groups', 'row', 'col')), parts along dimension 0, may hold values from -0.19921875 to 0.19921875
- tile_rows: int32 [3072], P(('groups', 'row', 'col')), parts along dimension 0, may hold values from 0 to 7
- tile_cols: int32 [3072], P(('groups', 'row', 'col')), parts along dimension 0, may hold values from 0 to 23
- tile_count: int32 [32], P(('groups', 'row', 'col')), parts along dimension 0, may hold values from 24 to 96, as said below
- channel_coupling: bfloat16 [48, 48], replicated, may hold values from -0.875 to 0.875
Outputs:
- new_positions: float32 [32768, 384], P(('groups', 'row', 'col')), parts along dimension 0
- new_momenta: float32 [32768, 384], P(('groups', 'row', 'col')), parts along dimension 0
- energy: float32 [16], P('groups'), parts along dimension 0
There are 2 independent parts, one for each index of `groups`. A program takes and returns all parts, laid end to end along the dimension named above; an argument that names none is the same for every part. Nothing has to cross between parts.
Inputs may be any that keep to these rules, and one draw needn't show every extreme that they name: tile_count[b] is the number of live slots of block b; slots at or past it are ignored; some block has exactly 96 live slots.
All inputs are finite; a program needn't handle non-finite values.
Results may differ from a plain program's by a relative error of at most 0.00079.
Values may be sent and summed in bfloat16 or wider, within the bound.
No kernel may reach another device: no remote copies, remote signals or barrier semaphores. Data moves between devices by JAX's collectives and lax.ppermute only.
A program may use at most 64 MiB of HBM per device.

v0:
```python
import jax
import jax.numpy as jnp
import ml_dtypes
import numpy as np
from jax import lax
from jax.experimental import pallas as pl
from jax.experimental.pallas import tpu as pltpu
from jax.sharding import PartitionSpec as P

STEPS = 2
LANES = 128
LONG, SHORT = 16, 4
VMEM_LIMIT = 14 * 1024 * 1024
F32 = jnp.float32
BF16 = jnp.bfloat16
RING = ("row", "col")


def cost(flops, moved):
    return pl.CostEstimate(
        flops=int(flops) // 1000, bytes_accessed=int(moved) // 1000, transcendentals=0
    )


def call(body, ins, outs, scratch, name, work=0):
    return pl.pallas_call(
        body,
        in_specs=[pl.BlockSpec(memory_space=pl.ANY if s is pltpu.HBM else s) for _, s in ins],
        out_specs=[pl.BlockSpec(memory_space=pl.ANY if s is pltpu.HBM else s) for *_, s in outs],
        out_shape=[
            jax.ShapeDtypeStruct(dims, kind) if s is pltpu.HBM else s(dims, kind)
            for dims, kind, s in outs
        ],
        scratch_shapes=scratch,
        compiler_params=pltpu.CompilerParams(vmem_limit_bytes=VMEM_LIMIT),
        cost_estimate=cost(work, work),
        name=name,
    )(*[pltpu.with_memory_space_constraint(a, s) for a, s in ins])


def vmem(*arrays):
    return [(a, pltpu.VMEM) for a in arrays]


def lanes(group):
    return slice(group * LANES, (group + 1) * LANES)


def spanned(group, channels, width):
    first = group * LANES // channels * channels
    last = -(-(group + 1) * LANES // channels) * channels
    return list(range(first // LANES, -(-min(last, width) // LANES)))


def span_lanes(near):
    return slice(near[0] * LANES, (near[-1] + 1) * LANES)


def split(x):
    high = x.astype(BF16)
    return high, (x - high.astype(F32)).astype(BF16)


def bases_into(outs, xs, ys, same, step, channels):
    groups = len(xs)
    width = groups * LANES
    detune = 1.0 - (step + 1.0) / (STEPS + 1.0)
    parts = [split(x) for x in xs]
    for g in range(groups):
        near = spanned(g, channels, width)
        ones = same[span_lanes(near), lanes(g)]
        totals = sum(
            jnp.dot(
                jnp.concatenate([parts[n][k] for n in near], axis=1),
                ones,
                preferred_element_type=F32,
            )
            for k in range(2)
        )
        penalty = 0.02 * (totals - (2.0 - channels))
        outs[g][...] = ys[g] + 0.5 * (-detune * xs[g] - 0.4 * penalty)


def mixed_of(fields, mixing, group, channels):
    near = spanned(group, channels, mixing.shape[0])
    return jnp.dot(
        jnp.concatenate([fields[n] for n in near], axis=1),
        mixing[span_lanes(near), lanes(group)],
        preferred_element_type=F32,
    )


def round_first(positions):
    cells = positions.shape[0]

    def body(x_ref, out_ref, buf, sem):
        copy = pltpu.make_async_copy(x_ref.at[:, lanes(0)], buf, sem)
        copy.start()
        copy.wait()
        out_ref[...] = buf[...].astype(BF16)

    return call(
        body,
        [(positions, pltpu.HBM)],
        [((cells, LANES), BF16, pltpu.VMEM)],
        [pltpu.VMEM((cells, LANES), F32), pltpu.SemaphoreType.DMA],
        "round_first",
    )[0]


def round_rest(positions, after):
    cells, width = positions.shape
    groups = width // LANES

    def body(x_ref, _, *outs):
        for g in range(1, groups):
            outs[g - 1][...] = x_ref[:, lanes(g)].astype(BF16)

    return call(
        body,
        vmem(positions, after),
        [((cells, LANES), BF16, pltpu.VMEM)] * (groups - 1),
        [],
        "round_rest",
    )


def section(slots, per):
    return -(-(slots + per) // (2 * SHORT)) * SHORT


def make_lists(rows, cols, count, mixing_parts, sent, slots, tile, cells, ring_index):
    per = cells // tile
    pairs = section(slots, per)
    same, spread, coupling = mixing_parts
    width = same.shape[0]

    def body(rows_ref, cols_ref, count_ref, same_ref, spread_ref, coupling_ref, sent_ref, list_ref, mixing_ref, copy_ref, held):
        odd = lax.rem(ring_index(), 2) == 1
        copy_ref[...] = sent_ref[...]
        tall = jnp.dot(spread_ref[...], coupling_ref[...], preferred_element_type=F32).astype(BF16)
        wide = lax.dot_general(
            tall, spread_ref[...], (((1,), (1,)), ((), ())), preferred_element_type=F32
        )
        mixing_ref[...] = (wide * same_ref[...].astype(F32)).astype(BF16)
        for k in range(2 * per):
            held[k] = -1
        far_third = jnp.where(odd, 2, 0)

        def visit(slot, totals):
            near_pairs, far_pairs = totals
            row, col = rows_ref[slot], cols_ref[slot]
            third = jnp.where(col >= 2 * per, 2, jnp.where(col >= per, 1, 0))
            source = col - third * per
            far = third == far_third
            source = jnp.where(far | (third == 1), source, source + per)
            key = row + jnp.where(far, per, 0)
            place = 2 * jnp.where(far, far_pairs + pairs, near_pairs)
            entry = slot * 65536 + source * 256 + row
            other = held[key]
            full = other >= 0
            list_ref[place] = other
            list_ref[place + 1] = entry
            held[key] = jnp.where(full, -1, entry)
            one = full.astype(jnp.int32)
            far_one = jnp.where(far, one, 0)
            return near_pairs + one - far_one, far_pairs + far_one

        totals = lax.fori_loop(0, count_ref[0], visit, (jnp.int32(0), jnp.int32(0)))
        for part, zero in enumerate((2 * per, per)):
            total = totals[part]
            start = part * pairs
            for k in range(per):
                other = held[part * per + k]
                list_ref[2 * (start + total)] = other
                list_ref[2 * (start + total) + 1] = zero * 256 + k
                total = total + (other >= 0).astype(jnp.int32)
            short_turns = (total + SHORT - 1) // SHORT

            def pad(pair, carry, start=start, zero=zero):
                for e in range(2):
                    list_ref[2 * (start + pair) + e] = zero * 256 + per
                return carry

            lax.fori_loop(total, short_turns * SHORT, pad, 0)
            list_ref[4 * pairs + 2 * part] = short_turns // (LONG // SHORT)
            list_ref[4 * pairs + 2 * part + 1] = short_turns % (LONG // SHORT)

    return call(
        body,
        [(rows, pltpu.SMEM), (cols, pltpu.SMEM), (count, pltpu.SMEM)]
        + vmem(same, spread, coupling, sent),
        [
            ((4 * pairs + 4 + 2,), jnp.int32, pltpu.SMEM),
            ((width, width), BF16, pltpu.VMEM),
            (sent.shape, BF16, pltpu.VMEM),
        ],
        [pltpu.SMEM((2 * per,), jnp.int32)],
        "make_lists",
    )


def add_pairs(part, list_ref, tiles, field, window, pairs):
    def turn(first, length):
        for u in range(length):
            place = 2 * (part * pairs + first + u)
            entries = [list_ref[place + e] for e in range(2)]
            left = jnp.concatenate([tiles[n >> 16] for n in entries], axis=1)
            right = jnp.concatenate([window[(n >> 8) & 255] for n in entries], axis=0)
            field[entries[1] & 255] += jnp.dot(left, right, preferred_element_type=F32)

    def long(i, carry):
        turn(i * LONG, LONG)
        return carry

    def short(i, carry):
        turn(long_turns * LONG + i * SHORT, SHORT)
        return carry

    long_turns = list_ref[4 * pairs + 2 * part]
    lax.fori_loop(0, long_turns, long, 0)
    lax.fori_loop(0, list_ref[4 * pairs + 2 * part + 1], short, 0)


def near_fields(lists, tiles, owns, others, far_part, sent, name):
    slots, tile, _ = tiles.shape
    cells = owns[0].shape[0]
    groups = len(owns)
    width = groups * LANES
    per = cells // tile
    pairs = section(slots, per)

    def body(list_ref, tiles_ref, *refs):
        own_refs, other_refs, refs = refs[:groups], refs[groups : 2 * groups], refs[2 * groups :]
        part_ref, sent_refs, refs = refs[0], refs[1 : 1 + len(sent)], refs[1 + len(sent) :]
        field_outs, copy_outs, (field, window) = refs[:groups], refs[groups:-2], refs[-2:]
        for out, ref in zip(copy_outs, sent_refs):
            out[...] = ref[...]
        for g in range(groups):
            window[:per, :, lanes(g)] = own_refs[g][...].reshape(per, tile, LANES)
            window[per : 2 * per, :, lanes(g)] = other_refs[g][...].reshape(per, tile, LANES)
        window[2 * per] = jnp.zeros((tile, width), BF16)
        field[:per, :, lanes(0)] = part_ref[...].reshape(per, tile, LANES)
        if groups > 1:
            field[:per, :, LANES:] = jnp.zeros((per, tile, width - LANES), F32)
        add_pairs(0, list_ref, tiles_ref, field, window, pairs)
        for g, out in enumerate(field_outs):
            out[...] = field[:per, :, lanes(g)].reshape(cells, LANES).astype(out.dtype)

    outs = call(
        body,
        [(lists, pltpu.SMEM)] + vmem(tiles, *owns, *others, far_part, *sent),
        [((cells, LANES), BF16 if g == 0 else F32, pltpu.VMEM) for g in range(groups)]
        + [((cells, LANES), BF16, pltpu.VMEM)] * len(sent),
        [
            pltpu.VMEM((per + 1, tile, width), F32),
            pltpu.VMEM((2 * per + 1, tile, width), BF16),
        ],
        name,
    )
    return outs[:groups], outs[groups:]


def far_fields(lists, tiles, near, far, extra, outs_of, work, name):
    slots, tile, _ = tiles.shape
    cells = far.shape[0]
    per = cells // tile
    pairs = section(slots, per)
    start = [] if near is None else [near]

    def body(list_ref, tiles_ref, far_ref, *refs):
        near_refs, refs = refs[: len(start)], refs[len(start) :]
        extra_refs, out_refs, (field, window) = refs[: len(extra)], refs[len(extra) : -2], refs[-2:]
        window[:per] = far_ref[...].reshape(per, tile, LANES)
        window[per] = jnp.zeros((tile, LANES), BF16)
        if start:
            field[:per] = near_refs[0][...].reshape(per, tile, LANES)
        else:
            field[:per] = jnp.zeros((per, tile, LANES), F32)
        add_pairs(1, list_ref, tiles_ref, field, window, pairs)
        work(field[:per].reshape(cells, LANES), extra_refs, out_refs)

    return call(
        body,
        [(lists, pltpu.SMEM)] + vmem(tiles, far, *start, *extra),
        [(*out, pltpu.VMEM) for out in outs_of],
        [
            pltpu.VMEM((per + 1, tile, LANES), F32),
            pltpu.VMEM((per + 1, tile, LANES), BF16),
        ],
        name,
    )


def bases(xs, ys, same, step, channels, after, name):
    cells = xs[0].shape[0]
    groups = same.shape[0] // LANES

    def body(*refs):
        x_refs, y_refs = refs[: len(xs)], refs[len(xs) : 2 * len(xs)]
        if len(xs) == 1:
            x, y = [[r[0][:, lanes(g)] for g in range(groups)] for r in (x_refs, y_refs)]
        else:
            x, y = [[r[...] for r in refs_of] for refs_of in (x_refs, y_refs)]
        bases_into(refs[2 * len(xs) + 2 :], x, y, refs[2 * len(xs)], step, channels)

    return call(
        body,
        vmem(*xs, *ys, same, after),
        [((cells, LANES), F32, pltpu.VMEM)] * groups,
        [],
        name,
    )


def assemble(xs, ys):
    groups = len(xs)
    cells = xs[0].shape[0]
    width = groups * LANES

    def body(*refs):
        outs, sems = refs[2 * groups : -1], refs[-1]
        copies = [
            pltpu.make_async_copy(
                refs[k * groups + g], outs[k].at[:, lanes(g)], sems.at[k * groups + g]
            )
            for g in range(groups)
            for k in range(2)
        ]
        for copy in copies:
            copy.start()
        for copy in copies:
            copy.wait()

    return call(
        body,
        vmem(*xs, *ys),
        [((cells, width), F32, pltpu.HBM)] * 2,
        [pltpu.SemaphoreType.DMA((2 * groups,))],
        "assemble",
    )


def local(positions, momenta, tile_values, tile_rows, tile_cols, tile_count, channel_coupling):
    cells, width = positions.shape
    slots, tile, _ = tile_values.shape
    channels = channel_coupling.shape[0]
    replicas = width // channels
    groups = width // LANES
    ring = lax.axis_size("row") * lax.axis_size("col")
    where = np.arange(width)
    same = jnp.asarray((where[:, None] // channels == where[None] // channels).astype(ml_dtypes.bfloat16))
    spread = jnp.asarray((where[:, None] % channels == np.arange(channels)[None]).astype(ml_dtypes.bfloat16))
    on_chip = [(i, i ^ 1) for i in range(ring)]
    off_chip = [(i, (i + 1) % ring if i % 2 else (i - 1) % ring) for i in range(ring)]
    wide = (cells, LANES)

    def ring_index():
        return lax.axis_index("row") * lax.axis_size("col") + lax.axis_index("col")

    def far_swap(mine):
        return lax.ppermute(mine, RING, off_chip)

    def near_swap(mine):
        return lax.ppermute(mine, RING, on_chip)

    ready = {g: [] for g in range(groups)}
    for g in range(groups):
        ready[max(max(spanned(g, channels, width)), 1)].append(g)

    def keep(field, _, outs):
        outs[0][...] = field

    owns = [round_first(positions)]
    far = {0: far_swap(owns[0])}
    owns += round_rest(positions, owns[0])
    others = [near_swap(r) for r in owns]
    lists, mixing, sent = make_lists(
        tile_rows, tile_cols, tile_count, (same, spread, channel_coupling), owns[1], slots, tile, cells, ring_index
    )
    far[1] = far_swap(sent)
    (part,) = far_fields(lists, tile_values, None, far[0], [], [(wide, F32)], keep, "far_first_0")
    near, sent = near_fields(lists, tile_values, owns, others, part, owns[2:], "near_first")
    for g in range(2, groups):
        far[g] = far_swap(sent[g - 2])
    base = bases([positions], [momenta], same, 0, channels, near[-1], "base_first")

    fields, xs, ys, rounded, new_far = {0: near[0]}, {}, {}, {}, {}
    for g in range(1, groups):
        todo = ready[g]
        known = sorted({n for t in todo for n in spanned(t, channels, width)} - {g})

        def work(field, ins, outs, g=g, todo=todo, known=known):
            own = field.astype(BF16)
            outs[0][...] = own
            held = {n: ins[1 + i][...] for i, n in enumerate(known)}
            held[g] = own
            x_ref, base_refs = ins[1 + len(known)], ins[2 + len(known) :]
            for i, t in enumerate(todo):
                y_new = base_refs[i][...] - 0.2 * mixed_of(held, ins[0], t, channels)
                x_new = jnp.clip(x_ref[:, lanes(t)] + 0.5 * y_new, -1.0, 1.0)
                outs[1 + 3 * i][...] = x_new
                outs[2 + 3 * i][...] = y_new
                outs[3 + 3 * i][...] = x_new.astype(BF16)

        fields[g], *results = far_fields(
            lists,
            tile_values,
            near[g],
            far[g],
            [mixing] + [fields[n] for n in known] + [positions] + [base[t] for t in todo],
            [(wide, BF16)] + [(wide, F32), (wide, F32), (wide, BF16)] * len(todo),
            work,
            f"far_first_{g}",
        )
        for i, t in enumerate(todo):
            xs[t], ys[t], rounded[t] = results[3 * i : 3 * i + 3]
            if t < 2:
                new_far[t] = far_swap(rounded[t])

    owns = [rounded[g] for g in range(groups)]
    others = [near_swap(r) for r in owns]
    (part,) = far_fields(
        lists, tile_values, None, new_far[0], [], [(wide, F32)], keep, "far_second_0"
    )
    near, sent = near_fields(lists, tile_values, owns, others, part, owns[2:], "near_second")
    for g in range(2, groups):
        new_far[g] = far_swap(sent[g - 2])
    base = bases(
        [xs[g] for g in range(groups)],
        [ys[g] for g in range(groups)],
        same,
        1,
        channels,
        near[-1],
        "base_second",
    )
    fields, last_x, last_y, energies = {0: near[0]}, {}, {}, {}
    for g in range(1, groups):
        todo = ready[g]
        known = sorted({n for t in todo for n in spanned(t, channels, width)} - {g})
        done = sorted(energies)
        last = g == groups - 1

        def work(field, ins, outs, g=g, todo=todo, known=known, done=done, last=last):
            own = field.astype(BF16)
            held = {n: ins[1 + i][...] for i, n in enumerate(known)}
            held[g] = own
            ins_of = ins[1 + len(known) :]
            sums = {}
            for i, t in enumerate(todo):
                base_ref, x_ref, rounded_ref = ins_of[3 * i : 3 * i + 3]
                mixed = mixed_of(held, ins[0], t, channels)
                y_new = base_ref[...] - 0.2 * mixed
                outs[1 + 3 * i][...] = jnp.clip(x_ref[...] + 0.5 * y_new, -1.0, 1.0)
                outs[2 + 3 * i][...] = y_new
                sums[t] = jnp.sum(rounded_ref[...].astype(F32) * mixed, axis=0, keepdims=True)
                outs[3 + 3 * i][...] = sums[t]
            if not last:
                outs[0][...] = own
                return
            for t, ref in zip(done, ins_of[3 * len(todo) :]):
                sums[t] = ref[...]
            row = jnp.concatenate([sums[t] for t in range(groups)], axis=1)
            lane = lax.broadcasted_iota(jnp.int32, (1, width), 1)
            place = lax.broadcasted_iota(jnp.int32, (1, LANES), 1)
            total = jnp.zeros((1, LANES), F32)
            for r in range(replicas):
                inside = (lane >= r * channels) & (lane < (r + 1) * channels)
                value = jnp.sum(jnp.where(inside, row, 0.0), axis=1, keepdims=True)
                total = jnp.where(place == r, value, total)
            outs[0][...] = jnp.broadcast_to(total, (ring, LANES))

        first, *results = far_fields(
            lists,
            tile_values,
            near[g],
            new_far[g],
            [mixing]
            + [fields[n] for n in known]
            + [a for t in todo for a in (base[t], xs[t], rounded[t])]
            + ([energies[t] for t in done] if last else []),
            [((ring, LANES), F32) if last else (wide, BF16)]
            + [(wide, F32), (wide, F32), ((1, LANES), F32)] * len(todo),
            work,
            f"far_second_{g}",
        )
        if last:
            partial = first
        else:
            fields[g] = first
        for i, t in enumerate(todo):
            last_x[t], last_y[t], energies[t] = results[3 * i : 3 * i + 3]

    everyone = lax.all_to_all(partial, RING, 0, 0, tiled=True)
    energy = jnp.sum(everyone, axis=0)[:replicas] / jnp.sqrt(jnp.float32(cells * ring * channels))
    x_new, y_new = assemble(
        [last_x[g] for g in range(groups)], [last_y[g] for g in range(groups)]
    )
    return (x_new, y_new, energy)


def solution(mesh):
    cells = P(("groups", "row", "col"), None)
    slots = P(("groups", "row", "col"))
    return jax.shard_map(
        local,
        mesh=mesh,
        in_specs=(cells, cells, P(("groups", "row", "col"), None, None), slots, slots, slots, P()),
        out_specs=(cells, cells, P("groups")),
        check_vma=False,
    )
```

profile of v0, /device:TPU:0, one launch (start us, length us, event | category | flops | bytes accessed | tf_op | source)
XLA Modules:
  0.0 57.9 jit_solution(1933499718154925904)
XLA Ops:
  0.6 1.2 %round_first.1._.refs_0_ = bf16[1024,128]{1,0:T(8,128)(2,1)S(1)} custom-call(f32[1024,384]{1,0:T(8,128)} %refs_4_.1), custom_call_target="tpu_custom_call" | custom-call | tf_op jit(solution)/shard_map/round_first/pallas_call | solution.py:26
  1.9 5.5 %collective-permute-start.3 = (bf16[1024,128]{1,0:T(8,128)(2,1)S(1)}, bf16[1024,128]{1,0:T(8,128)(2,1)S(1)}, u32[]{:S(2)}, u32[]{:S(2)}) collective-permute-start(bf16[1024,128]{1,0:T(8,128)(2,1)S(1)} %round_first.1._.refs_0_), channel_id=1, source_target_pairs={{0,15},{1,2},{2,1},{3,4},{4,3},{5,6},{6,5},{7,8},{8,7},{9,10},{10,... | collective-permute-start | bytes 786440 | tf_op jit(solution)/shard_map/ppermute | solution.py:362
  7.4 1.4 %copy-done.1 = f32[1024,384]{1,0:T(8,128)S(1)} copy-done((f32[1024,384]{1,0:T(8,128)S(1)}, f32[1024,384]{1,0:T(8,128)}, u32[]{:S(2)}) %copy-start.1) | copy-done | bytes 1572888
  8.8 0.1 round_rest.1
  8.9 0.1 collective-permute-start.1
  9.0 0.5 collective-permute-start.2
  9.5 0.1 collective-permute-start
  10.2 1.4 %make_lists.1 = (s32[214]{0:T(256)S(4)}, bf16[384,384]{1,0:T(8,128)(2,1)S(1)}, bf16[1024,128]{1,0:T(8,128)(2,1)S(1)}) custom-call(s32[96]{0:T(128)S(1)} %copy-done.7, s32[96]{0:T(128)S(1)} %copy-done.8, s32[1]{0:T(128)S(6)} %copy.13.count_ref, bf16[384,384]{1,0:T(8,128)(2,1)S(1)} %copy-done.3, bf16[384,48]{1,0:T(8,128)(2,1)S(1)} %copy-done.5, ...), custom_call_target="tpu_custom_call" | custom-call | tf_op jit(solution)/shard_map/make_lists/pallas_call | solution.py:26
  11.7 1.5 %collective-permute-start.5 = (bf16[1024,128]{1,0:T(8,128)(2,1)S(1)}, bf16[1024,128]{1,0:T(8,128)(2,1)S(1)}, u32[]{:S(2)}, u32[]{:S(2)}) collective-permute-start(bf16[1024,128]{1,0:T(8,128)(2,1)S(1)} %get-tuple-element.50), channel_id=1, source_target_pairs={{0,15},{1,2},{2,1},{3,4},{4,3},{5,6},{6,5},{7,8},{8,7},{9,10},{10,... | collective-permute-start | bytes 786440 | tf_op jit(solution)/shard_map/ppermute | solution.py:362
  13.2 0.3 far_first_0.1.refs_6_
  13.6 1.4 %near_first.1 = (bf16[1024,128]{1,0:T(8,128)(2,1)S(1)}, f32[1024,128]{1,0:T(8,128)S(1)}, f32[1024,128]{1,0:T(8,128)S(1)}, bf16[1024,128]{1,0:T(8,128)(2,1)S(1)}) custom-call(s32[214]{0:T(256)S(4)} %get-tuple-element.44.list_ref, bf16[96,128,128]{2,1,0:T(8,128)(2,1)S(1)} %copy-done, bf16[1024,128]{1,0:T(8,128)(2,1)S(1)} %round_first.1._.refs_0_, ...), custom_call_target="tpu_custom_call" | custom-call | tf_op jit(solution)/shard_map/near_first/pallas_call | solution.py:26
  15.0 4.2 %collective-permute-start.4 = (bf16[1024,128]{1,0:T(8,128)(2,1)S(1)}, bf16[1024,128]{1,0:T(8,128)(2,1)S(1)}, u32[]{:S(2)}, u32[]{:S(2)}) collective-permute-start(bf16[1024,128]{1,0:T(8,128)(2,1)S(1)} %get-tuple-element.46), channel_id=1, source_target_pairs={{0,15},{1,2},{2,1},{3,4},{4,3},{5,6},{6,5},{7,8},{8,7},{9,10},{10,... | collective-permute-start | bytes 786440 | tf_op jit(solution)/shard_map/ppermute | solution.py:362
  19.2 1.1 %base_first.1 = (f32[1024,128]{1,0:T(8,128)S(1)}, f32[1024,128]{1,0:T(8,128)S(1)}, f32[1024,128]{1,0:T(8,128)S(1)}) custom-call(f32[1024,384]{1,0:T(8,128)S(1)} %copy-done.2, f32[1024,384]{1,0:T(8,128)S(1)} %copy-done.4, bf16[384,384]{1,0:T(8,128)(2,1)S(1)} %copy-done.3, f32[1024,128]{1,0:T(8,128)S(1)} %get-tuple-element.47.refs_3_.refs_0_), custom_call_target="tpu_custom_call" | custom-call | tf_op jit(solution)/shard_map/base_first/pallas_call | solution.py:26
  20.3 0.6 %far_first_1.1 = (bf16[1024,128]{1,0:T(8,128)(2,1)S(1)}, f32[1024,128]{1,0:T(8,128)S(1)}, f32[1024,128]{1,0:T(8,128)S(1)}, bf16[1024,128]{1,0:T(8,128)(2,1)S(1)}) custom-call(s32[214]{0:T(256)S(4)} %get-tuple-element.44.list_ref, bf16[96,128,128]{2,1,0:T(8,128)(2,1)S(1)} %copy-done, bf16[1024,128]{1,0:T(8,128)(2,1)S(1)} %collective-permute-done.5.far_ref, ...), custom_call_target="tpu_custom_call" | custom-call | tf_op jit(solution)/shard_map/far_first_1/pallas_call | solution.py:26
  20.9 1.9 %collective-permute-start.10 = (bf16[1024,128]{1,0:T(8,128)(2,1)S(1)}, bf16[1024,128]{1,0:T(8,128)(2,1)S(1)}, u32[]{:S(2)}, u32[]{:S(2)}) collective-permute-start(bf16[1024,128]{1,0:T(8,128)(2,1)S(1)} %get-tuple-element.57.refs_0_.refs_5_), channel_id=1, source_target_pairs={{0,15},{1,2},{2,1},{3,4},{4,3},{5,6},{6,5},{7,8},{8,7},{9,10},{10,... | collective-permute-start | bytes 786440 | tf_op jit(solution)/shard_map/ppermute | solution.py:362
  22.9 5.6 %collective-permute-start.7 = (bf16[1024,128]{1,0:T(8,128)(2,1)S(1)}, bf16[1024,128]{1,0:T(8,128)(2,1)S(1)}, u32[]{:S(2)}, u32[]{:S(2)}) collective-permute-start(bf16[1024,128]{1,0:T(8,128)(2,1)S(1)} %get-tuple-element.57.refs_0_.refs_5_), channel_id=1, source_target_pairs={{0,1},{1,0},{2,3},{3,2},{4,5},{5,4},{6,7},{7,6},{8,9},{9,8},{10,11... | collective-permute-start | bytes 786440 | tf_op jit(solution)/shard_map/ppermute | solution.py:365
  28.5 1.1 %far_first_2.1 = (bf16[1024,128]{1,0:T(8,128)(2,1)}, f32[1024,128]{1,0:T(8,128)S(1)}, f32[1024,128]{1,0:T(8,128)S(1)}, bf16[1024,128]{1,0:T(8,128)(2,1)S(1)}, f3...) custom-call(s32[214]{0:T(256)S(4)} %get-tuple-element.44.list_ref, ...), custom_call_target="tpu_custom_call" | custom-call | tf_op jit(solution)/shard_map/far_first_2/pallas_call | solution.py:26
  29.7 1.9 %collective-permute-start.8 = (bf16[1024,128]{1,0:T(8,128)(2,1)S(1)}, bf16[1024,128]{1,0:T(8,128)(2,1)S(1)}, u32[]{:S(2)}, u32[]{:S(2)}) collective-permute-start(bf16[1024,128]{1,0:T(8,128)(2,1)S(1)} %get-tuple-element.56.refs_1_.refs_6_), channel_id=1, source_target_pairs={{0,1},{1,0},{2,3},{3,2},{4,5},{5,4},{6,7},{7,6},{8,9},{9,8},{10,11... | collective-permute-start | bytes 786440 | tf_op jit(solution)/shard_map/ppermute | solution.py:365
  31.6 0.9 %collective-permute-start.6 = (bf16[1024,128]{1,0:T(8,128)(2,1)S(1)}, bf16[1024,128]{1,0:T(8,128)(2,1)S(1)}, u32[]{:S(2)}, u32[]{:S(2)}) collective-permute-start(bf16[1024,128]{1,0:T(8,128)(2,1)S(1)} %get-tuple-element.56.refs_1_.refs_6_), channel_id=1, source_target_pairs={{0,15},{1,2},{2,1},{3,4},{4,3},{5,6},{6,5},{7,8},{8,7},{9,10},{10,... | collective-permute-start | bytes 786440 | tf_op jit(solution)/shard_map/ppermute | solution.py:362
  32.5 0.3 far_second_0.1.refs_6_
  32.8 0.2 collective-permute-done.9.refs_5_
  33.1 1.4 %near_second.1 = (bf16[1024,128]{1,0:T(8,128)(2,1)S(1)}, f32[1024,128]{1,0:T(8,128)S(1)}, f32[1024,128]{1,0:T(8,128)S(1)}, bf16[1024,128]{1,0:T(8,128)(2,1)S(1)}) custom-call(s32[214]{0:T(256)S(4)} %get-tuple-element.44.list_ref, bf16[96,128,128]{2,1,0:T(8,128)(2,1)S(1)} %copy-done, bf16[1024,128]{1,0:T(8,128)(2,1)S(1)} %get-tuple-element.57.refs_0_.refs_5_, ...), custom_call_target="tpu_custom_call" | custom-call | tf_op jit(solution)/shard_map/near_second/pallas_call | solution.py:26
  34.5 4.5 %collective-permute-start.11 = (bf16[1024,128]{1,0:T(8,128)(2,1)S(1)}, bf16[1024,128]{1,0:T(8,128)(2,1)S(1)}, u32[]{:S(2)}, u32[]{:S(2)}) collective-permute-start(bf16[1024,128]{1,0:T(8,128)(2,1)S(1)} %get-tuple-element.70), channel_id=1, source_target_pairs={{0,15},{1,2},{2,1},{3,4},{4,3},{5,6},{6,5},{7,8},{8,7},{9,10},{10,... | collective-permute-start | bytes 786440 | tf_op jit(solution)/shard_map/ppermute | solution.py:362
  39.0 1.1 %base_second.1 = (f32[1024,128]{1,0:T(8,128)S(1)}, f32[1024,128]{1,0:T(8,128)S(1)}, f32[1024,128]{1,0:T(8,128)S(1)}) custom-call(f32[1024,128]{1,0:T(8,128)S(1)} %get-tuple-element.61.refs_0_.refs_4_, f32[1024,128]{1,0:T(8,128)S(1)} %get-tuple-element.62.refs_1_.refs_5_, f32[1024,128]{1,0:T(8,128)S(1)} %get-tuple-element.63.refs_2_.refs_8_, ...), custom_call_target="tpu_custom_call" | custom-call | tf_op jit(solution)/shard_map/base_second/pallas_call | solution.py:26
  40.1 0.0 collective-permute-done.6.far_ref
  40.2 0.7 %far_second_1.1 = (bf16[1024,128]{1,0:T(8,128)(2,1)S(1)}, f32[1024,128]{1,0:T(8,128)S(1)}, f32[1024,128]{1,0:T(8,128)S(1)}, f32[1,128]{1,0:T(1,128)S(1)}) custom-call(s32[214]{0:T(256)S(4)} %get-tuple-element.44.list_ref, bf16[96,128,128]{2,1,0:T(8,128)(2,1)S(1)} %copy-done, bf16[1024,128]{1,0:T(8,128)(2,1)S(1)} %collective-permute-done.6.far_ref, ...), custom_call_target="tpu_custom_call" | custom-call | tf_op jit(solution)/shard_map/far_second_1/pallas_call | solution.py:26
  40.8 2.3 %collective-permute-done.11.far_ref = bf16[1024,128]{1,0:T(8,128)(2,1)S(1)} collective-permute-done((bf16[1024,128]{1,0:T(8,128)(2,1)S(1)}, bf16[1024,128]{1,0:T(8,128)(2,1)S(1)}, u32[]{:S(2)}, u32[]{:S(2)}) %collective-permute-start.11) | collective-permute-done | bytes 262176 | tf_op jit(solution)/shard_map/ppermute | solution.py:362
  43.1 1.6 %far_second_2.1 = (f32[16,128]{1,0:T(8,128)}, f32[1024,128]{1,0:T(8,128)S(1)}, f32[1024,128]{1,0:T(8,128)S(1)}, f32[1,128]{1,0:T(1,128)}, f32[1024,128]{1,0:T(8,...) custom-call(s32[214]{0:T(256)S(4)} %get-tuple-element.44.list_ref, bf16[96,128,128]{2,1,0:T(8,128)(2,1)S(1)} %copy-done, ...), custom_call_target="tpu_custom_call" | custom-call | tf_op jit(solution)/shard_map/far_second_2/pallas_call | solution.py:26
  44.7 6.2 %all-to-all-start = ((f32[16,1,128]{2,1,0:T(1,128)}), f32[16,1,128]{2,1,0:T(1,128)S(1)}, u32[]{:S(2)}, u32[]{:S(2)}) async-start(f32[16,1,128]{2,1,0:T(1,128)} %bitcast.1), calls=%async_computation | async-start | bytes 16384 | tf_op jit(solution)/shard_map/all_to_all | solution.py:495
  50.9 1.7 %assemble.1 = (f32[1024,384]{1,0:T(8,128)}, f32[1024,384]{1,0:T(8,128)}) custom-call(f32[1024,128]{1,0:T(8,128)S(1)} %get-tuple-element.69.refs_0_, f32[1024,128]{1,0:T(8,128)S(1)} %get-tuple-element.75.refs_1_, f32[1024,128]{1,0:T(8,128)S(1)} %get-tuple-element.76.refs_2_, f32[1024,128]{1,0:T(8,128)S(1)} %get-tuple-element.77.refs_3_, ...), custom_call_target="tpu_custom_call" | custom-call | tf_op jit(solution)/shard_map/assemble/pallas_call | solution.py:26
  52.6 4.7 %all-to-all-done = f32[16,1,128]{2,1,0:T(1,128)S(1)} async-done(((f32[16,1,128]{2,1,0:T(1,128)}), f32[16,1,128]{2,1,0:T(1,128)S(1)}, u32[]{:S(2)}, u32[]{:S(2)}) %all-to-all-start) | async-done | bytes 8224 | tf_op jit(solution)/shard_map/all_to_all | solution.py:495
  57.3 0.5 slice_multiply_fusion
  (28 shorter events, 0.1 us)
Async XLA Ops:
  0.6 12.6 %copy-start = (bf16[96,128,128]{2,1,0:T(8,128)(2,1)S(1)}, bf16[96,128,128]{2,1,0:T(8,128)(2,1)}, u32[]{:S(2)}) copy-start(bf16[96,128,128]{2,1,0:T(8,128)(2,1)} %tiles_ref.15) | copy-start | bytes 9437188
  1.9 11.3 %collective-permute-start.3 = (bf16[1024,128]{1,0:T(8,128)(2,1)S(1)}, bf16[1024,128]{1,0:T(8,128)(2,1)S(1)}, u32[]{:S(2)}, u32[]{:S(2)}) collective-permute-start(bf16[1024,128]{1,0:T(8,128)(2,1)S(1)} %round_first.1._.refs_0_), channel_id=1, source_target_pairs={{0,15},{1,2},{2,1},{3,4},{4,3},{5,6},{6,5},{7,8},{8,7},{9,10},{10,... | collective-permute-start | bytes 786440 | tf_op jit(solution)/shard_map/ppermute | solution.py:362
  7.4 1.4 %copy-start.1 = (f32[1024,384]{1,0:T(8,128)S(1)}, f32[1024,384]{1,0:T(8,128)}, u32[]{:S(2)}) copy-start(f32[1024,384]{1,0:T(8,128)} %refs_4_.1) | copy-start | bytes 4718596
  8.8 1.4 %copy-start.3 = (bf16[384,384]{1,0:T(8,128)(2,1)S(1)}, bf16[384,384]{1,0:T(8,128)(2,1)}, u32[]{:S(2)}) copy-start(bf16[384,384]{1,0:T(8,128)(2,1)} %constant.9.clone.same_ref.refs_2_.refs_6_) | copy-start | bytes 884740
  8.8 1.4 %copy-start.5 = (bf16[384,48]{1,0:T(8,128)(2,1)S(1)}, bf16[384,48]{1,0:T(8,128)(2,1)}, u32[]{:S(2)}) copy-start(bf16[384,48]{1,0:T(8,128)(2,1)} %constant.10.clone.spread_ref) | copy-start | bytes 110596
  8.8 1.4 %copy-start.6 = (bf16[48,48]{1,0:T(8,128)(2,1)S(1)}, bf16[48,48]{1,0:T(8,128)(2,1)}, u32[]{:S(2)}) copy-start(bf16[48,48]{1,0:T(8,128)(2,1)} %coupling_ref.1) | copy-start | bytes 13828
  8.8 1.4 %copy-start.7 = (s32[96]{0:T(128)S(1)}, s32[96]{0:T(128)}, u32[]{:S(2)}) copy-start(s32[96]{0:T(128)} %rows_ref.1) | copy-start | bytes 1156
  8.8 1.4 %copy-start.8 = (s32[96]{0:T(128)S(1)}, s32[96]{0:T(128)}, u32[]{:S(2)}) copy-start(s32[96]{0:T(128)} %cols_ref.1) | copy-start | bytes 1156
  8.9 4.7 %collective-permute-start.1 = (bf16[1024,128]{1,0:T(8,128)(2,1)S(1)}, bf16[1024,128]{1,0:T(8,128)(2,1)S(1)}, u32[]{:S(2)}, u32[]{:S(2)}) collective-permute-start(bf16[1024,128]{1,0:T(8,128)(2,1)S(1)} %get-tuple-element.43.sent_ref.refs_1_), channel_id=1, source_target_pairs={{0,1},{1,0},{2,3},{3,2},{4,5},{5,4},{6,7},{7,6},{8,9},{9,8},{10,11... | collective-permute-start | bytes 786440 | tf_op jit(solution)/shard_map/ppermute | solution.py:365
  9.0 4.6 %collective-permute-start.2 = (bf16[1024,128]{1,0:T(8,128)(2,1)S(1)}, bf16[1024,128]{1,0:T(8,128)(2,1)S(1)}, u32[]{:S(2)}, u32[]{:S(2)}) collective-permute-start(bf16[1024,128]{1,0:T(8,128)(2,1)S(1)} %get-tuple-element.45.refs_2_.refs_7_), channel_id=1, source_target_pairs={{0,1},{1,0},{2,3},{3,2},{4,5},{5,4},{6,7},{7,6},{8,9},{9,8},{10,11... | collective-permute-start | bytes 786440 | tf_op jit(solution)/shard_map/ppermute | solution.py:365
  9.5 4.1 %collective-permute-start = (bf16[1024,128]{1,0:T(8,128)(2,1)S(1)}, bf16[1024,128]{1,0:T(8,128)(2,1)S(1)}, u32[]{:S(2)}, u32[]{:S(2)}) collective-permute-start(bf16[1024,128]{1,0:T(8,128)(2,1)S(1)} %round_first.1._.refs_0_), channel_id=1, source_target_pairs={{0,1},{1,0},{2,3},{3,2},{4,5},{5,4},{6,7},{7,6},{8,9},{9,8},{10,11... | collective-permute-start | bytes 786440 | tf_op jit(solution)/shard_map/ppermute | solution.py:365
  11.7 8.7 %collective-permute-start.5 = (bf16[1024,128]{1,0:T(8,128)(2,1)S(1)}, bf16[1024,128]{1,0:T(8,128)(2,1)S(1)}, u32[]{:S(2)}, u32[]{:S(2)}) collective-permute-start(bf16[1024,128]{1,0:T(8,128)(2,1)S(1)} %get-tuple-element.50), channel_id=1, source_target_pairs={{0,15},{1,2},{2,1},{3,4},{4,3},{5,6},{6,5},{7,8},{8,7},{9,10},{10,... | collective-permute-start | bytes 786440 | tf_op jit(solution)/shard_map/ppermute | solution.py:362
  13.5 5.7 %copy-start.2 = (f32[1024,384]{1,0:T(8,128)S(1)}, f32[1024,384]{1,0:T(8,128)}, u32[]{:S(2)}) copy-start(f32[1024,384]{1,0:T(8,128)} %refs_4_.1) | copy-start | bytes 4718596
  13.5 5.6 %copy-start.4 = (f32[1024,384]{1,0:T(8,128)S(1)}, f32[1024,384]{1,0:T(8,128)}, u32[]{:S(2)}) copy-start(f32[1024,384]{1,0:T(8,128)} %refs_1_.1) | copy-start | bytes 4718596
  15.0 13.5 %collective-permute-start.4 = (bf16[1024,128]{1,0:T(8,128)(2,1)S(1)}, bf16[1024,128]{1,0:T(8,128)(2,1)S(1)}, u32[]{:S(2)}, u32[]{:S(2)}) collective-permute-start(bf16[1024,128]{1,0:T(8,128)(2,1)S(1)} %get-tuple-element.46), channel_id=1, source_target_pairs={{0,15},{1,2},{2,1},{3,4},{4,3},{5,6},{6,5},{7,8},{8,7},{9,10},{10,... | collective-permute-start | bytes 786440 | tf_op jit(solution)/shard_map/ppermute | solution.py:362
  20.9 11.5 %collective-permute-start.10 = (bf16[1024,128]{1,0:T(8,128)(2,1)S(1)}, bf16[1024,128]{1,0:T(8,128)(2,1)S(1)}, u32[]{:S(2)}, u32[]{:S(2)}) collective-permute-start(bf16[1024,128]{1,0:T(8,128)(2,1)S(1)} %get-tuple-element.57.refs_0_.refs_5_), channel_id=1, source_target_pairs={{0,15},{1,2},{2,1},{3,4},{4,3},{5,6},{6,5},{7,8},{8,7},{9,10},{10,... | collective-permute-start | bytes 786440 | tf_op jit(solution)/shard_map/ppermute | solution.py:362
  22.9 9.9 %collective-permute-start.7 = (bf16[1024,128]{1,0:T(8,128)(2,1)S(1)}, bf16[1024,128]{1,0:T(8,128)(2,1)S(1)}, u32[]{:S(2)}, u32[]{:S(2)}) collective-permute-start(bf16[1024,128]{1,0:T(8,128)(2,1)S(1)} %get-tuple-element.57.refs_0_.refs_5_), channel_id=1, source_target_pairs={{0,1},{1,0},{2,3},{3,2},{4,5},{5,4},{6,7},{7,6},{8,9},{9,8},{10,11... | collective-permute-start | bytes 786440 | tf_op jit(solution)/shard_map/ppermute | solution.py:365
  29.7 3.2 %collective-permute-start.8 = (bf16[1024,128]{1,0:T(8,128)(2,1)S(1)}, bf16[1024,128]{1,0:T(8,128)(2,1)S(1)}, u32[]{:S(2)}, u32[]{:S(2)}) collective-permute-start(bf16[1024,128]{1,0:T(8,128)(2,1)S(1)} %get-tuple-element.56.refs_1_.refs_6_), channel_id=1, source_target_pairs={{0,1},{1,0},{2,3},{3,2},{4,5},{5,4},{6,7},{7,6},{8,9},{9,8},{10,11... | collective-permute-start | bytes 786440 | tf_op jit(solution)/shard_map/ppermute | solution.py:365
  31.5 1.5 %collective-permute-start.9 = (bf16[1024,128]{1,0:T(8,128)(2,1)S(1)}, bf16[1024,128]{1,0:T(8,128)(2,1)S(1)}, u32[]{:S(2)}, u32[]{:S(2)}) collective-permute-start(bf16[1024,128]{1,0:T(8,128)(2,1)S(1)} %get-tuple-element.58.refs_2_.refs_7_.refs_9_), channel_id=1, source_target_pairs={{0,1},{1,0},{2,3},{3,2},{4,5},{5,4},{6,7},{7,6},{8,9},{9,8},{10,11... | collective-permute-start | bytes 786440 | tf_op jit(solution)/shard_map/ppermute | solution.py:365
  31.6 8.6 %collective-permute-start.6 = (bf16[1024,128]{1,0:T(8,128)(2,1)S(1)}, bf16[1024,128]{1,0:T(8,128)(2,1)S(1)}, u32[]{:S(2)}, u32[]{:S(2)}) collective-permute-start(bf16[1024,128]{1,0:T(8,128)(2,1)S(1)} %get-tuple-element.56.refs_1_.refs_6_), channel_id=1, source_target_pairs={{0,15},{1,2},{2,1},{3,4},{4,3},{5,6},{6,5},{7,8},{8,7},{9,10},{10,... | collective-permute-start | bytes 786440 | tf_op jit(solution)/shard_map/ppermute | solution.py:362
  34.5 8.6 %collective-permute-start.11 = (bf16[1024,128]{1,0:T(8,128)(2,1)S(1)}, bf16[1024,128]{1,0:T(8,128)(2,1)S(1)}, u32[]{:S(2)}, u32[]{:S(2)}) collective-permute-start(bf16[1024,128]{1,0:T(8,128)(2,1)S(1)} %get-tuple-element.70), channel_id=1, source_target_pairs={{0,15},{1,2},{2,1},{3,4},{4,3},{5,6},{6,5},{7,8},{8,7},{9,10},{10,... | collective-permute-start | bytes 786440 | tf_op jit(solution)/shard_map/ppermute | solution.py:362
  44.7 12.6 %all-to-all-start = ((f32[16,1,128]{2,1,0:T(1,128)}), f32[16,1,128]{2,1,0:T(1,128)S(1)}, u32[]{:S(2)}, u32[]{:S(2)}) async-start(f32[16,1,128]{2,1,0:T(1,128)} %bitcast.1), calls=%async_computation | async-start | bytes 16384 | tf_op jit(solution)/shard_map/all_to_all | solution.py:495
where the time goes:
time: 57.8 us; the launch traced here: 57.9 us
  starting transfers between devices  33 us (57%)
  Pallas kernels  14.1 us (24%)
  waiting for transfers between devices  7.25 us (13%)
  between operations  1.51 us (3%)
  local copies, waits for them, and re-layouts  1.45 us (3%)
    ppermute x6, starting transfers between devices, far_swap(): return lax.ppermute(mine, RING, off_chip)  18.6 us
    pallas_call x14, Pallas kernels, call(): pl.pallas_call(body, in_specs=[pl.BlockSpec(memory_space=pl.ANY if s is p...  14.1 us
    ppermute x6, starting transfers between devices, near_swap(): return lax.ppermute(mine, RING, on_chip)  8.15 us
    all_to_all x1, starting transfers between devices, local(): everyone = lax.all_to_all(partial, RING, 0, 0, tiled=True)  6.21 us
    all_to_all x1, waiting for transfers between devices, local(): everyone = lax.all_to_all(partial, RING, 0, 0, tiled=True)  4.69 us
    ppermute x6, waiting for transfers between devices, far_swap(): return lax.ppermute(mine, RING, off_chip)  2.3 us
    unnamed x18, local copies, waits for them, and re-layouts  1.45 us
  transfers between devices with their start and end apart: 13, of which 3 were waited for; matrix products, arithmetic and copies ran while one was open for 0% of the time, Pallas kernels for 20%

commit v1 on v0

v1 whole, which is shorter than its diff:
```python
import jax
import jax.numpy as jnp
import ml_dtypes
import numpy as np
from jax import lax
from jax.experimental import pallas as pl
from jax.experimental.pallas import tpu as pltpu
from jax.sharding import PartitionSpec as P

STEPS = 2
LANES = 128
LONG, SHORT = 16, 4
VMEM_LIMIT = 14 * 1024 * 1024
NEAR_FLOPS = 10**10
F32 = jnp.float32
BF16 = jnp.bfloat16
RING = ("row", "col")


def call(body, ins, outs, scratch, name, flops=0):
    return pl.pallas_call(
        body,
        in_specs=[pl.BlockSpec(memory_space=pl.ANY if s is pltpu.HBM else s) for _, s in ins],
        out_specs=[pl.BlockSpec(memory_space=pl.ANY if s is pltpu.HBM else s) for *_, s in outs],
        out_shape=[
            jax.ShapeDtypeStruct(dims, kind) if s is pltpu.HBM else s(dims, kind)
            for dims, kind, s in outs
        ],
        scratch_shapes=scratch,
        compiler_params=pltpu.CompilerParams(vmem_limit_bytes=VMEM_LIMIT),
        cost_estimate=pl.CostEstimate(
            flops=int(flops) or 1000, bytes_accessed=1000, transcendentals=0
        ),
        name=name,
    )(*[pltpu.with_memory_space_constraint(a, s) for a, s in ins])


def vmem(*arrays):
    return [(a, pltpu.VMEM) for a in arrays]


def lanes(group):
    return slice(group * LANES, (group + 1) * LANES)


def spanned(group, channels, width):
    first = group * LANES // channels * channels
    last = -(-(group + 1) * LANES // channels) * channels
    return list(range(first // LANES, -(-min(last, width) // LANES)))


def span_lanes(near):
    return slice(near[0] * LANES, (near[-1] + 1) * LANES)


def split(x):
    high = x.astype(BF16)
    return high, (x - high.astype(F32)).astype(BF16)


def bases_into(outs, xs, ys, same, step, channels):
    groups = len(xs)
    width = groups * LANES
    detune = 1.0 - (step + 1.0) / (STEPS + 1.0)
    parts = [split(x) for x in xs]
    for g in range(groups):
        near = spanned(g, channels, width)
        ones = same[span_lanes(near), lanes(g)]
        totals = sum(
            jnp.dot(
                jnp.concatenate([parts[n][k] for n in near], axis=1),
                ones,
                preferred_element_type=F32,
            )
            for k in range(2)
        )
        penalty = 0.02 * (totals - (2.0 - channels))
        outs[g][...] = ys[g] + 0.5 * (-detune * xs[g] - 0.4 * penalty)


def mixed_of(fields, mixing, group, channels):
    near = spanned(group, channels, mixing.shape[0])
    return jnp.dot(
        jnp.concatenate([fields[n] for n in near], axis=1),
        mixing[span_lanes(near), lanes(group)],
        preferred_element_type=F32,
    )


def load_first(positions, groups_of):
    cells = positions.shape[0]
    n = len(groups_of)

    def body(x_ref, *refs):
        x_outs, r_outs, sent, sems = refs[:n], refs[n : 2 * n], refs[2 * n], refs[-1]
        copies = [
            pltpu.make_async_copy(x_ref.at[:, lanes(g)], x_outs[i], sems.at[i])
            for i, g in enumerate(groups_of)
        ]
        for copy in copies:
            copy.start()
        for i, copy in enumerate(copies):
            copy.wait()
            rounded = x_outs[i][...].astype(BF16)
            r_outs[i][...] = rounded
            sent[:, lanes(i)] = rounded

    outs = call(
        body,
        [(positions, pltpu.HBM)],
        [((cells, LANES), F32, pltpu.VMEM)] * n
        + [((cells, LANES), BF16, pltpu.VMEM)] * n
        + [((cells, n * LANES), BF16, pltpu.VMEM)],
        [pltpu.SemaphoreType.DMA((n,))],
        "load_first",
    )
    return outs[:n], outs[n : 2 * n], outs[2 * n]


def section(slots, per):
    return -(-(slots + per) // (2 * SHORT)) * SHORT


def make_lists(rows, cols, count, positions, groups_of, after, slots, tile, ring_index):
    cells = positions.shape[0]
    per = cells // tile
    pairs = section(slots, per)
    n = len(groups_of)

    def body(rows_hbm, cols_hbm, count_hbm, x_ref, _, list_ref, *refs):
        x_outs, r_outs = refs[:n], refs[n : 2 * n]
        rows_ref, cols_ref, count_ref, held, sems = refs[2 * n :]
        copies = [
            pltpu.make_async_copy(*ends, sems.at[k])
            for k, ends in enumerate(
                [(rows_hbm, rows_ref), (cols_hbm, cols_ref), (count_hbm, count_ref)]
                + [(x_ref.at[:, lanes(g)], x_outs[i]) for i, g in enumerate(groups_of)]
            )
        ]
        for copy in copies:
            copy.start()
        for k in range(2 * per):
            held[k] = -1
        far_third = jnp.where(lax.rem(ring_index(), 2) == 1, 2, 0)
        for copy in copies[:3]:
            copy.wait()

        def visit(slot, totals):
            near_pairs, far_pairs = totals
            row, col = rows_ref[slot], cols_ref[slot]
            third = jnp.where(col >= 2 * per, 2, jnp.where(col >= per, 1, 0))
            source = col - third * per
            far = third == far_third
            source = jnp.where(far | (third == 1), source, source + per)
            key = row + jnp.where(far, per, 0)
            place = 2 * jnp.where(far, far_pairs + pairs, near_pairs)
            entry = slot * 65536 + source * 256 + row
            other = held[key]
            full = other >= 0
            list_ref[place] = other
            list_ref[place + 1] = entry
            held[key] = jnp.where(full, -1, entry)
            one = full.astype(jnp.int32)
            far_one = jnp.where(far, one, 0)
            return near_pairs + one - far_one, far_pairs + far_one

        totals = lax.fori_loop(0, count_ref[0], visit, (jnp.int32(0), jnp.int32(0)))
        for part, zero in enumerate((2 * per, per)):
            total = totals[part]
            start = part * pairs
            for k in range(per):
                other = held[part * per + k]
                list_ref[2 * (start + total)] = other
                list_ref[2 * (start + total) + 1] = zero * 256 + k
                total = total + (other >= 0).astype(jnp.int32)
            short_turns = (total + SHORT - 1) // SHORT

            def pad(pair, carry, start=start, zero=zero):
                for e in range(2):
                    list_ref[2 * (start + pair) + e] = zero * 256 + per
                return carry

            lax.fori_loop(total, short_turns * SHORT, pad, 0)
            list_ref[4 * pairs + 2 * part] = short_turns // (LONG // SHORT)
            list_ref[4 * pairs + 2 * part + 1] = short_turns % (LONG // SHORT)
        for i, copy in enumerate(copies[3:]):
            copy.wait()
            r_outs[i][...] = x_outs[i][...].astype(BF16)

    outs = call(
        body,
        [(a, pl.ANY) for a in (rows, cols, count)] + [(positions, pltpu.HBM)] + vmem(after),
        [((4 * pairs + 4 + 2,), jnp.int32, pltpu.SMEM)]
        + [((cells, LANES), F32, pltpu.VMEM)] * n
        + [((cells, LANES), BF16, pltpu.VMEM)] * n,
        [
            pltpu.SMEM(rows.shape, jnp.int32),
            pltpu.SMEM(cols.shape, jnp.int32),
            pltpu.SMEM(count.shape, jnp.int32),
            pltpu.SMEM((2 * per,), jnp.int32),
            pltpu.SemaphoreType.DMA((3 + n,)),
        ],
        "make_lists",
    )
    return outs[0], outs[1 : 1 + n], outs[1 + n :]


def add_pairs(part, list_ref, tiles, field, window, pairs):
    def turn(first, length):
        for u in range(length):
            place = 2 * (part * pairs + first + u)
            entries = [list_ref[place + e] for e in range(2)]
            left = jnp.concatenate([tiles[n >> 16] for n in entries], axis=1)
            right = jnp.concatenate([window[(n >> 8) & 255] for n in entries], axis=0)
            field[entries[1] & 255] += jnp.dot(left, right, preferred_element_type=F32)

    def long(i, carry):
        turn(i * LONG, LONG)
        return carry

    def short(i, carry):
        turn(long_turns * LONG + i * SHORT, SHORT)
        return carry

    long_turns = list_ref[4 * pairs + 2 * part]
    lax.fori_loop(0, long_turns, long, 0)
    lax.fori_loop(0, list_ref[4 * pairs + 2 * part + 1], short, 0)


def near_fields(lists, tiles, owns, others, far_part, sent, after, flops, name):
    slots, tile, _ = tiles.shape
    cells = owns[0].shape[0]
    groups = len(owns)
    width = groups * LANES
    per = cells // tile
    pairs = section(slots, per)
    start = [] if far_part is None else [far_part]

    def body(list_ref, tiles_ref, *refs):
        own_refs, other_refs, refs = refs[:groups], refs[groups : 2 * groups], refs[2 * groups :]
        start_refs, refs = refs[: len(start)], refs[len(start) :]
        sent_refs, refs = refs[: len(sent)], refs[len(sent) + len(after) :]
        field_outs, sent_outs, (field, window) = refs[:groups], refs[groups:-2], refs[-2:]
        for out, ref in zip(sent_outs, sent_refs):
            out[...] = ref[...]
        for g in range(groups):
            window[:per, :, lanes(g)] = own_refs[g][...].reshape(per, tile, LANES)
            window[per : 2 * per, :, lanes(g)] = other_refs[g][...].reshape(per, tile, LANES)
        window[2 * per] = jnp.zeros((tile, width), BF16)
        field[:per] = jnp.zeros((per, tile, width), F32)
        for ref in start_refs:
            field[:per, :, lanes(0)] = ref[...].reshape(per, tile, LANES)
        add_pairs(0, list_ref, tiles_ref, field, window, pairs)
        for g, out in enumerate(field_outs):
            out[...] = field[:per, :, lanes(g)].reshape(cells, LANES).astype(out.dtype)

    outs = call(
        body,
        [(lists, pltpu.SMEM)] + vmem(tiles, *owns, *others, *start, *sent, *after),
        [
            ((cells, LANES), BF16 if start and g == 0 else F32, pltpu.VMEM)
            for g in range(groups)
        ]
        + [(a.shape, BF16, pltpu.VMEM) for a in sent],
        [
            pltpu.VMEM((per + 1, tile, width), F32),
            pltpu.VMEM((2 * per + 1, tile, width), BF16),
        ],
        name,
        flops,
    )
    return outs[:groups], outs[groups:]


def far_fields(lists, tiles, nears, far, extra, outs_of, work, name, flops=0):
    slots, tile, _ = tiles.shape
    cells, width = far.shape
    per = cells // tile
    pairs = section(slots, per)
    n = width // LANES
    m = len(nears)

    def body(list_ref, tiles_ref, far_ref, *refs):
        near_refs, extra_refs = refs[:m], refs[m : m + len(extra)]
        out_refs, (field, window) = refs[m + len(extra) : -2], refs[-2:]
        window[:per] = far_ref[...].reshape(per, tile, width)
        window[per] = jnp.zeros((tile, width), BF16)
        if not near_refs:
            field[:per] = jnp.zeros((per, tile, width), F32)
        for i, ref in enumerate(near_refs):
            field[:per, :, lanes(i)] = ref[...].reshape(per, tile, LANES)
        add_pairs(1, list_ref, tiles_ref, field, window, pairs)
        work([field[:per, :, lanes(i)].reshape(cells, LANES) for i in range(n)], extra_refs, out_refs)

    return call(
        body,
        [(lists, pltpu.SMEM)] + vmem(tiles, far, *nears, *extra),
        [(*out, pltpu.VMEM) for out in outs_of],
        [pltpu.VMEM((per + 1, tile, width), F32), pltpu.VMEM((per + 1, tile, width), BF16)],
        name,
        flops,
    )


def first_base(xs, momenta, same, spread, coupling, channels):
    cells, width = momenta.shape
    groups = len(xs)

    def body(*refs):
        x_refs, (y_ref, same_ref, spread_ref, coupling_ref) = refs[:groups], refs[groups : groups + 4]
        outs = refs[groups + 4 :]
        tall = jnp.dot(spread_ref[...], coupling_ref[...], preferred_element_type=F32).astype(BF16)
        wide = lax.dot_general(
            tall, spread_ref[...], (((1,), (1,)), ((), ())), preferred_element_type=F32
        )
        outs[groups][...] = (wide * same_ref[...].astype(F32)).astype(BF16)
        x = [ref[...] for ref in x_refs]
        y = [y_ref[:, lanes(g)] for g in range(groups)]
        bases_into(outs[:groups], x, y, same_ref, 0, channels)

    outs = call(
        body,
        vmem(*xs, momenta, same, spread, coupling),
        [((cells, LANES), F32, pltpu.VMEM)] * groups + [((width, width), BF16, pltpu.VMEM)],
        [],
        "first_base",
    )
    return outs[:groups], outs[groups]


def second_base(xs, ys, same, channels):
    groups = len(xs)

    def body(*refs):
        x = [ref[...] for ref in refs[:groups]]
        y = [ref[...] for ref in refs[groups : 2 * groups]]
        bases_into(refs[2 * groups + 1 :], x, y, refs[2 * groups], 1, channels)

    return call(
        body,
        vmem(*xs, *ys, same),
        [(xs[0].shape, F32, pltpu.VMEM)] * groups,
        [],
        "second_base",
    )


def finish(xs, bases, mixed):
    groups = len(xs)
    cells = xs[0].shape[0]
    width = groups * LANES

    def body(*refs):
        x_refs, base_refs, mixed_refs = [refs[k * groups : (k + 1) * groups] for k in range(3)]
        x_out, y_out, x_buf, y_buf, sems = refs[3 * groups :]
        copies = []
        for g in range(groups):
            y_new = base_refs[g][...] - 0.2 * mixed_refs[g][...]
            y_buf[g] = y_new
            x_buf[g] = jnp.clip(x_refs[g][...] + 0.5 * y_new, -1.0, 1.0)
            for k, (buf, out) in enumerate(((y_buf, y_out), (x_buf, x_out))):
                copies.append(
                    pltpu.make_async_copy(buf.at[g], out.at[:, lanes(g)], sems.at[g, k])
                )
                copies[-1].start()
        for copy in copies:
            copy.wait()

    return call(
        body,
        vmem(*xs, *bases, *mixed),
        [((cells, width), F32, pltpu.HBM)] * 2,
        [
            pltpu.VMEM((groups, cells, LANES), F32),
            pltpu.VMEM((groups, cells, LANES), F32),
            pltpu.SemaphoreType.DMA((groups, 2)),
        ],
        "finish",
    )


def local(positions, momenta, tile_values, tile_rows, tile_cols, tile_count, channel_coupling):
    cells, width = positions.shape
    slots, tile, _ = tile_values.shape
    channels = channel_coupling.shape[0]
    replicas = width // channels
    groups = width // LANES
    ring = lax.axis_size("row") * lax.axis_size("col")
    where = np.arange(width)
    same = jnp.asarray(
        (where[:, None] // channels == where[None] // channels).astype(ml_dtypes.bfloat16)
    )
    spread = jnp.asarray(
        (where[:, None] % channels == np.arange(channels)[None]).astype(ml_dtypes.bfloat16)
    )
    on_chip = [(i, i ^ 1) for i in range(ring)]
    off_chip = [(i, (i + 1) % ring if i % 2 else (i - 1) % ring) for i in range(ring)]
    wide = (cells, LANES)
    every = list(range(groups))
    first_pieces = [every[:-1], every[-1:]]
    second_pieces = [every[:1], every[1:]]

    def ring_index():
        return lax.axis_index("row") * lax.axis_size("col") + lax.axis_index("col")

    def far_swap(mine):
        return lax.ppermute(mine, RING, off_chip)

    def near_swap(mine):
        return lax.ppermute(mine, RING, on_chip)

    def ready(piece, done):
        return [
            t for t in every if t not in done and max(spanned(t, channels, width)) <= piece[-1]
        ]

    def keep(done, _, outs):
        outs[0][...] = done[0]

    def needed(todo, piece):
        return sorted({n for t in todo for n in spanned(t, channels, width)} - set(piece))

    xs, owns, sent = load_first(positions, first_pieces[0])
    fars = [far_swap(sent)]
    lists, more_x, more_own = make_lists(
        tile_rows, tile_cols, tile_count, positions, first_pieces[1], sent, slots, tile, ring_index
    )
    xs, owns = [*xs, *more_x], [*owns, *more_own]
    others = [near_swap(r) for r in owns]
    base, mixing = first_base(xs, momenta, same, spread, channel_coupling, channels)
    near, sent = near_fields(
        lists, tile_values, owns, others, None, more_own, [mixing], 0, "near_first"
    )
    fars.append(far_swap(sent[0]))

    fields, new_x, new_y, rounded, new_fars = {}, {}, {}, {}, []
    for p, piece in enumerate(first_pieces):
        todo = ready(piece, new_x)
        known = needed(todo, piece)
        going = second_pieces[p]
        assert going == todo
        last = p == len(first_pieces) - 1

        def work(done, ins, outs, piece=piece, todo=todo, known=known, last=last):
            held = {n: ins[1 + i][...] for i, n in enumerate(known)}
            done = [field.astype(BF16) for field in done]
            held.update(zip(piece, done))
            rest = ins[1 + len(known) :]
            for i, t in enumerate(todo):
                y_new = rest[2 * i][...] - 0.2 * mixed_of(held, ins[0], t, channels)
                x_new = jnp.clip(rest[2 * i + 1][...] + 0.5 * y_new, -1.0, 1.0)
                r_new = x_new.astype(BF16)
                outs[3 * i][...] = x_new
                outs[3 * i + 1][...] = y_new
                outs[3 * i + 2][...] = r_new
                outs[3 * len(todo)][:, lanes(i)] = r_new
            if not last:
                for i, field in enumerate(done):
                    outs[3 * len(todo) + 1 + i][...] = field

        results = far_fields(
            lists,
            tile_values,
            [near[n] for n in piece],
            fars[p],
            [mixing] + [fields[n] for n in known] + [a for t in todo for a in (base[t], xs[t])],
            [(wide, F32), (wide, F32), (wide, BF16)] * len(todo)
            + [((cells, len(todo) * LANES), BF16)]
            + ([] if last else [(wide, BF16)] * len(piece)),
            work,
            f"far_first_{p}",
        )
        for i, t in enumerate(todo):
            new_x[t], new_y[t], rounded[t] = results[3 * i : 3 * i + 3]
        new_fars.append(far_swap(results[3 * len(todo)]))
        fields.update(zip(piece, results[3 * len(todo) + 1 :]))

    xs, ys, owns = [[of[g] for g in every] for of in (new_x, new_y, rounded)]
    others = [near_swap(r) for r in owns]
    (part,) = far_fields(
        lists, tile_values, [], new_fars[0], [], [(wide, F32)], keep, "far_second_0", NEAR_FLOPS
    )
    near, _ = near_fields(
        lists, tile_values, owns, others, part, [], [], NEAR_FLOPS, "near_second"
    )
    base = second_base(xs, ys, same, channels)
    piece = second_pieces[1]

    def last_work(done, ins, outs):
        held = {n: field.astype(BF16) for n, field in zip(piece, done)}
        held[0] = ins[1][...]
        sums = []
        for t in every:
            value = mixed_of(held, ins[0], t, channels)
            outs[t][...] = value
            sums.append(jnp.sum(ins[2 + t][...].astype(F32) * value, axis=0, keepdims=True))
        row = jnp.concatenate(sums, axis=1)
        lane = lax.broadcasted_iota(jnp.int32, (1, width), 1)
        place = lax.broadcasted_iota(jnp.int32, (1, LANES), 1)
        total = jnp.zeros((1, LANES), F32)
        for r in range(replicas):
            inside = (lane >= r * channels) & (lane < (r + 1) * channels)
            value = jnp.sum(jnp.where(inside, row, 0.0), axis=1, keepdims=True)
            total = jnp.where(place == r, value, total)
        outs[groups][...] = jnp.broadcast_to(total, (ring, LANES))

    *mixed, partial = far_fields(
        lists,
        tile_values,
        near[1:],
        new_fars[1],
        [mixing, near[0]] + owns,
        [(wide, F32)] * groups + [((ring, LANES), F32)],
        last_work,
        "far_second_1",
    )

    everyone = lax.all_to_all(partial, RING, 0, 0, tiled=True)
    energy = jnp.sum(everyone, axis=0)[:replicas] / jnp.sqrt(jnp.float32(cells * ring * channels))
    x_new, y_new = finish(xs, base, mixed)
    return (x_new, y_new, energy)


def solution(mesh):
    cells = P(("groups", "row", "col"), None)
    slots = P(("groups", "row", "col"))
    return jax.shard_map(
        local,
        mesh=mesh,
        in_specs=(cells, cells, P(("groups", "row", "col"), None, None), slots, slots, slots, P()),
        out_specs=(cells, cells, P("groups")),
        check_vma=False,
    )
```

time: 57.8 us -> 57.8 us (level); the launches traced: 57.9 us -> 57.1 us
  starting transfers between devices: 33 us -> 29.8 us
  local copies, waits for them, and re-layouts: 1.45 us -> 3.38 us
    ppermute x6 -> x4, waiting for transfers between devices: 2.3 us -> 7.07 us  [far_swap(): return lax.ppermute(mine, RING, off_chip)]
    all_to_all x1, waiting for transfers between devices: 4.69 us -> 0.29 us  [local(): everyone = lax.all_to_all(partial, RING, 0, 0, tiled=True)]
    ppermute x6 -> x4, starting transfers between devices: 18.6 us -> 15.7 us  [far_swap(): return lax.ppermute(mine, RING, off_chip)]
    ppermute x6, starting transfers between devices: 8.15 us -> 5.47 us  [near_swap(): return lax.ppermute(mine, RING, on_chip)]
    all_to_all x1, starting transfers between devices: 6.21 us -> 8.63 us  [local(): everyone = lax.all_to_all(partial, RING, 0, 0, tiled=True)]
    unnamed x18 -> x26, local copies, waits for them, and re-layouts: 1.45 us -> 3.38 us
    pallas_call x14 -> x11, Pallas kernels: 14.1 us -> 14.3 us  [call(): pl.pallas_call(body, in_specs=[pl.BlockSpec(memory_space=pl.ANY if s is p...]
  transfers between devices with their start and end apart: 13 -> 11, of which waited for: 3 -> 4; matrix products, arithmetic and copies ran while one was open for 0% -> 0% of each run, Pallas kernels for 20% -> 19%
where the time goes in v1:
time: 57.8 us; the launch traced here: 57.1 us
  starting transfers between devices  29.8 us (52%)
  Pallas kernels  14.3 us (25%)
  waiting for transfers between devices  7.62 us (13%)
  local copies, waits for them, and re-layouts  3.38 us (6%)
  between operations  1.55 us (3%)
    ppermute x4, starting transfers between devices, far_swap(): return lax.ppermute(mine, RING, off_chip)  15.7 us
    pallas_call x11, Pallas kernels, call(): pl.pallas_call(body, in_specs=[pl.BlockSpec(memory_space=pl.ANY if s is p...  14.3 us
    all_to_all x1, starting transfers between devices, local(): everyone = lax.all_to_all(partial, RING, 0, 0, tiled=True)  8.63 us
    ppermute x4, waiting for transfers between devices, far_swap(): return lax.ppermute(mine, RING, off_chip)  7.07 us
    ppermute x6, starting transfers between devices, near_swap(): return lax.ppermute(mine, RING, on_chip)  5.47 us
    unnamed x26, local copies, waits for them, and re-layouts  3.38 us
  transfers between devices with their start and end apart: 11, of which 4 were waited for; matrix products, arithmetic and copies ran while one was open for 0% of the time, Pallas kernels for 19%

profile of v1, /device:TPU:0, one launch (start us, length us, event | category | flops | bytes accessed | tf_op | source)
XLA Modules:
  0.0 57.1 jit_solution(445436751640975985)
XLA Ops:
  0.6 0.0 copy-start.2
  0.7 1.4 %load_first.1 = (f32[1024,128]{1,0:T(8,128)S(1)}, f32[1024,128]{1,0:T(8,128)S(1)}, bf16[1024,128]{1,0:T(8,128)(2,1)S(1)}, bf16[1024,128]{1,0:T(8,128)(2,1)S(1)}, bf16[1024,256]{1,0:T(8,128)(2,1)S(1)}) custom-call(f32[1024,384]{1,0:T(8,128)} %x_ref.3), custom_call_target="tpu_custom_call" | custom-call | flops 1000 | bytes 1000 | tf_op jit(solution)/shard_map/load_first/pallas_call | solution.py:21
  2.1 5.5 %collective-permute-start = (bf16[1024,256]{1,0:T(8,128)(2,1)S(1)}, bf16[1024,256]{1,0:T(8,128)(2,1)S(1)}, u32[]{:S(2)}, u32[]{:S(2)}) collective-permute-start(bf16[1024,256]{1,0:T(8,128)(2,1)S(1)} %get-tuple-element.44._), channel_id=1, source_target_pairs={{0,15},{1,2},{2,1},{3,4},{4,3},{5,6},{6,5},{7,8},{8,7},{9,10},{10,... | collective-permute-start | bytes 1572872 | tf_op jit(solution)/shard_map/ppermute | solution.py:407
  8.3 1.3 %make_lists.1 = (s32[214]{0:T(256)S(4)}, f32[1024,128]{1,0:T(8,128)S(1)}, bf16[1024,128]{1,0:T(8,128)(2,1)S(1)}) custom-call(s32[96]{0:T(128)S(1)} %copy-done.11, s32[96]{0:T(128)S(1)} %copy-done.12, s32[1]{0:T(128)S(6)} %copy.13.count_hbm, f32[1024,384]{1,0:T(8,128)} %x_ref.3, bf16[1024,256]{1,0:T(8,128)(2,1)S(1)} %get-tuple-element.44._), custom_call_target="tpu_custom_call" | custom-call | flops 1000 | bytes 1000 | tf_op jit(solution)/shard_map/make_lists/pallas_call | solution.py:21
  9.6 0.1 collective-permute-start.3
  9.6 0.5 collective-permute-start.1
  10.1 0.1 collective-permute-start.2
  10.2 1.4 %first_base.1 = (f32[1024,128]{1,0:T(8,128)S(1)}, f32[1024,128]{1,0:T(8,128)S(1)}, f32[1024,128]{1,0:T(8,128)S(1)}, bf16[384,384]{1,0:T(8,128)(2,1)S(1)}) custom-call(f32[1024,128]{1,0:T(8,128)S(1)} %get-tuple-element.49.refs_0_.refs_4_, f32[1024,128]{1,0:T(8,128)S(1)} %get-tuple-element.50.refs_1_.refs_5_, ...), custom_call_target="tpu_custom_call" | custom-call | flops 1000 | bytes 1000 | tf_op jit(solution)/shard_map/first_base/pallas_call | solution.py:21
  11.7 0.2 collective-permute-done.2.refs_4_
  11.9 0.2 copy-done
  12.1 1.4 %near_first.1 = (f32[1024,128]{1,0:T(8,128)S(1)}, f32[1024,128]{1,0:T(8,128)S(1)}, f32[1024,128]{1,0:T(8,128)S(1)}, bf16[1024,128]{1,0:T(8,128)(2,1)S(1)}) custom-call(s32[214]{0:T(256)S(4)} %get-tuple-element.45.list_ref, bf16[96,128,128]{2,1,0:T(8,128)(2,1)S(1)} %copy-done, bf16[1024,128]{1,0:T(8,128)(2,1)S(1)} %get-tuple-element.46.refs_0_, ...), custom_call_target="tpu_custom_call" | custom-call | flops 1000 | bytes 1000 | tf_op jit(solution)/shard_map/near_first/pallas_call | solution.py:21
  13.5 2.1 %collective-permute-start.4 = (bf16[1024,128]{1,0:T(8,128)(2,1)S(1)}, bf16[1024,128]{1,0:T(8,128)(2,1)S(1)}, u32[]{:S(2)}, u32[]{:S(2)}) collective-permute-start(bf16[1024,128]{1,0:T(8,128)(2,1)S(1)} %get-tuple-element.57), channel_id=1, source_target_pairs={{0,15},{1,2},{2,1},{3,4},{4,3},{5,6},{6,5},{7,8},{8,7},{9,10},{10,... | collective-permute-start | bytes 786440 | tf_op jit(solution)/shard_map/ppermute | solution.py:407
  15.6 0.9 %far_first_0.1 = (f32[1024,128]{1,0:T(8,128)S(1)}, f32[1024,128]{1,0:T(8,128)S(1)}, bf16[1024,128]{1,0:T(8,128)(2,1)S(1)}, bf16[1024,128]{1,0:T(8,128)(2,1)S(1)}...) custom-call(s32[214]{0:T(256)S(4)} %get-tuple-element.45.list_ref, bf16[96,128,128]{2,1,0:T(8,128)(2,1)S(1)} %copy-done, ...), custom_call_target="tpu_custom_call" | custom-call | flops 1000 | bytes 1000 | tf_op jit(solution)/shard_map/far_first_0/pallas_call | solution.py:21
  16.5 3.6 %collective-permute-start.9 = (bf16[1024,128]{1,0:T(8,128)(2,1)S(1)}, bf16[1024,128]{1,0:T(8,128)(2,1)S(1)}, u32[]{:S(2)}, u32[]{:S(2)}) collective-permute-start(bf16[1024,128]{1,0:T(8,128)(2,1)S(1)} %get-tuple-element.75), channel_id=1, source_target_pairs={{0,15},{1,2},{2,1},{3,4},{4,3},{5,6},{6,5},{7,8},{8,7},{9,10},{10,... | collective-permute-start | bytes 786440 | tf_op jit(solution)/shard_map/ppermute | solution.py:407
  20.1 2.1 %collective-permute-done.4.far_ref = bf16[1024,128]{1,0:T(8,128)(2,1)S(1)} collective-permute-done((bf16[1024,128]{1,0:T(8,128)(2,1)S(1)}, bf16[1024,128]{1,0:T(8,128)(2,1)S(1)}, u32[]{:S(2)}, u32[]{:S(2)}) %collective-permute-start.4) | collective-permute-done | bytes 262176 | tf_op jit(solution)/shard_map/ppermute | solution.py:407
  22.2 1.0 %far_first_1.1 = (f32[1024,128]{1,0:T(8,128)S(1)}, f32[1024,128]{1,0:T(8,128)S(1)}, bf16[1024,128]{1,0:T(8,128)(2,1)S(1)}, f32[1024,128]{1,0:T(8,128)S(1)}, f32[...) custom-call(s32[214]{0:T(256)S(4)} %get-tuple-element.45.list_ref, ...), custom_call_target="tpu_custom_call" | custom-call | flops 1000 | bytes 1000 | tf_op jit(solution)/shard_map/far_first_1/pallas_call | solution.py:21
  23.3 4.3 %collective-permute-start.7 = (bf16[1024,128]{1,0:T(8,128)(2,1)S(1)}, bf16[1024,128]{1,0:T(8,128)(2,1)S(1)}, u32[]{:S(2)}, u32[]{:S(2)}) collective-permute-start(bf16[1024,128]{1,0:T(8,128)(2,1)S(1)} %get-tuple-element.73.refs_1_.refs_5_), channel_id=1, source_target_pairs={{0,1},{1,0},{2,3},{3,2},{4,5},{5,4},{6,7},{7,6},{8,9},{9,8},{10,11... | collective-permute-start | bytes 786440 | tf_op jit(solution)/shard_map/ppermute | solution.py:410
  27.6 0.1 collective-permute-start.8
  27.7 0.4 collective-permute-start.6
  28.1 4.5 %collective-permute-start.5 = (bf16[1024,256]{1,0:T(8,128)(2,1)S(1)}, bf16[1024,256]{1,0:T(8,128)(2,1)S(1)}, u32[]{:S(2)}, u32[]{:S(2)}) collective-permute-start(bf16[1024,256]{1,0:T(8,128)(2,1)S(1)} %get-tuple-element.71), channel_id=1, source_target_pairs={{0,15},{1,2},{2,1},{3,4},{4,3},{5,6},{6,5},{7,8},{8,7},{9,10},{10,... | collective-permute-start | bytes 1572872 | tf_op jit(solution)/shard_map/ppermute | solution.py:407
  32.6 0.5 far_second_0.1.refs_6_
  33.2 1.4 %near_second.1 = (bf16[1024,128]{1,0:T(8,128)(2,1)S(1)}, f32[1024,128]{1,0:T(8,128)S(1)}, f32[1024,128]{1,0:T(8,128)S(1)}) custom-call(s32[214]{0:T(256)S(4)} %get-tuple-element.45.list_ref, bf16[96,128,128]{2,1,0:T(8,128)(2,1)S(1)} %copy-done, bf16[1024,128]{1,0:T(8,128)(2,1)S(1)} %get-tuple-element.72.refs_0_.refs_4_, ...), custom_call_target="tpu_custom_call" | custom-call | flops 10000000000 | bytes 1000 | tf_op jit(solution)/shard_map/near_second/pallas_call | solution.py:21
  34.6 5.0 %collective-permute-done.5.far_ref = bf16[1024,256]{1,0:T(8,128)(2,1)S(1)} collective-permute-done((bf16[1024,256]{1,0:T(8,128)(2,1)S(1)}, bf16[1024,256]{1,0:T(8,128)(2,1)S(1)}, u32[]{:S(2)}, u32[]{:S(2)}) %collective-permute-start.5) | collective-permute-done | bytes 524320 | tf_op jit(solution)/shard_map/ppermute | solution.py:407
  39.6 2.0 %far_second_1.1 = (f32[1024,128]{1,0:T(8,128)S(1)}, f32[1024,128]{1,0:T(8,128)S(1)}, f32[1024,128]{1,0:T(8,128)S(1)}, f32[16,128]{1,0:T(8,128)}) custom-call(s32[214]{0:T(256)S(4)} %get-tuple-element.45.list_ref, bf16[96,128,128]{2,1,0:T(8,128)(2,1)S(1)} %copy-done, bf16[1024,256]{1,0:T(8,128)(2,1)S(1)} %collective-permute-done.5.far_ref, ...), custom_call_target="tpu_custom_call" | custom-call | flops 1000 | bytes 1000 | tf_op jit(solution)/shard_map/far_second_1/pallas_call | solution.py:21
  41.6 8.6 %all-to-all-start = ((f32[16,1,128]{2,1,0:T(1,128)}), f32[16,1,128]{2,1,0:T(1,128)S(1)}, u32[]{:S(2)}, u32[]{:S(2)}) async-start(f32[16,1,128]{2,1,0:T(1,128)} %bitcast.1), calls=%async_computation | async-start | bytes 16384 | tf_op jit(solution)/shard_map/all_to_all | solution.py:518
  50.2 1.0 %copy-done.4 = f32[1024,128]{1,0:T(8,128)S(1)} copy-done((f32[1024,128]{1,0:T(8,128)S(1)}, f32[1024,128]{1,0:T(8,128)}, u32[]{:S(2)}) %copy-start.4) | copy-done | bytes 524312
  51.2 1.0 %copy-done.6 = f32[1024,128]{1,0:T(8,128)S(1)} copy-done((f32[1024,128]{1,0:T(8,128)S(1)}, f32[1024,128]{1,0:T(8,128)}, u32[]{:S(2)}) %copy-start.6) | copy-done | bytes 524312
  52.3 1.0 %copy-done.8 = f32[1024,128]{1,0:T(8,128)S(1)} copy-done((f32[1024,128]{1,0:T(8,128)S(1)}, f32[1024,128]{1,0:T(8,128)}, u32[]{:S(2)}) %copy-start.8) | copy-done | bytes 524312
  53.3 1.2 %second_base.1 = (f32[1024,128]{1,0:T(8,128)S(1)}, f32[1024,128]{1,0:T(8,128)S(1)}, f32[1024,128]{1,0:T(8,128)S(1)}) custom-call(f32[1024,128]{1,0:T(8,128)S(1)} %get-tuple-element.56.refs_0_, f32[1024,128]{1,0:T(8,128)S(1)} %get-tuple-element.63.refs_1_, f32[1024,128]{1,0:T(8,128)S(1)} %get-tuple-element.64.refs_2_, f32[1024,128]{1,0:T(8,128)S(1)} %copy-done.4, ...), custom_call_target="tpu_custom_call" | custom-call | flops 1000 | bytes 1000 | tf_op jit(solution)/shard_map/second_base/pallas_call | solution.py:21
  54.5 1.8 %finish.1 = (f32[1024,384]{1,0:T(8,128)}, f32[1024,384]{1,0:T(8,128)}) custom-call(f32[1024,128]{1,0:T(8,128)S(1)} %get-tuple-element.56.refs_0_, f32[1024,128]{1,0:T(8,128)S(1)} %get-tuple-element.63.refs_1_, f32[1024,128]{1,0:T(8,128)S(1)} %get-tuple-element.64.refs_2_, f32[1024,128]{1,0:T(8,128)S(1)} %get-tuple-element.68.refs_3_, ...), custom_call_target="tpu_custom_call" | custom-call | flops 1000 | bytes 1000 | tf_op jit(solution)/shard_map/finish/pallas_call | solution.py:21
  56.3 0.3 all-to-all-done
  56.6 0.5 slice_multiply_fusion
  (29 shorter events, 0.1 us)
Async XLA Ops:
  0.6 9.6 %copy-start.2 = (bf16[384,384]{1,0:T(8,128)(2,1)S(1)}, bf16[384,384]{1,0:T(8,128)(2,1)}, u32[]{:S(2)}) copy-start(bf16[384,384]{1,0:T(8,128)(2,1)} %constant.9.clone.refs_4_.refs_6_) | copy-start | bytes 884740
  0.6 9.6 %copy-start.9 = (bf16[384,48]{1,0:T(8,128)(2,1)S(1)}, bf16[384,48]{1,0:T(8,128)(2,1)}, u32[]{:S(2)}) copy-start(bf16[384,48]{1,0:T(8,128)(2,1)} %constant.10.clone.refs_5_) | copy-start | bytes 110596
  0.7 7.6 %copy-start.11 = (s32[96]{0:T(128)S(1)}, s32[96]{0:T(128)}, u32[]{:S(2)}) copy-start(s32[96]{0:T(128)} %rows_hbm.1) | copy-start | bytes 1156
  0.7 7.6 %copy-start.12 = (s32[96]{0:T(128)S(1)}, s32[96]{0:T(128)}, u32[]{:S(2)}) copy-start(s32[96]{0:T(128)} %cols_hbm.1) | copy-start | bytes 1156
  0.7 9.5 %copy-start.1 = (f32[1024,384]{1,0:T(8,128)S(1)}, f32[1024,384]{1,0:T(8,128)}, u32[]{:S(2)}) copy-start(f32[1024,384]{1,0:T(8,128)} %refs_3_.1) | copy-start | bytes 4718596
  0.7 9.5 %copy-start.10 = (bf16[48,48]{1,0:T(8,128)(2,1)S(1)}, bf16[48,48]{1,0:T(8,128)(2,1)}, u32[]{:S(2)}) copy-start(bf16[48,48]{1,0:T(8,128)(2,1)} %refs_6_.2) | copy-start | bytes 13828
  2.1 13.5 %collective-permute-start = (bf16[1024,256]{1,0:T(8,128)(2,1)S(1)}, bf16[1024,256]{1,0:T(8,128)(2,1)S(1)}, u32[]{:S(2)}, u32[]{:S(2)}) collective-permute-start(bf16[1024,256]{1,0:T(8,128)(2,1)S(1)} %get-tuple-element.44._), channel_id=1, source_target_pairs={{0,15},{1,2},{2,1},{3,4},{4,3},{5,6},{6,5},{7,8},{8,7},{9,10},{10,... | collective-permute-start | bytes 1572872 | tf_op jit(solution)/shard_map/ppermute | solution.py:407
  9.6 2.1 %collective-permute-start.3 = (bf16[1024,128]{1,0:T(8,128)(2,1)S(1)}, bf16[1024,128]{1,0:T(8,128)(2,1)S(1)}, u32[]{:S(2)}, u32[]{:S(2)}) collective-permute-start(bf16[1024,128]{1,0:T(8,128)(2,1)S(1)} %get-tuple-element.48.refs_2_.refs_6_), channel_id=1, source_target_pairs={{0,1},{1,0},{2,3},{3,2},{4,5},{5,4},{6,7},{7,6},{8,9},{9,8},{10,11... | collective-permute-start | bytes 786440 | tf_op jit(solution)/shard_map/ppermute | solution.py:410
  9.6 2.0 %collective-permute-start.1 = (bf16[1024,128]{1,0:T(8,128)(2,1)S(1)}, bf16[1024,128]{1,0:T(8,128)(2,1)S(1)}, u32[]{:S(2)}, u32[]{:S(2)}) collective-permute-start(bf16[1024,128]{1,0:T(8,128)(2,1)S(1)} %get-tuple-element.46.refs_0_), channel_id=1, source_target_pairs={{0,1},{1,0},{2,3},{3,2},{4,5},{5,4},{6,7},{7,6},{8,9},{9,8},{10,11... | collective-permute-start | bytes 786440 | tf_op jit(solution)/shard_map/ppermute | solution.py:410
  10.1 1.8 %collective-permute-start.2 = (bf16[1024,128]{1,0:T(8,128)(2,1)S(1)}, bf16[1024,128]{1,0:T(8,128)(2,1)S(1)}, u32[]{:S(2)}, u32[]{:S(2)}) collective-permute-start(bf16[1024,128]{1,0:T(8,128)(2,1)S(1)} %get-tuple-element.47.refs_1_), channel_id=1, source_target_pairs={{0,1},{1,0},{2,3},{3,2},{4,5},{5,4},{6,7},{7,6},{8,9},{9,8},{10,11... | collective-permute-start | bytes 786440 | tf_op jit(solution)/shard_map/ppermute | solution.py:410
  10.2 1.9 %copy-start = (bf16[96,128,128]{2,1,0:T(8,128)(2,1)S(1)}, bf16[96,128,128]{2,1,0:T(8,128)(2,1)}, u32[]{:S(2)}) copy-start(bf16[96,128,128]{2,1,0:T(8,128)(2,1)} %tiles_ref.11) | copy-start | bytes 9437188
  13.5 8.7 %collective-permute-start.4 = (bf16[1024,128]{1,0:T(8,128)(2,1)S(1)}, bf16[1024,128]{1,0:T(8,128)(2,1)S(1)}, u32[]{:S(2)}, u32[]{:S(2)}) collective-permute-start(bf16[1024,128]{1,0:T(8,128)(2,1)S(1)} %get-tuple-element.57), channel_id=1, source_target_pairs={{0,15},{1,2},{2,1},{3,4},{4,3},{5,6},{6,5},{7,8},{8,7},{9,10},{10,... | collective-permute-start | bytes 786440 | tf_op jit(solution)/shard_map/ppermute | solution.py:407
  16.5 6.7 %copy-start.3 = (f32[1024,128]{1,0:T(8,128)}, f32[1024,128]{1,0:T(8,128)S(1)}, u32[]{:S(2)}) copy-start(f32[1024,128]{1,0:T(8,128)S(1)} %get-tuple-element.65.refs_3_) | copy-start | bytes 1572868
  16.5 16.1 %collective-permute-start.9 = (bf16[1024,128]{1,0:T(8,128)(2,1)S(1)}, bf16[1024,128]{1,0:T(8,128)(2,1)S(1)}, u32[]{:S(2)}, u32[]{:S(2)}) collective-permute-start(bf16[1024,128]{1,0:T(8,128)(2,1)S(1)} %get-tuple-element.75), channel_id=1, source_target_pairs={{0,15},{1,2},{2,1},{3,4},{4,3},{5,6},{6,5},{7,8},{8,7},{9,10},{10,... | collective-permute-start | bytes 786440 | tf_op jit(solution)/shard_map/ppermute | solution.py:407
  23.2 9.9 %copy-start.5 = (f32[1024,128]{1,0:T(8,128)}, f32[1024,128]{1,0:T(8,128)S(1)}, u32[]{:S(2)}) copy-start(f32[1024,128]{1,0:T(8,128)S(1)} %get-tuple-element.66.refs_4_) | copy-start | bytes 1572868
  23.3 9.9 %copy-start.7 = (f32[1024,128]{1,0:T(8,128)}, f32[1024,128]{1,0:T(8,128)S(1)}, u32[]{:S(2)}) copy-start(f32[1024,128]{1,0:T(8,128)S(1)} %get-tuple-element.67.refs_5_) | copy-start | bytes 1572868
  23.3 9.9 %collective-permute-start.7 = (bf16[1024,128]{1,0:T(8,128)(2,1)S(1)}, bf16[1024,128]{1,0:T(8,128)(2,1)S(1)}, u32[]{:S(2)}, u32[]{:S(2)}) collective-permute-start(bf16[1024,128]{1,0:T(8,128)(2,1)S(1)} %get-tuple-element.73.refs_1_.refs_5_), channel_id=1, source_target_pairs={{0,1},{1,0},{2,3},{3,2},{4,5},{5,4},{6,7},{7,6},{8,9},{9,8},{10,11... | collective-permute-start | bytes 786440 | tf_op jit(solution)/shard_map/ppermute | solution.py:410
  27.6 5.6 %collective-permute-start.8 = (bf16[1024,128]{1,0:T(8,128)(2,1)S(1)}, bf16[1024,128]{1,0:T(8,128)(2,1)S(1)}, u32[]{:S(2)}, u32[]{:S(2)}) collective-permute-start(bf16[1024,128]{1,0:T(8,128)(2,1)S(1)} %get-tuple-element.74.refs_2_.refs_6_), channel_id=1, source_target_pairs={{0,1},{1,0},{2,3},{3,2},{4,5},{5,4},{6,7},{7,6},{8,9},{9,8},{10,11... | collective-permute-start | bytes 786440 | tf_op jit(solution)/shard_map/ppermute | solution.py:410
  27.7 5.6 %collective-permute-start.6 = (bf16[1024,128]{1,0:T(8,128)(2,1)S(1)}, bf16[1024,128]{1,0:T(8,128)(2,1)S(1)}, u32[]{:S(2)}, u32[]{:S(2)}) collective-permute-start(bf16[1024,128]{1,0:T(8,128)(2,1)S(1)} %get-tuple-element.72.refs_0_.refs_4_), channel_id=1, source_target_pairs={{0,1},{1,0},{2,3},{3,2},{4,5},{5,4},{6,7},{7,6},{8,9},{9,8},{10,11... | collective-permute-start | bytes 786440 | tf_op jit(solution)/shard_map/ppermute | solution.py:410
  28.1 11.5 %collective-permute-start.5 = (bf16[1024,256]{1,0:T(8,128)(2,1)S(1)}, bf16[1024,256]{1,0:T(8,128)(2,1)S(1)}, u32[]{:S(2)}, u32[]{:S(2)}) collective-permute-start(bf16[1024,256]{1,0:T(8,128)(2,1)S(1)} %get-tuple-element.71), channel_id=1, source_target_pairs={{0,15},{1,2},{2,1},{3,4},{4,3},{5,6},{6,5},{7,8},{8,7},{9,10},{10,... | collective-permute-start | bytes 1572872 | tf_op jit(solution)/shard_map/ppermute | solution.py:407
  41.6 15.0 %all-to-all-start = ((f32[16,1,128]{2,1,0:T(1,128)}), f32[16,1,128]{2,1,0:T(1,128)S(1)}, u32[]{:S(2)}, u32[]{:S(2)}) async-start(f32[16,1,128]{2,1,0:T(1,128)} %bitcast.1), calls=%async_computation | async-start | bytes 16384 | tf_op jit(solution)/shard_map/all_to_all | solution.py:518
  50.2 1.0 %copy-start.4 = (f32[1024,128]{1,0:T(8,128)S(1)}, f32[1024,128]{1,0:T(8,128)}, u32[]{:S(2)}) copy-start(f32[1024,128]{1,0:T(8,128)} %copy-done.3) | copy-start | bytes 1572868
  51.2 1.0 %copy-start.6 = (f32[1024,128]{1,0:T(8,128)S(1)}, f32[1024,128]{1,0:T(8,128)}, u32[]{:S(2)}) copy-start(f32[1024,128]{1,0:T(8,128)} %copy-done.5) | copy-start | bytes 1572868
  52.3 1.0 %copy-start.8 = (f32[1024,128]{1,0:T(8,128)S(1)}, f32[1024,128]{1,0:T(8,128)}, u32[]{:S(2)}) copy-start(f32[1024,128]{1,0:T(8,128)} %copy-done.7) | copy-start | bytes 1572868

commit v2 on v1

--- a/solution.py
+++ b/solution.py
@@ -11,7 +11,7 @@
 LANES = 128
 LONG, SHORT = 16, 4
 VMEM_LIMIT = 14 * 1024 * 1024
-NEAR_FLOPS = 10**10
+NEAR_FLOPS = 4 * 10**9
 F32 = jnp.float32
 BF16 = jnp.bfloat16
 RING = ("row", "col")
@@ -480,9 +480,7 @@
     (part,) = far_fields(
         lists, tile_values, [], new_fars[0], [], [(wide, F32)], keep, "far_second_0", NEAR_FLOPS
     )
-    near, _ = near_fields(
-        lists, tile_values, owns, others, part, [], [], NEAR_FLOPS, "near_second"
-    )
+    near, _ = near_fields(lists, tile_values, owns, others, part, [], [], 0, "near_second")
     base = second_base(xs, ys, same, channels)
     piece = second_pieces[1]
 
@@ -509,7 +507,7 @@
         tile_values,
         near[1:],
         new_fars[1],
-        [mixing, near[0]] + owns,
+        [mixing, near[0], *owns, base[0]],
         [(wide, F32)] * groups + [((ring, LANES), F32)],
         last_work,
         "far_second_1",

time: 57.8 us -> 58.3 us (level)
  waiting for transfers between devices: 7.62 us -> 4.6 us
  local copies, waits for them, and re-layouts: 3.38 us -> 5.76 us
  Pallas kernels: 14.3 us -> 16.3 us
  starting transfers between devices: 29.8 us -> 29.2 us
    ppermute x6, starting transfers between devices: 5.47 us -> 10.9 us  [near_swap(): return lax.ppermute(mine, RING, on_chip)]
    ppermute x4, starting transfers between devices: 15.7 us -> 10.8 us  [far_swap(): return lax.ppermute(mine, RING, off_chip)]
    ppermute x4, waiting for transfers between devices: 7.07 us -> 2.89 us  [far_swap(): return lax.ppermute(mine, RING, off_chip)]
    unnamed x26, local copies, waits for them, and re-layouts: 3.38 us -> 5.76 us
    pallas_call x11, Pallas kernels: 14.3 us -> 16.3 us  [call(): pl.pallas_call(body, in_specs=[pl.BlockSpec(memory_space=pl.ANY if s is p...]
    all_to_all x1, starting transfers between devices: 8.63 us -> 7.47 us  [local(): everyone = lax.all_to_all(partial, RING, 0, 0, tiled=True)]
    all_to_all x1, waiting for transfers between devices: 0.29 us -> 1.45 us  [local(): everyone = lax.all_to_all(partial, RING, 0, 0, tiled=True)]
  transfers between devices with their start and end apart: 11 -> 11, of which waited for: 4 -> 3; matrix products, arithmetic and copies ran while one was open for 0% -> 0% of each run, Pallas kernels for 19% -> 22%
where the time goes in v2:
time: 58.3 us; the launch traced here: 57.9 us
  starting transfers between devices  29.2 us (50%)
  Pallas kernels  16.3 us (28%)
  local copies, waits for them, and re-layouts  5.76 us (10%)
  waiting for transfers between devices  4.6 us (8%)
  between operations  1.52 us (3%)
    pallas_call x11, Pallas kernels, call(): pl.pallas_call(body, in_specs=[pl.BlockSpec(memory_space=pl.ANY if s is p...  16.3 us
    ppermute x6, starting transfers between devices, near_swap(): return lax.ppermute(mine, RING, on_chip)  10.9 us
    ppermute x4, starting transfers between devices, far_swap(): return lax.ppermute(mine, RING, off_chip)  10.8 us
    all_to_all x1, starting transfers between devices, local(): everyone = lax.all_to_all(partial, RING, 0, 0, tiled=True)  7.47 us
    unnamed x26, local copies, waits for them, and re-layouts  5.76 us
    ppermute x4, waiting for transfers between devices, far_swap(): return lax.ppermute(mine, RING, off_chip)  2.89 us
    all_to_all x1, waiting for transfers between devices, local(): everyone = lax.all_to_all(partial, RING, 0, 0, tiled=True)  1.45 us
  transfers between devices with their start and end apart: 11, of which 3 were waited for; matrix products, arithmetic and copies ran while one was open for 0% of the time, Pallas kernels for 22%

profile of v2, /device:TPU:0, one launch (start us, length us, event | category | flops | bytes accessed | tf_op | source)
XLA Modules:
  0.0 57.9 jit_solution(5877258575675726113)
XLA Ops:
  0.7 1.4 %load_first.1 = (f32[1024,128]{1,0:T(8,128)S(1)}, f32[1024,128]{1,0:T(8,128)S(1)}, bf16[1024,128]{1,0:T(8,128)(2,1)S(1)}, bf16[1024,128]{1,0:T(8,128)(2,1)S(1)}, bf16[1024,256]{1,0:T(8,128)(2,1)S(1)}) custom-call(f32[1024,384]{1,0:T(8,128)} %x_ref.3), custom_call_target="tpu_custom_call" | custom-call | flops 1000 | bytes 1000 | tf_op jit(solution)/shard_map/load_first/pallas_call | solution.py:21
  2.1 5.5 %collective-permute-start = (bf16[1024,256]{1,0:T(8,128)(2,1)S(1)}, bf16[1024,256]{1,0:T(8,128)(2,1)S(1)}, u32[]{:S(2)}, u32[]{:S(2)}) collective-permute-start(bf16[1024,256]{1,0:T(8,128)(2,1)S(1)} %get-tuple-element.44._), channel_id=1, source_target_pairs={{0,15},{1,2},{2,1},{3,4},{4,3},{5,6},{6,5},{7,8},{8,7},{9,10},{10,... | collective-permute-start | bytes 1572872 | tf_op jit(solution)/shard_map/ppermute | solution.py:407
  8.3 2.1 %make_lists.1 = (s32[214]{0:T(256)S(4)}, f32[1024,128]{1,0:T(8,128)S(1)}, bf16[1024,128]{1,0:T(8,128)(2,1)S(1)}) custom-call(s32[96]{0:T(128)S(1)} %copy-done.11, s32[96]{0:T(128)S(1)} %copy-done.12, s32[1]{0:T(128)S(6)} %copy.13.count_hbm, f32[1024,384]{1,0:T(8,128)} %x_ref.3, bf16[1024,256]{1,0:T(8,128)(2,1)S(1)} %get-tuple-element.44._), custom_call_target="tpu_custom_call" | custom-call | flops 1000 | bytes 1000 | tf_op jit(solution)/shard_map/make_lists/pallas_call | solution.py:21
  10.4 0.1 collective-permute-start.3
  10.5 0.5 collective-permute-start.1
  11.0 0.1 collective-permute-start.2
  11.1 1.4 %first_base.1 = (f32[1024,128]{1,0:T(8,128)S(1)}, f32[1024,128]{1,0:T(8,128)S(1)}, f32[1024,128]{1,0:T(8,128)S(1)}, bf16[384,384]{1,0:T(8,128)(2,1)S(1)}) custom-call(f32[1024,128]{1,0:T(8,128)S(1)} %get-tuple-element.49.refs_0_.refs_4_, f32[1024,128]{1,0:T(8,128)S(1)} %get-tuple-element.50.refs_1_.refs_5_, ...), custom_call_target="tpu_custom_call" | custom-call | flops 1000 | bytes 1000 | tf_op jit(solution)/shard_map/first_base/pallas_call | solution.py:21
  12.5 0.2 collective-permute-done.2.refs_4_
  12.7 0.2 copy-done
  12.9 1.9 %near_first.1 = (f32[1024,128]{1,0:T(8,128)S(1)}, f32[1024,128]{1,0:T(8,128)S(1)}, f32[1024,128]{1,0:T(8,128)S(1)}, bf16[1024,128]{1,0:T(8,128)(2,1)S(1)}) custom-call(s32[214]{0:T(256)S(4)} %get-tuple-element.45.list_ref, bf16[96,128,128]{2,1,0:T(8,128)(2,1)S(1)} %copy-done, bf16[1024,128]{1,0:T(8,128)(2,1)S(1)} %get-tuple-element.46.refs_0_, ...), custom_call_target="tpu_custom_call" | custom-call | flops 1000 | bytes 1000 | tf_op jit(solution)/shard_map/near_first/pallas_call | solution.py:21
  14.9 0.3 collective-permute-start.4
  15.2 1.0 %far_first_0.1 = (f32[1024,128]{1,0:T(8,128)S(1)}, f32[1024,128]{1,0:T(8,128)S(1)}, bf16[1024,128]{1,0:T(8,128)(2,1)S(1)}, bf16[1024,128]{1,0:T(8,128)(2,1)S(1)}...) custom-call(s32[214]{0:T(256)S(4)} %get-tuple-element.45.list_ref, bf16[96,128,128]{2,1,0:T(8,128)(2,1)S(1)} %copy-done, ...), custom_call_target="tpu_custom_call" | custom-call | flops 1000 | bytes 1000 | tf_op jit(solution)/shard_map/far_first_0/pallas_call | solution.py:21
  16.1 4.5 %collective-permute-start.9 = (bf16[1024,128]{1,0:T(8,128)(2,1)S(1)}, bf16[1024,128]{1,0:T(8,128)(2,1)S(1)}, u32[]{:S(2)}, u32[]{:S(2)}) collective-permute-start(bf16[1024,128]{1,0:T(8,128)(2,1)S(1)} %get-tuple-element.75), channel_id=1, source_target_pairs={{0,15},{1,2},{2,1},{3,4},{4,3},{5,6},{6,5},{7,8},{8,7},{9,10},{10,... | collective-permute-start | bytes 786440 | tf_op jit(solution)/shard_map/ppermute | solution.py:407
  20.7 2.9 %collective-permute-done.4.far_ref = bf16[1024,128]{1,0:T(8,128)(2,1)S(1)} collective-permute-done((bf16[1024,128]{1,0:T(8,128)(2,1)S(1)}, bf16[1024,128]{1,0:T(8,128)(2,1)S(1)}, u32[]{:S(2)}, u32[]{:S(2)}) %collective-permute-start.4) | collective-permute-done | bytes 262176 | tf_op jit(solution)/shard_map/ppermute | solution.py:407
  23.5 1.0 %far_first_1.1 = (f32[1024,128]{1,0:T(8,128)S(1)}, f32[1024,128]{1,0:T(8,128)S(1)}, bf16[1024,128]{1,0:T(8,128)(2,1)S(1)}, f32[1024,128]{1,0:T(8,128)S(1)}, f32[...) custom-call(s32[214]{0:T(256)S(4)} %get-tuple-element.45.list_ref, ...), custom_call_target="tpu_custom_call" | custom-call | flops 1000 | bytes 1000 | tf_op jit(solution)/shard_map/far_first_1/pallas_call | solution.py:21
  24.6 0.5 collective-permute-start.5
  25.1 9.8 %collective-permute-start.7 = (bf16[1024,128]{1,0:T(8,128)(2,1)S(1)}, bf16[1024,128]{1,0:T(8,128)(2,1)S(1)}, u32[]{:S(2)}, u32[]{:S(2)}) collective-permute-start(bf16[1024,128]{1,0:T(8,128)(2,1)S(1)} %get-tuple-element.73.refs_1_.refs_5_), channel_id=1, source_target_pairs={{0,1},{1,0},{2,3},{3,2},{4,5},{5,4},{6,7},{7,6},{8,9},{9,8},{10,11... | collective-permute-start | bytes 786440 | tf_op jit(solution)/shard_map/ppermute | solution.py:410
  34.9 0.5 collective-permute-start.6
  35.4 1.2 %second_base.1 = (f32[1024,128]{1,0:T(8,128)S(1)}, f32[1024,128]{1,0:T(8,128)S(1)}, f32[1024,128]{1,0:T(8,128)S(1)}) custom-call(f32[1024,128]{1,0:T(8,128)S(1)} %get-tuple-element.56.refs_0_, f32[1024,128]{1,0:T(8,128)S(1)} %get-tuple-element.63.refs_1_, f32[1024,128]{1,0:T(8,128)S(1)} %get-tuple-element.64.refs_2_, ...), custom_call_target="tpu_custom_call" | custom-call | flops 1000 | bytes 1000 | tf_op jit(solution)/shard_map/second_base/pallas_call | solution.py:21
  36.6 0.5 far_second_0.1.refs_6_
  37.2 1.9 %near_second.1 = (bf16[1024,128]{1,0:T(8,128)(2,1)S(1)}, f32[1024,128]{1,0:T(8,128)S(1)}, f32[1024,128]{1,0:T(8,128)S(1)}) custom-call(s32[214]{0:T(256)S(4)} %get-tuple-element.45.list_ref, bf16[96,128,128]{2,1,0:T(8,128)(2,1)S(1)} %copy-done, bf16[1024,128]{1,0:T(8,128)(2,1)S(1)} %get-tuple-element.72.refs_0_.refs_4_, ...), custom_call_target="tpu_custom_call" | custom-call | flops 1000 | bytes 1000 | tf_op jit(solution)/shard_map/near_second/pallas_call | solution.py:21
  39.1 2.0 %far_second_1.1 = (f32[1024,128]{1,0:T(8,128)S(1)}, f32[1024,128]{1,0:T(8,128)S(1)}, f32[1024,128]{1,0:T(8,128)S(1)}, f32[16,128]{1,0:T(8,128)}) custom-call(s32[214]{0:T(256)S(4)} %get-tuple-element.45.list_ref, bf16[96,128,128]{2,1,0:T(8,128)(2,1)S(1)} %copy-done, bf16[1024,256]{1,0:T(8,128)(2,1)S(1)} %collective-permute-done.5.far_ref, ...), custom_call_target="tpu_custom_call" | custom-call | flops 1000 | bytes 1000 | tf_op jit(solution)/shard_map/far_second_1/pallas_call | solution.py:21
  41.1 0.8 %copy-done.3 = f32[1024,128]{1,0:T(8,128)} copy-done((f32[1024,128]{1,0:T(8,128)}, f32[1024,128]{1,0:T(8,128)S(1)}, u32[]{:S(2)}) %copy-start.3) | copy-done | bytes 524312
  41.9 0.8 %copy-done.5 = f32[1024,128]{1,0:T(8,128)} copy-done((f32[1024,128]{1,0:T(8,128)}, f32[1024,128]{1,0:T(8,128)S(1)}, u32[]{:S(2)}) %copy-start.5) | copy-done | bytes 524312
  42.7 0.8 %copy-done.7 = f32[1024,128]{1,0:T(8,128)} copy-done((f32[1024,128]{1,0:T(8,128)}, f32[1024,128]{1,0:T(8,128)S(1)}, u32[]{:S(2)}) %copy-start.7) | copy-done | bytes 524312
  43.5 7.5 %all-to-all-start = ((f32[16,1,128]{2,1,0:T(1,128)}), f32[16,1,128]{2,1,0:T(1,128)S(1)}, u32[]{:S(2)}, u32[]{:S(2)}) async-start(f32[16,1,128]{2,1,0:T(1,128)} %bitcast.1), calls=%async_computation | async-start | bytes 16384 | tf_op jit(solution)/shard_map/all_to_all | solution.py:516
  51.0 1.0 %copy-done.4 = f32[1024,128]{1,0:T(8,128)S(1)} copy-done((f32[1024,128]{1,0:T(8,128)S(1)}, f32[1024,128]{1,0:T(8,128)}, u32[]{:S(2)}) %copy-start.4) | copy-done | bytes 524312
  52.0 1.0 %copy-done.6 = f32[1024,128]{1,0:T(8,128)S(1)} copy-done((f32[1024,128]{1,0:T(8,128)S(1)}, f32[1024,128]{1,0:T(8,128)}, u32[]{:S(2)}) %copy-start.6) | copy-done | bytes 524312
  53.0 1.0 %copy-done.8 = f32[1024,128]{1,0:T(8,128)S(1)} copy-done((f32[1024,128]{1,0:T(8,128)S(1)}, f32[1024,128]{1,0:T(8,128)}, u32[]{:S(2)}) %copy-start.8) | copy-done | bytes 524312
  54.1 1.8 %finish.1 = (f32[1024,384]{1,0:T(8,128)}, f32[1024,384]{1,0:T(8,128)}) custom-call(f32[1024,128]{1,0:T(8,128)S(1)} %get-tuple-element.56.refs_0_, f32[1024,128]{1,0:T(8,128)S(1)} %get-tuple-element.63.refs_1_, f32[1024,128]{1,0:T(8,128)S(1)} %get-tuple-element.64.refs_2_, f32[1024,128]{1,0:T(8,128)S(1)} %get-tuple-element.68.refs_7_.refs_3_, ...), custom_call_target="tpu_custom_call" | custom-call | flops 1000 | bytes 1000 | tf_op jit(solution)/shard_map/finish/pallas_call | solution.py:21
  55.9 1.5 %all-to-all-done = f32[16,1,128]{2,1,0:T(1,128)S(1)} async-done(((f32[16,1,128]{2,1,0:T(1,128)}), f32[16,1,128]{2,1,0:T(1,128)S(1)}, u32[]{:S(2)}, u32[]{:S(2)}) %all-to-all-start) | async-done | bytes 8224 | tf_op jit(solution)/shard_map/all_to_all | solution.py:516
  57.4 0.5 slice_multiply_fusion
  (29 shorter events, 0.1 us)
Async XLA Ops:
  0.6 10.4 %copy-start.2 = (bf16[384,384]{1,0:T(8,128)(2,1)S(1)}, bf16[384,384]{1,0:T(8,128)(2,1)}, u32[]{:S(2)}) copy-start(bf16[384,384]{1,0:T(8,128)(2,1)} %constant.9.clone.refs_4_.refs_6_) | copy-start | bytes 884740
  0.6 10.4 %copy-start.9 = (bf16[384,48]{1,0:T(8,128)(2,1)S(1)}, bf16[384,48]{1,0:T(8,128)(2,1)}, u32[]{:S(2)}) copy-start(bf16[384,48]{1,0:T(8,128)(2,1)} %constant.10.clone.refs_5_) | copy-start | bytes 110596
  0.7 7.6 %copy-start.11 = (s32[96]{0:T(128)S(1)}, s32[96]{0:T(128)}, u32[]{:S(2)}) copy-start(s32[96]{0:T(128)} %rows_hbm.1) | copy-start | bytes 1156
  0.7 7.6 %copy-start.12 = (s32[96]{0:T(128)S(1)}, s32[96]{0:T(128)}, u32[]{:S(2)}) copy-start(s32[96]{0:T(128)} %cols_hbm.1) | copy-start | bytes 1156
  0.7 10.4 %copy-start.1 = (f32[1024,384]{1,0:T(8,128)S(1)}, f32[1024,384]{1,0:T(8,128)}, u32[]{:S(2)}) copy-start(f32[1024,384]{1,0:T(8,128)} %refs_3_.1) | copy-start | bytes 4718596
  0.7 10.4 %copy-start.10 = (bf16[48,48]{1,0:T(8,128)(2,1)S(1)}, bf16[48,48]{1,0:T(8,128)(2,1)}, u32[]{:S(2)}) copy-start(bf16[48,48]{1,0:T(8,128)(2,1)} %refs_6_.2) | copy-start | bytes 13828
  2.1 13.0 %collective-permute-start = (bf16[1024,256]{1,0:T(8,128)(2,1)S(1)}, bf16[1024,256]{1,0:T(8,128)(2,1)S(1)}, u32[]{:S(2)}, u32[]{:S(2)}) collective-permute-start(bf16[1024,256]{1,0:T(8,128)(2,1)S(1)} %get-tuple-element.44._), channel_id=1, source_target_pairs={{0,15},{1,2},{2,1},{3,4},{4,3},{5,6},{6,5},{7,8},{8,7},{9,10},{10,... | collective-permute-start | bytes 1572872 | tf_op jit(solution)/shard_map/ppermute | solution.py:407
  10.4 2.1 %collective-permute-start.3 = (bf16[1024,128]{1,0:T(8,128)(2,1)S(1)}, bf16[1024,128]{1,0:T(8,128)(2,1)S(1)}, u32[]{:S(2)}, u32[]{:S(2)}) collective-permute-start(bf16[1024,128]{1,0:T(8,128)(2,1)S(1)} %get-tuple-element.48.refs_2_.refs_6_), channel_id=1, source_target_pairs={{0,1},{1,0},{2,3},{3,2},{4,5},{5,4},{6,7},{7,6},{8,9},{9,8},{10,11... | collective-permute-start | bytes 786440 | tf_op jit(solution)/shard_map/ppermute | solution.py:410
  10.5 2.0 %collective-permute-start.1 = (bf16[1024,128]{1,0:T(8,128)(2,1)S(1)}, bf16[1024,128]{1,0:T(8,128)(2,1)S(1)}, u32[]{:S(2)}, u32[]{:S(2)}) collective-permute-start(bf16[1024,128]{1,0:T(8,128)(2,1)S(1)} %get-tuple-element.46.refs_0_), channel_id=1, source_target_pairs={{0,1},{1,0},{2,3},{3,2},{4,5},{5,4},{6,7},{7,6},{8,9},{9,8},{10,11... | collective-permute-start | bytes 786440 | tf_op jit(solution)/shard_map/ppermute | solution.py:410
  11.0 1.8 %collective-permute-start.2 = (bf16[1024,128]{1,0:T(8,128)(2,1)S(1)}, bf16[1024,128]{1,0:T(8,128)(2,1)S(1)}, u32[]{:S(2)}, u32[]{:S(2)}) collective-permute-start(bf16[1024,128]{1,0:T(8,128)(2,1)S(1)} %get-tuple-element.47.refs_1_), channel_id=1, source_target_pairs={{0,1},{1,0},{2,3},{3,2},{4,5},{5,4},{6,7},{7,6},{8,9},{9,8},{10,11... | collective-permute-start | bytes 786440 | tf_op jit(solution)/shard_map/ppermute | solution.py:410
  11.1 1.9 %copy-start = (bf16[96,128,128]{2,1,0:T(8,128)(2,1)S(1)}, bf16[96,128,128]{2,1,0:T(8,128)(2,1)}, u32[]{:S(2)}) copy-start(bf16[96,128,128]{2,1,0:T(8,128)(2,1)} %tiles_ref.11) | copy-start | bytes 9437188
  14.9 8.7 %collective-permute-start.4 = (bf16[1024,128]{1,0:T(8,128)(2,1)S(1)}, bf16[1024,128]{1,0:T(8,128)(2,1)S(1)}, u32[]{:S(2)}, u32[]{:S(2)}) collective-permute-start(bf16[1024,128]{1,0:T(8,128)(2,1)S(1)} %get-tuple-element.57), channel_id=1, source_target_pairs={{0,15},{1,2},{2,1},{3,4},{4,3},{5,6},{6,5},{7,8},{8,7},{9,10},{10,... | collective-permute-start | bytes 786440 | tf_op jit(solution)/shard_map/ppermute | solution.py:407
  16.1 20.4 %collective-permute-start.9 = (bf16[1024,128]{1,0:T(8,128)(2,1)S(1)}, bf16[1024,128]{1,0:T(8,128)(2,1)S(1)}, u32[]{:S(2)}, u32[]{:S(2)}) collective-permute-start(bf16[1024,128]{1,0:T(8,128)(2,1)S(1)} %get-tuple-element.75), channel_id=1, source_target_pairs={{0,15},{1,2},{2,1},{3,4},{4,3},{5,6},{6,5},{7,8},{8,7},{9,10},{10,... | collective-permute-start | bytes 786440 | tf_op jit(solution)/shard_map/ppermute | solution.py:407
  24.6 14.5 %collective-permute-start.5 = (bf16[1024,256]{1,0:T(8,128)(2,1)S(1)}, bf16[1024,256]{1,0:T(8,128)(2,1)S(1)}, u32[]{:S(2)}, u32[]{:S(2)}) collective-permute-start(bf16[1024,256]{1,0:T(8,128)(2,1)S(1)} %get-tuple-element.71), channel_id=1, source_target_pairs={{0,15},{1,2},{2,1},{3,4},{4,3},{5,6},{6,5},{7,8},{8,7},{9,10},{10,... | collective-permute-start | bytes 1572872 | tf_op jit(solution)/shard_map/ppermute | solution.py:407
  25.1 12.0 %collective-permute-start.7 = (bf16[1024,128]{1,0:T(8,128)(2,1)S(1)}, bf16[1024,128]{1,0:T(8,128)(2,1)S(1)}, u32[]{:S(2)}, u32[]{:S(2)}) collective-permute-start(bf16[1024,128]{1,0:T(8,128)(2,1)S(1)} %get-tuple-element.73.refs_1_.refs_5_), channel_id=1, source_target_pairs={{0,1},{1,0},{2,3},{3,2},{4,5},{5,4},{6,7},{7,6},{8,9},{9,8},{10,11... | collective-permute-start | bytes 786440 | tf_op jit(solution)/shard_map/ppermute | solution.py:410
  34.9 2.3 %collective-permute-start.8 = (bf16[1024,128]{1,0:T(8,128)(2,1)S(1)}, bf16[1024,128]{1,0:T(8,128)(2,1)S(1)}, u32[]{:S(2)}, u32[]{:S(2)}) collective-permute-start(bf16[1024,128]{1,0:T(8,128)(2,1)S(1)} %get-tuple-element.74.refs_2_.refs_6_), channel_id=1, source_target_pairs={{0,1},{1,0},{2,3},{3,2},{4,5},{5,4},{6,7},{7,6},{8,9},{9,8},{10,11... | collective-permute-start | bytes 786440 | tf_op jit(solution)/shard_map/ppermute | solution.py:410
  34.9 2.3 %collective-permute-start.6 = (bf16[1024,128]{1,0:T(8,128)(2,1)S(1)}, bf16[1024,128]{1,0:T(8,128)(2,1)S(1)}, u32[]{:S(2)}, u32[]{:S(2)}) collective-permute-start(bf16[1024,128]{1,0:T(8,128)(2,1)S(1)} %get-tuple-element.72.refs_0_.refs_4_), channel_id=1, source_target_pairs={{0,1},{1,0},{2,3},{3,2},{4,5},{5,4},{6,7},{7,6},{8,9},{9,8},{10,11... | collective-permute-start | bytes 786440 | tf_op jit(solution)/shard_map/ppermute | solution.py:410
  41.1 0.8 %copy-start.3 = (f32[1024,128]{1,0:T(8,128)}, f32[1024,128]{1,0:T(8,128)S(1)}, u32[]{:S(2)}) copy-start(f32[1024,128]{1,0:T(8,128)S(1)} %get-tuple-element.79.refs_6_) | copy-start | bytes 1572868
  41.9 0.8 %copy-start.5 = (f32[1024,128]{1,0:T(8,128)}, f32[1024,128]{1,0:T(8,128)S(1)}, u32[]{:S(2)}) copy-start(f32[1024,128]{1,0:T(8,128)S(1)} %get-tuple-element.80.refs_7_) | copy-start | bytes 1572868
  42.7 0.8 %copy-start.7 = (f32[1024,128]{1,0:T(8,128)}, f32[1024,128]{1,0:T(8,128)S(1)}, u32[]{:S(2)}) copy-start(f32[1024,128]{1,0:T(8,128)S(1)} %get-tuple-element.81.refs_8_) | copy-start | bytes 1572868
  43.5 13.9 %all-to-all-start = ((f32[16,1,128]{2,1,0:T(1,128)}), f32[16,1,128]{2,1,0:T(1,128)S(1)}, u32[]{:S(2)}, u32[]{:S(2)}) async-start(f32[16,1,128]{2,1,0:T(1,128)} %bitcast.1), calls=%async_computation | async-start | bytes 16384 | tf_op jit(solution)/shard_map/all_to_all | solution.py:516
  51.0 1.0 %copy-start.4 = (f32[1024,128]{1,0:T(8,128)S(1)}, f32[1024,128]{1,0:T(8,128)}, u32[]{:S(2)}) copy-start(f32[1024,128]{1,0:T(8,128)} %copy-done.3) | copy-start | bytes 1572868
  52.0 1.0 %copy-start.6 = (f32[1024,128]{1,0:T(8,128)S(1)}, f32[1024,128]{1,0:T(8,128)}, u32[]{:S(2)}) copy-start(f32[1024,128]{1,0:T(8,128)} %copy-done.5) | copy-start | bytes 1572868
  53.0 1.0 %copy-start.8 = (f32[1024,128]{1,0:T(8,128)S(1)}, f32[1024,128]{1,0:T(8,128)}, u32[]{:S(2)}) copy-start(f32[1024,128]{1,0:T(8,128)} %copy-done.7) | copy-start | bytes 1572868

commit v3 on v2

--- a/solution.py
+++ b/solution.py
@@ -345,37 +345,31 @@
     )
 
 
-def finish(xs, bases, mixed):
+def assemble(xs, ys):
     groups = len(xs)
     cells = xs[0].shape[0]
     width = groups * LANES
 
     def body(*refs):
-        x_refs, base_refs, mixed_refs = [refs[k * groups : (k + 1) * groups] for k in range(3)]
-        x_out, y_out, x_buf, y_buf, sems = refs[3 * groups :]
-        copies = []
-        for g in range(groups):
-            y_new = base_refs[g][...] - 0.2 * mixed_refs[g][...]
-            y_buf[g] = y_new
-            x_buf[g] = jnp.clip(x_refs[g][...] + 0.5 * y_new, -1.0, 1.0)
-            for k, (buf, out) in enumerate(((y_buf, y_out), (x_buf, x_out))):
-                copies.append(
-                    pltpu.make_async_copy(buf.at[g], out.at[:, lanes(g)], sems.at[g, k])
-                )
-                copies[-1].start()
+        outs, sems = refs[2 * groups : -1], refs[-1]
+        copies = [
+            pltpu.make_async_copy(
+                refs[k * groups + g], outs[k].at[:, lanes(g)], sems.at[k * groups + g]
+            )
+            for g in range(groups)
+            for k in range(2)
+        ]
+        for copy in copies:
+            copy.start()
         for copy in copies:
             copy.wait()
 
     return call(
         body,
-        vmem(*xs, *bases, *mixed),
+        vmem(*xs, *ys),
         [((cells, width), F32, pltpu.HBM)] * 2,
-        [
-            pltpu.VMEM((groups, cells, LANES), F32),
-            pltpu.VMEM((groups, cells, LANES), F32),
-            pltpu.SemaphoreType.DMA((groups, 2)),
-        ],
-        "finish",
+        [pltpu.SemaphoreType.DMA((2 * groups,))],
+        "assemble",
     )
 
 
@@ -487,35 +481,38 @@
     def last_work(done, ins, outs):
         held = {n: field.astype(BF16) for n, field in zip(piece, done)}
         held[0] = ins[1][...]
+        x_refs, base_refs, rounded_refs = [ins[2 + k * groups : 2 + (k + 1) * groups] for k in range(3)]
         sums = []
         for t in every:
             value = mixed_of(held, ins[0], t, channels)
-            outs[t][...] = value
-            sums.append(jnp.sum(ins[2 + t][...].astype(F32) * value, axis=0, keepdims=True))
-        row = jnp.concatenate(sums, axis=1)
-        lane = lax.broadcasted_iota(jnp.int32, (1, width), 1)
-        place = lax.broadcasted_iota(jnp.int32, (1, LANES), 1)
-        total = jnp.zeros((1, LANES), F32)
-        for r in range(replicas):
-            inside = (lane >= r * channels) & (lane < (r + 1) * channels)
-            value = jnp.sum(jnp.where(inside, row, 0.0), axis=1, keepdims=True)
-            total = jnp.where(place == r, value, total)
-        outs[groups][...] = jnp.broadcast_to(total, (ring, LANES))
-
-    *mixed, partial = far_fields(
+            y_new = base_refs[t][...] - 0.2 * value
+            outs[t][...] = jnp.clip(x_refs[t][...] + 0.5 * y_new, -1.0, 1.0)
+            outs[groups + t][...] = y_new
+            sums.append(jnp.sum(rounded_refs[t][...].astype(F32) * value, axis=0, keepdims=True))
+        row = jnp.broadcast_to(jnp.concatenate(sums, axis=1), (replicas, width))
+        lane = lax.broadcasted_iota(jnp.int32, (replicas, width), 1)
+        first = lax.broadcasted_iota(jnp.int32, (replicas, width), 0) * channels
+        inside = (lane >= first) & (lane < first + channels)
+        total = jnp.sum(jnp.where(inside, row, 0.0), axis=1, keepdims=True)
+        place = lax.broadcasted_iota(jnp.int32, (replicas, LANES), 1)
+        which = lax.broadcasted_iota(jnp.int32, (replicas, LANES), 0)
+        flat = jnp.sum(jnp.where(place == which, total, 0.0), axis=0, keepdims=True)
+        outs[2 * groups][...] = jnp.broadcast_to(flat, (ring, LANES))
+
+    *results, partial = far_fields(
         lists,
         tile_values,
         near[1:],
         new_fars[1],
-        [mixing, near[0], *owns, base[0]],
-        [(wide, F32)] * groups + [((ring, LANES), F32)],
+        [mixing, near[0], *xs, *base, *owns],
+        [(wide, F32)] * (2 * groups) + [((ring, LANES), F32)],
         last_work,
         "far_second_1",
     )
 
     everyone = lax.all_to_all(partial, RING, 0, 0, tiled=True)
     energy = jnp.sum(everyone, axis=0)[:replicas] / jnp.sqrt(jnp.float32(cells * ring * channels))
-    x_new, y_new = finish(xs, base, mixed)
+    x_new, y_new = assemble(results[:groups], results[groups:])
     return (x_new, y_new, energy)
 
 

time: 58.3 us -> 56.2 us (0.964)
  local copies, waits for them, and re-layouts: 5.76 us -> 0.45 us
  waiting for transfers between devices: 4.6 us -> 7.1 us
  starting transfers between devices: 29.2 us -> 31.4 us
  Pallas kernels: 16.3 us -> 15.3 us
    unnamed x26 -> x14, local copies, waits for them, and re-layouts: 5.76 us -> 0.45 us
    all_to_all x1, waiting for transfers between devices: 1.45 us -> 4.69 us  [local(): everyone = lax.all_to_all(partial, RING, 0, 0, tiled=True)]
    pallas_call x11, Pallas kernels: 16.3 us -> 15.3 us  [call(): pl.pallas_call(body, in_specs=[pl.BlockSpec(memory_space=pl.ANY if s is p...]
    ppermute x4, starting transfers between devices: 10.8 us -> 11.8 us  [far_swap(): return lax.ppermute(mine, RING, off_chip)]
    all_to_all x1, starting transfers between devices: 7.47 us -> 8.35 us  [local(): everyone = lax.all_to_all(partial, RING, 0, 0, tiled=True)]
  transfers between devices with their start and end apart: 11 -> 11, of which waited for: 3 -> 3; matrix products, arithmetic and copies ran while one was open for 0% -> 0% of each run, Pallas kernels for 22% -> 20%
where the time goes in v3:
time: 56.2 us
  starting transfers between devices  31.4 us (56%)
  Pallas kernels  15.3 us (27%)
  waiting for transfers between devices  7.1 us (13%)
  between operations  1.5 us (3%)
    pallas_call x11, Pallas kernels, call(): pl.pallas_call(body, in_specs=[pl.BlockSpec(memory_space=pl.ANY if s is p...  15.3 us
    ppermute x4, starting transfers between devices, far_swap(): return lax.ppermute(mine, RING, off_chip)  11.8 us
    ppermute x6, starting transfers between devices, near_swap(): return lax.ppermute(mine, RING, on_chip)  11.2 us
    all_to_all x1, starting transfers between devices, local(): everyone = lax.all_to_all(partial, RING, 0, 0, tiled=True)  8.35 us
    all_to_all x1, waiting for transfers between devices, local(): everyone = lax.all_to_all(partial, RING, 0, 0, tiled=True)  4.69 us
    ppermute x4, waiting for transfers between devices, far_swap(): return lax.ppermute(mine, RING, off_chip)  2.32 us
  transfers between devices with their start and end apart: 11, of which 3 were waited for; matrix products, arithmetic and copies ran while one was open for 0% of the time, Pallas kernels for 20%

profile of v3, /device:TPU:0, one launch (start us, length us, event | category | flops | bytes accessed | tf_op | source)
XLA Modules:
  0.0 56.2 jit_solution(6081070721537300342)
XLA Ops:
  0.6 0.0 copy-start.2
  0.6 0.0 copy-start.3
  0.7 1.4 %load_first.1 = (f32[1024,128]{1,0:T(8,128)S(1)}, f32[1024,128]{1,0:T(8,128)S(1)}, bf16[1024,128]{1,0:T(8,128)(2,1)S(1)}, bf16[1024,128]{1,0:T(8,128)(2,1)S(1)}, bf16[1024,256]{1,0:T(8,128)(2,1)S(1)}) custom-call(f32[1024,384]{1,0:T(8,128)} %x_ref.3), custom_call_target="tpu_custom_call" | custom-call | flops 1000 | bytes 1000 | tf_op jit(solution)/shard_map/load_first/pallas_call | solution.py:21
  2.1 5.5 %collective-permute-start.4 = (bf16[1024,256]{1,0:T(8,128)(2,1)S(1)}, bf16[1024,256]{1,0:T(8,128)(2,1)S(1)}, u32[]{:S(2)}, u32[]{:S(2)}) collective-permute-start(bf16[1024,256]{1,0:T(8,128)(2,1)S(1)} %get-tuple-element.47._), channel_id=1, source_target_pairs={{0,15},{1,2},{2,1},{3,4},{4,3},{5,6},{6,5},{7,8},{8,7},{9,10},{10,... | collective-permute-start | bytes 1572872 | tf_op jit(solution)/shard_map/ppermute | solution.py:401
  7.6 0.0 collective-permute-start
  7.6 0.5 collective-permute-start.1
  8.8 1.3 %make_lists.1 = (s32[214]{0:T(256)S(4)}, f32[1024,128]{1,0:T(8,128)S(1)}, bf16[1024,128]{1,0:T(8,128)(2,1)S(1)}) custom-call(s32[96]{0:T(128)S(1)} %copy-done.5, s32[96]{0:T(128)S(1)} %copy-done.6, s32[1]{0:T(128)S(6)} %copy.13.count_hbm, f32[1024,384]{1,0:T(8,128)} %x_ref.3, bf16[1024,256]{1,0:T(8,128)(2,1)S(1)} %get-tuple-element.47._), custom_call_target="tpu_custom_call" | custom-call | flops 1000 | bytes 1000 | tf_op jit(solution)/shard_map/make_lists/pallas_call | solution.py:21
  10.1 0.1 collective-permute-start.2
  10.3 0.0 copy-start
  10.3 1.4 %first_base.1 = (f32[1024,128]{1,0:T(8,128)S(1)}, f32[1024,128]{1,0:T(8,128)S(1)}, f32[1024,128]{1,0:T(8,128)S(1)}, bf16[384,384]{1,0:T(8,128)(2,1)S(1)}) custom-call(f32[1024,128]{1,0:T(8,128)S(1)} %get-tuple-element.52.refs_0_.refs_4_, f32[1024,128]{1,0:T(8,128)S(1)} %get-tuple-element.53.refs_1_.refs_5_, ...), custom_call_target="tpu_custom_call" | custom-call | flops 1000 | bytes 1000 | tf_op jit(solution)/shard_map/first_base/pallas_call | solution.py:21
  11.7 0.1 collective-permute-done.2.refs_5_
  11.7 0.4 copy-done
  12.2 1.3 %near_first.1 = (f32[1024,128]{1,0:T(8,128)S(1)}, f32[1024,128]{1,0:T(8,128)S(1)}, f32[1024,128]{1,0:T(8,128)S(1)}, bf16[1024,128]{1,0:T(8,128)(2,1)S(1)}) custom-call(s32[214]{0:T(256)S(4)} %get-tuple-element.48.list_ref, bf16[96,128,128]{2,1,0:T(8,128)(2,1)S(1)} %copy-done, bf16[1024,128]{1,0:T(8,128)(2,1)S(1)} %get-tuple-element.49.refs_0_, ...), custom_call_target="tpu_custom_call" | custom-call | flops 1000 | bytes 1000 | tf_op jit(solution)/shard_map/near_first/pallas_call | solution.py:21
  13.4 1.6 %collective-permute-start.3 = (bf16[1024,128]{1,0:T(8,128)(2,1)S(1)}, bf16[1024,128]{1,0:T(8,128)(2,1)S(1)}, u32[]{:S(2)}, u32[]{:S(2)}) collective-permute-start(bf16[1024,128]{1,0:T(8,128)(2,1)S(1)} %get-tuple-element.56), channel_id=1, source_target_pairs={{0,15},{1,2},{2,1},{3,4},{4,3},{5,6},{6,5},{7,8},{8,7},{9,10},{10,... | collective-permute-start | bytes 786440 | tf_op jit(solution)/shard_map/ppermute | solution.py:401
  15.1 1.2 %far_first_0.1 = (f32[1024,128]{1,0:T(8,128)S(1)}, f32[1024,128]{1,0:T(8,128)S(1)}, bf16[1024,128]{1,0:T(8,128)(2,1)S(1)}, bf16[1024,128]{1,0:T(8,128)(2,1)S(1)}...) custom-call(s32[214]{0:T(256)S(4)} %get-tuple-element.48.list_ref, bf16[96,128,128]{2,1,0:T(8,128)(2,1)S(1)} %copy-done, ...), custom_call_target="tpu_custom_call" | custom-call | flops 1000 | bytes 1000 | tf_op jit(solution)/shard_map/far_first_0/pallas_call | solution.py:21
  16.3 3.5 %collective-permute-start.9 = (bf16[1024,128]{1,0:T(8,128)(2,1)S(1)}, bf16[1024,128]{1,0:T(8,128)(2,1)S(1)}, u32[]{:S(2)}, u32[]{:S(2)}) collective-permute-start(bf16[1024,128]{1,0:T(8,128)(2,1)S(1)} %get-tuple-element.69), channel_id=1, source_target_pairs={{0,15},{1,2},{2,1},{3,4},{4,3},{5,6},{6,5},{7,8},{8,7},{9,10},{10,... | collective-permute-start | bytes 786440 | tf_op jit(solution)/shard_map/ppermute | solution.py:401
  19.8 2.3 %collective-permute-done.3.far_ref = bf16[1024,128]{1,0:T(8,128)(2,1)S(1)} collective-permute-done((bf16[1024,128]{1,0:T(8,128)(2,1)S(1)}, bf16[1024,128]{1,0:T(8,128)(2,1)S(1)}, u32[]{:S(2)}, u32[]{:S(2)}) %collective-permute-start.3) | collective-permute-done | bytes 262176 | tf_op jit(solution)/shard_map/ppermute | solution.py:401
  22.1 1.3 %far_first_1.1 = (f32[1024,128]{1,0:T(8,128)S(1)}, f32[1024,128]{1,0:T(8,128)S(1)}, bf16[1024,128]{1,0:T(8,128)(2,1)S(1)}, f32[1024,128]{1,0:T(8,128)S(1)}, f32[...) custom-call(s32[214]{0:T(256)S(4)} %get-tuple-element.48.list_ref, ...), custom_call_target="tpu_custom_call" | custom-call | flops 1000 | bytes 1000 | tf_op jit(solution)/shard_map/far_first_1/pallas_call | solution.py:21
  23.4 1.2 %collective-permute-start.5 = (bf16[1024,256]{1,0:T(8,128)(2,1)S(1)}, bf16[1024,256]{1,0:T(8,128)(2,1)S(1)}, u32[]{:S(2)}, u32[]{:S(2)}) collective-permute-start(bf16[1024,256]{1,0:T(8,128)(2,1)S(1)} %get-tuple-element.65), channel_id=1, source_target_pairs={{0,15},{1,2},{2,1},{3,4},{4,3},{5,6},{6,5},{7,8},{8,7},{9,10},{10,... | collective-permute-start | bytes 1572872 | tf_op jit(solution)/shard_map/ppermute | solution.py:401
  24.6 10.1 %collective-permute-start.7 = (bf16[1024,128]{1,0:T(8,128)(2,1)S(1)}, bf16[1024,128]{1,0:T(8,128)(2,1)S(1)}, u32[]{:S(2)}, u32[]{:S(2)}) collective-permute-start(bf16[1024,128]{1,0:T(8,128)(2,1)S(1)} %get-tuple-element.67.refs_1_.refs_11_), channel_id=1, source_target_pairs={{0,1},{1,0},{2,3},{3,2},{4,5},{5,4},{6,7},{7,6},{8,9},{9,8},{10,11... | collective-permute-start | bytes 786440 | tf_op jit(solution)/shard_map/ppermute | solution.py:404
  34.7 0.0 collective-permute-start.8
  34.7 0.5 collective-permute-start.6
  35.2 1.2 %second_base.1 = (f32[1024,128]{1,0:T(8,128)S(1)}, f32[1024,128]{1,0:T(8,128)S(1)}, f32[1024,128]{1,0:T(8,128)S(1)}) custom-call(f32[1024,128]{1,0:T(8,128)S(1)} %get-tuple-element.73.refs_0_.refs_4_, f32[1024,128]{1,0:T(8,128)S(1)} %get-tuple-element.74.refs_1_.refs_5_, f32[1024,128]{1,0:T(8,128)S(1)} %get-tuple-element.75.refs_2_.refs_6_, ...), custom_call_target="tpu_custom_call" | custom-call | flops 1000 | bytes 1000 | tf_op jit(solution)/shard_map/second_base/pallas_call | solution.py:21
  36.4 0.8 %far_second_0.1.refs_6_ = f32[1024,128]{1,0:T(8,128)S(1)} custom-call(s32[214]{0:T(256)S(4)} %get-tuple-element.48.list_ref, bf16[96,128,128]{2,1,0:T(8,128)(2,1)S(1)} %copy-done, bf16[1024,128]{1,0:T(8,128)(2,1)S(1)} %collective-permute-done.9.far_ref), custom_call_target="tpu_custom_call" | custom-call | flops 4000000000 | bytes 1000 | tf_op jit(solution)/shard_map/far_second_0/pallas_call | solution.py:21
  37.2 0.0 collective-permute-done.7.refs_4_
  37.2 0.0 collective-permute-done.8.refs_5_
  37.2 1.2 %near_second.1 = (bf16[1024,128]{1,0:T(8,128)(2,1)S(1)}, f32[1024,128]{1,0:T(8,128)S(1)}, f32[1024,128]{1,0:T(8,128)S(1)}) custom-call(s32[214]{0:T(256)S(4)} %get-tuple-element.48.list_ref, bf16[96,128,128]{2,1,0:T(8,128)(2,1)S(1)} %copy-done, bf16[1024,128]{1,0:T(8,128)(2,1)S(1)} %get-tuple-element.66.refs_0_.refs_10_, ...), custom_call_target="tpu_custom_call" | custom-call | flops 1000 | bytes 1000 | tf_op jit(solution)/shard_map/near_second/pallas_call | solution.py:21
  38.5 2.4 %far_second_1.1 = (f32[1024,128]{1,0:T(8,128)S(1)}, f32[1024,128]{1,0:T(8,128)S(1)}, f32[1024,128]{1,0:T(8,128)S(1)}, f32[1024,128]{1,0:T(8,128)S(1)}, f32[1024,...) custom-call(s32[214]{0:T(256)S(4)} %get-tuple-element.48.list_ref, bf16[96,128,128]{2,1,0:T(8,128)(2,1)S(1)} %copy-done, ...), custom_call_target="tpu_custom_call" | custom-call | flops 1000 | bytes 1000 | tf_op jit(solution)/shard_map/far_second_1/pallas_call | solution.py:21
  40.9 8.4 %all-to-all-start = ((f32[16,1,128]{2,1,0:T(1,128)}), f32[16,1,128]{2,1,0:T(1,128)S(1)}, u32[]{:S(2)}, u32[]{:S(2)}) async-start(f32[16,1,128]{2,1,0:T(1,128)} %bitcast.1), calls=%async_computation | async-start | bytes 16384 | tf_op jit(solution)/shard_map/all_to_all | solution.py:513
  49.3 1.7 %assemble.1 = (f32[1024,384]{1,0:T(8,128)}, f32[1024,384]{1,0:T(8,128)}) custom-call(f32[1024,128]{1,0:T(8,128)S(1)} %get-tuple-element.82.refs_0_, f32[1024,128]{1,0:T(8,128)S(1)} %get-tuple-element.83.refs_1_, f32[1024,128]{1,0:T(8,128)S(1)} %get-tuple-element.84.refs_2_, f32[1024,128]{1,0:T(8,128)S(1)} %get-tuple-element.85.refs_3_, ...), custom_call_target="tpu_custom_call" | custom-call | flops 1000 | bytes 1000 | tf_op jit(solution)/shard_map/assemble/pallas_call | solution.py:21
  51.0 4.7 %all-to-all-done = f32[16,1,128]{2,1,0:T(1,128)S(1)} async-done(((f32[16,1,128]{2,1,0:T(1,128)}), f32[16,1,128]{2,1,0:T(1,128)S(1)}, u32[]{:S(2)}, u32[]{:S(2)}) %all-to-all-start) | async-done | bytes 8224 | tf_op jit(solution)/shard_map/all_to_all | solution.py:513
  55.7 0.5 slice_multiply_fusion
  (17 shorter events, 0.1 us)
Async XLA Ops:
  0.6 9.6 %copy-start.2 = (bf16[384,384]{1,0:T(8,128)(2,1)S(1)}, bf16[384,384]{1,0:T(8,128)(2,1)}, u32[]{:S(2)}) copy-start(bf16[384,384]{1,0:T(8,128)(2,1)} %constant.9.clone.refs_4_.refs_6_) | copy-start | bytes 884740
  0.6 9.6 %copy-start.3 = (bf16[384,48]{1,0:T(8,128)(2,1)S(1)}, bf16[384,48]{1,0:T(8,128)(2,1)}, u32[]{:S(2)}) copy-start(bf16[384,48]{1,0:T(8,128)(2,1)} %constant.10.clone.refs_5_) | copy-start | bytes 110596
  0.7 8.1 %copy-start.6 = (s32[96]{0:T(128)S(1)}, s32[96]{0:T(128)}, u32[]{:S(2)}) copy-start(s32[96]{0:T(128)} %cols_hbm.1) | copy-start | bytes 1156
  0.7 8.1 %copy-start.5 = (s32[96]{0:T(128)S(1)}, s32[96]{0:T(128)}, u32[]{:S(2)}) copy-start(s32[96]{0:T(128)} %rows_hbm.1) | copy-start | bytes 1156
  0.7 9.6 %copy-start.4 = (bf16[48,48]{1,0:T(8,128)(2,1)S(1)}, bf16[48,48]{1,0:T(8,128)(2,1)}, u32[]{:S(2)}) copy-start(bf16[48,48]{1,0:T(8,128)(2,1)} %refs_6_.2) | copy-start | bytes 13828
  0.7 9.6 %copy-start.1 = (f32[1024,384]{1,0:T(8,128)S(1)}, f32[1024,384]{1,0:T(8,128)}, u32[]{:S(2)}) copy-start(f32[1024,384]{1,0:T(8,128)} %refs_3_.1) | copy-start | bytes 4718596
  2.1 13.0 %collective-permute-start.4 = (bf16[1024,256]{1,0:T(8,128)(2,1)S(1)}, bf16[1024,256]{1,0:T(8,128)(2,1)S(1)}, u32[]{:S(2)}, u32[]{:S(2)}) collective-permute-start(bf16[1024,256]{1,0:T(8,128)(2,1)S(1)} %get-tuple-element.47._), channel_id=1, source_target_pairs={{0,15},{1,2},{2,1},{3,4},{4,3},{5,6},{6,5},{7,8},{8,7},{9,10},{10,... | collective-permute-start | bytes 1572872 | tf_op jit(solution)/shard_map/ppermute | solution.py:401
  7.6 4.0 %collective-permute-start = (bf16[1024,128]{1,0:T(8,128)(2,1)S(1)}, bf16[1024,128]{1,0:T(8,128)(2,1)S(1)}, u32[]{:S(2)}, u32[]{:S(2)}) collective-permute-start(bf16[1024,128]{1,0:T(8,128)(2,1)S(1)} %get-tuple-element.49.refs_0_), channel_id=1, source_target_pairs={{0,1},{1,0},{2,3},{3,2},{4,5},{5,4},{6,7},{7,6},{8,9},{9,8},{10,11... | collective-permute-start | bytes 786440 | tf_op jit(solution)/shard_map/ppermute | solution.py:404
  7.6 4.0 %collective-permute-start.1 = (bf16[1024,128]{1,0:T(8,128)(2,1)S(1)}, bf16[1024,128]{1,0:T(8,128)(2,1)S(1)}, u32[]{:S(2)}, u32[]{:S(2)}) collective-permute-start(bf16[1024,128]{1,0:T(8,128)(2,1)S(1)} %get-tuple-element.50.refs_1_), channel_id=1, source_target_pairs={{0,1},{1,0},{2,3},{3,2},{4,5},{5,4},{6,7},{7,6},{8,9},{9,8},{10,11... | collective-permute-start | bytes 786440 | tf_op jit(solution)/shard_map/ppermute | solution.py:404
  10.1 1.6 %collective-permute-start.2 = (bf16[1024,128]{1,0:T(8,128)(2,1)S(1)}, bf16[1024,128]{1,0:T(8,128)(2,1)S(1)}, u32[]{:S(2)}, u32[]{:S(2)}) collective-permute-start(bf16[1024,128]{1,0:T(8,128)(2,1)S(1)} %get-tuple-element.51.refs_2_.refs_6_), channel_id=1, source_target_pairs={{0,1},{1,0},{2,3},{3,2},{4,5},{5,4},{6,7},{7,6},{8,9},{9,8},{10,11... | collective-permute-start | bytes 786440 | tf_op jit(solution)/shard_map/ppermute | solution.py:404
  10.3 1.9 %copy-start = (bf16[96,128,128]{2,1,0:T(8,128)(2,1)S(1)}, bf16[96,128,128]{2,1,0:T(8,128)(2,1)}, u32[]{:S(2)}) copy-start(bf16[96,128,128]{2,1,0:T(8,128)(2,1)} %tiles_ref.11) | copy-start | bytes 9437188
  13.4 8.7 %collective-permute-start.3 = (bf16[1024,128]{1,0:T(8,128)(2,1)S(1)}, bf16[1024,128]{1,0:T(8,128)(2,1)S(1)}, u32[]{:S(2)}, u32[]{:S(2)}) collective-permute-start(bf16[1024,128]{1,0:T(8,128)(2,1)S(1)} %get-tuple-element.56), channel_id=1, source_target_pairs={{0,15},{1,2},{2,1},{3,4},{4,3},{5,6},{6,5},{7,8},{8,7},{9,10},{10,... | collective-permute-start | bytes 786440 | tf_op jit(solution)/shard_map/ppermute | solution.py:401
  16.3 20.0 %collective-permute-start.9 = (bf16[1024,128]{1,0:T(8,128)(2,1)S(1)}, bf16[1024,128]{1,0:T(8,128)(2,1)S(1)}, u32[]{:S(2)}, u32[]{:S(2)}) collective-permute-start(bf16[1024,128]{1,0:T(8,128)(2,1)S(1)} %get-tuple-element.69), channel_id=1, source_target_pairs={{0,15},{1,2},{2,1},{3,4},{4,3},{5,6},{6,5},{7,8},{8,7},{9,10},{10,... | collective-permute-start | bytes 786440 | tf_op jit(solution)/shard_map/ppermute | solution.py:401
  23.4 15.1 %collective-permute-start.5 = (bf16[1024,256]{1,0:T(8,128)(2,1)S(1)}, bf16[1024,256]{1,0:T(8,128)(2,1)S(1)}, u32[]{:S(2)}, u32[]{:S(2)}) collective-permute-start(bf16[1024,256]{1,0:T(8,128)(2,1)S(1)} %get-tuple-element.65), channel_id=1, source_target_pairs={{0,15},{1,2},{2,1},{3,4},{4,3},{5,6},{6,5},{7,8},{8,7},{9,10},{10,... | collective-permute-start | bytes 1572872 | tf_op jit(solution)/shard_map/ppermute | solution.py:401
  24.6 12.6 %collective-permute-start.7 = (bf16[1024,128]{1,0:T(8,128)(2,1)S(1)}, bf16[1024,128]{1,0:T(8,128)(2,1)S(1)}, u32[]{:S(2)}, u32[]{:S(2)}) collective-permute-start(bf16[1024,128]{1,0:T(8,128)(2,1)S(1)} %get-tuple-element.67.refs_1_.refs_11_), channel_id=1, source_target_pairs={{0,1},{1,0},{2,3},{3,2},{4,5},{5,4},{6,7},{7,6},{8,9},{9,8},{10,11... | collective-permute-start | bytes 786440 | tf_op jit(solution)/shard_map/ppermute | solution.py:404
  34.7 2.5 %collective-permute-start.8 = (bf16[1024,128]{1,0:T(8,128)(2,1)S(1)}, bf16[1024,128]{1,0:T(8,128)(2,1)S(1)}, u32[]{:S(2)}, u32[]{:S(2)}) collective-permute-start(bf16[1024,128]{1,0:T(8,128)(2,1)S(1)} %get-tuple-element.68.refs_2_.refs_12_), channel_id=1, source_target_pairs={{0,1},{1,0},{2,3},{3,2},{4,5},{5,4},{6,7},{7,6},{8,9},{9,8},{10,11... | collective-permute-start | bytes 786440 | tf_op jit(solution)/shard_map/ppermute | solution.py:404
  34.7 2.5 %collective-permute-start.6 = (bf16[1024,128]{1,0:T(8,128)(2,1)S(1)}, bf16[1024,128]{1,0:T(8,128)(2,1)S(1)}, u32[]{:S(2)}, u32[]{:S(2)}) collective-permute-start(bf16[1024,128]{1,0:T(8,128)(2,1)S(1)} %get-tuple-element.66.refs_0_.refs_10_), channel_id=1, source_target_pairs={{0,1},{1,0},{2,3},{3,2},{4,5},{5,4},{6,7},{7,6},{8,9},{9,8},{10,11... | collective-permute-start | bytes 786440 | tf_op jit(solution)/shard_map/ppermute | solution.py:404
  40.9 14.8 %all-to-all-start = ((f32[16,1,128]{2,1,0:T(1,128)}), f32[16,1,128]{2,1,0:T(1,128)S(1)}, u32[]{:S(2)}, u32[]{:S(2)}) async-start(f32[16,1,128]{2,1,0:T(1,128)} %bitcast.1), calls=%async_computation | async-start | bytes 16384 | tf_op jit(solution)/shard_map/all_to_all | solution.py:513

commit v4 on v2

--- a/solution.py
+++ b/solution.py
@@ -17,7 +17,7 @@
 RING = ("row", "col")
 
 
-def call(body, ins, outs, scratch, name, flops=0):
+def call(body, ins, outs, scratch, name, flops=0, aliases=()):
     return pl.pallas_call(
         body,
         in_specs=[pl.BlockSpec(memory_space=pl.ANY if s is pltpu.HBM else s) for _, s in ins],
@@ -27,6 +27,7 @@
             for dims, kind, s in outs
         ],
         scratch_shapes=scratch,
+        input_output_aliases=dict(aliases),
         compiler_params=pltpu.CompilerParams(vmem_limit_bytes=VMEM_LIMIT),
         cost_estimate=pl.CostEstimate(
             flops=int(flops) or 1000, bytes_accessed=1000, transcendentals=0
@@ -272,7 +273,7 @@
     return outs[:groups], outs[groups:]
 
 
-def far_fields(lists, tiles, nears, far, extra, outs_of, work, name, flops=0):
+def far_fields(lists, tiles, nears, far, extra, outs_of, work, name, flops=0, through=()):
     slots, tile, _ = tiles.shape
     cells, width = far.shape
     per = cells // tile
@@ -282,7 +283,8 @@
 
     def body(list_ref, tiles_ref, far_ref, *refs):
         near_refs, extra_refs = refs[:m], refs[m : m + len(extra)]
-        out_refs, (field, window) = refs[m + len(extra) : -2], refs[-2:]
+        through_refs = refs[m + len(extra) : m + len(extra) + len(through)]
+        out_refs, (field, window) = refs[m + len(extra) + len(through) : -2], refs[-2:]
         window[:per] = far_ref[...].reshape(per, tile, width)
         window[per] = jnp.zeros((tile, width), BF16)
         if not near_refs:
@@ -290,15 +292,17 @@
         for i, ref in enumerate(near_refs):
             field[:per, :, lanes(i)] = ref[...].reshape(per, tile, LANES)
         add_pairs(1, list_ref, tiles_ref, field, window, pairs)
-        work([field[:per, :, lanes(i)].reshape(cells, LANES) for i in range(n)], extra_refs, out_refs)
+        done = [field[:per, :, lanes(i)].reshape(cells, LANES) for i in range(n)]
+        work(done, [*extra_refs, *through_refs], out_refs[: len(outs_of)])
 
     return call(
         body,
-        [(lists, pltpu.SMEM)] + vmem(tiles, far, *nears, *extra),
-        [(*out, pltpu.VMEM) for out in outs_of],
+        [(lists, pltpu.SMEM)] + vmem(tiles, far, *nears, *extra, *through),
+        [(*out, pltpu.VMEM) for out in outs_of] + [(a.shape, a.dtype, pltpu.VMEM) for a in through],
         [pltpu.VMEM((per + 1, tile, width), F32), pltpu.VMEM((per + 1, tile, width), BF16)],
         name,
         flops,
+        [(3 + m + len(extra) + i, len(outs_of) + i) for i in range(len(through))],
     )
 
 
@@ -328,34 +332,47 @@
     return outs[:groups], outs[groups]
 
 
-def second_base(xs, ys, same, channels):
-    groups = len(xs)
-
-    def body(*refs):
-        x = [ref[...] for ref in refs[:groups]]
-        y = [ref[...] for ref in refs[groups : 2 * groups]]
-        bases_into(refs[2 * groups + 1 :], x, y, refs[2 * groups], 1, channels)
-
-    return call(
-        body,
-        vmem(*xs, *ys, same),
-        [(xs[0].shape, F32, pltpu.VMEM)] * groups,
-        [],
-        "second_base",
-    )
-
-
-def finish(xs, bases, mixed):
+def second_base(xs, ys, rounded, same, mixing, channels):
     groups = len(xs)
     cells = xs[0].shape[0]
     width = groups * LANES
 
     def body(*refs):
-        x_refs, base_refs, mixed_refs = [refs[k * groups : (k + 1) * groups] for k in range(3)]
-        x_out, y_out, x_buf, y_buf, sems = refs[3 * groups :]
+        x, y, r = [[ref[...] for ref in refs[k * groups : (k + 1) * groups]] for k in range(3)]
+        same_ref, mixing_ref = refs[3 * groups : 3 * groups + 2]
+        outs = refs[3 * groups + 2 :]
+        bases_into(outs[:groups], x, y, same_ref, 1, channels)
+        for g in range(groups):
+            near = spanned(g, channels, width)
+            outs[groups + g][...] = lax.dot_general(
+                jnp.concatenate([r[n] for n in near], axis=1),
+                mixing_ref[lanes(g), span_lanes(near)],
+                (((1,), (1,)), ((), ())),
+                preferred_element_type=F32,
+            )
+
+    outs = call(
+        body,
+        vmem(*xs, *ys, *rounded, same, mixing),
+        [((cells, LANES), F32, pltpu.VMEM)] * (2 * groups),
+        [],
+        "second_base",
+    )
+    return outs[:groups], outs[groups:]
+
+
+def finish(fields, xs, bases, mixing, channels):
+    groups = len(xs)
+    cells = xs[0].shape[0]
+    width = groups * LANES
+
+    def body(*refs):
+        field_refs, x_refs, base_refs = [refs[k * groups : (k + 1) * groups] for k in range(3)]
+        mixing_ref, x_out, y_out, x_buf, y_buf, sems = refs[3 * groups :]
+        held = [ref[...] for ref in field_refs]
         copies = []
         for g in range(groups):
-            y_new = base_refs[g][...] - 0.2 * mixed_refs[g][...]
+            y_new = base_refs[g][...] - 0.2 * mixed_of(held, mixing_ref, g, channels)
             y_buf[g] = y_new
             x_buf[g] = jnp.clip(x_refs[g][...] + 0.5 * y_new, -1.0, 1.0)
             for k, (buf, out) in enumerate(((y_buf, y_out), (x_buf, x_out))):
@@ -368,7 +385,7 @@
 
     return call(
         body,
-        vmem(*xs, *bases, *mixed),
+        vmem(*fields, *xs, *bases, mixing),
         [((cells, width), F32, pltpu.HBM)] * 2,
         [
             pltpu.VMEM((groups, cells, LANES), F32),
@@ -481,41 +498,49 @@
         lists, tile_values, [], new_fars[0], [], [(wide, F32)], keep, "far_second_0", NEAR_FLOPS
     )
     near, _ = near_fields(lists, tile_values, owns, others, part, [], [], 0, "near_second")
-    base = second_base(xs, ys, same, channels)
+    base, weights = second_base(xs, ys, owns, same, mixing, channels)
     piece = second_pieces[1]
 
     def last_work(done, ins, outs):
-        held = {n: field.astype(BF16) for n, field in zip(piece, done)}
-        held[0] = ins[1][...]
-        sums = []
-        for t in every:
-            value = mixed_of(held, ins[0], t, channels)
-            outs[t][...] = value
-            sums.append(jnp.sum(ins[2 + t][...].astype(F32) * value, axis=0, keepdims=True))
-        row = jnp.concatenate(sums, axis=1)
-        lane = lax.broadcasted_iota(jnp.int32, (1, width), 1)
-        place = lax.broadcasted_iota(jnp.int32, (1, LANES), 1)
-        total = jnp.zeros((1, LANES), F32)
-        for r in range(replicas):
-            inside = (lane >= r * channels) & (lane < (r + 1) * channels)
-            value = jnp.sum(jnp.where(inside, row, 0.0), axis=1, keepdims=True)
-            total = jnp.where(place == r, value, total)
-        outs[groups][...] = jnp.broadcast_to(total, (ring, LANES))
-
-    *mixed, partial = far_fields(
+        held = [ins[groups][...]] + [field.astype(BF16) for field in done]
+        for out, field in zip(outs, held[1:]):
+            out[...] = field
+        row = jnp.concatenate(
+            [
+                jnp.sum(field.astype(F32) * ref[...], axis=0, keepdims=True)
+                for field, ref in zip(held, ins[:groups])
+            ],
+            axis=1,
+        )
+        row = jnp.broadcast_to(row, (replicas, width))
+        lane = lax.broadcasted_iota(jnp.int32, (replicas, width), 1)
+        first = lax.broadcasted_iota(jnp.int32, (replicas, width), 0) * channels
+        inside = (lane >= first) & (lane < first + channels)
+        total = jnp.sum(jnp.where(inside, row, 0.0), axis=1, keepdims=True)
+        place = lax.broadcasted_iota(jnp.int32, (replicas, LANES), 1)
+        which = lax.broadcasted_iota(jnp.int32, (replicas, LANES), 0)
+        flat = jnp.sum(jnp.where(place == which, total, 0.0), axis=0, keepdims=True)
+        outs[len(piece)][...] = jnp.broadcast_to(flat, (ring, LANES))
+
+    results = far_fields(
         lists,
         tile_values,
         near[1:],
         new_fars[1],
-        [mixing, near[0], *owns, base[0]],
-        [(wide, F32)] * groups + [((ring, LANES), F32)],
+        weights,
+        [(wide, BF16)] * len(piece) + [((ring, LANES), F32)],
         last_work,
         "far_second_1",
-    )
+        through=[near[0], *xs, *base, mixing],
+    )
+    fields, partial, kept = results[: len(piece)], results[len(piece)], results[len(piece) + 1 :]
+    fields, kept = [kept[0], *fields], kept[1:]
 
     everyone = lax.all_to_all(partial, RING, 0, 0, tiled=True)
     energy = jnp.sum(everyone, axis=0)[:replicas] / jnp.sqrt(jnp.float32(cells * ring * channels))
-    x_new, y_new = finish(xs, base, mixed)
+    x_new, y_new = finish(
+        fields, kept[:groups], kept[groups : 2 * groups], kept[2 * groups], channels
+    )
     return (x_new, y_new, energy)
 
 

time: 58.3 us -> 57.8 us (level)
  starting transfers between devices: 29.2 us -> 31.5 us
  Pallas kernels: 16.3 us -> 14.6 us
  waiting for transfers between devices: 4.6 us -> 3.66 us
    ppermute x4, starting transfers between devices: 10.8 us -> 13.1 us  [far_swap(): return lax.ppermute(mine, RING, off_chip)]
    pallas_call x11, Pallas kernels: 16.3 us -> 14.6 us  [call(): pl.pallas_call(body, in_specs=[pl.BlockSpec(memory_space=pl.ANY if s is p...]
    ppermute x4, waiting for transfers between devices: 2.89 us -> 2.25 us  [far_swap(): return lax.ppermute(mine, RING, off_chip)]
  transfers between devices with their start and end apart: 11 -> 11, of which waited for: 3 -> 2; matrix products, arithmetic and copies ran while one was open for 0% -> 0% of each run, Pallas kernels for 22% -> 20%
where the time goes in v4:
time: 57.8 us; the launch traced here: 57.2 us
  starting transfers between devices  31.5 us (54%)
  Pallas kernels  14.6 us (25%)
  local copies, waits for them, and re-layouts  5.42 us (9%)
  waiting for transfers between devices  3.66 us (6%)
  between operations  1.52 us (3%)
    pallas_call x11, Pallas kernels, call(): pl.pallas_call(body, in_specs=[pl.BlockSpec(memory_space=pl.ANY if s is p...  14.6 us
    ppermute x4, starting transfers between devices, far_swap(): return lax.ppermute(mine, RING, off_chip)  13.1 us
    ppermute x6, starting transfers between devices, near_swap(): return lax.ppermute(mine, RING, on_chip)  10.5 us
    all_to_all x1, starting transfers between devices, local(): everyone = lax.all_to_all(partial, RING, 0, 0, tiled=True)  7.83 us
    unnamed x26, local copies, waits for them, and re-layouts  5.42 us
    ppermute x4, waiting for transfers between devices, far_swap(): return lax.ppermute(mine, RING, off_chip)  2.25 us
    all_to_all x1, waiting for transfers between devices, local(): everyone = lax.all_to_all(partial, RING, 0, 0, tiled=True)  1.39 us
  transfers between devices with their start and end apart: 11, of which 2 were waited for; matrix products, arithmetic and copies ran while one was open for 0% of the time, Pallas kernels for 20%

profile of v4, /device:TPU:0, one launch (start us, length us, event | category | flops | bytes accessed | tf_op | source)
XLA Modules:
  0.0 57.2 jit_solution(4397679978654835274)
XLA Ops:
  0.6 0.0 copy-start.2
  0.6 0.0 copy-start.9
  0.7 1.4 %load_first.1 = (f32[1024,128]{1,0:T(8,128)S(1)}, f32[1024,128]{1,0:T(8,128)S(1)}, bf16[1024,128]{1,0:T(8,128)(2,1)S(1)}, bf16[1024,128]{1,0:T(8,128)(2,1)S(1)}, bf16[1024,256]{1,0:T(8,128)(2,1)S(1)}) custom-call(f32[1024,384]{1,0:T(8,128)} %x_ref.3), custom_call_target="tpu_custom_call" | custom-call | flops 1000 | bytes 1000 | tf_op jit(solution)/shard_map/load_first/pallas_call | solution.py:21
  2.1 5.5 %collective-permute-start.4 = (bf16[1024,256]{1,0:T(8,128)(2,1)S(1)}, bf16[1024,256]{1,0:T(8,128)(2,1)S(1)}, u32[]{:S(2)}, u32[]{:S(2)}) collective-permute-start(bf16[1024,256]{1,0:T(8,128)(2,1)S(1)} %get-tuple-element.54._), channel_id=1, source_target_pairs={{0,15},{1,2},{2,1},{3,4},{4,3},{5,6},{6,5},{7,8},{8,7},{9,10},{10,... | collective-permute-start | bytes 1572872 | tf_op jit(solution)/shard_map/ppermute | solution.py:424
  7.6 0.5 collective-permute-start.1
  8.8 1.3 %make_lists.1 = (s32[214]{0:T(256)S(4)}, f32[1024,128]{1,0:T(8,128)S(1)}, bf16[1024,128]{1,0:T(8,128)(2,1)S(1)}) custom-call(s32[96]{0:T(128)S(1)} %copy-done.11, s32[96]{0:T(128)S(1)} %copy-done.12, s32[1]{0:T(128)S(6)} %copy.29.count_hbm, f32[1024,384]{1,0:T(8,128)} %x_ref.3, bf16[1024,256]{1,0:T(8,128)(2,1)S(1)} %get-tuple-element.54._), custom_call_target="tpu_custom_call" | custom-call | flops 1000 | bytes 1000 | tf_op jit(solution)/shard_map/make_lists/pallas_call | solution.py:21
  10.1 0.7 %collective-permute-start.2 = (bf16[1024,128]{1,0:T(8,128)(2,1)S(1)}, bf16[1024,128]{1,0:T(8,128)(2,1)S(1)}, u32[]{:S(2)}, u32[]{:S(2)}) collective-permute-start(bf16[1024,128]{1,0:T(8,128)(2,1)S(1)} %get-tuple-element.58.refs_2_.refs_6_), channel_id=1, source_target_pairs={{0,1},{1,0},{2,3},{3,2},{4,5},{5,4},{6,7},{7,6},{8,9},{9,8},{10,11... | collective-permute-start | bytes 786440 | tf_op jit(solution)/shard_map/ppermute | solution.py:427
  10.8 1.4 %first_base.1 = (f32[1024,128]{1,0:T(8,128)S(1)}, f32[1024,128]{1,0:T(8,128)S(1)}, f32[1024,128]{1,0:T(8,128)S(1)}, bf16[384,384]{1,0:T(8,128)(2,1)S(1)}) custom-call(f32[1024,128]{1,0:T(8,128)S(1)} %get-tuple-element.59.refs_0_.refs_4_, f32[1024,128]{1,0:T(8,128)S(1)} %get-tuple-element.60.refs_1_.refs_5_, ...), custom_call_target="tpu_custom_call" | custom-call | flops 1000 | bytes 1000 | tf_op jit(solution)/shard_map/first_base/pallas_call | solution.py:21
  12.3 0.4 copy-done
  12.7 1.3 %near_first.1 = (f32[1024,128]{1,0:T(8,128)S(1)}, f32[1024,128]{1,0:T(8,128)S(1)}, f32[1024,128]{1,0:T(8,128)S(1)}, bf16[1024,128]{1,0:T(8,128)(2,1)S(1)}) custom-call(s32[214]{0:T(256)S(4)} %get-tuple-element.55.list_ref, bf16[96,128,128]{2,1,0:T(8,128)(2,1)S(1)} %copy-done, bf16[1024,128]{1,0:T(8,128)(2,1)S(1)} %get-tuple-element.56.refs_0_, ...), custom_call_target="tpu_custom_call" | custom-call | flops 1000 | bytes 1000 | tf_op jit(solution)/shard_map/near_first/pallas_call | solution.py:21
  14.0 1.9 %collective-permute-start.3 = (bf16[1024,128]{1,0:T(8,128)(2,1)S(1)}, bf16[1024,128]{1,0:T(8,128)(2,1)S(1)}, u32[]{:S(2)}, u32[]{:S(2)}) collective-permute-start(bf16[1024,128]{1,0:T(8,128)(2,1)S(1)} %get-tuple-element.63), channel_id=1, source_target_pairs={{0,15},{1,2},{2,1},{3,4},{4,3},{5,6},{6,5},{7,8},{8,7},{9,10},{10,... | collective-permute-start | bytes 786440 | tf_op jit(solution)/shard_map/ppermute | solution.py:424
  15.9 1.0 %far_first_0.1 = (f32[1024,128]{1,0:T(8,128)S(1)}, f32[1024,128]{1,0:T(8,128)S(1)}, bf16[1024,128]{1,0:T(8,128)(2,1)S(1)}, bf16[1024,128]{1,0:T(8,128)(2,1)S(1)}...) custom-call(s32[214]{0:T(256)S(4)} %get-tuple-element.55.list_ref, bf16[96,128,128]{2,1,0:T(8,128)(2,1)S(1)} %copy-done, ...), custom_call_target="tpu_custom_call" | custom-call | flops 1000 | bytes 1000 | tf_op jit(solution)/shard_map/far_first_0/pallas_call | solution.py:21
  16.9 3.5 %collective-permute-start.9 = (bf16[1024,128]{1,0:T(8,128)(2,1)S(1)}, bf16[1024,128]{1,0:T(8,128)(2,1)S(1)}, u32[]{:S(2)}, u32[]{:S(2)}) collective-permute-start(bf16[1024,128]{1,0:T(8,128)(2,1)S(1)} %get-tuple-element.76), channel_id=1, source_target_pairs={{0,15},{1,2},{2,1},{3,4},{4,3},{5,6},{6,5},{7,8},{8,7},{9,10},{10,... | collective-permute-start | bytes 786440 | tf_op jit(solution)/shard_map/ppermute | solution.py:424
  20.4 2.2 %collective-permute-done.3.far_ref = bf16[1024,128]{1,0:T(8,128)(2,1)S(1)} collective-permute-done((bf16[1024,128]{1,0:T(8,128)(2,1)S(1)}, bf16[1024,128]{1,0:T(8,128)(2,1)S(1)}, u32[]{:S(2)}, u32[]{:S(2)}) %collective-permute-start.3) | collective-permute-done | bytes 262176 | tf_op jit(solution)/shard_map/ppermute | solution.py:424
  22.6 1.1 %far_first_1.1 = (f32[1024,128]{1,0:T(8,128)S(1)}, f32[1024,128]{1,0:T(8,128)S(1)}, bf16[1024,128]{1,0:T(8,128)(2,1)S(1)}, f32[1024,128]{1,0:T(8,128)S(1)}, f32[...) custom-call(s32[214]{0:T(256)S(4)} %get-tuple-element.55.list_ref, ...), custom_call_target="tpu_custom_call" | custom-call | flops 1000 | bytes 1000 | tf_op jit(solution)/shard_map/far_first_1/pallas_call | solution.py:21
  23.7 2.2 %collective-permute-start.5 = (bf16[1024,256]{1,0:T(8,128)(2,1)S(1)}, bf16[1024,256]{1,0:T(8,128)(2,1)S(1)}, u32[]{:S(2)}, u32[]{:S(2)}) collective-permute-start(bf16[1024,256]{1,0:T(8,128)(2,1)S(1)} %get-tuple-element.72), channel_id=1, source_target_pairs={{0,15},{1,2},{2,1},{3,4},{4,3},{5,6},{6,5},{7,8},{8,7},{9,10},{10,... | collective-permute-start | bytes 1572872 | tf_op jit(solution)/shard_map/ppermute | solution.py:424
  25.9 8.8 %collective-permute-start.7 = (bf16[1024,128]{1,0:T(8,128)(2,1)S(1)}, bf16[1024,128]{1,0:T(8,128)(2,1)S(1)}, u32[]{:S(2)}, u32[]{:S(2)}) collective-permute-start(bf16[1024,128]{1,0:T(8,128)(2,1)S(1)} %get-tuple-element.74.refs_1_.refs_7_), channel_id=1, source_target_pairs={{0,1},{1,0},{2,3},{3,2},{4,5},{5,4},{6,7},{7,6},{8,9},{9,8},{10,11... | collective-permute-start | bytes 786440 | tf_op jit(solution)/shard_map/ppermute | solution.py:427
  34.7 0.5 collective-permute-start.6
  35.2 1.6 %second_base.1 = (f32[1024,128]{1,0:T(8,128)S(1)}, f32[1024,128]{1,0:T(8,128)S(1)}, f32[1024,128]{1,0:T(8,128)S(1)}, f32[1024,128]{1,0:T(8,128)S(1)}, f32[1024,128]{1,0:T(8,128)S(1)}, /*index=5*/f32[1024,128]{1,0:T(8,128)S(1)}) custom-call(f32[1024,128]{1,0:T(8,128)S(1)} %get-tuple-element.79.refs_0_.refs_6_, ...), custom_call_target="tpu_custom_call" | custom-call | flops 1000 | bytes 1000 | tf_op jit(solution)/shard_map/second_base/pallas_call | solution.py:21
  36.8 0.6 far_second_0.1.refs_6_
  37.5 1.2 %near_second.1 = (bf16[1024,128]{1,0:T(8,128)(2,1)S(1)}, f32[1024,128]{1,0:T(8,128)S(1)}, f32[1024,128]{1,0:T(8,128)S(1)}) custom-call(s32[214]{0:T(256)S(4)} %get-tuple-element.55.list_ref, bf16[96,128,128]{2,1,0:T(8,128)(2,1)S(1)} %copy-done, bf16[1024,128]{1,0:T(8,128)(2,1)S(1)} %get-tuple-element.73.refs_0_.refs_6_, ...), custom_call_target="tpu_custom_call" | custom-call | flops 1000 | bytes 1000 | tf_op jit(solution)/shard_map/near_second/pallas_call | solution.py:21
  38.7 1.6 %far_second_1.1 = (bf16[1024,128]{1,0:T(8,128)(2,1)S(1)}, bf16[1024,128]{1,0:T(8,128)(2,1)S(1)}, f32[16,128]{1,0:T(8,128)}, bf16[1024,128]{1,0:T(8,128)(2,1)S(1)...) custom-call(s32[214]{0:T(256)S(4)} %get-tuple-element.55.list_ref, ...), custom_call_target="tpu_custom_call", output_to_operand_aliasing={{3}: (8, {}), {4}: (9, {}), {5}: (10, {}), {6}: (11, {}), {... | custom-call | flops 1000 | bytes 1000 | tf_op jit(solution)/shard_map/far_second_1/pallas_call | solution.py:21
  40.3 0.7 %copy-done.3 = bf16[1024,128]{1,0:T(8,128)(2,1)} copy-done((bf16[1024,128]{1,0:T(8,128)(2,1)}, bf16[1024,128]{1,0:T(8,128)(2,1)S(1)}, u32[]{:S(2)}) %copy-start.3) | copy-done | bytes 262168
  41.1 0.7 %copy-done.5 = bf16[1024,128]{1,0:T(8,128)(2,1)} copy-done((bf16[1024,128]{1,0:T(8,128)(2,1)}, bf16[1024,128]{1,0:T(8,128)(2,1)S(1)}, u32[]{:S(2)}) %copy-start.5) | copy-done | bytes 262168
  41.8 0.7 %copy-done.7 = bf16[1024,128]{1,0:T(8,128)(2,1)} copy-done((bf16[1024,128]{1,0:T(8,128)(2,1)}, bf16[1024,128]{1,0:T(8,128)(2,1)S(1)}, u32[]{:S(2)}) %copy-start.7) | copy-done | bytes 262168
  42.4 7.8 %all-to-all-start = ((f32[16,1,128]{2,1,0:T(1,128)}), f32[16,1,128]{2,1,0:T(1,128)S(1)}, u32[]{:S(2)}, u32[]{:S(2)}) async-start(f32[16,1,128]{2,1,0:T(1,128)} %bitcast.1), calls=%async_computation | async-start | bytes 16384 | tf_op jit(solution)/shard_map/all_to_all | solution.py:539
  50.3 0.9 %copy-done.4 = bf16[1024,128]{1,0:T(8,128)(2,1)S(1)} copy-done((bf16[1024,128]{1,0:T(8,128)(2,1)S(1)}, bf16[1024,128]{1,0:T(8,128)(2,1)}, u32[]{:S(2)}) %copy-start.4) | copy-done | bytes 262168
  51.2 0.9 %copy-done.6 = bf16[1024,128]{1,0:T(8,128)(2,1)S(1)} copy-done((bf16[1024,128]{1,0:T(8,128)(2,1)S(1)}, bf16[1024,128]{1,0:T(8,128)(2,1)}, u32[]{:S(2)}) %copy-start.6) | copy-done | bytes 262168
  52.2 0.9 %copy-done.8 = bf16[1024,128]{1,0:T(8,128)(2,1)S(1)} copy-done((bf16[1024,128]{1,0:T(8,128)(2,1)S(1)}, bf16[1024,128]{1,0:T(8,128)(2,1)}, u32[]{:S(2)}) %copy-start.8) | copy-done | bytes 262168
  53.1 2.1 %finish.1 = (f32[1024,384]{1,0:T(8,128)}, f32[1024,384]{1,0:T(8,128)}) custom-call(bf16[1024,128]{1,0:T(8,128)(2,1)S(1)} %copy-done.4, bf16[1024,128]{1,0:T(8,128)(2,1)S(1)} %copy-done.6, bf16[1024,128]{1,0:T(8,128)(2,1)S(1)} %copy-done.8, f32[1024,128]{1,0:T(8,128)S(1)} %get-tuple-element.95.refs_3_, f32[1024,128]{1,0:T(8,128)S(1)} %get-tuple-element.96.refs_4_, ...), custom_call_target="tpu_custom_call" | custom-call | flops 1000 | bytes 1000 | tf_op jit(solution)/shard_map/finish/pallas_call | solution.py:21
  55.3 1.4 %all-to-all-done = f32[16,1,128]{2,1,0:T(1,128)S(1)} async-done(((f32[16,1,128]{2,1,0:T(1,128)}), f32[16,1,128]{2,1,0:T(1,128)S(1)}, u32[]{:S(2)}, u32[]{:S(2)}) %all-to-all-start) | async-done | bytes 8224 | tf_op jit(solution)/shard_map/all_to_all | solution.py:539
  56.7 0.5 slice_multiply_fusion
  (29 shorter events, 0.1 us)
Async XLA Ops:
  0.6 10.2 %copy-start.2 = (bf16[384,384]{1,0:T(8,128)(2,1)S(1)}, bf16[384,384]{1,0:T(8,128)(2,1)}, u32[]{:S(2)}) copy-start(bf16[384,384]{1,0:T(8,128)(2,1)} %constant.9.clone.refs_4_.refs_9_) | copy-start | bytes 884740
  0.6 10.2 %copy-start.9 = (bf16[384,48]{1,0:T(8,128)(2,1)S(1)}, bf16[384,48]{1,0:T(8,128)(2,1)}, u32[]{:S(2)}) copy-start(bf16[384,48]{1,0:T(8,128)(2,1)} %constant.10.clone.refs_5_) | copy-start | bytes 110596
  0.7 8.1 %copy-start.12 = (s32[96]{0:T(128)S(1)}, s32[96]{0:T(128)}, u32[]{:S(2)}) copy-start(s32[96]{0:T(128)} %cols_hbm.1) | copy-start | bytes 1156
  0.7 8.1 %copy-start.11 = (s32[96]{0:T(128)S(1)}, s32[96]{0:T(128)}, u32[]{:S(2)}) copy-start(s32[96]{0:T(128)} %rows_hbm.1) | copy-start | bytes 1156
  0.7 10.1 %copy-start.10 = (bf16[48,48]{1,0:T(8,128)(2,1)S(1)}, bf16[48,48]{1,0:T(8,128)(2,1)}, u32[]{:S(2)}) copy-start(bf16[48,48]{1,0:T(8,128)(2,1)} %refs_6_.1) | copy-start | bytes 13828
  0.7 10.1 %copy-start.1 = (f32[1024,384]{1,0:T(8,128)S(1)}, f32[1024,384]{1,0:T(8,128)}, u32[]{:S(2)}) copy-start(f32[1024,384]{1,0:T(8,128)} %refs_3_.1) | copy-start | bytes 4718596
  2.1 13.8 %collective-permute-start.4 = (bf16[1024,256]{1,0:T(8,128)(2,1)S(1)}, bf16[1024,256]{1,0:T(8,128)(2,1)S(1)}, u32[]{:S(2)}, u32[]{:S(2)}) collective-permute-start(bf16[1024,256]{1,0:T(8,128)(2,1)S(1)} %get-tuple-element.54._), channel_id=1, source_target_pairs={{0,15},{1,2},{2,1},{3,4},{4,3},{5,6},{6,5},{7,8},{8,7},{9,10},{10,... | collective-permute-start | bytes 1572872 | tf_op jit(solution)/shard_map/ppermute | solution.py:424
  7.6 4.6 %collective-permute-start = (bf16[1024,128]{1,0:T(8,128)(2,1)S(1)}, bf16[1024,128]{1,0:T(8,128)(2,1)S(1)}, u32[]{:S(2)}, u32[]{:S(2)}) collective-permute-start(bf16[1024,128]{1,0:T(8,128)(2,1)S(1)} %get-tuple-element.56.refs_0_), channel_id=1, source_target_pairs={{0,1},{1,0},{2,3},{3,2},{4,5},{5,4},{6,7},{7,6},{8,9},{9,8},{10,11... | collective-permute-start | bytes 786440 | tf_op jit(solution)/shard_map/ppermute | solution.py:427
  7.6 4.6 %collective-permute-start.1 = (bf16[1024,128]{1,0:T(8,128)(2,1)S(1)}, bf16[1024,128]{1,0:T(8,128)(2,1)S(1)}, u32[]{:S(2)}, u32[]{:S(2)}) collective-permute-start(bf16[1024,128]{1,0:T(8,128)(2,1)S(1)} %get-tuple-element.57.refs_1_), channel_id=1, source_target_pairs={{0,1},{1,0},{2,3},{3,2},{4,5},{5,4},{6,7},{7,6},{8,9},{9,8},{10,11... | collective-permute-start | bytes 786440 | tf_op jit(solution)/shard_map/ppermute | solution.py:427
  10.1 2.2 %collective-permute-start.2 = (bf16[1024,128]{1,0:T(8,128)(2,1)S(1)}, bf16[1024,128]{1,0:T(8,128)(2,1)S(1)}, u32[]{:S(2)}, u32[]{:S(2)}) collective-permute-start(bf16[1024,128]{1,0:T(8,128)(2,1)S(1)} %get-tuple-element.58.refs_2_.refs_6_), channel_id=1, source_target_pairs={{0,1},{1,0},{2,3},{3,2},{4,5},{5,4},{6,7},{7,6},{8,9},{9,8},{10,11... | collective-permute-start | bytes 786440 | tf_op jit(solution)/shard_map/ppermute | solution.py:427
  10.8 1.9 %copy-start = (bf16[96,128,128]{2,1,0:T(8,128)(2,1)S(1)}, bf16[96,128,128]{2,1,0:T(8,128)(2,1)}, u32[]{:S(2)}) copy-start(bf16[96,128,128]{2,1,0:T(8,128)(2,1)} %tiles_ref.11) | copy-start | bytes 9437188
  14.0 8.7 %collective-permute-start.3 = (bf16[1024,128]{1,0:T(8,128)(2,1)S(1)}, bf16[1024,128]{1,0:T(8,128)(2,1)S(1)}, u32[]{:S(2)}, u32[]{:S(2)}) collective-permute-start(bf16[1024,128]{1,0:T(8,128)(2,1)S(1)} %get-tuple-element.63), channel_id=1, source_target_pairs={{0,15},{1,2},{2,1},{3,4},{4,3},{5,6},{6,5},{7,8},{8,7},{9,10},{10,... | collective-permute-start | bytes 786440 | tf_op jit(solution)/shard_map/ppermute | solution.py:424
  16.9 20.0 %collective-permute-start.9 = (bf16[1024,128]{1,0:T(8,128)(2,1)S(1)}, bf16[1024,128]{1,0:T(8,128)(2,1)S(1)}, u32[]{:S(2)}, u32[]{:S(2)}) collective-permute-start(bf16[1024,128]{1,0:T(8,128)(2,1)S(1)} %get-tuple-element.76), channel_id=1, source_target_pairs={{0,15},{1,2},{2,1},{3,4},{4,3},{5,6},{6,5},{7,8},{8,7},{9,10},{10,... | collective-permute-start | bytes 786440 | tf_op jit(solution)/shard_map/ppermute | solution.py:424
  23.7 15.0 %collective-permute-start.5 = (bf16[1024,256]{1,0:T(8,128)(2,1)S(1)}, bf16[1024,256]{1,0:T(8,128)(2,1)S(1)}, u32[]{:S(2)}, u32[]{:S(2)}) collective-permute-start(bf16[1024,256]{1,0:T(8,128)(2,1)S(1)} %get-tuple-element.72), channel_id=1, source_target_pairs={{0,15},{1,2},{2,1},{3,4},{4,3},{5,6},{6,5},{7,8},{8,7},{9,10},{10,... | collective-permute-start | bytes 1572872 | tf_op jit(solution)/shard_map/ppermute | solution.py:424
  25.9 11.5 %collective-permute-start.7 = (bf16[1024,128]{1,0:T(8,128)(2,1)S(1)}, bf16[1024,128]{1,0:T(8,128)(2,1)S(1)}, u32[]{:S(2)}, u32[]{:S(2)}) collective-permute-start(bf16[1024,128]{1,0:T(8,128)(2,1)S(1)} %get-tuple-element.74.refs_1_.refs_7_), channel_id=1, source_target_pairs={{0,1},{1,0},{2,3},{3,2},{4,5},{5,4},{6,7},{7,6},{8,9},{9,8},{10,11... | collective-permute-start | bytes 786440 | tf_op jit(solution)/shard_map/ppermute | solution.py:427
  34.7 2.8 %collective-permute-start.8 = (bf16[1024,128]{1,0:T(8,128)(2,1)S(1)}, bf16[1024,128]{1,0:T(8,128)(2,1)S(1)}, u32[]{:S(2)}, u32[]{:S(2)}) collective-permute-start(bf16[1024,128]{1,0:T(8,128)(2,1)S(1)} %get-tuple-element.75.refs_2_.refs_8_), channel_id=1, source_target_pairs={{0,1},{1,0},{2,3},{3,2},{4,5},{5,4},{6,7},{7,6},{8,9},{9,8},{10,11... | collective-permute-start | bytes 786440 | tf_op jit(solution)/shard_map/ppermute | solution.py:427
  34.7 2.8 %collective-permute-start.6 = (bf16[1024,128]{1,0:T(8,128)(2,1)S(1)}, bf16[1024,128]{1,0:T(8,128)(2,1)S(1)}, u32[]{:S(2)}, u32[]{:S(2)}) collective-permute-start(bf16[1024,128]{1,0:T(8,128)(2,1)S(1)} %get-tuple-element.73.refs_0_.refs_6_), channel_id=1, source_target_pairs={{0,1},{1,0},{2,3},{3,2},{4,5},{5,4},{6,7},{7,6},{8,9},{9,8},{10,11... | collective-permute-start | bytes 786440 | tf_op jit(solution)/shard_map/ppermute | solution.py:427
  40.3 0.7 %copy-start.3 = (bf16[1024,128]{1,0:T(8,128)(2,1)}, bf16[1024,128]{1,0:T(8,128)(2,1)S(1)}, u32[]{:S(2)}) copy-start(bf16[1024,128]{1,0:T(8,128)(2,1)S(1)} %get-tuple-element.92.refs_0_) | copy-start | bytes 786436
  41.0 0.7 %copy-start.5 = (bf16[1024,128]{1,0:T(8,128)(2,1)}, bf16[1024,128]{1,0:T(8,128)(2,1)S(1)}, u32[]{:S(2)}) copy-start(bf16[1024,128]{1,0:T(8,128)(2,1)S(1)} %get-tuple-element.93.refs_1_) | copy-start | bytes 786436
  41.8 0.7 %copy-start.7 = (bf16[1024,128]{1,0:T(8,128)(2,1)}, bf16[1024,128]{1,0:T(8,128)(2,1)S(1)}, u32[]{:S(2)}) copy-start(bf16[1024,128]{1,0:T(8,128)(2,1)S(1)} %get-tuple-element.94.refs_2_) | copy-start | bytes 786436
  42.4 14.2 %all-to-all-start = ((f32[16,1,128]{2,1,0:T(1,128)}), f32[16,1,128]{2,1,0:T(1,128)S(1)}, u32[]{:S(2)}, u32[]{:S(2)}) async-start(f32[16,1,128]{2,1,0:T(1,128)} %bitcast.1), calls=%async_computation | async-start | bytes 16384 | tf_op jit(solution)/shard_map/all_to_all | solution.py:539
  50.3 1.0 %copy-start.4 = (bf16[1024,128]{1,0:T(8,128)(2,1)S(1)}, bf16[1024,128]{1,0:T(8,128)(2,1)}, u32[]{:S(2)}) copy-start(bf16[1024,128]{1,0:T(8,128)(2,1)} %copy-done.3) | copy-start | bytes 786436
  51.2 0.9 %copy-start.6 = (bf16[1024,128]{1,0:T(8,128)(2,1)S(1)}, bf16[1024,128]{1,0:T(8,128)(2,1)}, u32[]{:S(2)}) copy-start(bf16[1024,128]{1,0:T(8,128)(2,1)} %copy-done.5) | copy-start | bytes 786436
  52.2 0.9 %copy-start.8 = (bf16[1024,128]{1,0:T(8,128)(2,1)S(1)}, bf16[1024,128]{1,0:T(8,128)(2,1)}, u32[]{:S(2)}) copy-start(bf16[1024,128]{1,0:T(8,128)(2,1)} %copy-done.7) | copy-start | bytes 786436

commit v5 on v4

--- a/solution.py
+++ b/solution.py
@@ -394,6 +394,19 @@
         ],
         "finish",
     )
+
+
+def sum_over_ring(value, ring):
+    if ring & (ring - 1):
+        return lax.psum(value, RING)
+    size = 1
+    while size < ring:
+        digits = (1, 2, 3) if 4 * size <= ring else (1,)
+        value = value + sum(
+            lax.ppermute(value, RING, [(i, i ^ (size * d)) for i in range(ring)]) for d in digits
+        )
+        size *= len(digits) + 1
+    return value
 
 
 def local(positions, momenta, tile_values, tile_rows, tile_cols, tile_count, channel_coupling):
@@ -520,7 +533,7 @@
         place = lax.broadcasted_iota(jnp.int32, (replicas, LANES), 1)
         which = lax.broadcasted_iota(jnp.int32, (replicas, LANES), 0)
         flat = jnp.sum(jnp.where(place == which, total, 0.0), axis=0, keepdims=True)
-        outs[len(piece)][...] = jnp.broadcast_to(flat, (ring, LANES))
+        outs[len(piece)][...] = jnp.broadcast_to(flat, (8, LANES))
 
     results = far_fields(
         lists,
@@ -528,7 +541,7 @@
         near[1:],
         new_fars[1],
         weights,
-        [(wide, BF16)] * len(piece) + [((ring, LANES), F32)],
+        [(wide, BF16)] * len(piece) + [((8, LANES), F32)],
         last_work,
         "far_second_1",
         through=[near[0], *xs, *base, mixing],
@@ -536,8 +549,8 @@
     fields, partial, kept = results[: len(piece)], results[len(piece)], results[len(piece) + 1 :]
     fields, kept = [kept[0], *fields], kept[1:]
 
-    everyone = lax.all_to_all(partial, RING, 0, 0, tiled=True)
-    energy = jnp.sum(everyone, axis=0)[:replicas] / jnp.sqrt(jnp.float32(cells * ring * channels))
+    total = sum_over_ring(partial, ring)
+    energy = total[0, :replicas] / jnp.sqrt(jnp.float32(cells * ring * channels))
     x_new, y_new = finish(
         fields, kept[:groups], kept[groups : 2 * groups], kept[2 * groups], channels
     )

time: 57.8 us -> 55 us (0.952)
  local copies, waits for them, and re-layouts: 5.42 us -> 0.44 us
  waiting for transfers between devices: 3.66 us -> 5.38 us
  Pallas kernels: 14.6 us -> 15.9 us
  starting transfers between devices: 31.5 us -> 30.7 us
    ppermute x0 -> x6, starting transfers between devices: none -> 8.57 us  [sum_over_ring(): lax.ppermute(value, RING, [(i, i ^ size * d) for i in range(ring)])]
    all_to_all x1 -> x0, starting transfers between devices: 7.83 us -> none  [local(): everyone = lax.all_to_all(partial, RING, 0, 0, tiled=True)]
    unnamed x26 -> x14, local copies, waits for them, and re-layouts: 5.42 us -> 0.44 us
    ppermute x0 -> x6, waiting for transfers between devices: none -> 2.55 us  [sum_over_ring(): lax.ppermute(value, RING, [(i, i ^ size * d) for i in range(ring)])]
    all_to_all x1 -> x0, waiting for transfers between devices: 1.39 us -> none  [local(): everyone = lax.all_to_all(partial, RING, 0, 0, tiled=True)]
    pallas_call x11, Pallas kernels: 14.6 us -> 15.9 us  [call(): pl.pallas_call(body, in_specs=[pl.BlockSpec(memory_space=pl.ANY if s is p...]
    ppermute x4, starting transfers between devices: 13.1 us -> 12 us  [far_swap(): return lax.ppermute(mine, RING, off_chip)]
  transfers between devices with their start and end apart: 11 -> 16, of which waited for: 2 -> 3; matrix products, arithmetic and copies ran while one was open for 0% -> 0% of each run, Pallas kernels for 20% -> 25%
where the time goes in v5:
time: 55 us; the launch traced here: 54.5 us
  starting transfers between devices  30.7 us (56%)
  Pallas kernels  15.9 us (29%)
  waiting for transfers between devices  5.38 us (10%)
  between operations  1.55 us (3%)
    pallas_call x11, Pallas kernels, call(): pl.pallas_call(body, in_specs=[pl.BlockSpec(memory_space=pl.ANY if s is p...  15.9 us
    ppermute x4, starting transfers between devices, far_swap(): return lax.ppermute(mine, RING, off_chip)  12 us
    ppermute x6, starting transfers between devices, near_swap(): return lax.ppermute(mine, RING, on_chip)  10.2 us
    ppermute x6, starting transfers between devices, sum_over_ring(): lax.ppermute(value, RING, [(i, i ^ size * d) for i in range(ring)])  8.57 us
    ppermute x4, waiting for transfers between devices, far_swap(): return lax.ppermute(mine, RING, off_chip)  2.77 us
    ppermute x6, waiting for transfers between devices, sum_over_ring(): lax.ppermute(value, RING, [(i, i ^ size * d) for i in range(ring)])  2.55 us
  transfers between devices with their start and end apart: 16, of which 3 were waited for; matrix products, arithmetic and copies ran while one was open for 0% of the time, Pallas kernels for 25%

profile of v5, /device:TPU:0, one launch (start us, length us, event | category | flops | bytes accessed | tf_op | source)
XLA Modules:
  0.0 54.5 jit_solution(16597397079370302311)
XLA Ops:
  0.6 0.0 copy-start.2
  0.6 0.0 copy-start.3
  0.7 1.4 %load_first.1 = (f32[1024,128]{1,0:T(8,128)S(1)}, f32[1024,128]{1,0:T(8,128)S(1)}, bf16[1024,128]{1,0:T(8,128)(2,1)S(1)}, bf16[1024,128]{1,0:T(8,128)(2,1)S(1)}, bf16[1024,256]{1,0:T(8,128)(2,1)S(1)}) custom-call(f32[1024,384]{1,0:T(8,128)} %x_ref.3), custom_call_target="tpu_custom_call" | custom-call | flops 1000 | bytes 1000 | tf_op jit(solution)/shard_map/load_first/pallas_call | solution.py:21
  2.1 5.5 %collective-permute-start.4 = (bf16[1024,256]{1,0:T(8,128)(2,1)S(1)}, bf16[1024,256]{1,0:T(8,128)(2,1)S(1)}, u32[]{:S(2)}, u32[]{:S(2)}) collective-permute-start(bf16[1024,256]{1,0:T(8,128)(2,1)S(1)} %get-tuple-element.54._), channel_id=1, source_target_pairs={{0,15},{1,2},{2,1},{3,4},{4,3},{5,6},{6,5},{7,8},{8,7},{9,10},{10,... | collective-permute-start | bytes 1572872 | tf_op jit(solution)/shard_map/ppermute | solution.py:437
  7.6 0.5 collective-permute-start.1
  8.8 1.8 %make_lists.1 = (s32[214]{0:T(256)S(4)}, f32[1024,128]{1,0:T(8,128)S(1)}, bf16[1024,128]{1,0:T(8,128)(2,1)S(1)}) custom-call(s32[96]{0:T(128)S(1)} %copy-done.5, s32[96]{0:T(128)S(1)} %copy-done.6, s32[1]{0:T(128)S(6)} %copy.28.count_hbm, f32[1024,384]{1,0:T(8,128)} %x_ref.3, bf16[1024,256]{1,0:T(8,128)(2,1)S(1)} %get-tuple-element.54._), custom_call_target="tpu_custom_call" | custom-call | flops 1000 | bytes 1000 | tf_op jit(solution)/shard_map/make_lists/pallas_call | solution.py:21
  10.6 0.1 collective-permute-start.2
  10.7 0.0 copy-start
  10.7 1.4 %first_base.1 = (f32[1024,128]{1,0:T(8,128)S(1)}, f32[1024,128]{1,0:T(8,128)S(1)}, f32[1024,128]{1,0:T(8,128)S(1)}, bf16[384,384]{1,0:T(8,128)(2,1)S(1)}) custom-call(f32[1024,128]{1,0:T(8,128)S(1)} %get-tuple-element.59.refs_0_.refs_4_, f32[1024,128]{1,0:T(8,128)S(1)} %get-tuple-element.60.refs_1_.refs_5_, ...), custom_call_target="tpu_custom_call" | custom-call | flops 1000 | bytes 1000 | tf_op jit(solution)/shard_map/first_base/pallas_call | solution.py:21
  12.1 0.0 collective-permute-done.2.refs_5_
  12.2 0.4 copy-done
  12.6 1.9 %near_first.1 = (f32[1024,128]{1,0:T(8,128)S(1)}, f32[1024,128]{1,0:T(8,128)S(1)}, f32[1024,128]{1,0:T(8,128)S(1)}, bf16[1024,128]{1,0:T(8,128)(2,1)S(1)}) custom-call(s32[214]{0:T(256)S(4)} %get-tuple-element.55.list_ref, bf16[96,128,128]{2,1,0:T(8,128)(2,1)S(1)} %copy-done, bf16[1024,128]{1,0:T(8,128)(2,1)S(1)} %get-tuple-element.56.refs_0_, ...), custom_call_target="tpu_custom_call" | custom-call | flops 1000 | bytes 1000 | tf_op jit(solution)/shard_map/near_first/pallas_call | solution.py:21
  14.5 1.4 %collective-permute-start.3 = (bf16[1024,128]{1,0:T(8,128)(2,1)S(1)}, bf16[1024,128]{1,0:T(8,128)(2,1)S(1)}, u32[]{:S(2)}, u32[]{:S(2)}) collective-permute-start(bf16[1024,128]{1,0:T(8,128)(2,1)S(1)} %get-tuple-element.63), channel_id=1, source_target_pairs={{0,15},{1,2},{2,1},{3,4},{4,3},{5,6},{6,5},{7,8},{8,7},{9,10},{10,... | collective-permute-start | bytes 786440 | tf_op jit(solution)/shard_map/ppermute | solution.py:437
  15.9 1.0 %far_first_0.1 = (f32[1024,128]{1,0:T(8,128)S(1)}, f32[1024,128]{1,0:T(8,128)S(1)}, bf16[1024,128]{1,0:T(8,128)(2,1)S(1)}, bf16[1024,128]{1,0:T(8,128)(2,1)S(1)}...) custom-call(s32[214]{0:T(256)S(4)} %get-tuple-element.55.list_ref, bf16[96,128,128]{2,1,0:T(8,128)(2,1)S(1)} %copy-done, ...), custom_call_target="tpu_custom_call" | custom-call | flops 1000 | bytes 1000 | tf_op jit(solution)/shard_map/far_first_0/pallas_call | solution.py:21
  16.9 3.5 %collective-permute-start.9 = (bf16[1024,128]{1,0:T(8,128)(2,1)S(1)}, bf16[1024,128]{1,0:T(8,128)(2,1)S(1)}, u32[]{:S(2)}, u32[]{:S(2)}) collective-permute-start(bf16[1024,128]{1,0:T(8,128)(2,1)S(1)} %get-tuple-element.76), channel_id=1, source_target_pairs={{0,15},{1,2},{2,1},{3,4},{4,3},{5,6},{6,5},{7,8},{8,7},{9,10},{10,... | collective-permute-start | bytes 786440 | tf_op jit(solution)/shard_map/ppermute | solution.py:437
  20.4 2.8 %collective-permute-done.3.far_ref = bf16[1024,128]{1,0:T(8,128)(2,1)S(1)} collective-permute-done((bf16[1024,128]{1,0:T(8,128)(2,1)S(1)}, bf16[1024,128]{1,0:T(8,128)(2,1)S(1)}, u32[]{:S(2)}, u32[]{:S(2)}) %collective-permute-start.3) | collective-permute-done | bytes 262176 | tf_op jit(solution)/shard_map/ppermute | solution.py:437
  23.1 1.1 %far_first_1.1 = (f32[1024,128]{1,0:T(8,128)S(1)}, f32[1024,128]{1,0:T(8,128)S(1)}, bf16[1024,128]{1,0:T(8,128)(2,1)S(1)}, f32[1024,128]{1,0:T(8,128)S(1)}, f32[...) custom-call(s32[214]{0:T(256)S(4)} %get-tuple-element.55.list_ref, ...), custom_call_target="tpu_custom_call" | custom-call | flops 1000 | bytes 1000 | tf_op jit(solution)/shard_map/far_first_1/pallas_call | solution.py:21
  24.2 1.6 %collective-permute-start.5 = (bf16[1024,256]{1,0:T(8,128)(2,1)S(1)}, bf16[1024,256]{1,0:T(8,128)(2,1)S(1)}, u32[]{:S(2)}, u32[]{:S(2)}) collective-permute-start(bf16[1024,256]{1,0:T(8,128)(2,1)S(1)} %get-tuple-element.72), channel_id=1, source_target_pairs={{0,15},{1,2},{2,1},{3,4},{4,3},{5,6},{6,5},{7,8},{8,7},{9,10},{10,... | collective-permute-start | bytes 1572872 | tf_op jit(solution)/shard_map/ppermute | solution.py:437
  25.8 9.1 %collective-permute-start.7 = (bf16[1024,128]{1,0:T(8,128)(2,1)S(1)}, bf16[1024,128]{1,0:T(8,128)(2,1)S(1)}, u32[]{:S(2)}, u32[]{:S(2)}) collective-permute-start(bf16[1024,128]{1,0:T(8,128)(2,1)S(1)} %get-tuple-element.74.refs_1_.refs_7_), channel_id=1, source_target_pairs={{0,1},{1,0},{2,3},{3,2},{4,5},{5,4},{6,7},{7,6},{8,9},{9,8},{10,11... | collective-permute-start | bytes 786440 | tf_op jit(solution)/shard_map/ppermute | solution.py:440
  34.9 0.5 collective-permute-start.6
  35.4 1.7 %second_base.1 = (f32[1024,128]{1,0:T(8,128)S(1)}, f32[1024,128]{1,0:T(8,128)S(1)}, f32[1024,128]{1,0:T(8,128)S(1)}, f32[1024,128]{1,0:T(8,128)S(1)}, f32[1024,128]{1,0:T(8,128)S(1)}, /*index=5*/f32[1024,128]{1,0:T(8,128)S(1)}) custom-call(f32[1024,128]{1,0:T(8,128)S(1)} %get-tuple-element.79.refs_0_.refs_6_, ...), custom_call_target="tpu_custom_call" | custom-call | flops 1000 | bytes 1000 | tf_op jit(solution)/shard_map/second_base/pallas_call | solution.py:21
  37.1 0.6 %far_second_0.1.refs_6_ = f32[1024,128]{1,0:T(8,128)S(1)} custom-call(s32[214]{0:T(256)S(4)} %get-tuple-element.55.list_ref, bf16[96,128,128]{2,1,0:T(8,128)(2,1)S(1)} %copy-done, bf16[1024,128]{1,0:T(8,128)(2,1)S(1)} %collective-permute-done.9.far_ref), custom_call_target="tpu_custom_call" | custom-call | flops 4000000000 | bytes 1000 | tf_op jit(solution)/shard_map/far_second_0/pallas_call | solution.py:21
  37.7 1.8 %near_second.1 = (bf16[1024,128]{1,0:T(8,128)(2,1)S(1)}, f32[1024,128]{1,0:T(8,128)S(1)}, f32[1024,128]{1,0:T(8,128)S(1)}) custom-call(s32[214]{0:T(256)S(4)} %get-tuple-element.55.list_ref, bf16[96,128,128]{2,1,0:T(8,128)(2,1)S(1)} %copy-done, bf16[1024,128]{1,0:T(8,128)(2,1)S(1)} %get-tuple-element.73.refs_0_.refs_6_, ...), custom_call_target="tpu_custom_call" | custom-call | flops 1000 | bytes 1000 | tf_op jit(solution)/shard_map/near_second/pallas_call | solution.py:21
  39.6 1.1 %far_second_1.1 = (bf16[1024,128]{1,0:T(8,128)(2,1)S(1)}, bf16[1024,128]{1,0:T(8,128)(2,1)S(1)}, f32[8,128]{1,0:T(8,128)S(1)}, bf16[1024,128]{1,0:T(8,128)(2,1)S...) custom-call(s32[214]{0:T(256)S(4)} %get-tuple-element.55.list_ref, ...), custom_call_target="tpu_custom_call", output_to_operand_aliasing={{3}: (8, {}), {4}: (9, {}), {5}: (10, {}), {6}: (11, {}), {... | custom-call | flops 1000 | bytes 1000 | tf_op jit(solution)/shard_map/far_second_1/pallas_call | solution.py:21
  40.7 4.1 %collective-permute-start.11 = (f32[8,128]{1,0:T(8,128)S(1)}, f32[8,128]{1,0:T(8,128)S(1)}, u32[]{:S(2)}, u32[]{:S(2)}) collective-permute-start(f32[8,128]{1,0:T(8,128)S(1)} %get-tuple-element.104), channel_id=1, source_target_pairs={{0,2},{1,3},{2,0},{3,1},{4,6},{5,7},{6,4},{7,5},{8,10},{9,11},{10,... | collective-permute-start | bytes 12296 | tf_op jit(solution)/shard_map/ppermute | solution.py:406
  44.7 0.1 collective-permute-start.10
  44.8 1.5 %collective-permute-done.11 = f32[8,128]{1,0:T(8,128)S(1)} collective-permute-done((f32[8,128]{1,0:T(8,128)S(1)}, f32[8,128]{1,0:T(8,128)S(1)}, u32[]{:S(2)}, u32[]{:S(2)}) %collective-permute-start.11) | collective-permute-done | bytes 4128 | tf_op jit(solution)/shard_map/ppermute | solution.py:406
  46.3 3.2 %collective-permute-start.15 = (f32[8,128]{1,0:T(8,128)S(1)}, f32[8,128]{1,0:T(8,128)S(1)}, u32[]{:S(2)}, u32[]{:S(2)}) collective-permute-start(f32[8,128]{1,0:T(8,128)S(1)} %add_add_fusion.1), channel_id=1, source_target_pairs={{0,12},{1,13},{2,14},{3,15},{4,8},{5,9},{6,10},{7,11},{8,4},{9,5},... | collective-permute-start | bytes 12296 | tf_op jit(solution)/shard_map/ppermute | solution.py:406
  49.5 1.3 %collective-permute-start.13 = (f32[8,128]{1,0:T(8,128)S(1)}, f32[8,128]{1,0:T(8,128)S(1)}, u32[]{:S(2)}, u32[]{:S(2)}) collective-permute-start(f32[8,128]{1,0:T(8,128)S(1)} %add_add_fusion.1), channel_id=1, source_target_pairs={{0,4},{1,5},{2,6},{3,7},{4,0},{5,1},{6,2},{7,3},{8,12},{9,13},{10,... | collective-permute-start | bytes 12296 | tf_op jit(solution)/shard_map/ppermute | solution.py:406
  50.8 2.2 %finish.1 = (f32[1024,384]{1,0:T(8,128)}, f32[1024,384]{1,0:T(8,128)}) custom-call(bf16[1024,128]{1,0:T(8,128)(2,1)S(1)} %get-tuple-element.92.refs_0_, bf16[1024,128]{1,0:T(8,128)(2,1)S(1)} %get-tuple-element.93.refs_1_, bf16[1024,128]{1,0:T(8,128)(2,1)S(1)} %get-tuple-element.94.refs_2_, f32[1024,128]{1,0:T(8,128)S(1)} %get-tuple-element.95.refs_3_, ...), custom_call_target="tpu_custom_call" | custom-call | flops 1000 | bytes 1000 | tf_op jit(solution)/shard_map/finish/pallas_call | solution.py:21
  53.0 1.0 %collective-permute-done.14 = f32[8,128]{1,0:T(8,128)S(1)} collective-permute-done((f32[8,128]{1,0:T(8,128)S(1)}, f32[8,128]{1,0:T(8,128)S(1)}, u32[]{:S(2)}, u32[]{:S(2)}) %collective-permute-start.14) | collective-permute-done | bytes 4128 | tf_op jit(solution)/shard_map/ppermute | solution.py:406
  54.0 0.5 multiply_bitcast_fusion
  (28 shorter events, 0.1 us)
Async XLA Ops:
  0.6 10.0 %copy-start.2 = (bf16[384,384]{1,0:T(8,128)(2,1)S(1)}, bf16[384,384]{1,0:T(8,128)(2,1)}, u32[]{:S(2)}) copy-start(bf16[384,384]{1,0:T(8,128)(2,1)} %constant.7.clone.refs_4_.refs_9_) | copy-start | bytes 884740
  0.6 10.0 %copy-start.3 = (bf16[384,48]{1,0:T(8,128)(2,1)S(1)}, bf16[384,48]{1,0:T(8,128)(2,1)}, u32[]{:S(2)}) copy-start(bf16[384,48]{1,0:T(8,128)(2,1)} %constant.8.clone.refs_5_) | copy-start | bytes 110596
  0.7 8.1 %copy-start.6 = (s32[96]{0:T(128)S(1)}, s32[96]{0:T(128)}, u32[]{:S(2)}) copy-start(s32[96]{0:T(128)} %cols_hbm.1) | copy-start | bytes 1156
  0.7 8.1 %copy-start.5 = (s32[96]{0:T(128)S(1)}, s32[96]{0:T(128)}, u32[]{:S(2)}) copy-start(s32[96]{0:T(128)} %rows_hbm.1) | copy-start | bytes 1156
  0.7 10.0 %copy-start.4 = (bf16[48,48]{1,0:T(8,128)(2,1)S(1)}, bf16[48,48]{1,0:T(8,128)(2,1)}, u32[]{:S(2)}) copy-start(bf16[48,48]{1,0:T(8,128)(2,1)} %refs_6_.1) | copy-start | bytes 13828
  0.7 10.0 %copy-start.1 = (f32[1024,384]{1,0:T(8,128)S(1)}, f32[1024,384]{1,0:T(8,128)}, u32[]{:S(2)}) copy-start(f32[1024,384]{1,0:T(8,128)} %refs_3_.1) | copy-start | bytes 4718596
  2.1 13.7 %collective-permute-start.4 = (bf16[1024,256]{1,0:T(8,128)(2,1)S(1)}, bf16[1024,256]{1,0:T(8,128)(2,1)S(1)}, u32[]{:S(2)}, u32[]{:S(2)}) collective-permute-start(bf16[1024,256]{1,0:T(8,128)(2,1)S(1)} %get-tuple-element.54._), channel_id=1, source_target_pairs={{0,15},{1,2},{2,1},{3,4},{4,3},{5,6},{6,5},{7,8},{8,7},{9,10},{10,... | collective-permute-start | bytes 1572872 | tf_op jit(solution)/shard_map/ppermute | solution.py:437
  7.6 4.5 %collective-permute-start = (bf16[1024,128]{1,0:T(8,128)(2,1)S(1)}, bf16[1024,128]{1,0:T(8,128)(2,1)S(1)}, u32[]{:S(2)}, u32[]{:S(2)}) collective-permute-start(bf16[1024,128]{1,0:T(8,128)(2,1)S(1)} %get-tuple-element.56.refs_0_), channel_id=1, source_target_pairs={{0,1},{1,0},{2,3},{3,2},{4,5},{5,4},{6,7},{7,6},{8,9},{9,8},{10,11... | collective-permute-start | bytes 786440 | tf_op jit(solution)/shard_map/ppermute | solution.py:440
  7.6 4.5 %collective-permute-start.1 = (bf16[1024,128]{1,0:T(8,128)(2,1)S(1)}, bf16[1024,128]{1,0:T(8,128)(2,1)S(1)}, u32[]{:S(2)}, u32[]{:S(2)}) collective-permute-start(bf16[1024,128]{1,0:T(8,128)(2,1)S(1)} %get-tuple-element.57.refs_1_), channel_id=1, source_target_pairs={{0,1},{1,0},{2,3},{3,2},{4,5},{5,4},{6,7},{7,6},{8,9},{9,8},{10,11... | collective-permute-start | bytes 786440 | tf_op jit(solution)/shard_map/ppermute | solution.py:440
  10.6 1.6 %collective-permute-start.2 = (bf16[1024,128]{1,0:T(8,128)(2,1)S(1)}, bf16[1024,128]{1,0:T(8,128)(2,1)S(1)}, u32[]{:S(2)}, u32[]{:S(2)}) collective-permute-start(bf16[1024,128]{1,0:T(8,128)(2,1)S(1)} %get-tuple-element.58.refs_2_.refs_6_), channel_id=1, source_target_pairs={{0,1},{1,0},{2,3},{3,2},{4,5},{5,4},{6,7},{7,6},{8,9},{9,8},{10,11... | collective-permute-start | bytes 786440 | tf_op jit(solution)/shard_map/ppermute | solution.py:440
  10.7 1.9 %copy-start = (bf16[96,128,128]{2,1,0:T(8,128)(2,1)S(1)}, bf16[96,128,128]{2,1,0:T(8,128)(2,1)}, u32[]{:S(2)}) copy-start(bf16[96,128,128]{2,1,0:T(8,128)(2,1)} %tiles_ref.11) | copy-start | bytes 9437188
  14.5 8.7 %collective-permute-start.3 = (bf16[1024,128]{1,0:T(8,128)(2,1)S(1)}, bf16[1024,128]{1,0:T(8,128)(2,1)S(1)}, u32[]{:S(2)}, u32[]{:S(2)}) collective-permute-start(bf16[1024,128]{1,0:T(8,128)(2,1)S(1)} %get-tuple-element.63), channel_id=1, source_target_pairs={{0,15},{1,2},{2,1},{3,4},{4,3},{5,6},{6,5},{7,8},{8,7},{9,10},{10,... | collective-permute-start | bytes 786440 | tf_op jit(solution)/shard_map/ppermute | solution.py:437
  16.9 20.2 %collective-permute-start.9 = (bf16[1024,128]{1,0:T(8,128)(2,1)S(1)}, bf16[1024,128]{1,0:T(8,128)(2,1)S(1)}, u32[]{:S(2)}, u32[]{:S(2)}) collective-permute-start(bf16[1024,128]{1,0:T(8,128)(2,1)S(1)} %get-tuple-element.76), channel_id=1, source_target_pairs={{0,15},{1,2},{2,1},{3,4},{4,3},{5,6},{6,5},{7,8},{8,7},{9,10},{10,... | collective-permute-start | bytes 786440 | tf_op jit(solution)/shard_map/ppermute | solution.py:437
  24.2 15.4 %collective-permute-start.5 = (bf16[1024,256]{1,0:T(8,128)(2,1)S(1)}, bf16[1024,256]{1,0:T(8,128)(2,1)S(1)}, u32[]{:S(2)}, u32[]{:S(2)}) collective-permute-start(bf16[1024,256]{1,0:T(8,128)(2,1)S(1)} %get-tuple-element.72), channel_id=1, source_target_pairs={{0,15},{1,2},{2,1},{3,4},{4,3},{5,6},{6,5},{7,8},{8,7},{9,10},{10,... | collective-permute-start | bytes 1572872 | tf_op jit(solution)/shard_map/ppermute | solution.py:437
  25.8 11.9 %collective-permute-start.7 = (bf16[1024,128]{1,0:T(8,128)(2,1)S(1)}, bf16[1024,128]{1,0:T(8,128)(2,1)S(1)}, u32[]{:S(2)}, u32[]{:S(2)}) collective-permute-start(bf16[1024,128]{1,0:T(8,128)(2,1)S(1)} %get-tuple-element.74.refs_1_.refs_7_), channel_id=1, source_target_pairs={{0,1},{1,0},{2,3},{3,2},{4,5},{5,4},{6,7},{7,6},{8,9},{9,8},{10,11... | collective-permute-start | bytes 786440 | tf_op jit(solution)/shard_map/ppermute | solution.py:440
  34.9 2.8 %collective-permute-start.8 = (bf16[1024,128]{1,0:T(8,128)(2,1)S(1)}, bf16[1024,128]{1,0:T(8,128)(2,1)S(1)}, u32[]{:S(2)}, u32[]{:S(2)}) collective-permute-start(bf16[1024,128]{1,0:T(8,128)(2,1)S(1)} %get-tuple-element.75.refs_2_.refs_8_), channel_id=1, source_target_pairs={{0,1},{1,0},{2,3},{3,2},{4,5},{5,4},{6,7},{7,6},{8,9},{9,8},{10,11... | collective-permute-start | bytes 786440 | tf_op jit(solution)/shard_map/ppermute | solution.py:440
  34.9 2.8 %collective-permute-start.6 = (bf16[1024,128]{1,0:T(8,128)(2,1)S(1)}, bf16[1024,128]{1,0:T(8,128)(2,1)S(1)}, u32[]{:S(2)}, u32[]{:S(2)}) collective-permute-start(bf16[1024,128]{1,0:T(8,128)(2,1)S(1)} %get-tuple-element.73.refs_0_.refs_6_), channel_id=1, source_target_pairs={{0,1},{1,0},{2,3},{3,2},{4,5},{5,4},{6,7},{7,6},{8,9},{9,8},{10,11... | collective-permute-start | bytes 786440 | tf_op jit(solution)/shard_map/ppermute | solution.py:440
  40.7 4.1 %collective-permute-start.12 = (f32[8,128]{1,0:T(8,128)S(1)}, f32[8,128]{1,0:T(8,128)S(1)}, u32[]{:S(2)}, u32[]{:S(2)}) collective-permute-start(f32[8,128]{1,0:T(8,128)S(1)} %get-tuple-element.104), channel_id=1, source_target_pairs={{0,3},{1,2},{2,1},{3,0},{4,7},{5,6},{6,5},{7,4},{8,11},{9,10},{10,... | collective-permute-start | bytes 12296 | tf_op jit(solution)/shard_map/ppermute | solution.py:406
  40.7 5.6 %collective-permute-start.11 = (f32[8,128]{1,0:T(8,128)S(1)}, f32[8,128]{1,0:T(8,128)S(1)}, u32[]{:S(2)}, u32[]{:S(2)}) collective-permute-start(f32[8,128]{1,0:T(8,128)S(1)} %get-tuple-element.104), channel_id=1, source_target_pairs={{0,2},{1,3},{2,0},{3,1},{4,6},{5,7},{6,4},{7,5},{8,10},{9,11},{10,... | collective-permute-start | bytes 12296 | tf_op jit(solution)/shard_map/ppermute | solution.py:406
  44.7 1.6 %collective-permute-start.10 = (f32[8,128]{1,0:T(8,128)S(1)}, f32[8,128]{1,0:T(8,128)S(1)}, u32[]{:S(2)}, u32[]{:S(2)}) collective-permute-start(f32[8,128]{1,0:T(8,128)S(1)} %get-tuple-element.104), channel_id=1, source_target_pairs={{0,1},{1,0},{2,3},{3,2},{4,5},{5,4},{6,7},{7,6},{8,9},{9,8},{10,11... | collective-permute-start | bytes 12296 | tf_op jit(solution)/shard_map/ppermute | solution.py:406
  46.3 6.6 %collective-permute-start.15 = (f32[8,128]{1,0:T(8,128)S(1)}, f32[8,128]{1,0:T(8,128)S(1)}, u32[]{:S(2)}, u32[]{:S(2)}) collective-permute-start(f32[8,128]{1,0:T(8,128)S(1)} %add_add_fusion.1), channel_id=1, source_target_pairs={{0,12},{1,13},{2,14},{3,15},{4,8},{5,9},{6,10},{7,11},{8,4},{9,5},... | collective-permute-start | bytes 12296 | tf_op jit(solution)/shard_map/ppermute | solution.py:406
  49.5 4.5 %collective-permute-start.14 = (f32[8,128]{1,0:T(8,128)S(1)}, f32[8,128]{1,0:T(8,128)S(1)}, u32[]{:S(2)}, u32[]{:S(2)}) collective-permute-start(f32[8,128]{1,0:T(8,128)S(1)} %add_add_fusion.1), channel_id=1, source_target_pairs={{0,8},{1,9},{2,10},{3,11},{4,12},{5,13},{6,14},{7,15},{8,0},{9,1},... | collective-permute-start | bytes 12296 | tf_op jit(solution)/shard_map/ppermute | solution.py:406
  49.5 4.5 %collective-permute-start.13 = (f32[8,128]{1,0:T(8,128)S(1)}, f32[8,128]{1,0:T(8,128)S(1)}, u32[]{:S(2)}, u32[]{:S(2)}) collective-permute-start(f32[8,128]{1,0:T(8,128)S(1)} %add_add_fusion.1), channel_id=1, source_target_pairs={{0,4},{1,5},{2,6},{3,7},{4,0},{5,1},{6,2},{7,3},{8,12},{9,13},{10,... | collective-permute-start | bytes 12296 | tf_op jit(solution)/shard_map/ppermute | solution.py:406

commit v6 on v5

--- a/solution.py
+++ b/solution.py
@@ -361,50 +361,71 @@
     return outs[:groups], outs[groups:]
 
 
-def finish(fields, xs, bases, mixing, channels):
-    groups = len(xs)
+def finish(todo, fields, xs, bases, mixing, channels, outputs, name):
+    width = mixing.shape[0]
     cells = xs[0].shape[0]
-    width = groups * LANES
+    near = sorted({n for t in todo for n in spanned(t, channels, width)})
+    m, n = len(near), len(todo)
 
     def body(*refs):
-        field_refs, x_refs, base_refs = [refs[k * groups : (k + 1) * groups] for k in range(3)]
-        mixing_ref, x_out, y_out, x_buf, y_buf, sems = refs[3 * groups :]
-        held = [ref[...] for ref in field_refs]
+        field_refs, x_refs, base_refs = refs[:m], refs[m : m + n], refs[m + n : m + 2 * n]
+        mixing_ref = refs[m + 2 * n]
+        x_out, y_out, token, x_buf, y_buf, sems = refs[-6:]
+        held = {g: ref[...] for g, ref in zip(near, field_refs)}
         copies = []
-        for g in range(groups):
-            y_new = base_refs[g][...] - 0.2 * mixed_of(held, mixing_ref, g, channels)
-            y_buf[g] = y_new
-            x_buf[g] = jnp.clip(x_refs[g][...] + 0.5 * y_new, -1.0, 1.0)
+        for i, t in enumerate(todo):
+            y_new = base_refs[i][...] - 0.2 * mixed_of(held, mixing_ref, t, channels)
+            y_buf[i] = y_new
+            x_buf[i] = jnp.clip(x_refs[i][...] + 0.5 * y_new, -1.0, 1.0)
             for k, (buf, out) in enumerate(((y_buf, y_out), (x_buf, x_out))):
                 copies.append(
-                    pltpu.make_async_copy(buf.at[g], out.at[:, lanes(g)], sems.at[g, k])
+                    pltpu.make_async_copy(buf.at[i], out.at[:, lanes(t)], sems.at[i, k])
                 )
                 copies[-1].start()
+        token[...] = jnp.zeros_like(token)
         for copy in copies:
             copy.wait()
 
+    ins = vmem(*[fields[g] for g in near], *[xs[t] for t in todo], *[bases[t] for t in todo], mixing)
+    first = len(ins)
     return call(
         body,
-        vmem(*fields, *xs, *bases, mixing),
-        [((cells, width), F32, pltpu.HBM)] * 2,
+        ins + [(a, pltpu.HBM) for a in outputs],
+        [((cells, width), F32, pltpu.HBM)] * 2 + [((8, LANES), F32, pltpu.VMEM)],
         [
-            pltpu.VMEM((groups, cells, LANES), F32),
-            pltpu.VMEM((groups, cells, LANES), F32),
-            pltpu.SemaphoreType.DMA((groups, 2)),
+            pltpu.VMEM((n, cells, LANES), F32),
+            pltpu.VMEM((n, cells, LANES), F32),
+            pltpu.SemaphoreType.DMA((n, 2)),
         ],
-        "finish",
-    )
-
-
-def sum_over_ring(value, ring):
+        name,
+        0,
+        [(first + i, i) for i in range(len(outputs))],
+    )
+
+
+def add_up(arrays, token):
+    def body(*refs):
+        refs[-1][...] = sum(ref[...] for ref in refs[:-2])
+
+    return call(
+        body,
+        vmem(*arrays, token),
+        [(arrays[0].shape, F32, pltpu.VMEM)],
+        [],
+        "add_up",
+    )[0]
+
+
+def sum_over_ring(value, ring, token):
     if ring & (ring - 1):
         return lax.psum(value, RING)
     size = 1
     while size < ring:
         digits = (1, 2, 3) if 4 * size <= ring else (1,)
-        value = value + sum(
+        parts = [value] + [
             lax.ppermute(value, RING, [(i, i ^ (size * d)) for i in range(ring)]) for d in digits
-        )
+        ]
+        value = add_up(parts, token) if size == 1 else sum(parts)
         size *= len(digits) + 1
     return value
 
@@ -549,11 +570,22 @@
     fields, partial, kept = results[: len(piece)], results[len(piece)], results[len(piece) + 1 :]
     fields, kept = [kept[0], *fields], kept[1:]
 
-    total = sum_over_ring(partial, ring)
+    outputs = []
+    for part, todo in enumerate((every[:-1], every[-1:])):
+        *outputs, token = finish(
+            todo,
+            fields,
+            kept[:groups],
+            kept[groups : 2 * groups],
+            kept[2 * groups],
+            channels,
+            outputs,
+            f"finish_{part}",
+        )
+        if part == 0:
+            total = sum_over_ring(partial, ring, token)
     energy = total[0, :replicas] / jnp.sqrt(jnp.float32(cells * ring * channels))
-    x_new, y_new = finish(
-        fields, kept[:groups], kept[groups : 2 * groups], kept[2 * groups], channels
-    )
+    x_new, y_new = outputs
     return (x_new, y_new, energy)
 
 

time: 55 us -> 55.1 us (level)
  Pallas kernels: 15.9 us -> 18.1 us
  waiting for transfers between devices: 5.38 us -> 4.1 us
  starting transfers between devices: 30.7 us -> 30 us
    pallas_call x11 -> x13, Pallas kernels: 15.9 us -> 18.1 us  [call(): pl.pallas_call(body, in_specs=[pl.BlockSpec(memory_space=pl.ANY if s is p...]
    ppermute x6, waiting for transfers between devices: 2.55 us -> 1.2 us  [sum_over_ring(): lax.ppermute(value, RING, [(i, i ^ size * d) for i in range(ring)])]
    ppermute x4, starting transfers between devices: 12 us -> 10.8 us  [far_swap(): return lax.ppermute(mine, RING, off_chip)]
    ppermute x6, starting transfers between devices: 10.2 us -> 10.9 us  [near_swap(): return lax.ppermute(mine, RING, on_chip)]
  transfers between devices with their start and end apart: 16 -> 16, of which waited for: 3 -> 2; matrix products, arithmetic and copies ran while one was open for 0% -> 0% of each run, Pallas kernels for 25% -> 28%
where the time goes in v6:
time: 55.1 us; the launch traced here: 54.7 us
  starting transfers between devices  30 us (54%)
  Pallas kernels  18.1 us (33%)
  waiting for transfers between devices  4.1 us (7%)
  between operations  1.55 us (3%)
    pallas_call x13, Pallas kernels, call(): pl.pallas_call(body, in_specs=[pl.BlockSpec(memory_space=pl.ANY if s is p...  18.1 us
    ppermute x6, starting transfers between devices, near_swap(): return lax.ppermute(mine, RING, on_chip)  10.9 us
    ppermute x4, starting transfers between devices, far_swap(): return lax.ppermute(mine, RING, off_chip)  10.8 us
    ppermute x6, starting transfers between devices, sum_over_ring(): lax.ppermute(value, RING, [(i, i ^ size * d) for i in range(ring)])  8.31 us
    ppermute x4, waiting for transfers between devices, far_swap(): return lax.ppermute(mine, RING, off_chip)  2.88 us
    ppermute x6, waiting for transfers between devices, sum_over_ring(): lax.ppermute(value, RING, [(i, i ^ size * d) for i in range(ring)])  1.2 us
  transfers between devices with their start and end apart: 16, of which 2 were waited for; matrix products, arithmetic and copies ran while one was open for 0% of the time, Pallas kernels for 28%

profile of v6, /device:TPU:0, one launch (start us, length us, event | category | flops | bytes accessed | tf_op | source)
XLA Modules:
  0.0 54.7 jit_solution(15488458037885750060)
XLA Ops:
  0.6 0.0 copy-start.2
  0.6 0.0 copy-start.3
  0.7 1.4 %load_first.1 = (f32[1024,128]{1,0:T(8,128)S(1)}, f32[1024,128]{1,0:T(8,128)S(1)}, bf16[1024,128]{1,0:T(8,128)(2,1)S(1)}, bf16[1024,128]{1,0:T(8,128)(2,1)S(1)}, bf16[1024,256]{1,0:T(8,128)(2,1)S(1)}) custom-call(f32[1024,384]{1,0:T(8,128)} %x_ref.3), custom_call_target="tpu_custom_call" | custom-call | flops 1000 | bytes 1000 | tf_op jit(solution)/shard_map/load_first/pallas_call | solution.py:21
  2.1 5.5 %collective-permute-start.4 = (bf16[1024,256]{1,0:T(8,128)(2,1)S(1)}, bf16[1024,256]{1,0:T(8,128)(2,1)S(1)}, u32[]{:S(2)}, u32[]{:S(2)}) collective-permute-start(bf16[1024,256]{1,0:T(8,128)(2,1)S(1)} %get-tuple-element.57._), channel_id=1, source_target_pairs={{0,15},{1,2},{2,1},{3,4},{4,3},{5,6},{6,5},{7,8},{8,7},{9,10},{10,... | collective-permute-start | bytes 1572872 | tf_op jit(solution)/shard_map/ppermute | solution.py:458
  7.6 0.5 collective-permute-start.1
  8.8 1.9 %make_lists.1 = (s32[214]{0:T(256)S(4)}, f32[1024,128]{1,0:T(8,128)S(1)}, bf16[1024,128]{1,0:T(8,128)(2,1)S(1)}) custom-call(s32[96]{0:T(128)S(1)} %copy-done.5, s32[96]{0:T(128)S(1)} %copy-done.6, s32[1]{0:T(128)S(6)} %copy.32.count_hbm, f32[1024,384]{1,0:T(8,128)} %x_ref.3, bf16[1024,256]{1,0:T(8,128)(2,1)S(1)} %get-tuple-element.57._), custom_call_target="tpu_custom_call" | custom-call | flops 1000 | bytes 1000 | tf_op jit(solution)/shard_map/make_lists/pallas_call | solution.py:21
  10.7 0.5 collective-permute-start.2
  11.2 0.0 copy-start
  11.2 1.4 %first_base.1 = (f32[1024,128]{1,0:T(8,128)S(1)}, f32[1024,128]{1,0:T(8,128)S(1)}, f32[1024,128]{1,0:T(8,128)S(1)}, bf16[384,384]{1,0:T(8,128)(2,1)S(1)}) custom-call(f32[1024,128]{1,0:T(8,128)S(1)} %get-tuple-element.62.refs_0_.refs_4_, f32[1024,128]{1,0:T(8,128)S(1)} %get-tuple-element.63.refs_1_.refs_5_, ...), custom_call_target="tpu_custom_call" | custom-call | flops 1000 | bytes 1000 | tf_op jit(solution)/shard_map/first_base/pallas_call | solution.py:21
  12.7 0.0 collective-permute-done.2.refs_5_
  12.7 0.4 copy-done
  13.1 2.2 %near_first.1 = (f32[1024,128]{1,0:T(8,128)S(1)}, f32[1024,128]{1,0:T(8,128)S(1)}, f32[1024,128]{1,0:T(8,128)S(1)}, bf16[1024,128]{1,0:T(8,128)(2,1)S(1)}) custom-call(s32[214]{0:T(256)S(4)} %get-tuple-element.58.list_ref, bf16[96,128,128]{2,1,0:T(8,128)(2,1)S(1)} %copy-done, bf16[1024,128]{1,0:T(8,128)(2,1)S(1)} %get-tuple-element.59.refs_0_, ...), custom_call_target="tpu_custom_call" | custom-call | flops 1000 | bytes 1000 | tf_op jit(solution)/shard_map/near_first/pallas_call | solution.py:21
  15.3 0.3 collective-permute-start.3
  15.6 1.0 %far_first_0.1 = (f32[1024,128]{1,0:T(8,128)S(1)}, f32[1024,128]{1,0:T(8,128)S(1)}, bf16[1024,128]{1,0:T(8,128)(2,1)S(1)}, bf16[1024,128]{1,0:T(8,128)(2,1)S(1)}...) custom-call(s32[214]{0:T(256)S(4)} %get-tuple-element.58.list_ref, bf16[96,128,128]{2,1,0:T(8,128)(2,1)S(1)} %copy-done, ...), custom_call_target="tpu_custom_call" | custom-call | flops 1000 | bytes 1000 | tf_op jit(solution)/shard_map/far_first_0/pallas_call | solution.py:21
  16.6 4.5 %collective-permute-start.9 = (bf16[1024,128]{1,0:T(8,128)(2,1)S(1)}, bf16[1024,128]{1,0:T(8,128)(2,1)S(1)}, u32[]{:S(2)}, u32[]{:S(2)}) collective-permute-start(bf16[1024,128]{1,0:T(8,128)(2,1)S(1)} %get-tuple-element.79), channel_id=1, source_target_pairs={{0,15},{1,2},{2,1},{3,4},{4,3},{5,6},{6,5},{7,8},{8,7},{9,10},{10,... | collective-permute-start | bytes 786440 | tf_op jit(solution)/shard_map/ppermute | solution.py:458
  21.1 2.9 %collective-permute-done.3.far_ref = bf16[1024,128]{1,0:T(8,128)(2,1)S(1)} collective-permute-done((bf16[1024,128]{1,0:T(8,128)(2,1)S(1)}, bf16[1024,128]{1,0:T(8,128)(2,1)S(1)}, u32[]{:S(2)}, u32[]{:S(2)}) %collective-permute-start.3) | collective-permute-done | bytes 262176 | tf_op jit(solution)/shard_map/ppermute | solution.py:458
  23.9 1.1 %far_first_1.1 = (f32[1024,128]{1,0:T(8,128)S(1)}, f32[1024,128]{1,0:T(8,128)S(1)}, bf16[1024,128]{1,0:T(8,128)(2,1)S(1)}, f32[1024,128]{1,0:T(8,128)S(1)}, f32[...) custom-call(s32[214]{0:T(256)S(4)} %get-tuple-element.58.list_ref, ...), custom_call_target="tpu_custom_call" | custom-call | flops 1000 | bytes 1000 | tf_op jit(solution)/shard_map/far_first_1/pallas_call | solution.py:21
  25.0 0.5 collective-permute-start.5
  25.5 9.4 %collective-permute-start.7 = (bf16[1024,128]{1,0:T(8,128)(2,1)S(1)}, bf16[1024,128]{1,0:T(8,128)(2,1)S(1)}, u32[]{:S(2)}, u32[]{:S(2)}) collective-permute-start(bf16[1024,128]{1,0:T(8,128)(2,1)S(1)} %get-tuple-element.77.refs_1_.refs_7_), channel_id=1, source_target_pairs={{0,1},{1,0},{2,3},{3,2},{4,5},{5,4},{6,7},{7,6},{8,9},{9,8},{10,11... | collective-permute-start | bytes 786440 | tf_op jit(solution)/shard_map/ppermute | solution.py:461
  34.9 0.5 collective-permute-start.6
  35.4 1.7 %second_base.1 = (f32[1024,128]{1,0:T(8,128)S(1)}, f32[1024,128]{1,0:T(8,128)S(1)}, f32[1024,128]{1,0:T(8,128)S(1)}, f32[1024,128]{1,0:T(8,128)S(1)}, f32[1024,128]{1,0:T(8,128)S(1)}, /*index=5*/f32[1024,128]{1,0:T(8,128)S(1)}) custom-call(f32[1024,128]{1,0:T(8,128)S(1)} %get-tuple-element.82.refs_0_.refs_6_, ...), custom_call_target="tpu_custom_call" | custom-call | flops 1000 | bytes 1000 | tf_op jit(solution)/shard_map/second_base/pallas_call | solution.py:21
  37.1 0.6 %far_second_0.1.refs_6_ = f32[1024,128]{1,0:T(8,128)S(1)} custom-call(s32[214]{0:T(256)S(4)} %get-tuple-element.58.list_ref, bf16[96,128,128]{2,1,0:T(8,128)(2,1)S(1)} %copy-done, bf16[1024,128]{1,0:T(8,128)(2,1)S(1)} %collective-permute-done.9.far_ref), custom_call_target="tpu_custom_call" | custom-call | flops 4000000000 | bytes 1000 | tf_op jit(solution)/shard_map/far_second_0/pallas_call | solution.py:21
  37.7 2.1 %near_second.1 = (bf16[1024,128]{1,0:T(8,128)(2,1)S(1)}, f32[1024,128]{1,0:T(8,128)S(1)}, f32[1024,128]{1,0:T(8,128)S(1)}) custom-call(s32[214]{0:T(256)S(4)} %get-tuple-element.58.list_ref, bf16[96,128,128]{2,1,0:T(8,128)(2,1)S(1)} %copy-done, bf16[1024,128]{1,0:T(8,128)(2,1)S(1)} %get-tuple-element.76.refs_0_.refs_6_, ...), custom_call_target="tpu_custom_call" | custom-call | flops 1000 | bytes 1000 | tf_op jit(solution)/shard_map/near_second/pallas_call | solution.py:21
  39.9 1.1 %far_second_1.1 = (bf16[1024,128]{1,0:T(8,128)(2,1)S(1)}, bf16[1024,128]{1,0:T(8,128)(2,1)S(1)}, f32[8,128]{1,0:T(8,128)S(1)}, bf16[1024,128]{1,0:T(8,128)(2,1)S...) custom-call(s32[214]{0:T(256)S(4)} %get-tuple-element.58.list_ref, ...), custom_call_target="tpu_custom_call", output_to_operand_aliasing={{3}: (8, {}), {4}: (9, {}), {5}: (10, {}), {6}: (11, {}), {... | custom-call | flops 1000 | bytes 1000 | tf_op jit(solution)/shard_map/far_second_1/pallas_call | solution.py:21
  41.0 0.5 collective-permute-start.12
  41.4 3.4 %collective-permute-start.11 = (f32[8,128]{1,0:T(8,128)S(1)}, f32[8,128]{1,0:T(8,128)S(1)}, u32[]{:S(2)}, u32[]{:S(2)}) collective-permute-start(f32[8,128]{1,0:T(8,128)S(1)} %get-tuple-element.109.refs_0_), channel_id=1, source_target_pairs={{0,2},{1,3},{2,0},{3,1},{4,6},{5,7},{6,4},{7,5},{8,10},{9,11},{10,... | collective-permute-start | bytes 12296 | tf_op jit(solution)/shard_map/ppermute | solution.py:426
  44.8 1.7 %finish_0.1 = (f32[1024,384]{1,0:T(8,128)}, f32[1024,384]{1,0:T(8,128)}, f32[8,128]{1,0:T(8,128)S(1)}) custom-call(bf16[1024,128]{1,0:T(8,128)(2,1)S(1)} %get-tuple-element.100.refs_0_, bf16[1024,128]{1,0:T(8,128)(2,1)S(1)} %get-tuple-element.95.refs_1_.refs_0_, bf16[1024,128]{1,0:T(8,128)(2,1)S(1)} %get-tuple-element.96.refs_2_.refs_1_, ...), custom_call_target="tpu_custom_call" | custom-call | flops 1000 | bytes 1000 | tf_op jit(solution)/shard_map/finish_0/pallas_call | solution.py:21
  46.6 3.1 %collective-permute-start.15 = (f32[8,128]{1,0:T(8,128)S(1)}, f32[8,128]{1,0:T(8,128)S(1)}, u32[]{:S(2)}, u32[]{:S(2)}) collective-permute-start(f32[8,128]{1,0:T(8,128)S(1)} %add_up.1), channel_id=1, source_target_pairs={{0,12},{1,13},{2,14},{3,15},{4,8},{5,9},{6,10},{7,11},{8,4},{9,5},... | collective-permute-start | bytes 12296 | tf_op jit(solution)/shard_map/ppermute | solution.py:426
  49.6 1.4 %collective-permute-start.13 = (f32[8,128]{1,0:T(8,128)S(1)}, f32[8,128]{1,0:T(8,128)S(1)}, u32[]{:S(2)}, u32[]{:S(2)}) collective-permute-start(f32[8,128]{1,0:T(8,128)S(1)} %add_up.1), channel_id=1, source_target_pairs={{0,4},{1,5},{2,6},{3,7},{4,0},{5,1},{6,2},{7,3},{8,12},{9,13},{10,... | collective-permute-start | bytes 12296 | tf_op jit(solution)/shard_map/ppermute | solution.py:426
  51.1 1.9 %finish_1.1 = (f32[1024,384]{1,0:T(8,128)}, f32[1024,384]{1,0:T(8,128)}, f32[8,128]{1,0:T(8,128)}) custom-call(bf16[1024,128]{1,0:T(8,128)(2,1)S(1)} %get-tuple-element.95.refs_1_.refs_0_, bf16[1024,128]{1,0:T(8,128)(2,1)S(1)} %get-tuple-element.96.refs_2_.refs_1_, ...), custom_call_target="tpu_custom_call", output_to_operand_aliasing={{0}: (5, {}), {1}: (6, {})} | custom-call | flops 1000 | bytes 1000 | tf_op jit(solution)/shard_map/finish_1/pallas_call | solution.py:21
  53.0 1.2 %collective-permute-done.14 = f32[8,128]{1,0:T(8,128)S(1)} collective-permute-done((f32[8,128]{1,0:T(8,128)S(1)}, f32[8,128]{1,0:T(8,128)S(1)}, u32[]{:S(2)}, u32[]{:S(2)}) %collective-permute-start.14) | collective-permute-done | bytes 4128 | tf_op jit(solution)/shard_map/ppermute | solution.py:426
  54.2 0.5 multiply_bitcast_fusion
  (29 shorter events, 0.1 us)
Async XLA Ops:
  0.6 10.6 %copy-start.2 = (bf16[384,384]{1,0:T(8,128)(2,1)S(1)}, bf16[384,384]{1,0:T(8,128)(2,1)}, u32[]{:S(2)}) copy-start(bf16[384,384]{1,0:T(8,128)(2,1)} %constant.7.clone.refs_4_.refs_9_) | copy-start | bytes 884740
  0.6 10.6 %copy-start.3 = (bf16[384,48]{1,0:T(8,128)(2,1)S(1)}, bf16[384,48]{1,0:T(8,128)(2,1)}, u32[]{:S(2)}) copy-start(bf16[384,48]{1,0:T(8,128)(2,1)} %constant.8.clone.refs_5_) | copy-start | bytes 110596
  0.7 8.1 %copy-start.6 = (s32[96]{0:T(128)S(1)}, s32[96]{0:T(128)}, u32[]{:S(2)}) copy-start(s32[96]{0:T(128)} %cols_hbm.1) | copy-start | bytes 1156
  0.7 8.1 %copy-start.5 = (s32[96]{0:T(128)S(1)}, s32[96]{0:T(128)}, u32[]{:S(2)}) copy-start(s32[96]{0:T(128)} %rows_hbm.1) | copy-start | bytes 1156
  0.7 10.5 %copy-start.4 = (bf16[48,48]{1,0:T(8,128)(2,1)S(1)}, bf16[48,48]{1,0:T(8,128)(2,1)}, u32[]{:S(2)}) copy-start(bf16[48,48]{1,0:T(8,128)(2,1)} %refs_6_.1) | copy-start | bytes 13828
  0.7 10.5 %copy-start.1 = (f32[1024,384]{1,0:T(8,128)S(1)}, f32[1024,384]{1,0:T(8,128)}, u32[]{:S(2)}) copy-start(f32[1024,384]{1,0:T(8,128)} %refs_3_.1) | copy-start | bytes 4718596
  2.1 13.4 %collective-permute-start.4 = (bf16[1024,256]{1,0:T(8,128)(2,1)S(1)}, bf16[1024,256]{1,0:T(8,128)(2,1)S(1)}, u32[]{:S(2)}, u32[]{:S(2)}) collective-permute-start(bf16[1024,256]{1,0:T(8,128)(2,1)S(1)} %get-tuple-element.57._), channel_id=1, source_target_pairs={{0,15},{1,2},{2,1},{3,4},{4,3},{5,6},{6,5},{7,8},{8,7},{9,10},{10,... | collective-permute-start | bytes 1572872 | tf_op jit(solution)/shard_map/ppermute | solution.py:458
  7.6 5.0 %collective-permute-start = (bf16[1024,128]{1,0:T(8,128)(2,1)S(1)}, bf16[1024,128]{1,0:T(8,128)(2,1)S(1)}, u32[]{:S(2)}, u32[]{:S(2)}) collective-permute-start(bf16[1024,128]{1,0:T(8,128)(2,1)S(1)} %get-tuple-element.59.refs_0_), channel_id=1, source_target_pairs={{0,1},{1,0},{2,3},{3,2},{4,5},{5,4},{6,7},{7,6},{8,9},{9,8},{10,11... | collective-permute-start | bytes 786440 | tf_op jit(solution)/shard_map/ppermute | solution.py:461
  7.6 5.0 %collective-permute-start.1 = (bf16[1024,128]{1,0:T(8,128)(2,1)S(1)}, bf16[1024,128]{1,0:T(8,128)(2,1)S(1)}, u32[]{:S(2)}, u32[]{:S(2)}) collective-permute-start(bf16[1024,128]{1,0:T(8,128)(2,1)S(1)} %get-tuple-element.60.refs_1_), channel_id=1, source_target_pairs={{0,1},{1,0},{2,3},{3,2},{4,5},{5,4},{6,7},{7,6},{8,9},{9,8},{10,11... | collective-permute-start | bytes 786440 | tf_op jit(solution)/shard_map/ppermute | solution.py:461
  10.7 1.9 %collective-permute-start.2 = (bf16[1024,128]{1,0:T(8,128)(2,1)S(1)}, bf16[1024,128]{1,0:T(8,128)(2,1)S(1)}, u32[]{:S(2)}, u32[]{:S(2)}) collective-permute-start(bf16[1024,128]{1,0:T(8,128)(2,1)S(1)} %get-tuple-element.61.refs_2_.refs_6_), channel_id=1, source_target_pairs={{0,1},{1,0},{2,3},{3,2},{4,5},{5,4},{6,7},{7,6},{8,9},{9,8},{10,11... | collective-permute-start | bytes 786440 | tf_op jit(solution)/shard_map/ppermute | solution.py:461
  11.2 1.9 %copy-start = (bf16[96,128,128]{2,1,0:T(8,128)(2,1)S(1)}, bf16[96,128,128]{2,1,0:T(8,128)(2,1)}, u32[]{:S(2)}) copy-start(bf16[96,128,128]{2,1,0:T(8,128)(2,1)} %tiles_ref.11) | copy-start | bytes 9437188
  15.3 8.7 %collective-permute-start.3 = (bf16[1024,128]{1,0:T(8,128)(2,1)S(1)}, bf16[1024,128]{1,0:T(8,128)(2,1)S(1)}, u32[]{:S(2)}, u32[]{:S(2)}) collective-permute-start(bf16[1024,128]{1,0:T(8,128)(2,1)S(1)} %get-tuple-element.66), channel_id=1, source_target_pairs={{0,15},{1,2},{2,1},{3,4},{4,3},{5,6},{6,5},{7,8},{8,7},{9,10},{10,... | collective-permute-start | bytes 786440 | tf_op jit(solution)/shard_map/ppermute | solution.py:458
  16.6 20.6 %collective-permute-start.9 = (bf16[1024,128]{1,0:T(8,128)(2,1)S(1)}, bf16[1024,128]{1,0:T(8,128)(2,1)S(1)}, u32[]{:S(2)}, u32[]{:S(2)}) collective-permute-start(bf16[1024,128]{1,0:T(8,128)(2,1)S(1)} %get-tuple-element.79), channel_id=1, source_target_pairs={{0,15},{1,2},{2,1},{3,4},{4,3},{5,6},{6,5},{7,8},{8,7},{9,10},{10,... | collective-permute-start | bytes 786440 | tf_op jit(solution)/shard_map/ppermute | solution.py:458
  25.0 14.9 %collective-permute-start.5 = (bf16[1024,256]{1,0:T(8,128)(2,1)S(1)}, bf16[1024,256]{1,0:T(8,128)(2,1)S(1)}, u32[]{:S(2)}, u32[]{:S(2)}) collective-permute-start(bf16[1024,256]{1,0:T(8,128)(2,1)S(1)} %get-tuple-element.75), channel_id=1, source_target_pairs={{0,15},{1,2},{2,1},{3,4},{4,3},{5,6},{6,5},{7,8},{8,7},{9,10},{10,... | collective-permute-start | bytes 1572872 | tf_op jit(solution)/shard_map/ppermute | solution.py:458
  25.5 12.2 %collective-permute-start.7 = (bf16[1024,128]{1,0:T(8,128)(2,1)S(1)}, bf16[1024,128]{1,0:T(8,128)(2,1)S(1)}, u32[]{:S(2)}, u32[]{:S(2)}) collective-permute-start(bf16[1024,128]{1,0:T(8,128)(2,1)S(1)} %get-tuple-element.77.refs_1_.refs_7_), channel_id=1, source_target_pairs={{0,1},{1,0},{2,3},{3,2},{4,5},{5,4},{6,7},{7,6},{8,9},{9,8},{10,11... | collective-permute-start | bytes 786440 | tf_op jit(solution)/shard_map/ppermute | solution.py:461
  34.9 2.8 %collective-permute-start.8 = (bf16[1024,128]{1,0:T(8,128)(2,1)S(1)}, bf16[1024,128]{1,0:T(8,128)(2,1)S(1)}, u32[]{:S(2)}, u32[]{:S(2)}) collective-permute-start(bf16[1024,128]{1,0:T(8,128)(2,1)S(1)} %get-tuple-element.78.refs_2_.refs_8_), channel_id=1, source_target_pairs={{0,1},{1,0},{2,3},{3,2},{4,5},{5,4},{6,7},{7,6},{8,9},{9,8},{10,11... | collective-permute-start | bytes 786440 | tf_op jit(solution)/shard_map/ppermute | solution.py:461
  34.9 2.8 %collective-permute-start.6 = (bf16[1024,128]{1,0:T(8,128)(2,1)S(1)}, bf16[1024,128]{1,0:T(8,128)(2,1)S(1)}, u32[]{:S(2)}, u32[]{:S(2)}) collective-permute-start(bf16[1024,128]{1,0:T(8,128)(2,1)S(1)} %get-tuple-element.76.refs_0_.refs_6_), channel_id=1, source_target_pairs={{0,1},{1,0},{2,3},{3,2},{4,5},{5,4},{6,7},{7,6},{8,9},{9,8},{10,11... | collective-permute-start | bytes 786440 | tf_op jit(solution)/shard_map/ppermute | solution.py:461
  41.0 5.6 %collective-permute-start.12 = (f32[8,128]{1,0:T(8,128)S(1)}, f32[8,128]{1,0:T(8,128)S(1)}, u32[]{:S(2)}, u32[]{:S(2)}) collective-permute-start(f32[8,128]{1,0:T(8,128)S(1)} %get-tuple-element.109.refs_0_), channel_id=1, source_target_pairs={{0,3},{1,2},{2,1},{3,0},{4,7},{5,6},{6,5},{7,4},{8,11},{9,10},{10,... | collective-permute-start | bytes 12296 | tf_op jit(solution)/shard_map/ppermute | solution.py:426
  41.4 5.1 %collective-permute-start.11 = (f32[8,128]{1,0:T(8,128)S(1)}, f32[8,128]{1,0:T(8,128)S(1)}, u32[]{:S(2)}, u32[]{:S(2)}) collective-permute-start(f32[8,128]{1,0:T(8,128)S(1)} %get-tuple-element.109.refs_0_), channel_id=1, source_target_pairs={{0,2},{1,3},{2,0},{3,1},{4,6},{5,7},{6,4},{7,5},{8,10},{9,11},{10,... | collective-permute-start | bytes 12296 | tf_op jit(solution)/shard_map/ppermute | solution.py:426
  44.8 1.8 %collective-permute-start.10 = (f32[8,128]{1,0:T(8,128)S(1)}, f32[8,128]{1,0:T(8,128)S(1)}, u32[]{:S(2)}, u32[]{:S(2)}) collective-permute-start(f32[8,128]{1,0:T(8,128)S(1)} %get-tuple-element.109.refs_0_), channel_id=1, source_target_pairs={{0,1},{1,0},{2,3},{3,2},{4,5},{5,4},{6,7},{7,6},{8,9},{9,8},{10,11... | collective-permute-start | bytes 12296 | tf_op jit(solution)/shard_map/ppermute | solution.py:426
  46.6 6.4 %collective-permute-start.15 = (f32[8,128]{1,0:T(8,128)S(1)}, f32[8,128]{1,0:T(8,128)S(1)}, u32[]{:S(2)}, u32[]{:S(2)}) collective-permute-start(f32[8,128]{1,0:T(8,128)S(1)} %add_up.1), channel_id=1, source_target_pairs={{0,12},{1,13},{2,14},{3,15},{4,8},{5,9},{6,10},{7,11},{8,4},{9,5},... | collective-permute-start | bytes 12296 | tf_op jit(solution)/shard_map/ppermute | solution.py:426
  49.6 4.5 %collective-permute-start.14 = (f32[8,128]{1,0:T(8,128)S(1)}, f32[8,128]{1,0:T(8,128)S(1)}, u32[]{:S(2)}, u32[]{:S(2)}) collective-permute-start(f32[8,128]{1,0:T(8,128)S(1)} %add_up.1), channel_id=1, source_target_pairs={{0,8},{1,9},{2,10},{3,11},{4,12},{5,13},{6,14},{7,15},{8,0},{9,1},... | collective-permute-start | bytes 12296 | tf_op jit(solution)/shard_map/ppermute | solution.py:426
  49.6 4.5 %collective-permute-start.13 = (f32[8,128]{1,0:T(8,128)S(1)}, f32[8,128]{1,0:T(8,128)S(1)}, u32[]{:S(2)}, u32[]{:S(2)}) collective-permute-start(f32[8,128]{1,0:T(8,128)S(1)} %add_up.1), channel_id=1, source_target_pairs={{0,4},{1,5},{2,6},{3,7},{4,0},{5,1},{6,2},{7,3},{8,12},{9,13},{10,... | collective-permute-start | bytes 12296 | tf_op jit(solution)/shard_map/ppermute | solution.py:426

commit v7 on v5

--- a/solution.py
+++ b/solution.py
@@ -368,7 +368,7 @@
 
     def body(*refs):
         field_refs, x_refs, base_refs = [refs[k * groups : (k + 1) * groups] for k in range(3)]
-        mixing_ref, x_out, y_out, x_buf, y_buf, sems = refs[3 * groups :]
+        mixing_ref, x_out, y_out, token, x_buf, y_buf, sems = refs[3 * groups :]
         held = [ref[...] for ref in field_refs]
         copies = []
         for g in range(groups):
@@ -380,13 +380,14 @@
                     pltpu.make_async_copy(buf.at[g], out.at[:, lanes(g)], sems.at[g, k])
                 )
                 copies[-1].start()
+        token[...] = jnp.zeros_like(token)
         for copy in copies:
             copy.wait()
 
     return call(
         body,
         vmem(*fields, *xs, *bases, mixing),
-        [((cells, width), F32, pltpu.HBM)] * 2,
+        [((cells, width), F32, pltpu.HBM)] * 2 + [((8, LANES), F32, pltpu.VMEM)],
         [
             pltpu.VMEM((groups, cells, LANES), F32),
             pltpu.VMEM((groups, cells, LANES), F32),
@@ -396,15 +397,29 @@
     )
 
 
-def sum_over_ring(value, ring):
+def add_up(arrays, token):
+    def body(*refs):
+        refs[-1][...] = sum(ref[...] for ref in refs[:-2])
+
+    return call(
+        body,
+        vmem(*arrays, token),
+        [(arrays[0].shape, F32, pltpu.VMEM)],
+        [],
+        "add_up",
+    )[0]
+
+
+def sum_over_ring(value, ring, token):
     if ring & (ring - 1):
         return lax.psum(value, RING)
     size = 1
     while size < ring:
         digits = (1, 2, 3) if 4 * size <= ring else (1,)
-        value = value + sum(
+        parts = [value] + [
             lax.ppermute(value, RING, [(i, i ^ (size * d)) for i in range(ring)]) for d in digits
-        )
+        ]
+        value = add_up(parts, token) if size == 1 else sum(parts)
         size *= len(digits) + 1
     return value
 
@@ -549,11 +564,11 @@
     fields, partial, kept = results[: len(piece)], results[len(piece)], results[len(piece) + 1 :]
     fields, kept = [kept[0], *fields], kept[1:]
 
-    total = sum_over_ring(partial, ring)
+    x_new, y_new, token = finish(
+        fields, kept[:groups], kept[groups : 2 * groups], kept[2 * groups], channels
+    )
+    total = sum_over_ring(partial, ring, token)
     energy = total[0, :replicas] / jnp.sqrt(jnp.float32(cells * ring * channels))
-    x_new, y_new = finish(
-        fields, kept[:groups], kept[groups : 2 * groups], kept[2 * groups], channels
-    )
     return (x_new, y_new, energy)
 
 

time: 55 us -> 55.8 us (1.015)
  starting transfers between devices: 30.7 us -> 28.9 us
  Pallas kernels: 15.9 us -> 17.6 us
  waiting for transfers between devices: 5.38 us -> 6.49 us
    ppermute x4, starting transfers between devices: 12 us -> 10.1 us  [far_swap(): return lax.ppermute(mine, RING, off_chip)]
    pallas_call x11 -> x12, Pallas kernels: 15.9 us -> 17.6 us  [call(): pl.pallas_call(body, in_specs=[pl.BlockSpec(memory_space=pl.ANY if s is p...]
    ppermute x6, waiting for transfers between devices: 2.55 us -> 3.55 us  [sum_over_ring(): lax.ppermute(value, RING, [(i, i ^ size * d) for i in range(ring)])]
    ppermute x6, starting transfers between devices: 10.2 us -> 10.9 us  [near_swap(): return lax.ppermute(mine, RING, on_chip)]
    ppermute x6, starting transfers between devices: 8.57 us -> 7.96 us  [sum_over_ring(): lax.ppermute(value, RING, [(i, i ^ size * d) for i in range(ring)])]
  transfers between devices with their start and end apart: 16 -> 16, of which waited for: 3 -> 3; matrix products, arithmetic and copies ran while one was open for 0% -> 0% of each run, Pallas kernels for 25% -> 27%
where the time goes in v7:
time: 55.8 us; the launch traced here: 55.6 us
  starting transfers between devices  28.9 us (52%)
  Pallas kernels  17.6 us (32%)
  waiting for transfers between devices  6.49 us (12%)
  between operations  1.59 us (3%)
    pallas_call x12, Pallas kernels, call(): pl.pallas_call(body, in_specs=[pl.BlockSpec(memory_space=pl.ANY if s is p...  17.6 us
    ppermute x6, starting transfers between devices, near_swap(): return lax.ppermute(mine, RING, on_chip)  10.9 us
    ppermute x4, starting transfers between devices, far_swap(): return lax.ppermute(mine, RING, off_chip)  10.1 us
    ppermute x6, starting transfers between devices, sum_over_ring(): lax.ppermute(value, RING, [(i, i ^ size * d) for i in range(ring)])  7.96 us
    ppermute x6, waiting for transfers between devices, sum_over_ring(): lax.ppermute(value, RING, [(i, i ^ size * d) for i in range(ring)])  3.55 us
    ppermute x4, waiting for transfers between devices, far_swap(): return lax.ppermute(mine, RING, off_chip)  2.88 us
  transfers between devices with their start and end apart: 16, of which 3 were waited for; matrix products, arithmetic and copies ran while one was open for 0% of the time, Pallas kernels for 27%

profile of v7, /device:TPU:0, one launch (start us, length us, event | category | flops | bytes accessed | tf_op | source)
XLA Modules:
  0.0 55.6 jit_solution(837385826613474657)
XLA Ops:
  0.6 0.0 copy-start.2
  0.6 0.0 copy-start.3
  0.7 1.4 %load_first.1 = (f32[1024,128]{1,0:T(8,128)S(1)}, f32[1024,128]{1,0:T(8,128)S(1)}, bf16[1024,128]{1,0:T(8,128)(2,1)S(1)}, bf16[1024,128]{1,0:T(8,128)(2,1)S(1)}, bf16[1024,256]{1,0:T(8,128)(2,1)S(1)}) custom-call(f32[1024,384]{1,0:T(8,128)} %x_ref.3), custom_call_target="tpu_custom_call" | custom-call | flops 1000 | bytes 1000 | tf_op jit(solution)/shard_map/load_first/pallas_call | solution.py:21
  2.1 5.5 %collective-permute-start.4 = (bf16[1024,256]{1,0:T(8,128)(2,1)S(1)}, bf16[1024,256]{1,0:T(8,128)(2,1)S(1)}, u32[]{:S(2)}, u32[]{:S(2)}) collective-permute-start(bf16[1024,256]{1,0:T(8,128)(2,1)S(1)} %get-tuple-element.55._), channel_id=1, source_target_pairs={{0,15},{1,2},{2,1},{3,4},{4,3},{5,6},{6,5},{7,8},{8,7},{9,10},{10,... | collective-permute-start | bytes 1572872 | tf_op jit(solution)/shard_map/ppermute | solution.py:452
  7.6 0.5 collective-permute-start.1
  8.8 2.2 %make_lists.1 = (s32[214]{0:T(256)S(4)}, f32[1024,128]{1,0:T(8,128)S(1)}, bf16[1024,128]{1,0:T(8,128)(2,1)S(1)}) custom-call(s32[96]{0:T(128)S(1)} %copy-done.5, s32[96]{0:T(128)S(1)} %copy-done.6, s32[1]{0:T(128)S(6)} %copy.28.count_hbm, f32[1024,384]{1,0:T(8,128)} %x_ref.3, bf16[1024,256]{1,0:T(8,128)(2,1)S(1)} %get-tuple-element.55._), custom_call_target="tpu_custom_call" | custom-call | flops 1000 | bytes 1000 | tf_op jit(solution)/shard_map/make_lists/pallas_call | solution.py:21
  11.0 0.1 collective-permute-start.2
  11.1 0.0 copy-start
  11.2 1.4 %first_base.1 = (f32[1024,128]{1,0:T(8,128)S(1)}, f32[1024,128]{1,0:T(8,128)S(1)}, f32[1024,128]{1,0:T(8,128)S(1)}, bf16[384,384]{1,0:T(8,128)(2,1)S(1)}) custom-call(f32[1024,128]{1,0:T(8,128)S(1)} %get-tuple-element.60.refs_0_.refs_4_, f32[1024,128]{1,0:T(8,128)S(1)} %get-tuple-element.61.refs_1_.refs_5_, ...), custom_call_target="tpu_custom_call" | custom-call | flops 1000 | bytes 1000 | tf_op jit(solution)/shard_map/first_base/pallas_call | solution.py:21
  12.6 0.0 collective-permute-done.2.refs_5_
  12.6 0.4 copy-done
  13.0 2.0 %near_first.1 = (f32[1024,128]{1,0:T(8,128)S(1)}, f32[1024,128]{1,0:T(8,128)S(1)}, f32[1024,128]{1,0:T(8,128)S(1)}, bf16[1024,128]{1,0:T(8,128)(2,1)S(1)}) custom-call(s32[214]{0:T(256)S(4)} %get-tuple-element.56.list_ref, bf16[96,128,128]{2,1,0:T(8,128)(2,1)S(1)} %copy-done, bf16[1024,128]{1,0:T(8,128)(2,1)S(1)} %get-tuple-element.57.refs_0_, ...), custom_call_target="tpu_custom_call" | custom-call | flops 1000 | bytes 1000 | tf_op jit(solution)/shard_map/near_first/pallas_call | solution.py:21
  15.1 0.1 collective-permute-start.3
  15.2 1.3 %far_first_0.1 = (f32[1024,128]{1,0:T(8,128)S(1)}, f32[1024,128]{1,0:T(8,128)S(1)}, bf16[1024,128]{1,0:T(8,128)(2,1)S(1)}, bf16[1024,128]{1,0:T(8,128)(2,1)S(1)}...) custom-call(s32[214]{0:T(256)S(4)} %get-tuple-element.56.list_ref, bf16[96,128,128]{2,1,0:T(8,128)(2,1)S(1)} %copy-done, ...), custom_call_target="tpu_custom_call" | custom-call | flops 1000 | bytes 1000 | tf_op jit(solution)/shard_map/far_first_0/pallas_call | solution.py:21
  16.5 4.4 %collective-permute-start.9 = (bf16[1024,128]{1,0:T(8,128)(2,1)S(1)}, bf16[1024,128]{1,0:T(8,128)(2,1)S(1)}, u32[]{:S(2)}, u32[]{:S(2)}) collective-permute-start(bf16[1024,128]{1,0:T(8,128)(2,1)S(1)} %get-tuple-element.77), channel_id=1, source_target_pairs={{0,15},{1,2},{2,1},{3,4},{4,3},{5,6},{6,5},{7,8},{8,7},{9,10},{10,... | collective-permute-start | bytes 786440 | tf_op jit(solution)/shard_map/ppermute | solution.py:452
  20.9 2.9 %collective-permute-done.3.far_ref = bf16[1024,128]{1,0:T(8,128)(2,1)S(1)} collective-permute-done((bf16[1024,128]{1,0:T(8,128)(2,1)S(1)}, bf16[1024,128]{1,0:T(8,128)(2,1)S(1)}, u32[]{:S(2)}, u32[]{:S(2)}) %collective-permute-start.3) | collective-permute-done | bytes 262176 | tf_op jit(solution)/shard_map/ppermute | solution.py:452
  23.8 1.3 %far_first_1.1 = (f32[1024,128]{1,0:T(8,128)S(1)}, f32[1024,128]{1,0:T(8,128)S(1)}, bf16[1024,128]{1,0:T(8,128)(2,1)S(1)}, f32[1024,128]{1,0:T(8,128)S(1)}, f32[...) custom-call(s32[214]{0:T(256)S(4)} %get-tuple-element.56.list_ref, ...), custom_call_target="tpu_custom_call" | custom-call | flops 1000 | bytes 1000 | tf_op jit(solution)/shard_map/far_first_1/pallas_call | solution.py:21
  25.1 0.1 collective-permute-start.5
  25.1 9.8 %collective-permute-start.7 = (bf16[1024,128]{1,0:T(8,128)(2,1)S(1)}, bf16[1024,128]{1,0:T(8,128)(2,1)S(1)}, u32[]{:S(2)}, u32[]{:S(2)}) collective-permute-start(bf16[1024,128]{1,0:T(8,128)(2,1)S(1)} %get-tuple-element.75.refs_1_.refs_7_), channel_id=1, source_target_pairs={{0,1},{1,0},{2,3},{3,2},{4,5},{5,4},{6,7},{7,6},{8,9},{9,8},{10,11... | collective-permute-start | bytes 786440 | tf_op jit(solution)/shard_map/ppermute | solution.py:455
  34.9 0.5 collective-permute-start.6
  35.4 1.7 %second_base.1 = (f32[1024,128]{1,0:T(8,128)S(1)}, f32[1024,128]{1,0:T(8,128)S(1)}, f32[1024,128]{1,0:T(8,128)S(1)}, f32[1024,128]{1,0:T(8,128)S(1)}, f32[1024,128]{1,0:T(8,128)S(1)}, /*index=5*/f32[1024,128]{1,0:T(8,128)S(1)}) custom-call(f32[1024,128]{1,0:T(8,128)S(1)} %get-tuple-element.80.refs_0_.refs_6_, ...), custom_call_target="tpu_custom_call" | custom-call | flops 1000 | bytes 1000 | tf_op jit(solution)/shard_map/second_base/pallas_call | solution.py:21
  37.1 0.8 %far_second_0.1.refs_6_ = f32[1024,128]{1,0:T(8,128)S(1)} custom-call(s32[214]{0:T(256)S(4)} %get-tuple-element.56.list_ref, bf16[96,128,128]{2,1,0:T(8,128)(2,1)S(1)} %copy-done, bf16[1024,128]{1,0:T(8,128)(2,1)S(1)} %collective-permute-done.9.far_ref), custom_call_target="tpu_custom_call" | custom-call | flops 4000000000 | bytes 1000 | tf_op jit(solution)/shard_map/far_second_0/pallas_call | solution.py:21
  38.0 2.0 %near_second.1 = (bf16[1024,128]{1,0:T(8,128)(2,1)S(1)}, f32[1024,128]{1,0:T(8,128)S(1)}, f32[1024,128]{1,0:T(8,128)S(1)}) custom-call(s32[214]{0:T(256)S(4)} %get-tuple-element.56.list_ref, bf16[96,128,128]{2,1,0:T(8,128)(2,1)S(1)} %copy-done, bf16[1024,128]{1,0:T(8,128)(2,1)S(1)} %get-tuple-element.74.refs_0_.refs_6_, ...), custom_call_target="tpu_custom_call" | custom-call | flops 1000 | bytes 1000 | tf_op jit(solution)/shard_map/near_second/pallas_call | solution.py:21
  40.0 1.3 %far_second_1.1 = (bf16[1024,128]{1,0:T(8,128)(2,1)S(1)}, bf16[1024,128]{1,0:T(8,128)(2,1)S(1)}, f32[8,128]{1,0:T(8,128)S(1)}, bf16[1024,128]{1,0:T(8,128)(2,1)S...) custom-call(s32[214]{0:T(256)S(4)} %get-tuple-element.56.list_ref, ...), custom_call_target="tpu_custom_call", output_to_operand_aliasing={{3}: (8, {}), {4}: (9, {}), {5}: (10, {}), {6}: (11, {}), {... | custom-call | flops 1000 | bytes 1000 | tf_op jit(solution)/shard_map/far_second_1/pallas_call | solution.py:21
  41.3 3.5 %collective-permute-start.11 = (f32[8,128]{1,0:T(8,128)S(1)}, f32[8,128]{1,0:T(8,128)S(1)}, u32[]{:S(2)}, u32[]{:S(2)}) collective-permute-start(f32[8,128]{1,0:T(8,128)S(1)} %get-tuple-element.105.refs_0_), channel_id=1, source_target_pairs={{0,2},{1,3},{2,0},{3,1},{4,6},{5,7},{6,4},{7,5},{8,10},{9,11},{10,... | collective-permute-start | bytes 12296 | tf_op jit(solution)/shard_map/ppermute | solution.py:420
  44.8 0.1 collective-permute-start.10
  44.8 2.2 %finish.1 = (f32[1024,384]{1,0:T(8,128)}, f32[1024,384]{1,0:T(8,128)}, f32[8,128]{1,0:T(8,128)S(1)}) custom-call(bf16[1024,128]{1,0:T(8,128)(2,1)S(1)} %get-tuple-element.93.refs_0_, bf16[1024,128]{1,0:T(8,128)(2,1)S(1)} %get-tuple-element.94.refs_1_, bf16[1024,128]{1,0:T(8,128)(2,1)S(1)} %get-tuple-element.95.refs_2_, ...), custom_call_target="tpu_custom_call" | custom-call | flops 1000 | bytes 1000 | tf_op jit(solution)/shard_map/finish/pallas_call | solution.py:21
  47.1 3.5 %collective-permute-start.15 = (f32[8,128]{1,0:T(8,128)S(1)}, f32[8,128]{1,0:T(8,128)S(1)}, u32[]{:S(2)}, u32[]{:S(2)}) collective-permute-start(f32[8,128]{1,0:T(8,128)S(1)} %add_up.1), channel_id=1, source_target_pairs={{0,12},{1,13},{2,14},{3,15},{4,8},{5,9},{6,10},{7,11},{8,4},{9,5},... | collective-permute-start | bytes 12296 | tf_op jit(solution)/shard_map/ppermute | solution.py:420
  50.5 1.0 %collective-permute-start.13 = (f32[8,128]{1,0:T(8,128)S(1)}, f32[8,128]{1,0:T(8,128)S(1)}, u32[]{:S(2)}, u32[]{:S(2)}) collective-permute-start(f32[8,128]{1,0:T(8,128)S(1)} %add_up.1), channel_id=1, source_target_pairs={{0,4},{1,5},{2,6},{3,7},{4,0},{5,1},{6,2},{7,3},{8,12},{9,13},{10,... | collective-permute-start | bytes 12296 | tf_op jit(solution)/shard_map/ppermute | solution.py:420
  51.5 1.0 %collective-permute-done.15 = f32[8,128]{1,0:T(8,128)S(1)} collective-permute-done((f32[8,128]{1,0:T(8,128)S(1)}, f32[8,128]{1,0:T(8,128)S(1)}, u32[]{:S(2)}, u32[]{:S(2)}) %collective-permute-start.15) | collective-permute-done | bytes 4128 | tf_op jit(solution)/shard_map/ppermute | solution.py:420
  52.5 2.5 %collective-permute-done.14 = f32[8,128]{1,0:T(8,128)S(1)} collective-permute-done((f32[8,128]{1,0:T(8,128)S(1)}, f32[8,128]{1,0:T(8,128)S(1)}, u32[]{:S(2)}, u32[]{:S(2)}) %collective-permute-start.14) | collective-permute-done | bytes 4128 | tf_op jit(solution)/shard_map/ppermute | solution.py:420
  55.1 0.5 multiply_bitcast_fusion
  (28 shorter events, 0.1 us)
Async XLA Ops:
  0.6 10.5 %copy-start.2 = (bf16[384,384]{1,0:T(8,128)(2,1)S(1)}, bf16[384,384]{1,0:T(8,128)(2,1)}, u32[]{:S(2)}) copy-start(bf16[384,384]{1,0:T(8,128)(2,1)} %constant.7.clone.refs_4_.refs_9_) | copy-start | bytes 884740
  0.6 10.5 %copy-start.3 = (bf16[384,48]{1,0:T(8,128)(2,1)S(1)}, bf16[384,48]{1,0:T(8,128)(2,1)}, u32[]{:S(2)}) copy-start(bf16[384,48]{1,0:T(8,128)(2,1)} %constant.8.clone.refs_5_) | copy-start | bytes 110596
  0.7 8.1 %copy-start.6 = (s32[96]{0:T(128)S(1)}, s32[96]{0:T(128)}, u32[]{:S(2)}) copy-start(s32[96]{0:T(128)} %cols_hbm.1) | copy-start | bytes 1156
  0.7 8.1 %copy-start.5 = (s32[96]{0:T(128)S(1)}, s32[96]{0:T(128)}, u32[]{:S(2)}) copy-start(s32[96]{0:T(128)} %rows_hbm.1) | copy-start | bytes 1156
  0.7 10.5 %copy-start.4 = (bf16[48,48]{1,0:T(8,128)(2,1)S(1)}, bf16[48,48]{1,0:T(8,128)(2,1)}, u32[]{:S(2)}) copy-start(bf16[48,48]{1,0:T(8,128)(2,1)} %refs_6_.1) | copy-start | bytes 13828
  0.7 10.5 %copy-start.1 = (f32[1024,384]{1,0:T(8,128)S(1)}, f32[1024,384]{1,0:T(8,128)}, u32[]{:S(2)}) copy-start(f32[1024,384]{1,0:T(8,128)} %refs_3_.1) | copy-start | bytes 4718596
  2.1 13.1 %collective-permute-start.4 = (bf16[1024,256]{1,0:T(8,128)(2,1)S(1)}, bf16[1024,256]{1,0:T(8,128)(2,1)S(1)}, u32[]{:S(2)}, u32[]{:S(2)}) collective-permute-start(bf16[1024,256]{1,0:T(8,128)(2,1)S(1)} %get-tuple-element.55._), channel_id=1, source_target_pairs={{0,15},{1,2},{2,1},{3,4},{4,3},{5,6},{6,5},{7,8},{8,7},{9,10},{10,... | collective-permute-start | bytes 1572872 | tf_op jit(solution)/shard_map/ppermute | solution.py:452
  7.6 4.9 %collective-permute-start = (bf16[1024,128]{1,0:T(8,128)(2,1)S(1)}, bf16[1024,128]{1,0:T(8,128)(2,1)S(1)}, u32[]{:S(2)}, u32[]{:S(2)}) collective-permute-start(bf16[1024,128]{1,0:T(8,128)(2,1)S(1)} %get-tuple-element.57.refs_0_), channel_id=1, source_target_pairs={{0,1},{1,0},{2,3},{3,2},{4,5},{5,4},{6,7},{7,6},{8,9},{9,8},{10,11... | collective-permute-start | bytes 786440 | tf_op jit(solution)/shard_map/ppermute | solution.py:455
  7.6 4.9 %collective-permute-start.1 = (bf16[1024,128]{1,0:T(8,128)(2,1)S(1)}, bf16[1024,128]{1,0:T(8,128)(2,1)S(1)}, u32[]{:S(2)}, u32[]{:S(2)}) collective-permute-start(bf16[1024,128]{1,0:T(8,128)(2,1)S(1)} %get-tuple-element.58.refs_1_), channel_id=1, source_target_pairs={{0,1},{1,0},{2,3},{3,2},{4,5},{5,4},{6,7},{7,6},{8,9},{9,8},{10,11... | collective-permute-start | bytes 786440 | tf_op jit(solution)/shard_map/ppermute | solution.py:455
  11.0 1.6 %collective-permute-start.2 = (bf16[1024,128]{1,0:T(8,128)(2,1)S(1)}, bf16[1024,128]{1,0:T(8,128)(2,1)S(1)}, u32[]{:S(2)}, u32[]{:S(2)}) collective-permute-start(bf16[1024,128]{1,0:T(8,128)(2,1)S(1)} %get-tuple-element.59.refs_2_.refs_6_), channel_id=1, source_target_pairs={{0,1},{1,0},{2,3},{3,2},{4,5},{5,4},{6,7},{7,6},{8,9},{9,8},{10,11... | collective-permute-start | bytes 786440 | tf_op jit(solution)/shard_map/ppermute | solution.py:455
  11.1 1.9 %copy-start = (bf16[96,128,128]{2,1,0:T(8,128)(2,1)S(1)}, bf16[96,128,128]{2,1,0:T(8,128)(2,1)}, u32[]{:S(2)}) copy-start(bf16[96,128,128]{2,1,0:T(8,128)(2,1)} %tiles_ref.11) | copy-start | bytes 9437188
  15.1 8.7 %collective-permute-start.3 = (bf16[1024,128]{1,0:T(8,128)(2,1)S(1)}, bf16[1024,128]{1,0:T(8,128)(2,1)S(1)}, u32[]{:S(2)}, u32[]{:S(2)}) collective-permute-start(bf16[1024,128]{1,0:T(8,128)(2,1)S(1)} %get-tuple-element.64), channel_id=1, source_target_pairs={{0,15},{1,2},{2,1},{3,4},{4,3},{5,6},{6,5},{7,8},{8,7},{9,10},{10,... | collective-permute-start | bytes 786440 | tf_op jit(solution)/shard_map/ppermute | solution.py:452
  16.5 20.7 %collective-permute-start.9 = (bf16[1024,128]{1,0:T(8,128)(2,1)S(1)}, bf16[1024,128]{1,0:T(8,128)(2,1)S(1)}, u32[]{:S(2)}, u32[]{:S(2)}) collective-permute-start(bf16[1024,128]{1,0:T(8,128)(2,1)S(1)} %get-tuple-element.77), channel_id=1, source_target_pairs={{0,15},{1,2},{2,1},{3,4},{4,3},{5,6},{6,5},{7,8},{8,7},{9,10},{10,... | collective-permute-start | bytes 786440 | tf_op jit(solution)/shard_map/ppermute | solution.py:452
  25.1 14.9 %collective-permute-start.5 = (bf16[1024,256]{1,0:T(8,128)(2,1)S(1)}, bf16[1024,256]{1,0:T(8,128)(2,1)S(1)}, u32[]{:S(2)}, u32[]{:S(2)}) collective-permute-start(bf16[1024,256]{1,0:T(8,128)(2,1)S(1)} %get-tuple-element.73), channel_id=1, source_target_pairs={{0,15},{1,2},{2,1},{3,4},{4,3},{5,6},{6,5},{7,8},{8,7},{9,10},{10,... | collective-permute-start | bytes 1572872 | tf_op jit(solution)/shard_map/ppermute | solution.py:452
  25.1 12.8 %collective-permute-start.7 = (bf16[1024,128]{1,0:T(8,128)(2,1)S(1)}, bf16[1024,128]{1,0:T(8,128)(2,1)S(1)}, u32[]{:S(2)}, u32[]{:S(2)}) collective-permute-start(bf16[1024,128]{1,0:T(8,128)(2,1)S(1)} %get-tuple-element.75.refs_1_.refs_7_), channel_id=1, source_target_pairs={{0,1},{1,0},{2,3},{3,2},{4,5},{5,4},{6,7},{7,6},{8,9},{9,8},{10,11... | collective-permute-start | bytes 786440 | tf_op jit(solution)/shard_map/ppermute | solution.py:455
  34.9 3.1 %collective-permute-start.8 = (bf16[1024,128]{1,0:T(8,128)(2,1)S(1)}, bf16[1024,128]{1,0:T(8,128)(2,1)S(1)}, u32[]{:S(2)}, u32[]{:S(2)}) collective-permute-start(bf16[1024,128]{1,0:T(8,128)(2,1)S(1)} %get-tuple-element.76.refs_2_.refs_8_), channel_id=1, source_target_pairs={{0,1},{1,0},{2,3},{3,2},{4,5},{5,4},{6,7},{7,6},{8,9},{9,8},{10,11... | collective-permute-start | bytes 786440 | tf_op jit(solution)/shard_map/ppermute | solution.py:455
  34.9 3.1 %collective-permute-start.6 = (bf16[1024,128]{1,0:T(8,128)(2,1)S(1)}, bf16[1024,128]{1,0:T(8,128)(2,1)S(1)}, u32[]{:S(2)}, u32[]{:S(2)}) collective-permute-start(bf16[1024,128]{1,0:T(8,128)(2,1)S(1)} %get-tuple-element.74.refs_0_.refs_6_), channel_id=1, source_target_pairs={{0,1},{1,0},{2,3},{3,2},{4,5},{5,4},{6,7},{7,6},{8,9},{9,8},{10,11... | collective-permute-start | bytes 786440 | tf_op jit(solution)/shard_map/ppermute | solution.py:455
  41.3 5.7 %collective-permute-start.12 = (f32[8,128]{1,0:T(8,128)S(1)}, f32[8,128]{1,0:T(8,128)S(1)}, u32[]{:S(2)}, u32[]{:S(2)}) collective-permute-start(f32[8,128]{1,0:T(8,128)S(1)} %get-tuple-element.105.refs_0_), channel_id=1, source_target_pairs={{0,3},{1,2},{2,1},{3,0},{4,7},{5,6},{6,5},{7,4},{8,11},{9,10},{10,... | collective-permute-start | bytes 12296 | tf_op jit(solution)/shard_map/ppermute | solution.py:420
  41.3 5.7 %collective-permute-start.11 = (f32[8,128]{1,0:T(8,128)S(1)}, f32[8,128]{1,0:T(8,128)S(1)}, u32[]{:S(2)}, u32[]{:S(2)}) collective-permute-start(f32[8,128]{1,0:T(8,128)S(1)} %get-tuple-element.105.refs_0_), channel_id=1, source_target_pairs={{0,2},{1,3},{2,0},{3,1},{4,6},{5,7},{6,4},{7,5},{8,10},{9,11},{10,... | collective-permute-start | bytes 12296 | tf_op jit(solution)/shard_map/ppermute | solution.py:420
  44.8 2.3 %collective-permute-start.10 = (f32[8,128]{1,0:T(8,128)S(1)}, f32[8,128]{1,0:T(8,128)S(1)}, u32[]{:S(2)}, u32[]{:S(2)}) collective-permute-start(f32[8,128]{1,0:T(8,128)S(1)} %get-tuple-element.105.refs_0_), channel_id=1, source_target_pairs={{0,1},{1,0},{2,3},{3,2},{4,5},{5,4},{6,7},{7,6},{8,9},{9,8},{10,11... | collective-permute-start | bytes 12296 | tf_op jit(solution)/shard_map/ppermute | solution.py:420
  47.1 5.5 %collective-permute-start.15 = (f32[8,128]{1,0:T(8,128)S(1)}, f32[8,128]{1,0:T(8,128)S(1)}, u32[]{:S(2)}, u32[]{:S(2)}) collective-permute-start(f32[8,128]{1,0:T(8,128)S(1)} %add_up.1), channel_id=1, source_target_pairs={{0,12},{1,13},{2,14},{3,15},{4,8},{5,9},{6,10},{7,11},{8,4},{9,5},... | collective-permute-start | bytes 12296 | tf_op jit(solution)/shard_map/ppermute | solution.py:420
  50.5 4.5 %collective-permute-start.14 = (f32[8,128]{1,0:T(8,128)S(1)}, f32[8,128]{1,0:T(8,128)S(1)}, u32[]{:S(2)}, u32[]{:S(2)}) collective-permute-start(f32[8,128]{1,0:T(8,128)S(1)} %add_up.1), channel_id=1, source_target_pairs={{0,8},{1,9},{2,10},{3,11},{4,12},{5,13},{6,14},{7,15},{8,0},{9,1},... | collective-permute-start | bytes 12296 | tf_op jit(solution)/shard_map/ppermute | solution.py:420
  50.5 4.5 %collective-permute-start.13 = (f32[8,128]{1,0:T(8,128)S(1)}, f32[8,128]{1,0:T(8,128)S(1)}, u32[]{:S(2)}, u32[]{:S(2)}) collective-permute-start(f32[8,128]{1,0:T(8,128)S(1)} %add_up.1), channel_id=1, source_target_pairs={{0,4},{1,5},{2,6},{3,7},{4,0},{5,1},{6,2},{7,3},{8,12},{9,13},{10,... | collective-permute-start | bytes 12296 | tf_op jit(solution)/shard_map/ppermute | solution.py:420

commit v8 on v5

--- a/solution.py
+++ b/solution.py
@@ -399,13 +399,15 @@
 def sum_over_ring(value, ring):
     if ring & (ring - 1):
         return lax.psum(value, RING)
-    size = 1
+    rounds, size = [], 1
     while size < ring:
         digits = (1, 2, 3) if 4 * size <= ring else (1,)
+        rounds.append([size * d for d in digits])
+        size *= len(digits) + 1
+    for bits in reversed(rounds):
         value = value + sum(
-            lax.ppermute(value, RING, [(i, i ^ (size * d)) for i in range(ring)]) for d in digits
+            lax.ppermute(value, RING, [(i, i ^ bit) for i in range(ring)]) for bit in bits
         )
-        size *= len(digits) + 1
     return value
 
 

time: 55 us -> 54.3 us (0.987)
  starting transfers between devices: 30.7 us -> 29.1 us
  Pallas kernels: 15.9 us -> 16.5 us
    ppermute x4, starting transfers between devices: 12 us -> 10.5 us  [far_swap(): return lax.ppermute(mine, RING, off_chip)]
    pallas_call x11, Pallas kernels: 15.9 us -> 16.5 us  [call(): pl.pallas_call(body, in_specs=[pl.BlockSpec(memory_space=pl.ANY if s is p...]
    ppermute x6, starting transfers between devices: 8.57 us -> 7.95 us  [sum_over_ring(): lax.ppermute(value, RING, [(i, i ^ bit) for i in range(ring)])]
  transfers between devices with their start and end apart: 16 -> 16, of which waited for: 3 -> 3; matrix products, arithmetic and copies ran while one was open for 0% -> 0% of each run, Pallas kernels for 25% -> 26%
where the time goes in v8:
time: 54.3 us; the launch traced here: 53.9 us
  starting transfers between devices  29.1 us (54%)
  Pallas kernels  16.5 us (30%)
  waiting for transfers between devices  5.75 us (11%)
  between operations  1.57 us (3%)
    pallas_call x11, Pallas kernels, call(): pl.pallas_call(body, in_specs=[pl.BlockSpec(memory_space=pl.ANY if s is p...  16.5 us
    ppermute x6, starting transfers between devices, near_swap(): return lax.ppermute(mine, RING, on_chip)  10.7 us
    ppermute x4, starting transfers between devices, far_swap(): return lax.ppermute(mine, RING, off_chip)  10.5 us
    ppermute x6, starting transfers between devices, sum_over_ring(): lax.ppermute(value, RING, [(i, i ^ bit) for i in range(ring)])  7.95 us
    ppermute x4, waiting for transfers between devices, far_swap(): return lax.ppermute(mine, RING, off_chip)  3.07 us
    ppermute x6, waiting for transfers between devices, sum_over_ring(): lax.ppermute(value, RING, [(i, i ^ bit) for i in range(ring)])  2.62 us
  transfers between devices with their start and end apart: 16, of which 3 were waited for; matrix products, arithmetic and copies ran while one was open for 0% of the time, Pallas kernels for 26%

profile of v8, /device:TPU:0, one launch (start us, length us, event | category | flops | bytes accessed | tf_op | source)
XLA Modules:
  0.0 53.9 jit_solution(9574740176523464075)
XLA Ops:
  0.6 0.0 copy-start.2
  0.7 1.4 %load_first.1 = (f32[1024,128]{1,0:T(8,128)S(1)}, f32[1024,128]{1,0:T(8,128)S(1)}, bf16[1024,128]{1,0:T(8,128)(2,1)S(1)}, bf16[1024,128]{1,0:T(8,128)(2,1)S(1)}, bf16[1024,256]{1,0:T(8,128)(2,1)S(1)}) custom-call(f32[1024,384]{1,0:T(8,128)} %x_ref.3), custom_call_target="tpu_custom_call" | custom-call | flops 1000 | bytes 1000 | tf_op jit(solution)/shard_map/load_first/pallas_call | solution.py:21
  2.1 5.5 %collective-permute-start.4 = (bf16[1024,256]{1,0:T(8,128)(2,1)S(1)}, bf16[1024,256]{1,0:T(8,128)(2,1)S(1)}, u32[]{:S(2)}, u32[]{:S(2)}) collective-permute-start(bf16[1024,256]{1,0:T(8,128)(2,1)S(1)} %get-tuple-element.54._), channel_id=1, source_target_pairs={{0,15},{1,2},{2,1},{3,4},{4,3},{5,6},{6,5},{7,8},{8,7},{9,10},{10,... | collective-permute-start | bytes 1572872 | tf_op jit(solution)/shard_map/ppermute | solution.py:439
  7.6 0.5 collective-permute-start.1
  8.8 2.1 %make_lists.1 = (s32[214]{0:T(256)S(4)}, f32[1024,128]{1,0:T(8,128)S(1)}, bf16[1024,128]{1,0:T(8,128)(2,1)S(1)}) custom-call(s32[96]{0:T(128)S(1)} %copy-done.5, s32[96]{0:T(128)S(1)} %copy-done.6, s32[1]{0:T(128)S(6)} %copy.28.count_hbm, f32[1024,384]{1,0:T(8,128)} %x_ref.3, bf16[1024,256]{1,0:T(8,128)(2,1)S(1)} %get-tuple-element.54._), custom_call_target="tpu_custom_call" | custom-call | flops 1000 | bytes 1000 | tf_op jit(solution)/shard_map/make_lists/pallas_call | solution.py:21
  10.9 0.1 collective-permute-start.2
  11.0 1.4 %first_base.1 = (f32[1024,128]{1,0:T(8,128)S(1)}, f32[1024,128]{1,0:T(8,128)S(1)}, f32[1024,128]{1,0:T(8,128)S(1)}, bf16[384,384]{1,0:T(8,128)(2,1)S(1)}) custom-call(f32[1024,128]{1,0:T(8,128)S(1)} %get-tuple-element.59.refs_0_.refs_4_, f32[1024,128]{1,0:T(8,128)S(1)} %get-tuple-element.60.refs_1_.refs_5_, ...), custom_call_target="tpu_custom_call" | custom-call | flops 1000 | bytes 1000 | tf_op jit(solution)/shard_map/first_base/pallas_call | solution.py:21
  12.4 0.0 collective-permute-done.2.refs_5_
  12.5 0.4 copy-done
  12.9 2.0 %near_first.1 = (f32[1024,128]{1,0:T(8,128)S(1)}, f32[1024,128]{1,0:T(8,128)S(1)}, f32[1024,128]{1,0:T(8,128)S(1)}, bf16[1024,128]{1,0:T(8,128)(2,1)S(1)}) custom-call(s32[214]{0:T(256)S(4)} %get-tuple-element.55.list_ref, bf16[96,128,128]{2,1,0:T(8,128)(2,1)S(1)} %copy-done, bf16[1024,128]{1,0:T(8,128)(2,1)S(1)} %get-tuple-element.56.refs_0_, ...), custom_call_target="tpu_custom_call" | custom-call | flops 1000 | bytes 1000 | tf_op jit(solution)/shard_map/near_first/pallas_call | solution.py:21
  14.9 0.4 collective-permute-start.3
  15.3 1.0 %far_first_0.1 = (f32[1024,128]{1,0:T(8,128)S(1)}, f32[1024,128]{1,0:T(8,128)S(1)}, bf16[1024,128]{1,0:T(8,128)(2,1)S(1)}, bf16[1024,128]{1,0:T(8,128)(2,1)S(1)}...) custom-call(s32[214]{0:T(256)S(4)} %get-tuple-element.55.list_ref, bf16[96,128,128]{2,1,0:T(8,128)(2,1)S(1)} %copy-done, ...), custom_call_target="tpu_custom_call" | custom-call | flops 1000 | bytes 1000 | tf_op jit(solution)/shard_map/far_first_0/pallas_call | solution.py:21
  16.3 4.2 %collective-permute-start.9 = (bf16[1024,128]{1,0:T(8,128)(2,1)S(1)}, bf16[1024,128]{1,0:T(8,128)(2,1)S(1)}, u32[]{:S(2)}, u32[]{:S(2)}) collective-permute-start(bf16[1024,128]{1,0:T(8,128)(2,1)S(1)} %get-tuple-element.76), channel_id=1, source_target_pairs={{0,15},{1,2},{2,1},{3,4},{4,3},{5,6},{6,5},{7,8},{8,7},{9,10},{10,... | collective-permute-start | bytes 786440 | tf_op jit(solution)/shard_map/ppermute | solution.py:439
  20.5 3.1 %collective-permute-done.3.far_ref = bf16[1024,128]{1,0:T(8,128)(2,1)S(1)} collective-permute-done((bf16[1024,128]{1,0:T(8,128)(2,1)S(1)}, bf16[1024,128]{1,0:T(8,128)(2,1)S(1)}, u32[]{:S(2)}, u32[]{:S(2)}) %collective-permute-start.3) | collective-permute-done | bytes 262176 | tf_op jit(solution)/shard_map/ppermute | solution.py:439
  23.6 1.1 %far_first_1.1 = (f32[1024,128]{1,0:T(8,128)S(1)}, f32[1024,128]{1,0:T(8,128)S(1)}, bf16[1024,128]{1,0:T(8,128)(2,1)S(1)}, f32[1024,128]{1,0:T(8,128)S(1)}, f32[...) custom-call(s32[214]{0:T(256)S(4)} %get-tuple-element.55.list_ref, ...), custom_call_target="tpu_custom_call" | custom-call | flops 1000 | bytes 1000 | tf_op jit(solution)/shard_map/far_first_1/pallas_call | solution.py:21
  24.7 0.4 collective-permute-start.5
  25.1 9.6 %collective-permute-start.7 = (bf16[1024,128]{1,0:T(8,128)(2,1)S(1)}, bf16[1024,128]{1,0:T(8,128)(2,1)S(1)}, u32[]{:S(2)}, u32[]{:S(2)}) collective-permute-start(bf16[1024,128]{1,0:T(8,128)(2,1)S(1)} %get-tuple-element.74.refs_1_.refs_7_), channel_id=1, source_target_pairs={{0,1},{1,0},{2,3},{3,2},{4,5},{5,4},{6,7},{7,6},{8,9},{9,8},{10,11... | collective-permute-start | bytes 786440 | tf_op jit(solution)/shard_map/ppermute | solution.py:442
  34.7 0.5 collective-permute-start.6
  35.2 1.7 %second_base.1 = (f32[1024,128]{1,0:T(8,128)S(1)}, f32[1024,128]{1,0:T(8,128)S(1)}, f32[1024,128]{1,0:T(8,128)S(1)}, f32[1024,128]{1,0:T(8,128)S(1)}, f32[1024,128]{1,0:T(8,128)S(1)}, /*index=5*/f32[1024,128]{1,0:T(8,128)S(1)}) custom-call(f32[1024,128]{1,0:T(8,128)S(1)} %get-tuple-element.79.refs_0_.refs_6_, ...), custom_call_target="tpu_custom_call" | custom-call | flops 1000 | bytes 1000 | tf_op jit(solution)/shard_map/second_base/pallas_call | solution.py:21
  36.9 0.6 %far_second_0.1.refs_6_ = f32[1024,128]{1,0:T(8,128)S(1)} custom-call(s32[214]{0:T(256)S(4)} %get-tuple-element.55.list_ref, bf16[96,128,128]{2,1,0:T(8,128)(2,1)S(1)} %copy-done, bf16[1024,128]{1,0:T(8,128)(2,1)S(1)} %collective-permute-done.9.far_ref), custom_call_target="tpu_custom_call" | custom-call | flops 4000000000 | bytes 1000 | tf_op jit(solution)/shard_map/far_second_0/pallas_call | solution.py:21
  37.5 2.0 %near_second.1 = (bf16[1024,128]{1,0:T(8,128)(2,1)S(1)}, f32[1024,128]{1,0:T(8,128)S(1)}, f32[1024,128]{1,0:T(8,128)S(1)}) custom-call(s32[214]{0:T(256)S(4)} %get-tuple-element.55.list_ref, bf16[96,128,128]{2,1,0:T(8,128)(2,1)S(1)} %copy-done, bf16[1024,128]{1,0:T(8,128)(2,1)S(1)} %get-tuple-element.73.refs_0_.refs_6_, ...), custom_call_target="tpu_custom_call" | custom-call | flops 1000 | bytes 1000 | tf_op jit(solution)/shard_map/near_second/pallas_call | solution.py:21
  39.6 1.1 %far_second_1.1 = (bf16[1024,128]{1,0:T(8,128)(2,1)S(1)}, bf16[1024,128]{1,0:T(8,128)(2,1)S(1)}, f32[8,128]{1,0:T(8,128)S(1)}, bf16[1024,128]{1,0:T(8,128)(2,1)S...) custom-call(s32[214]{0:T(256)S(4)} %get-tuple-element.55.list_ref, ...), custom_call_target="tpu_custom_call", output_to_operand_aliasing={{3}: (8, {}), {4}: (9, {}), {5}: (10, {}), {6}: (11, {}), {... | custom-call | flops 1000 | bytes 1000 | tf_op jit(solution)/shard_map/far_second_1/pallas_call | solution.py:21
  40.6 2.5 %collective-permute-start.12 = (f32[8,128]{1,0:T(8,128)S(1)}, f32[8,128]{1,0:T(8,128)S(1)}, u32[]{:S(2)}, u32[]{:S(2)}) collective-permute-start(f32[8,128]{1,0:T(8,128)S(1)} %get-tuple-element.104), channel_id=1, source_target_pairs={{0,12},{1,13},{2,14},{3,15},{4,8},{5,9},{6,10},{7,11},{8,4},{9,5},... | collective-permute-start | bytes 12296 | tf_op jit(solution)/shard_map/ppermute | solution.py:409
  43.1 0.4 collective-permute-start.11
  43.5 1.5 %collective-permute-start.10 = (f32[8,128]{1,0:T(8,128)S(1)}, f32[8,128]{1,0:T(8,128)S(1)}, u32[]{:S(2)}, u32[]{:S(2)}) collective-permute-start(f32[8,128]{1,0:T(8,128)S(1)} %get-tuple-element.104), channel_id=1, source_target_pairs={{0,4},{1,5},{2,6},{3,7},{4,0},{5,1},{6,2},{7,3},{8,12},{9,13},{10,... | collective-permute-start | bytes 12296 | tf_op jit(solution)/shard_map/ppermute | solution.py:409
  45.0 1.0 %collective-permute-done.12 = f32[8,128]{1,0:T(8,128)S(1)} collective-permute-done((f32[8,128]{1,0:T(8,128)S(1)}, f32[8,128]{1,0:T(8,128)S(1)}, u32[]{:S(2)}, u32[]{:S(2)}) %collective-permute-start.12) | collective-permute-done | bytes 4128 | tf_op jit(solution)/shard_map/ppermute | solution.py:409
  46.0 1.6 %collective-permute-done.11 = f32[8,128]{1,0:T(8,128)S(1)} collective-permute-done((f32[8,128]{1,0:T(8,128)S(1)}, f32[8,128]{1,0:T(8,128)S(1)}, u32[]{:S(2)}, u32[]{:S(2)}) %collective-permute-start.11) | collective-permute-done | bytes 4128 | tf_op jit(solution)/shard_map/ppermute | solution.py:409
  47.6 0.1 collective-permute-start.15
  47.7 3.5 %collective-permute-start.14 = (f32[8,128]{1,0:T(8,128)S(1)}, f32[8,128]{1,0:T(8,128)S(1)}, u32[]{:S(2)}, u32[]{:S(2)}) collective-permute-start(f32[8,128]{1,0:T(8,128)S(1)} %add_add_fusion.1), channel_id=1, source_target_pairs={{0,2},{1,3},{2,0},{3,1},{4,6},{5,7},{6,4},{7,5},{8,10},{9,11},{10,... | collective-permute-start | bytes 12296 | tf_op jit(solution)/shard_map/ppermute | solution.py:409
  51.2 0.0 collective-permute-start.13
  51.2 2.2 %finish.1 = (f32[1024,384]{1,0:T(8,128)}, f32[1024,384]{1,0:T(8,128)}) custom-call(bf16[1024,128]{1,0:T(8,128)(2,1)S(1)} %get-tuple-element.92.refs_0_, bf16[1024,128]{1,0:T(8,128)(2,1)S(1)} %get-tuple-element.93.refs_1_, bf16[1024,128]{1,0:T(8,128)(2,1)S(1)} %get-tuple-element.94.refs_2_, f32[1024,128]{1,0:T(8,128)S(1)} %get-tuple-element.95.refs_3_, ...), custom_call_target="tpu_custom_call" | custom-call | flops 1000 | bytes 1000 | tf_op jit(solution)/shard_map/finish/pallas_call | solution.py:21
  53.4 0.5 multiply_bitcast_fusion
  (28 shorter events, 0.1 us)
Async XLA Ops:
  0.6 10.3 %copy-start.2 = (bf16[384,384]{1,0:T(8,128)(2,1)S(1)}, bf16[384,384]{1,0:T(8,128)(2,1)}, u32[]{:S(2)}) copy-start(bf16[384,384]{1,0:T(8,128)(2,1)} %constant.7.clone.refs_4_.refs_9_) | copy-start | bytes 884740
  0.6 10.3 %copy-start.3 = (bf16[384,48]{1,0:T(8,128)(2,1)S(1)}, bf16[384,48]{1,0:T(8,128)(2,1)}, u32[]{:S(2)}) copy-start(bf16[384,48]{1,0:T(8,128)(2,1)} %constant.8.clone.refs_5_) | copy-start | bytes 110596
  0.7 8.1 %copy-start.6 = (s32[96]{0:T(128)S(1)}, s32[96]{0:T(128)}, u32[]{:S(2)}) copy-start(s32[96]{0:T(128)} %cols_hbm.1) | copy-start | bytes 1156
  0.7 8.1 %copy-start.5 = (s32[96]{0:T(128)S(1)}, s32[96]{0:T(128)}, u32[]{:S(2)}) copy-start(s32[96]{0:T(128)} %rows_hbm.1) | copy-start | bytes 1156
  0.7 10.3 %copy-start.4 = (bf16[48,48]{1,0:T(8,128)(2,1)S(1)}, bf16[48,48]{1,0:T(8,128)(2,1)}, u32[]{:S(2)}) copy-start(bf16[48,48]{1,0:T(8,128)(2,1)} %refs_6_.1) | copy-start | bytes 13828
  0.7 10.3 %copy-start.1 = (f32[1024,384]{1,0:T(8,128)S(1)}, f32[1024,384]{1,0:T(8,128)}, u32[]{:S(2)}) copy-start(f32[1024,384]{1,0:T(8,128)} %refs_3_.1) | copy-start | bytes 4718596
  2.1 13.2 %collective-permute-start.4 = (bf16[1024,256]{1,0:T(8,128)(2,1)S(1)}, bf16[1024,256]{1,0:T(8,128)(2,1)S(1)}, u32[]{:S(2)}, u32[]{:S(2)}) collective-permute-start(bf16[1024,256]{1,0:T(8,128)(2,1)S(1)} %get-tuple-element.54._), channel_id=1, source_target_pairs={{0,15},{1,2},{2,1},{3,4},{4,3},{5,6},{6,5},{7,8},{8,7},{9,10},{10,... | collective-permute-start | bytes 1572872 | tf_op jit(solution)/shard_map/ppermute | solution.py:439
  7.6 4.8 %collective-permute-start = (bf16[1024,128]{1,0:T(8,128)(2,1)S(1)}, bf16[1024,128]{1,0:T(8,128)(2,1)S(1)}, u32[]{:S(2)}, u32[]{:S(2)}) collective-permute-start(bf16[1024,128]{1,0:T(8,128)(2,1)S(1)} %get-tuple-element.56.refs_0_), channel_id=1, source_target_pairs={{0,1},{1,0},{2,3},{3,2},{4,5},{5,4},{6,7},{7,6},{8,9},{9,8},{10,11... | collective-permute-start | bytes 786440 | tf_op jit(solution)/shard_map/ppermute | solution.py:442
  7.6 4.8 %collective-permute-start.1 = (bf16[1024,128]{1,0:T(8,128)(2,1)S(1)}, bf16[1024,128]{1,0:T(8,128)(2,1)S(1)}, u32[]{:S(2)}, u32[]{:S(2)}) collective-permute-start(bf16[1024,128]{1,0:T(8,128)(2,1)S(1)} %get-tuple-element.57.refs_1_), channel_id=1, source_target_pairs={{0,1},{1,0},{2,3},{3,2},{4,5},{5,4},{6,7},{7,6},{8,9},{9,8},{10,11... | collective-permute-start | bytes 786440 | tf_op jit(solution)/shard_map/ppermute | solution.py:442
  10.9 1.6 %collective-permute-start.2 = (bf16[1024,128]{1,0:T(8,128)(2,1)S(1)}, bf16[1024,128]{1,0:T(8,128)(2,1)S(1)}, u32[]{:S(2)}, u32[]{:S(2)}) collective-permute-start(bf16[1024,128]{1,0:T(8,128)(2,1)S(1)} %get-tuple-element.58.refs_2_.refs_6_), channel_id=1, source_target_pairs={{0,1},{1,0},{2,3},{3,2},{4,5},{5,4},{6,7},{7,6},{8,9},{9,8},{10,11... | collective-permute-start | bytes 786440 | tf_op jit(solution)/shard_map/ppermute | solution.py:442
  11.0 1.9 %copy-start = (bf16[96,128,128]{2,1,0:T(8,128)(2,1)S(1)}, bf16[96,128,128]{2,1,0:T(8,128)(2,1)}, u32[]{:S(2)}) copy-start(bf16[96,128,128]{2,1,0:T(8,128)(2,1)} %tiles_ref.11) | copy-start | bytes 9437188
  14.9 8.7 %collective-permute-start.3 = (bf16[1024,128]{1,0:T(8,128)(2,1)S(1)}, bf16[1024,128]{1,0:T(8,128)(2,1)S(1)}, u32[]{:S(2)}, u32[]{:S(2)}) collective-permute-start(bf16[1024,128]{1,0:T(8,128)(2,1)S(1)} %get-tuple-element.63), channel_id=1, source_target_pairs={{0,15},{1,2},{2,1},{3,4},{4,3},{5,6},{6,5},{7,8},{8,7},{9,10},{10,... | collective-permute-start | bytes 786440 | tf_op jit(solution)/shard_map/ppermute | solution.py:439
  16.3 20.6 %collective-permute-start.9 = (bf16[1024,128]{1,0:T(8,128)(2,1)S(1)}, bf16[1024,128]{1,0:T(8,128)(2,1)S(1)}, u32[]{:S(2)}, u32[]{:S(2)}) collective-permute-start(bf16[1024,128]{1,0:T(8,128)(2,1)S(1)} %get-tuple-element.76), channel_id=1, source_target_pairs={{0,15},{1,2},{2,1},{3,4},{4,3},{5,6},{6,5},{7,8},{8,7},{9,10},{10,... | collective-permute-start | bytes 786440 | tf_op jit(solution)/shard_map/ppermute | solution.py:439
  24.7 14.9 %collective-permute-start.5 = (bf16[1024,256]{1,0:T(8,128)(2,1)S(1)}, bf16[1024,256]{1,0:T(8,128)(2,1)S(1)}, u32[]{:S(2)}, u32[]{:S(2)}) collective-permute-start(bf16[1024,256]{1,0:T(8,128)(2,1)S(1)} %get-tuple-element.72), channel_id=1, source_target_pairs={{0,15},{1,2},{2,1},{3,4},{4,3},{5,6},{6,5},{7,8},{8,7},{9,10},{10,... | collective-permute-start | bytes 1572872 | tf_op jit(solution)/shard_map/ppermute | solution.py:439
  25.1 12.4 %collective-permute-start.7 = (bf16[1024,128]{1,0:T(8,128)(2,1)S(1)}, bf16[1024,128]{1,0:T(8,128)(2,1)S(1)}, u32[]{:S(2)}, u32[]{:S(2)}) collective-permute-start(bf16[1024,128]{1,0:T(8,128)(2,1)S(1)} %get-tuple-element.74.refs_1_.refs_7_), channel_id=1, source_target_pairs={{0,1},{1,0},{2,3},{3,2},{4,5},{5,4},{6,7},{7,6},{8,9},{9,8},{10,11... | collective-permute-start | bytes 786440 | tf_op jit(solution)/shard_map/ppermute | solution.py:442
  34.7 2.8 %collective-permute-start.8 = (bf16[1024,128]{1,0:T(8,128)(2,1)S(1)}, bf16[1024,128]{1,0:T(8,128)(2,1)S(1)}, u32[]{:S(2)}, u32[]{:S(2)}) collective-permute-start(bf16[1024,128]{1,0:T(8,128)(2,1)S(1)} %get-tuple-element.75.refs_2_.refs_8_), channel_id=1, source_target_pairs={{0,1},{1,0},{2,3},{3,2},{4,5},{5,4},{6,7},{7,6},{8,9},{9,8},{10,11... | collective-permute-start | bytes 786440 | tf_op jit(solution)/shard_map/ppermute | solution.py:442
  34.7 2.8 %collective-permute-start.6 = (bf16[1024,128]{1,0:T(8,128)(2,1)S(1)}, bf16[1024,128]{1,0:T(8,128)(2,1)S(1)}, u32[]{:S(2)}, u32[]{:S(2)}) collective-permute-start(bf16[1024,128]{1,0:T(8,128)(2,1)S(1)} %get-tuple-element.73.refs_0_.refs_6_), channel_id=1, source_target_pairs={{0,1},{1,0},{2,3},{3,2},{4,5},{5,4},{6,7},{7,6},{8,9},{9,8},{10,11... | collective-permute-start | bytes 786440 | tf_op jit(solution)/shard_map/ppermute | solution.py:442
  40.6 5.4 %collective-permute-start.12 = (f32[8,128]{1,0:T(8,128)S(1)}, f32[8,128]{1,0:T(8,128)S(1)}, u32[]{:S(2)}, u32[]{:S(2)}) collective-permute-start(f32[8,128]{1,0:T(8,128)S(1)} %get-tuple-element.104), channel_id=1, source_target_pairs={{0,12},{1,13},{2,14},{3,15},{4,8},{5,9},{6,10},{7,11},{8,4},{9,5},... | collective-permute-start | bytes 12296 | tf_op jit(solution)/shard_map/ppermute | solution.py:409
  43.1 4.5 %collective-permute-start.11 = (f32[8,128]{1,0:T(8,128)S(1)}, f32[8,128]{1,0:T(8,128)S(1)}, u32[]{:S(2)}, u32[]{:S(2)}) collective-permute-start(f32[8,128]{1,0:T(8,128)S(1)} %get-tuple-element.104), channel_id=1, source_target_pairs={{0,8},{1,9},{2,10},{3,11},{4,12},{5,13},{6,14},{7,15},{8,0},{9,1},... | collective-permute-start | bytes 12296 | tf_op jit(solution)/shard_map/ppermute | solution.py:409
  43.5 4.1 %collective-permute-start.10 = (f32[8,128]{1,0:T(8,128)S(1)}, f32[8,128]{1,0:T(8,128)S(1)}, u32[]{:S(2)}, u32[]{:S(2)}) collective-permute-start(f32[8,128]{1,0:T(8,128)S(1)} %get-tuple-element.104), channel_id=1, source_target_pairs={{0,4},{1,5},{2,6},{3,7},{4,0},{5,1},{6,2},{7,3},{8,12},{9,13},{10,... | collective-permute-start | bytes 12296 | tf_op jit(solution)/shard_map/ppermute | solution.py:409
  47.6 5.7 %collective-permute-start.15 = (f32[8,128]{1,0:T(8,128)S(1)}, f32[8,128]{1,0:T(8,128)S(1)}, u32[]{:S(2)}, u32[]{:S(2)}) collective-permute-start(f32[8,128]{1,0:T(8,128)S(1)} %add_add_fusion.1), channel_id=1, source_target_pairs={{0,3},{1,2},{2,1},{3,0},{4,7},{5,6},{6,5},{7,4},{8,11},{9,10},{10,... | collective-permute-start | bytes 12296 | tf_op jit(solution)/shard_map/ppermute | solution.py:409
  47.7 5.7 %collective-permute-start.14 = (f32[8,128]{1,0:T(8,128)S(1)}, f32[8,128]{1,0:T(8,128)S(1)}, u32[]{:S(2)}, u32[]{:S(2)}) collective-permute-start(f32[8,128]{1,0:T(8,128)S(1)} %add_add_fusion.1), channel_id=1, source_target_pairs={{0,2},{1,3},{2,0},{3,1},{4,6},{5,7},{6,4},{7,5},{8,10},{9,11},{10,... | collective-permute-start | bytes 12296 | tf_op jit(solution)/shard_map/ppermute | solution.py:409
  51.2 2.2 %collective-permute-start.13 = (f32[8,128]{1,0:T(8,128)S(1)}, f32[8,128]{1,0:T(8,128)S(1)}, u32[]{:S(2)}, u32[]{:S(2)}) collective-permute-start(f32[8,128]{1,0:T(8,128)S(1)} %add_add_fusion.1), channel_id=1, source_target_pairs={{0,1},{1,0},{2,3},{3,2},{4,5},{5,4},{6,7},{7,6},{8,9},{9,8},{10,11... | collective-permute-start | bytes 12296 | tf_op jit(solution)/shard_map/ppermute | solution.py:409

commit v9 on v7

--- a/solution.py
+++ b/solution.py
@@ -413,14 +413,16 @@
 def sum_over_ring(value, ring, token):
     if ring & (ring - 1):
         return lax.psum(value, RING)
-    size = 1
+    rounds, size = [], 1
     while size < ring:
         digits = (1, 2, 3) if 4 * size <= ring else (1,)
+        rounds.append([size * d for d in digits])
+        size *= len(digits) + 1
+    for i, bits in enumerate(reversed(rounds)):
         parts = [value] + [
-            lax.ppermute(value, RING, [(i, i ^ (size * d)) for i in range(ring)]) for d in digits
+            lax.ppermute(value, RING, [(j, j ^ bit) for j in range(ring)]) for bit in bits
         ]
-        value = add_up(parts, token) if size == 1 else sum(parts)
-        size *= len(digits) + 1
+        value = add_up(parts, token) if i == 0 else sum(parts)
     return value
 
 

time: 55.8 us -> 54.2 us (0.971)
  waiting for transfers between devices: 6.49 us -> 4.6 us
  starting transfers between devices: 28.9 us -> 28 us
  Pallas kernels: 17.6 us -> 18.4 us
    ppermute x6, waiting for transfers between devices: 3.55 us -> 1.57 us  [sum_over_ring(): lax.ppermute(value, RING, [(j, j ^ bit) for j in range(ring)])]
    pallas_call x12, Pallas kernels: 17.6 us -> 18.4 us  [call(): pl.pallas_call(body, in_specs=[pl.BlockSpec(memory_space=pl.ANY if s is p...]
    ppermute x6, starting transfers between devices: 10.9 us -> 10.3 us  [near_swap(): return lax.ppermute(mine, RING, on_chip)]
  transfers between devices with their start and end apart: 16 -> 16, of which waited for: 3 -> 2; matrix products, arithmetic and copies ran while one was open for 0% -> 0% of each run, Pallas kernels for 27% -> 29%
where the time goes in v9:
time: 54.2 us; the launch traced here: 53.6 us
  starting transfers between devices  28 us (52%)
  Pallas kernels  18.4 us (34%)
  waiting for transfers between devices  4.6 us (8%)
  between operations  1.6 us (3%)
    pallas_call x12, Pallas kernels, call(): pl.pallas_call(body, in_specs=[pl.BlockSpec(memory_space=pl.ANY if s is p...  18.4 us
    ppermute x6, starting transfers between devices, near_swap(): return lax.ppermute(mine, RING, on_chip)  10.3 us
    ppermute x4, starting transfers between devices, far_swap(): return lax.ppermute(mine, RING, off_chip)  9.87 us
    ppermute x6, starting transfers between devices, sum_over_ring(): lax.ppermute(value, RING, [(j, j ^ bit) for j in range(ring)])  7.84 us
    ppermute x4, waiting for transfers between devices, far_swap(): return lax.ppermute(mine, RING, off_chip)  2.97 us
    ppermute x6, waiting for transfers between devices, sum_over_ring(): lax.ppermute(value, RING, [(j, j ^ bit) for j in range(ring)])  1.57 us
  transfers between devices with their start and end apart: 16, of which 2 were waited for; matrix products, arithmetic and copies ran while one was open for 0% of the time, Pallas kernels for 29%

profile of v9, /device:TPU:0, one launch (start us, length us, event | category | flops | bytes accessed | tf_op | source)
XLA Modules:
  0.0 53.6 jit_solution(3291770830110394286)
XLA Ops:
  0.6 0.0 copy-start.2
  0.6 0.0 copy-start.3
  0.7 1.4 %load_first.1 = (f32[1024,128]{1,0:T(8,128)S(1)}, f32[1024,128]{1,0:T(8,128)S(1)}, bf16[1024,128]{1,0:T(8,128)(2,1)S(1)}, bf16[1024,128]{1,0:T(8,128)(2,1)S(1)}, bf16[1024,256]{1,0:T(8,128)(2,1)S(1)}) custom-call(f32[1024,384]{1,0:T(8,128)} %x_ref.3), custom_call_target="tpu_custom_call" | custom-call | flops 1000 | bytes 1000 | tf_op jit(solution)/shard_map/load_first/pallas_call | solution.py:21
  2.1 5.5 %collective-permute-start.4 = (bf16[1024,256]{1,0:T(8,128)(2,1)S(1)}, bf16[1024,256]{1,0:T(8,128)(2,1)S(1)}, u32[]{:S(2)}, u32[]{:S(2)}) collective-permute-start(bf16[1024,256]{1,0:T(8,128)(2,1)S(1)} %get-tuple-element.55._), channel_id=1, source_target_pairs={{0,15},{1,2},{2,1},{3,4},{4,3},{5,6},{6,5},{7,8},{8,7},{9,10},{10,... | collective-permute-start | bytes 1572872 | tf_op jit(solution)/shard_map/ppermute | solution.py:454
  7.6 0.5 collective-permute-start.1
  8.8 2.3 %make_lists.1 = (s32[214]{0:T(256)S(4)}, f32[1024,128]{1,0:T(8,128)S(1)}, bf16[1024,128]{1,0:T(8,128)(2,1)S(1)}) custom-call(s32[96]{0:T(128)S(1)} %copy-done.5, s32[96]{0:T(128)S(1)} %copy-done.6, s32[1]{0:T(128)S(6)} %copy.28.count_hbm, f32[1024,384]{1,0:T(8,128)} %x_ref.3, bf16[1024,256]{1,0:T(8,128)(2,1)S(1)} %get-tuple-element.55._), custom_call_target="tpu_custom_call" | custom-call | flops 1000 | bytes 1000 | tf_op jit(solution)/shard_map/make_lists/pallas_call | solution.py:21
  11.2 0.1 collective-permute-start.2
  11.3 1.4 %first_base.1 = (f32[1024,128]{1,0:T(8,128)S(1)}, f32[1024,128]{1,0:T(8,128)S(1)}, f32[1024,128]{1,0:T(8,128)S(1)}, bf16[384,384]{1,0:T(8,128)(2,1)S(1)}) custom-call(f32[1024,128]{1,0:T(8,128)S(1)} %get-tuple-element.60.refs_0_.refs_4_, f32[1024,128]{1,0:T(8,128)S(1)} %get-tuple-element.61.refs_1_.refs_5_, ...), custom_call_target="tpu_custom_call" | custom-call | flops 1000 | bytes 1000 | tf_op jit(solution)/shard_map/first_base/pallas_call | solution.py:21
  12.7 0.0 collective-permute-done.2.refs_5_
  12.8 0.4 copy-done
  13.2 2.3 %near_first.1 = (f32[1024,128]{1,0:T(8,128)S(1)}, f32[1024,128]{1,0:T(8,128)S(1)}, f32[1024,128]{1,0:T(8,128)S(1)}, bf16[1024,128]{1,0:T(8,128)(2,1)S(1)}) custom-call(s32[214]{0:T(256)S(4)} %get-tuple-element.56.list_ref, bf16[96,128,128]{2,1,0:T(8,128)(2,1)S(1)} %copy-done, bf16[1024,128]{1,0:T(8,128)(2,1)S(1)} %get-tuple-element.57.refs_0_, ...), custom_call_target="tpu_custom_call" | custom-call | flops 1000 | bytes 1000 | tf_op jit(solution)/shard_map/near_first/pallas_call | solution.py:21
  15.5 0.1 collective-permute-start.3
  15.6 1.3 %far_first_0.1 = (f32[1024,128]{1,0:T(8,128)S(1)}, f32[1024,128]{1,0:T(8,128)S(1)}, bf16[1024,128]{1,0:T(8,128)(2,1)S(1)}, bf16[1024,128]{1,0:T(8,128)(2,1)S(1)}...) custom-call(s32[214]{0:T(256)S(4)} %get-tuple-element.56.list_ref, bf16[96,128,128]{2,1,0:T(8,128)(2,1)S(1)} %copy-done, ...), custom_call_target="tpu_custom_call" | custom-call | flops 1000 | bytes 1000 | tf_op jit(solution)/shard_map/far_first_0/pallas_call | solution.py:21
  16.9 4.2 %collective-permute-start.9 = (bf16[1024,128]{1,0:T(8,128)(2,1)S(1)}, bf16[1024,128]{1,0:T(8,128)(2,1)S(1)}, u32[]{:S(2)}, u32[]{:S(2)}) collective-permute-start(bf16[1024,128]{1,0:T(8,128)(2,1)S(1)} %get-tuple-element.77), channel_id=1, source_target_pairs={{0,15},{1,2},{2,1},{3,4},{4,3},{5,6},{6,5},{7,8},{8,7},{9,10},{10,... | collective-permute-start | bytes 786440 | tf_op jit(solution)/shard_map/ppermute | solution.py:454
  21.1 3.0 %collective-permute-done.3.far_ref = bf16[1024,128]{1,0:T(8,128)(2,1)S(1)} collective-permute-done((bf16[1024,128]{1,0:T(8,128)(2,1)S(1)}, bf16[1024,128]{1,0:T(8,128)(2,1)S(1)}, u32[]{:S(2)}, u32[]{:S(2)}) %collective-permute-start.3) | collective-permute-done | bytes 262176 | tf_op jit(solution)/shard_map/ppermute | solution.py:454
  24.1 1.3 %far_first_1.1 = (f32[1024,128]{1,0:T(8,128)S(1)}, f32[1024,128]{1,0:T(8,128)S(1)}, bf16[1024,128]{1,0:T(8,128)(2,1)S(1)}, f32[1024,128]{1,0:T(8,128)S(1)}, f32[...) custom-call(s32[214]{0:T(256)S(4)} %get-tuple-element.56.list_ref, ...), custom_call_target="tpu_custom_call" | custom-call | flops 1000 | bytes 1000 | tf_op jit(solution)/shard_map/far_first_1/pallas_call | solution.py:21
  25.4 0.1 collective-permute-start.5
  25.5 9.2 %collective-permute-start.7 = (bf16[1024,128]{1,0:T(8,128)(2,1)S(1)}, bf16[1024,128]{1,0:T(8,128)(2,1)S(1)}, u32[]{:S(2)}, u32[]{:S(2)}) collective-permute-start(bf16[1024,128]{1,0:T(8,128)(2,1)S(1)} %get-tuple-element.75.refs_1_.refs_7_), channel_id=1, source_target_pairs={{0,1},{1,0},{2,3},{3,2},{4,5},{5,4},{6,7},{7,6},{8,9},{9,8},{10,11... | collective-permute-start | bytes 786440 | tf_op jit(solution)/shard_map/ppermute | solution.py:457
  34.7 0.5 collective-permute-start.6
  35.2 1.7 %second_base.1 = (f32[1024,128]{1,0:T(8,128)S(1)}, f32[1024,128]{1,0:T(8,128)S(1)}, f32[1024,128]{1,0:T(8,128)S(1)}, f32[1024,128]{1,0:T(8,128)S(1)}, f32[1024,128]{1,0:T(8,128)S(1)}, /*index=5*/f32[1024,128]{1,0:T(8,128)S(1)}) custom-call(f32[1024,128]{1,0:T(8,128)S(1)} %get-tuple-element.80.refs_0_.refs_6_, ...), custom_call_target="tpu_custom_call" | custom-call | flops 1000 | bytes 1000 | tf_op jit(solution)/shard_map/second_base/pallas_call | solution.py:21
  36.9 0.8 %far_second_0.1.refs_6_ = f32[1024,128]{1,0:T(8,128)S(1)} custom-call(s32[214]{0:T(256)S(4)} %get-tuple-element.56.list_ref, bf16[96,128,128]{2,1,0:T(8,128)(2,1)S(1)} %copy-done, bf16[1024,128]{1,0:T(8,128)(2,1)S(1)} %collective-permute-done.9.far_ref), custom_call_target="tpu_custom_call" | custom-call | flops 4000000000 | bytes 1000 | tf_op jit(solution)/shard_map/far_second_0/pallas_call | solution.py:21
  37.8 2.3 %near_second.1 = (bf16[1024,128]{1,0:T(8,128)(2,1)S(1)}, f32[1024,128]{1,0:T(8,128)S(1)}, f32[1024,128]{1,0:T(8,128)S(1)}) custom-call(s32[214]{0:T(256)S(4)} %get-tuple-element.56.list_ref, bf16[96,128,128]{2,1,0:T(8,128)(2,1)S(1)} %copy-done, bf16[1024,128]{1,0:T(8,128)(2,1)S(1)} %get-tuple-element.74.refs_0_.refs_6_, ...), custom_call_target="tpu_custom_call" | custom-call | flops 1000 | bytes 1000 | tf_op jit(solution)/shard_map/near_second/pallas_call | solution.py:21
  40.1 1.3 %far_second_1.1 = (bf16[1024,128]{1,0:T(8,128)(2,1)S(1)}, bf16[1024,128]{1,0:T(8,128)(2,1)S(1)}, f32[8,128]{1,0:T(8,128)S(1)}, bf16[1024,128]{1,0:T(8,128)(2,1)S...) custom-call(s32[214]{0:T(256)S(4)} %get-tuple-element.56.list_ref, ...), custom_call_target="tpu_custom_call", output_to_operand_aliasing={{3}: (8, {}), {4}: (9, {}), {5}: (10, {}), {6}: (11, {}), {... | custom-call | flops 1000 | bytes 1000 | tf_op jit(solution)/shard_map/far_second_1/pallas_call | solution.py:21
  41.4 1.5 %collective-permute-start.12 = (f32[8,128]{1,0:T(8,128)S(1)}, f32[8,128]{1,0:T(8,128)S(1)}, u32[]{:S(2)}, u32[]{:S(2)}) collective-permute-start(f32[8,128]{1,0:T(8,128)S(1)} %get-tuple-element.105.refs_0_), channel_id=1, source_target_pairs={{0,12},{1,13},{2,14},{3,15},{4,8},{5,9},{6,10},{7,11},{8,4},{9,5},... | collective-permute-start | bytes 12296 | tf_op jit(solution)/shard_map/ppermute | solution.py:423
  42.9 1.0 %collective-permute-start.11 = (f32[8,128]{1,0:T(8,128)S(1)}, f32[8,128]{1,0:T(8,128)S(1)}, u32[]{:S(2)}, u32[]{:S(2)}) collective-permute-start(f32[8,128]{1,0:T(8,128)S(1)} %get-tuple-element.105.refs_0_), channel_id=1, source_target_pairs={{0,8},{1,9},{2,10},{3,11},{4,12},{5,13},{6,14},{7,15},{8,0},{9,1},... | collective-permute-start | bytes 12296 | tf_op jit(solution)/shard_map/ppermute | solution.py:423
  43.9 1.9 %collective-permute-start.10 = (f32[8,128]{1,0:T(8,128)S(1)}, f32[8,128]{1,0:T(8,128)S(1)}, u32[]{:S(2)}, u32[]{:S(2)}) collective-permute-start(f32[8,128]{1,0:T(8,128)S(1)} %get-tuple-element.105.refs_0_), channel_id=1, source_target_pairs={{0,4},{1,5},{2,6},{3,7},{4,0},{5,1},{6,2},{7,3},{8,12},{9,13},{10,... | collective-permute-start | bytes 12296 | tf_op jit(solution)/shard_map/ppermute | solution.py:423
  45.8 2.2 %finish.1 = (f32[1024,384]{1,0:T(8,128)}, f32[1024,384]{1,0:T(8,128)}, f32[8,128]{1,0:T(8,128)S(1)}) custom-call(bf16[1024,128]{1,0:T(8,128)(2,1)S(1)} %get-tuple-element.93.refs_0_, bf16[1024,128]{1,0:T(8,128)(2,1)S(1)} %get-tuple-element.94.refs_1_, bf16[1024,128]{1,0:T(8,128)(2,1)S(1)} %get-tuple-element.95.refs_2_, ...), custom_call_target="tpu_custom_call" | custom-call | flops 1000 | bytes 1000 | tf_op jit(solution)/shard_map/finish/pallas_call | solution.py:21
  48.0 0.1 collective-permute-start.15
  48.1 3.3 %collective-permute-start.14 = (f32[8,128]{1,0:T(8,128)S(1)}, f32[8,128]{1,0:T(8,128)S(1)}, u32[]{:S(2)}, u32[]{:S(2)}) collective-permute-start(f32[8,128]{1,0:T(8,128)S(1)} %add_up.1), channel_id=1, source_target_pairs={{0,2},{1,3},{2,0},{3,1},{4,6},{5,7},{6,4},{7,5},{8,10},{9,11},{10,... | collective-permute-start | bytes 12296 | tf_op jit(solution)/shard_map/ppermute | solution.py:423
  51.4 0.0 collective-permute-start.13
  51.5 1.6 %collective-permute-done.14 = f32[8,128]{1,0:T(8,128)S(1)} collective-permute-done((f32[8,128]{1,0:T(8,128)S(1)}, f32[8,128]{1,0:T(8,128)S(1)}, u32[]{:S(2)}, u32[]{:S(2)}) %collective-permute-start.14) | collective-permute-done | bytes 4128 | tf_op jit(solution)/shard_map/ppermute | solution.py:423
  53.0 0.5 multiply_bitcast_fusion
  (28 shorter events, 0.1 us)
Async XLA Ops:
  0.6 10.6 %copy-start.2 = (bf16[384,384]{1,0:T(8,128)(2,1)S(1)}, bf16[384,384]{1,0:T(8,128)(2,1)}, u32[]{:S(2)}) copy-start(bf16[384,384]{1,0:T(8,128)(2,1)} %constant.7.clone.refs_4_.refs_9_) | copy-start | bytes 884740
  0.6 10.6 %copy-start.3 = (bf16[384,48]{1,0:T(8,128)(2,1)S(1)}, bf16[384,48]{1,0:T(8,128)(2,1)}, u32[]{:S(2)}) copy-start(bf16[384,48]{1,0:T(8,128)(2,1)} %constant.8.clone.refs_5_) | copy-start | bytes 110596
  0.7 8.1 %copy-start.6 = (s32[96]{0:T(128)S(1)}, s32[96]{0:T(128)}, u32[]{:S(2)}) copy-start(s32[96]{0:T(128)} %cols_hbm.1) | copy-start | bytes 1156
  0.7 8.1 %copy-start.5 = (s32[96]{0:T(128)S(1)}, s32[96]{0:T(128)}, u32[]{:S(2)}) copy-start(s32[96]{0:T(128)} %rows_hbm.1) | copy-start | bytes 1156
  0.7 10.6 %copy-start.4 = (bf16[48,48]{1,0:T(8,128)(2,1)S(1)}, bf16[48,48]{1,0:T(8,128)(2,1)}, u32[]{:S(2)}) copy-start(bf16[48,48]{1,0:T(8,128)(2,1)} %refs_6_.1) | copy-start | bytes 13828
  0.7 10.6 %copy-start.1 = (f32[1024,384]{1,0:T(8,128)S(1)}, f32[1024,384]{1,0:T(8,128)}, u32[]{:S(2)}) copy-start(f32[1024,384]{1,0:T(8,128)} %refs_3_.1) | copy-start | bytes 4718596
  2.1 13.5 %collective-permute-start.4 = (bf16[1024,256]{1,0:T(8,128)(2,1)S(1)}, bf16[1024,256]{1,0:T(8,128)(2,1)S(1)}, u32[]{:S(2)}, u32[]{:S(2)}) collective-permute-start(bf16[1024,256]{1,0:T(8,128)(2,1)S(1)} %get-tuple-element.55._), channel_id=1, source_target_pairs={{0,15},{1,2},{2,1},{3,4},{4,3},{5,6},{6,5},{7,8},{8,7},{9,10},{10,... | collective-permute-start | bytes 1572872 | tf_op jit(solution)/shard_map/ppermute | solution.py:454
  7.6 5.1 %collective-permute-start = (bf16[1024,128]{1,0:T(8,128)(2,1)S(1)}, bf16[1024,128]{1,0:T(8,128)(2,1)S(1)}, u32[]{:S(2)}, u32[]{:S(2)}) collective-permute-start(bf16[1024,128]{1,0:T(8,128)(2,1)S(1)} %get-tuple-element.57.refs_0_), channel_id=1, source_target_pairs={{0,1},{1,0},{2,3},{3,2},{4,5},{5,4},{6,7},{7,6},{8,9},{9,8},{10,11... | collective-permute-start | bytes 786440 | tf_op jit(solution)/shard_map/ppermute | solution.py:457
  7.6 5.1 %collective-permute-start.1 = (bf16[1024,128]{1,0:T(8,128)(2,1)S(1)}, bf16[1024,128]{1,0:T(8,128)(2,1)S(1)}, u32[]{:S(2)}, u32[]{:S(2)}) collective-permute-start(bf16[1024,128]{1,0:T(8,128)(2,1)S(1)} %get-tuple-element.58.refs_1_), channel_id=1, source_target_pairs={{0,1},{1,0},{2,3},{3,2},{4,5},{5,4},{6,7},{7,6},{8,9},{9,8},{10,11... | collective-permute-start | bytes 786440 | tf_op jit(solution)/shard_map/ppermute | solution.py:457
  11.2 1.6 %collective-permute-start.2 = (bf16[1024,128]{1,0:T(8,128)(2,1)S(1)}, bf16[1024,128]{1,0:T(8,128)(2,1)S(1)}, u32[]{:S(2)}, u32[]{:S(2)}) collective-permute-start(bf16[1024,128]{1,0:T(8,128)(2,1)S(1)} %get-tuple-element.59.refs_2_.refs_6_), channel_id=1, source_target_pairs={{0,1},{1,0},{2,3},{3,2},{4,5},{5,4},{6,7},{7,6},{8,9},{9,8},{10,11... | collective-permute-start | bytes 786440 | tf_op jit(solution)/shard_map/ppermute | solution.py:457
  11.3 1.9 %copy-start = (bf16[96,128,128]{2,1,0:T(8,128)(2,1)S(1)}, bf16[96,128,128]{2,1,0:T(8,128)(2,1)}, u32[]{:S(2)}) copy-start(bf16[96,128,128]{2,1,0:T(8,128)(2,1)} %tiles_ref.11) | copy-start | bytes 9437188
  15.5 8.6 %collective-permute-start.3 = (bf16[1024,128]{1,0:T(8,128)(2,1)S(1)}, bf16[1024,128]{1,0:T(8,128)(2,1)S(1)}, u32[]{:S(2)}, u32[]{:S(2)}) collective-permute-start(bf16[1024,128]{1,0:T(8,128)(2,1)S(1)} %get-tuple-element.64), channel_id=1, source_target_pairs={{0,15},{1,2},{2,1},{3,4},{4,3},{5,6},{6,5},{7,8},{8,7},{9,10},{10,... | collective-permute-start | bytes 786440 | tf_op jit(solution)/shard_map/ppermute | solution.py:454
  16.9 20.0 %collective-permute-start.9 = (bf16[1024,128]{1,0:T(8,128)(2,1)S(1)}, bf16[1024,128]{1,0:T(8,128)(2,1)S(1)}, u32[]{:S(2)}, u32[]{:S(2)}) collective-permute-start(bf16[1024,128]{1,0:T(8,128)(2,1)S(1)} %get-tuple-element.77), channel_id=1, source_target_pairs={{0,15},{1,2},{2,1},{3,4},{4,3},{5,6},{6,5},{7,8},{8,7},{9,10},{10,... | collective-permute-start | bytes 786440 | tf_op jit(solution)/shard_map/ppermute | solution.py:454
  25.4 14.7 %collective-permute-start.5 = (bf16[1024,256]{1,0:T(8,128)(2,1)S(1)}, bf16[1024,256]{1,0:T(8,128)(2,1)S(1)}, u32[]{:S(2)}, u32[]{:S(2)}) collective-permute-start(bf16[1024,256]{1,0:T(8,128)(2,1)S(1)} %get-tuple-element.73), channel_id=1, source_target_pairs={{0,15},{1,2},{2,1},{3,4},{4,3},{5,6},{6,5},{7,8},{8,7},{9,10},{10,... | collective-permute-start | bytes 1572872 | tf_op jit(solution)/shard_map/ppermute | solution.py:454
  25.5 12.3 %collective-permute-start.7 = (bf16[1024,128]{1,0:T(8,128)(2,1)S(1)}, bf16[1024,128]{1,0:T(8,128)(2,1)S(1)}, u32[]{:S(2)}, u32[]{:S(2)}) collective-permute-start(bf16[1024,128]{1,0:T(8,128)(2,1)S(1)} %get-tuple-element.75.refs_1_.refs_7_), channel_id=1, source_target_pairs={{0,1},{1,0},{2,3},{3,2},{4,5},{5,4},{6,7},{7,6},{8,9},{9,8},{10,11... | collective-permute-start | bytes 786440 | tf_op jit(solution)/shard_map/ppermute | solution.py:457
  34.7 3.1 %collective-permute-start.8 = (bf16[1024,128]{1,0:T(8,128)(2,1)S(1)}, bf16[1024,128]{1,0:T(8,128)(2,1)S(1)}, u32[]{:S(2)}, u32[]{:S(2)}) collective-permute-start(bf16[1024,128]{1,0:T(8,128)(2,1)S(1)} %get-tuple-element.76.refs_2_.refs_8_), channel_id=1, source_target_pairs={{0,1},{1,0},{2,3},{3,2},{4,5},{5,4},{6,7},{7,6},{8,9},{9,8},{10,11... | collective-permute-start | bytes 786440 | tf_op jit(solution)/shard_map/ppermute | solution.py:457
  34.7 3.1 %collective-permute-start.6 = (bf16[1024,128]{1,0:T(8,128)(2,1)S(1)}, bf16[1024,128]{1,0:T(8,128)(2,1)S(1)}, u32[]{:S(2)}, u32[]{:S(2)}) collective-permute-start(bf16[1024,128]{1,0:T(8,128)(2,1)S(1)} %get-tuple-element.74.refs_0_.refs_6_), channel_id=1, source_target_pairs={{0,1},{1,0},{2,3},{3,2},{4,5},{5,4},{6,7},{7,6},{8,9},{9,8},{10,11... | collective-permute-start | bytes 786440 | tf_op jit(solution)/shard_map/ppermute | solution.py:457
  41.4 6.6 %collective-permute-start.12 = (f32[8,128]{1,0:T(8,128)S(1)}, f32[8,128]{1,0:T(8,128)S(1)}, u32[]{:S(2)}, u32[]{:S(2)}) collective-permute-start(f32[8,128]{1,0:T(8,128)S(1)} %get-tuple-element.105.refs_0_), channel_id=1, source_target_pairs={{0,12},{1,13},{2,14},{3,15},{4,8},{5,9},{6,10},{7,11},{8,4},{9,5},... | collective-permute-start | bytes 12296 | tf_op jit(solution)/shard_map/ppermute | solution.py:423
  42.9 5.1 %collective-permute-start.11 = (f32[8,128]{1,0:T(8,128)S(1)}, f32[8,128]{1,0:T(8,128)S(1)}, u32[]{:S(2)}, u32[]{:S(2)}) collective-permute-start(f32[8,128]{1,0:T(8,128)S(1)} %get-tuple-element.105.refs_0_), channel_id=1, source_target_pairs={{0,8},{1,9},{2,10},{3,11},{4,12},{5,13},{6,14},{7,15},{8,0},{9,1},... | collective-permute-start | bytes 12296 | tf_op jit(solution)/shard_map/ppermute | solution.py:423
  43.9 4.1 %collective-permute-start.10 = (f32[8,128]{1,0:T(8,128)S(1)}, f32[8,128]{1,0:T(8,128)S(1)}, u32[]{:S(2)}, u32[]{:S(2)}) collective-permute-start(f32[8,128]{1,0:T(8,128)S(1)} %get-tuple-element.105.refs_0_), channel_id=1, source_target_pairs={{0,4},{1,5},{2,6},{3,7},{4,0},{5,1},{6,2},{7,3},{8,12},{9,13},{10,... | collective-permute-start | bytes 12296 | tf_op jit(solution)/shard_map/ppermute | solution.py:423
  48.0 3.5 %collective-permute-start.15 = (f32[8,128]{1,0:T(8,128)S(1)}, f32[8,128]{1,0:T(8,128)S(1)}, u32[]{:S(2)}, u32[]{:S(2)}) collective-permute-start(f32[8,128]{1,0:T(8,128)S(1)} %add_up.1), channel_id=1, source_target_pairs={{0,3},{1,2},{2,1},{3,0},{4,7},{5,6},{6,5},{7,4},{8,11},{9,10},{10,... | collective-permute-start | bytes 12296 | tf_op jit(solution)/shard_map/ppermute | solution.py:423
  48.1 4.9 %collective-permute-start.14 = (f32[8,128]{1,0:T(8,128)S(1)}, f32[8,128]{1,0:T(8,128)S(1)}, u32[]{:S(2)}, u32[]{:S(2)}) collective-permute-start(f32[8,128]{1,0:T(8,128)S(1)} %add_up.1), channel_id=1, source_target_pairs={{0,2},{1,3},{2,0},{3,1},{4,6},{5,7},{6,4},{7,5},{8,10},{9,11},{10,... | collective-permute-start | bytes 12296 | tf_op jit(solution)/shard_map/ppermute | solution.py:423
  51.4 1.6 %collective-permute-start.13 = (f32[8,128]{1,0:T(8,128)S(1)}, f32[8,128]{1,0:T(8,128)S(1)}, u32[]{:S(2)}, u32[]{:S(2)}) collective-permute-start(f32[8,128]{1,0:T(8,128)S(1)} %add_up.1), channel_id=1, source_target_pairs={{0,1},{1,0},{2,3},{3,2},{4,5},{5,4},{6,7},{7,6},{8,9},{9,8},{10,11... | collective-permute-start | bytes 12296 | tf_op jit(solution)/shard_map/ppermute | solution.py:423

commit v10 on v9

--- a/solution.py
+++ b/solution.py
@@ -361,39 +361,46 @@
     return outs[:groups], outs[groups:]
 
 
-def finish(fields, xs, bases, mixing, channels):
+def finish(here, fields, xs, bases, mixing, channels, outputs, name):
     groups = len(xs)
     cells = xs[0].shape[0]
     width = groups * LANES
 
     def body(*refs):
         field_refs, x_refs, base_refs = [refs[k * groups : (k + 1) * groups] for k in range(3)]
-        mixing_ref, x_out, y_out, token, x_buf, y_buf, sems = refs[3 * groups :]
-        held = [ref[...] for ref in field_refs]
-        copies = []
-        for g in range(groups):
-            y_new = base_refs[g][...] - 0.2 * mixed_of(held, mixing_ref, g, channels)
-            y_buf[g] = y_new
-            x_buf[g] = jnp.clip(x_refs[g][...] + 0.5 * y_new, -1.0, 1.0)
-            for k, (buf, out) in enumerate(((y_buf, y_out), (x_buf, x_out))):
-                copies.append(
-                    pltpu.make_async_copy(buf.at[g], out.at[:, lanes(g)], sems.at[g, k])
-                )
-                copies[-1].start()
+        mixing_ref = refs[3 * groups]
+        x_out, y_out, token, x_buf, y_buf, sems = refs[-6:]
         token[...] = jnp.zeros_like(token)
-        for copy in copies:
-            copy.wait()
-
+
+        @pl.when(here())
+        def _():
+            held = [ref[...] for ref in field_refs]
+            copies = []
+            for g in range(groups):
+                y_new = base_refs[g][...] - 0.2 * mixed_of(held, mixing_ref, g, channels)
+                y_buf[g] = y_new
+                x_buf[g] = jnp.clip(x_refs[g][...] + 0.5 * y_new, -1.0, 1.0)
+                for k, (buf, out) in enumerate(((y_buf, y_out), (x_buf, x_out))):
+                    copies.append(
+                        pltpu.make_async_copy(buf.at[g], out.at[:, lanes(g)], sems.at[g, k])
+                    )
+                    copies[-1].start()
+            for copy in copies:
+                copy.wait()
+
+    ins = vmem(*fields, *xs, *bases, mixing)
     return call(
         body,
-        vmem(*fields, *xs, *bases, mixing),
+        ins + [(a, pltpu.HBM) for a in outputs],
         [((cells, width), F32, pltpu.HBM)] * 2 + [((8, LANES), F32, pltpu.VMEM)],
         [
             pltpu.VMEM((groups, cells, LANES), F32),
             pltpu.VMEM((groups, cells, LANES), F32),
             pltpu.SemaphoreType.DMA((groups, 2)),
         ],
-        "finish",
+        name,
+        0,
+        [(len(ins) + i, i) for i in range(len(outputs))],
     )
 
 
@@ -566,11 +573,17 @@
     fields, partial, kept = results[: len(piece)], results[len(piece)], results[len(piece) + 1 :]
     fields, kept = [kept[0], *fields], kept[1:]
 
-    x_new, y_new, token = finish(
-        fields, kept[:groups], kept[groups : 2 * groups], kept[2 * groups], channels
-    )
+    def early():
+        return ((ring_index() + 1) // 2) % 2 == 0
+
+    def late():
+        return ((ring_index() + 1) // 2) % 2 == 1
+
+    rest = (fields, kept[:groups], kept[groups : 2 * groups], kept[2 * groups], channels)
+    *outputs, token = finish(early, *rest, [], "finish_early")
     total = sum_over_ring(partial, ring, token)
     energy = total[0, :replicas] / jnp.sqrt(jnp.float32(cells * ring * channels))
+    x_new, y_new, _ = finish(late, *rest, outputs, "finish_late")
     return (x_new, y_new, energy)
 
 

time: 54.2 us -> 55.3 us (1.020)
  the two profiles are of different devices: /device:TPU:0 before, /device:TPU:1 now
where the time goes in v10:
time: 55.3 us; the launch traced here: 54.8 us
  starting transfers between devices  18.6 us (34%)
  waiting for transfers between devices  17 us (31%)
  Pallas kernels  16.6 us (30%)
  between operations  1.55 us (3%)
    pallas_call x13, Pallas kernels, call(): pl.pallas_call(body, in_specs=[pl.BlockSpec(memory_space=pl.ANY if s is p...  16.6 us
    ppermute x4, waiting for transfers between devices, far_swap(): return lax.ppermute(mine, RING, off_chip)  14.2 us
    ppermute x4, starting transfers between devices, far_swap(): return lax.ppermute(mine, RING, off_chip)  8.34 us
    ppermute x6, starting transfers between devices, sum_over_ring(): lax.ppermute(value, RING, [(j, j ^ bit) for j in range(ring)])  6.18 us
    ppermute x6, starting transfers between devices, near_swap(): return lax.ppermute(mine, RING, on_chip)  4.07 us
    ppermute x6, waiting for transfers between devices, sum_over_ring(): lax.ppermute(value, RING, [(j, j ^ bit) for j in range(ring)])  2.84 us
  transfers between devices with their start and end apart: 16, of which 5 were waited for; matrix products, arithmetic and copies ran while one was open for 0% of the time, Pallas kernels for 26%

profile of v10, /device:TPU:1, one launch (start us, length us, event | category | flops | bytes accessed | tf_op | source)
XLA Modules:
  0.0 54.8 jit_solution(9890072812039720748)
XLA Ops:
  0.6 0.0 copy-start.2
  0.6 0.0 copy-start.3
  0.7 1.4 %load_first.1 = (f32[1024,128]{1,0:T(8,128)S(1)}, f32[1024,128]{1,0:T(8,128)S(1)}, bf16[1024,128]{1,0:T(8,128)(2,1)S(1)}, bf16[1024,128]{1,0:T(8,128)(2,1)S(1)}, bf16[1024,256]{1,0:T(8,128)(2,1)S(1)}) custom-call(f32[1024,384]{1,0:T(8,128)} %x_ref.3), custom_call_target="tpu_custom_call" | custom-call | flops 1000 | bytes 1000 | tf_op jit(solution)/shard_map/load_first/pallas_call | solution.py:21
  2.1 2.7 %collective-permute-start.4 = (bf16[1024,256]{1,0:T(8,128)(2,1)S(1)}, bf16[1024,256]{1,0:T(8,128)(2,1)S(1)}, u32[]{:S(2)}, u32[]{:S(2)}) collective-permute-start(bf16[1024,256]{1,0:T(8,128)(2,1)S(1)} %get-tuple-element.57._), channel_id=1, source_target_pairs={{0,15},{1,2},{2,1},{3,4},{4,3},{5,6},{6,5},{7,8},{8,7},{9,10},{10,... | collective-permute-start | bytes 1572872 | tf_op jit(solution)/shard_map/ppermute | solution.py:461
  4.8 2.9 %collective-permute-start = (bf16[1024,128]{1,0:T(8,128)(2,1)S(1)}, bf16[1024,128]{1,0:T(8,128)(2,1)S(1)}, u32[]{:S(2)}, u32[]{:S(2)}) collective-permute-start(bf16[1024,128]{1,0:T(8,128)(2,1)S(1)} %get-tuple-element.59.refs_0_), channel_id=1, source_target_pairs={{0,1},{1,0},{2,3},{3,2},{4,5},{5,4},{6,7},{7,6},{8,9},{9,8},{10,11... | collective-permute-start | bytes 786440 | tf_op jit(solution)/shard_map/ppermute | solution.py:464
  8.4 1.9 %make_lists.1 = (s32[214]{0:T(256)S(4)}, f32[1024,128]{1,0:T(8,128)S(1)}, bf16[1024,128]{1,0:T(8,128)(2,1)S(1)}) custom-call(s32[96]{0:T(128)S(1)} %copy-done.5, s32[96]{0:T(128)S(1)} %copy-done.6, s32[1]{0:T(128)S(6)} %copy.32.count_hbm, f32[1024,384]{1,0:T(8,128)} %x_ref.3, bf16[1024,256]{1,0:T(8,128)(2,1)S(1)} %get-tuple-element.57._), custom_call_target="tpu_custom_call" | custom-call | flops 1000 | bytes 1000 | tf_op jit(solution)/shard_map/make_lists/pallas_call | solution.py:21
  10.2 0.7 %collective-permute-start.2 = (bf16[1024,128]{1,0:T(8,128)(2,1)S(1)}, bf16[1024,128]{1,0:T(8,128)(2,1)S(1)}, u32[]{:S(2)}, u32[]{:S(2)}) collective-permute-start(bf16[1024,128]{1,0:T(8,128)(2,1)S(1)} %get-tuple-element.61.refs_2_.refs_6_), channel_id=1, source_target_pairs={{0,1},{1,0},{2,3},{3,2},{4,5},{5,4},{6,7},{7,6},{8,9},{9,8},{10,11... | collective-permute-start | bytes 786440 | tf_op jit(solution)/shard_map/ppermute | solution.py:464
  10.9 1.4 %first_base.1 = (f32[1024,128]{1,0:T(8,128)S(1)}, f32[1024,128]{1,0:T(8,128)S(1)}, f32[1024,128]{1,0:T(8,128)S(1)}, bf16[384,384]{1,0:T(8,128)(2,1)S(1)}) custom-call(f32[1024,128]{1,0:T(8,128)S(1)} %get-tuple-element.62.refs_0_.refs_4_, f32[1024,128]{1,0:T(8,128)S(1)} %get-tuple-element.63.refs_1_.refs_5_, ...), custom_call_target="tpu_custom_call" | custom-call | flops 1000 | bytes 1000 | tf_op jit(solution)/shard_map/first_base/pallas_call | solution.py:21
  12.4 0.4 copy-done
  12.8 1.9 %near_first.1 = (f32[1024,128]{1,0:T(8,128)S(1)}, f32[1024,128]{1,0:T(8,128)S(1)}, f32[1024,128]{1,0:T(8,128)S(1)}, bf16[1024,128]{1,0:T(8,128)(2,1)S(1)}) custom-call(s32[214]{0:T(256)S(4)} %get-tuple-element.58.list_ref, bf16[96,128,128]{2,1,0:T(8,128)(2,1)S(1)} %copy-done, bf16[1024,128]{1,0:T(8,128)(2,1)S(1)} %get-tuple-element.59.refs_0_, ...), custom_call_target="tpu_custom_call" | custom-call | flops 1000 | bytes 1000 | tf_op jit(solution)/shard_map/near_first/pallas_call | solution.py:21
  14.7 0.1 collective-permute-start.3
  14.8 7.4 %collective-permute-done.4.far_ref = bf16[1024,256]{1,0:T(8,128)(2,1)S(1)} collective-permute-done((bf16[1024,256]{1,0:T(8,128)(2,1)S(1)}, bf16[1024,256]{1,0:T(8,128)(2,1)S(1)}, u32[]{:S(2)}, u32[]{:S(2)}) %collective-permute-start.4) | collective-permute-done | bytes 524320 | tf_op jit(solution)/shard_map/ppermute | solution.py:461
  22.2 1.0 %far_first_0.1 = (f32[1024,128]{1,0:T(8,128)S(1)}, f32[1024,128]{1,0:T(8,128)S(1)}, bf16[1024,128]{1,0:T(8,128)(2,1)S(1)}, bf16[1024,128]{1,0:T(8,128)(2,1)S(1)}...) custom-call(s32[214]{0:T(256)S(4)} %get-tuple-element.58.list_ref, bf16[96,128,128]{2,1,0:T(8,128)(2,1)S(1)} %copy-done, ...), custom_call_target="tpu_custom_call" | custom-call | flops 1000 | bytes 1000 | tf_op jit(solution)/shard_map/far_first_0/pallas_call | solution.py:21
  23.2 2.8 %collective-permute-start.9 = (bf16[1024,128]{1,0:T(8,128)(2,1)S(1)}, bf16[1024,128]{1,0:T(8,128)(2,1)S(1)}, u32[]{:S(2)}, u32[]{:S(2)}) collective-permute-start(bf16[1024,128]{1,0:T(8,128)(2,1)S(1)} %get-tuple-element.79), channel_id=1, source_target_pairs={{0,15},{1,2},{2,1},{3,4},{4,3},{5,6},{6,5},{7,8},{8,7},{9,10},{10,... | collective-permute-start | bytes 786440 | tf_op jit(solution)/shard_map/ppermute | solution.py:461
  26.0 4.6 %collective-permute-done.3.far_ref = bf16[1024,128]{1,0:T(8,128)(2,1)S(1)} collective-permute-done((bf16[1024,128]{1,0:T(8,128)(2,1)S(1)}, bf16[1024,128]{1,0:T(8,128)(2,1)S(1)}, u32[]{:S(2)}, u32[]{:S(2)}) %collective-permute-start.3) | collective-permute-done | bytes 262176 | tf_op jit(solution)/shard_map/ppermute | solution.py:461
  30.6 1.1 %far_first_1.1 = (f32[1024,128]{1,0:T(8,128)S(1)}, f32[1024,128]{1,0:T(8,128)S(1)}, bf16[1024,128]{1,0:T(8,128)(2,1)S(1)}, f32[1024,128]{1,0:T(8,128)S(1)}, f32[...) custom-call(s32[214]{0:T(256)S(4)} %get-tuple-element.58.list_ref, ...), custom_call_target="tpu_custom_call" | custom-call | flops 1000 | bytes 1000 | tf_op jit(solution)/shard_map/far_first_1/pallas_call | solution.py:21
  31.7 2.8 %collective-permute-start.5 = (bf16[1024,256]{1,0:T(8,128)(2,1)S(1)}, bf16[1024,256]{1,0:T(8,128)(2,1)S(1)}, u32[]{:S(2)}, u32[]{:S(2)}) collective-permute-start(bf16[1024,256]{1,0:T(8,128)(2,1)S(1)} %get-tuple-element.75), channel_id=1, source_target_pairs={{0,15},{1,2},{2,1},{3,4},{4,3},{5,6},{6,5},{7,8},{8,7},{9,10},{10,... | collective-permute-start | bytes 1572872 | tf_op jit(solution)/shard_map/ppermute | solution.py:461
  34.4 0.5 collective-permute-start.8
  35.0 1.7 %second_base.1 = (f32[1024,128]{1,0:T(8,128)S(1)}, f32[1024,128]{1,0:T(8,128)S(1)}, f32[1024,128]{1,0:T(8,128)S(1)}, f32[1024,128]{1,0:T(8,128)S(1)}, f32[1024,128]{1,0:T(8,128)S(1)}, /*index=5*/f32[1024,128]{1,0:T(8,128)S(1)}) custom-call(f32[1024,128]{1,0:T(8,128)S(1)} %get-tuple-element.82.refs_0_.refs_6_, ...), custom_call_target="tpu_custom_call" | custom-call | flops 1000 | bytes 1000 | tf_op jit(solution)/shard_map/second_base/pallas_call | solution.py:21
  36.7 0.6 %far_second_0.1.refs_6_ = f32[1024,128]{1,0:T(8,128)S(1)} custom-call(s32[214]{0:T(256)S(4)} %get-tuple-element.58.list_ref, bf16[96,128,128]{2,1,0:T(8,128)(2,1)S(1)} %copy-done, bf16[1024,128]{1,0:T(8,128)(2,1)S(1)} %collective-permute-done.9.far_ref), custom_call_target="tpu_custom_call" | custom-call | flops 4000000000 | bytes 1000 | tf_op jit(solution)/shard_map/far_second_0/pallas_call | solution.py:21
  37.3 1.8 %near_second.1 = (bf16[1024,128]{1,0:T(8,128)(2,1)S(1)}, f32[1024,128]{1,0:T(8,128)S(1)}, f32[1024,128]{1,0:T(8,128)S(1)}) custom-call(s32[214]{0:T(256)S(4)} %get-tuple-element.58.list_ref, bf16[96,128,128]{2,1,0:T(8,128)(2,1)S(1)} %copy-done, bf16[1024,128]{1,0:T(8,128)(2,1)S(1)} %get-tuple-element.76.refs_0_.refs_6_, ...), custom_call_target="tpu_custom_call" | custom-call | flops 1000 | bytes 1000 | tf_op jit(solution)/shard_map/near_second/pallas_call | solution.py:21
  39.2 2.2 %collective-permute-done.5.far_ref = bf16[1024,256]{1,0:T(8,128)(2,1)S(1)} collective-permute-done((bf16[1024,256]{1,0:T(8,128)(2,1)S(1)}, bf16[1024,256]{1,0:T(8,128)(2,1)S(1)}, u32[]{:S(2)}, u32[]{:S(2)}) %collective-permute-start.5) | collective-permute-done | bytes 524320 | tf_op jit(solution)/shard_map/ppermute | solution.py:461
  41.3 1.1 %far_second_1.1 = (bf16[1024,128]{1,0:T(8,128)(2,1)S(1)}, bf16[1024,128]{1,0:T(8,128)(2,1)S(1)}, f32[8,128]{1,0:T(8,128)S(1)}, bf16[1024,128]{1,0:T(8,128)(2,1)S...) custom-call(s32[214]{0:T(256)S(4)} %get-tuple-element.58.list_ref, ...), custom_call_target="tpu_custom_call", output_to_operand_aliasing={{3}: (8, {}), {4}: (9, {}), {5}: (10, {}), {6}: (11, {}), {... | custom-call | flops 1000 | bytes 1000 | tf_op jit(solution)/shard_map/far_second_1/pallas_call | solution.py:21
  42.4 3.1 %collective-permute-start.12 = (f32[8,128]{1,0:T(8,128)S(1)}, f32[8,128]{1,0:T(8,128)S(1)}, u32[]{:S(2)}, u32[]{:S(2)}) collective-permute-start(f32[8,128]{1,0:T(8,128)S(1)} %get-tuple-element.109.refs_0_), channel_id=1, source_target_pairs={{0,12},{1,13},{2,14},{3,15},{4,8},{5,9},{6,10},{7,11},{8,4},{9,5},... | collective-permute-start | bytes 12296 | tf_op jit(solution)/shard_map/ppermute | solution.py:430
  45.5 0.5 collective-permute-start.10
  45.9 0.1 finish_early.1
  46.0 0.6 %collective-permute-done.12.refs_3_ = f32[8,128]{1,0:T(8,128)S(1)} collective-permute-done((f32[8,128]{1,0:T(8,128)S(1)}, f32[8,128]{1,0:T(8,128)S(1)}, u32[]{:S(2)}, u32[]{:S(2)}) %collective-permute-start.12) | collective-permute-done | bytes 4128 | tf_op jit(solution)/shard_map/ppermute | solution.py:430
  46.6 2.2 %collective-permute-done.11.refs_2_ = f32[8,128]{1,0:T(8,128)S(1)} collective-permute-done((f32[8,128]{1,0:T(8,128)S(1)}, f32[8,128]{1,0:T(8,128)S(1)}, u32[]{:S(2)}, u32[]{:S(2)}) %collective-permute-start.11) | collective-permute-done | bytes 4128 | tf_op jit(solution)/shard_map/ppermute | solution.py:430
  48.8 2.2 %collective-permute-start.15 = (f32[8,128]{1,0:T(8,128)S(1)}, f32[8,128]{1,0:T(8,128)S(1)}, u32[]{:S(2)}, u32[]{:S(2)}) collective-permute-start(f32[8,128]{1,0:T(8,128)S(1)} %add_up.1), channel_id=1, source_target_pairs={{0,3},{1,2},{2,1},{3,0},{4,7},{5,6},{6,5},{7,4},{8,11},{9,10},{10,... | collective-permute-start | bytes 12296 | tf_op jit(solution)/shard_map/ppermute | solution.py:430
  51.0 0.5 collective-permute-start.13
  51.5 2.8 %finish_late.1 = (f32[1024,384]{1,0:T(8,128)}, f32[1024,384]{1,0:T(8,128)}, f32[8,128]{1,0:T(8,128)}) custom-call(bf16[1024,128]{1,0:T(8,128)(2,1)S(1)} %get-tuple-element.95.refs_0_, bf16[1024,128]{1,0:T(8,128)(2,1)S(1)} %get-tuple-element.96.refs_1_, ...), custom_call_target="tpu_custom_call", output_to_operand_aliasing={{0}: (10, {}), {1}: (11, {})} | custom-call | flops 1000 | bytes 1000 | tf_op jit(solution)/shard_map/finish_late/pallas_call | solution.py:21
  54.3 0.5 multiply_bitcast_fusion
  (29 shorter events, 0.1 us)
Async XLA Ops:
  0.6 10.3 %copy-start.2 = (bf16[384,384]{1,0:T(8,128)(2,1)S(1)}, bf16[384,384]{1,0:T(8,128)(2,1)}, u32[]{:S(2)}) copy-start(bf16[384,384]{1,0:T(8,128)(2,1)} %constant.7.clone.refs_4_.refs_9_) | copy-start | bytes 884740
  0.6 10.3 %copy-start.3 = (bf16[384,48]{1,0:T(8,128)(2,1)S(1)}, bf16[384,48]{1,0:T(8,128)(2,1)}, u32[]{:S(2)}) copy-start(bf16[384,48]{1,0:T(8,128)(2,1)} %constant.8.clone.refs_5_) | copy-start | bytes 110596
  0.7 7.7 %copy-start.6 = (s32[96]{0:T(128)S(1)}, s32[96]{0:T(128)}, u32[]{:S(2)}) copy-start(s32[96]{0:T(128)} %cols_hbm.1) | copy-start | bytes 1156
  0.7 7.7 %copy-start.5 = (s32[96]{0:T(128)S(1)}, s32[96]{0:T(128)}, u32[]{:S(2)}) copy-start(s32[96]{0:T(128)} %rows_hbm.1) | copy-start | bytes 1156
  0.7 10.2 %copy-start.4 = (bf16[48,48]{1,0:T(8,128)(2,1)S(1)}, bf16[48,48]{1,0:T(8,128)(2,1)}, u32[]{:S(2)}) copy-start(bf16[48,48]{1,0:T(8,128)(2,1)} %refs_6_.1) | copy-start | bytes 13828
  0.7 10.2 %copy-start.1 = (f32[1024,384]{1,0:T(8,128)S(1)}, f32[1024,384]{1,0:T(8,128)}, u32[]{:S(2)}) copy-start(f32[1024,384]{1,0:T(8,128)} %refs_3_.1) | copy-start | bytes 4718596
  2.1 20.1 %collective-permute-start.4 = (bf16[1024,256]{1,0:T(8,128)(2,1)S(1)}, bf16[1024,256]{1,0:T(8,128)(2,1)S(1)}, u32[]{:S(2)}, u32[]{:S(2)}) collective-permute-start(bf16[1024,256]{1,0:T(8,128)(2,1)S(1)} %get-tuple-element.57._), channel_id=1, source_target_pairs={{0,15},{1,2},{2,1},{3,4},{4,3},{5,6},{6,5},{7,8},{8,7},{9,10},{10,... | collective-permute-start | bytes 1572872 | tf_op jit(solution)/shard_map/ppermute | solution.py:461
  4.8 7.5 %collective-permute-start = (bf16[1024,128]{1,0:T(8,128)(2,1)S(1)}, bf16[1024,128]{1,0:T(8,128)(2,1)S(1)}, u32[]{:S(2)}, u32[]{:S(2)}) collective-permute-start(bf16[1024,128]{1,0:T(8,128)(2,1)S(1)} %get-tuple-element.59.refs_0_), channel_id=1, source_target_pairs={{0,1},{1,0},{2,3},{3,2},{4,5},{5,4},{6,7},{7,6},{8,9},{9,8},{10,11... | collective-permute-start | bytes 786440 | tf_op jit(solution)/shard_map/ppermute | solution.py:464
  7.7 4.7 %collective-permute-start.1 = (bf16[1024,128]{1,0:T(8,128)(2,1)S(1)}, bf16[1024,128]{1,0:T(8,128)(2,1)S(1)}, u32[]{:S(2)}, u32[]{:S(2)}) collective-permute-start(bf16[1024,128]{1,0:T(8,128)(2,1)S(1)} %get-tuple-element.60.refs_1_), channel_id=1, source_target_pairs={{0,1},{1,0},{2,3},{3,2},{4,5},{5,4},{6,7},{7,6},{8,9},{9,8},{10,11... | collective-permute-start | bytes 786440 | tf_op jit(solution)/shard_map/ppermute | solution.py:464
  10.2 2.1 %collective-permute-start.2 = (bf16[1024,128]{1,0:T(8,128)(2,1)S(1)}, bf16[1024,128]{1,0:T(8,128)(2,1)S(1)}, u32[]{:S(2)}, u32[]{:S(2)}) collective-permute-start(bf16[1024,128]{1,0:T(8,128)(2,1)S(1)} %get-tuple-element.61.refs_2_.refs_6_), channel_id=1, source_target_pairs={{0,1},{1,0},{2,3},{3,2},{4,5},{5,4},{6,7},{7,6},{8,9},{9,8},{10,11... | collective-permute-start | bytes 786440 | tf_op jit(solution)/shard_map/ppermute | solution.py:464
  10.9 1.9 %copy-start = (bf16[96,128,128]{2,1,0:T(8,128)(2,1)S(1)}, bf16[96,128,128]{2,1,0:T(8,128)(2,1)}, u32[]{:S(2)}) copy-start(bf16[96,128,128]{2,1,0:T(8,128)(2,1)} %tiles_ref.11) | copy-start | bytes 9437188
  14.7 15.9 %collective-permute-start.3 = (bf16[1024,128]{1,0:T(8,128)(2,1)S(1)}, bf16[1024,128]{1,0:T(8,128)(2,1)S(1)}, u32[]{:S(2)}, u32[]{:S(2)}) collective-permute-start(bf16[1024,128]{1,0:T(8,128)(2,1)S(1)} %get-tuple-element.66), channel_id=1, source_target_pairs={{0,15},{1,2},{2,1},{3,4},{4,3},{5,6},{6,5},{7,8},{8,7},{9,10},{10,... | collective-permute-start | bytes 786440 | tf_op jit(solution)/shard_map/ppermute | solution.py:461
  23.2 13.5 %collective-permute-start.9 = (bf16[1024,128]{1,0:T(8,128)(2,1)S(1)}, bf16[1024,128]{1,0:T(8,128)(2,1)S(1)}, u32[]{:S(2)}, u32[]{:S(2)}) collective-permute-start(bf16[1024,128]{1,0:T(8,128)(2,1)S(1)} %get-tuple-element.79), channel_id=1, source_target_pairs={{0,15},{1,2},{2,1},{3,4},{4,3},{5,6},{6,5},{7,8},{8,7},{9,10},{10,... | collective-permute-start | bytes 786440 | tf_op jit(solution)/shard_map/ppermute | solution.py:461
  31.7 9.6 %collective-permute-start.5 = (bf16[1024,256]{1,0:T(8,128)(2,1)S(1)}, bf16[1024,256]{1,0:T(8,128)(2,1)S(1)}, u32[]{:S(2)}, u32[]{:S(2)}) collective-permute-start(bf16[1024,256]{1,0:T(8,128)(2,1)S(1)} %get-tuple-element.75), channel_id=1, source_target_pairs={{0,15},{1,2},{2,1},{3,4},{4,3},{5,6},{6,5},{7,8},{8,7},{9,10},{10,... | collective-permute-start | bytes 1572872 | tf_op jit(solution)/shard_map/ppermute | solution.py:461
  34.4 2.8 %collective-permute-start.7 = (bf16[1024,128]{1,0:T(8,128)(2,1)S(1)}, bf16[1024,128]{1,0:T(8,128)(2,1)S(1)}, u32[]{:S(2)}, u32[]{:S(2)}) collective-permute-start(bf16[1024,128]{1,0:T(8,128)(2,1)S(1)} %get-tuple-element.77.refs_1_.refs_7_), channel_id=1, source_target_pairs={{0,1},{1,0},{2,3},{3,2},{4,5},{5,4},{6,7},{7,6},{8,9},{9,8},{10,11... | collective-permute-start | bytes 786440 | tf_op jit(solution)/shard_map/ppermute | solution.py:464
  34.4 2.8 %collective-permute-start.8 = (bf16[1024,128]{1,0:T(8,128)(2,1)S(1)}, bf16[1024,128]{1,0:T(8,128)(2,1)S(1)}, u32[]{:S(2)}, u32[]{:S(2)}) collective-permute-start(bf16[1024,128]{1,0:T(8,128)(2,1)S(1)} %get-tuple-element.78.refs_2_.refs_8_), channel_id=1, source_target_pairs={{0,1},{1,0},{2,3},{3,2},{4,5},{5,4},{6,7},{7,6},{8,9},{9,8},{10,11... | collective-permute-start | bytes 786440 | tf_op jit(solution)/shard_map/ppermute | solution.py:464
  35.0 2.3 %collective-permute-start.6 = (bf16[1024,128]{1,0:T(8,128)(2,1)S(1)}, bf16[1024,128]{1,0:T(8,128)(2,1)S(1)}, u32[]{:S(2)}, u32[]{:S(2)}) collective-permute-start(bf16[1024,128]{1,0:T(8,128)(2,1)S(1)} %get-tuple-element.76.refs_0_.refs_6_), channel_id=1, source_target_pairs={{0,1},{1,0},{2,3},{3,2},{4,5},{5,4},{6,7},{7,6},{8,9},{9,8},{10,11... | collective-permute-start | bytes 786440 | tf_op jit(solution)/shard_map/ppermute | solution.py:464
  42.4 4.3 %collective-permute-start.12 = (f32[8,128]{1,0:T(8,128)S(1)}, f32[8,128]{1,0:T(8,128)S(1)}, u32[]{:S(2)}, u32[]{:S(2)}) collective-permute-start(f32[8,128]{1,0:T(8,128)S(1)} %get-tuple-element.109.refs_0_), channel_id=1, source_target_pairs={{0,12},{1,13},{2,14},{3,15},{4,8},{5,9},{6,10},{7,11},{8,4},{9,5},... | collective-permute-start | bytes 12296 | tf_op jit(solution)/shard_map/ppermute | solution.py:430
  45.5 3.4 %collective-permute-start.11 = (f32[8,128]{1,0:T(8,128)S(1)}, f32[8,128]{1,0:T(8,128)S(1)}, u32[]{:S(2)}, u32[]{:S(2)}) collective-permute-start(f32[8,128]{1,0:T(8,128)S(1)} %get-tuple-element.109.refs_0_), channel_id=1, source_target_pairs={{0,8},{1,9},{2,10},{3,11},{4,12},{5,13},{6,14},{7,15},{8,0},{9,1},... | collective-permute-start | bytes 12296 | tf_op jit(solution)/shard_map/ppermute | solution.py:430
  45.5 3.4 %collective-permute-start.10 = (f32[8,128]{1,0:T(8,128)S(1)}, f32[8,128]{1,0:T(8,128)S(1)}, u32[]{:S(2)}, u32[]{:S(2)}) collective-permute-start(f32[8,128]{1,0:T(8,128)S(1)} %get-tuple-element.109.refs_0_), channel_id=1, source_target_pairs={{0,4},{1,5},{2,6},{3,7},{4,0},{5,1},{6,2},{7,3},{8,12},{9,13},{10,... | collective-permute-start | bytes 12296 | tf_op jit(solution)/shard_map/ppermute | solution.py:430
  48.8 5.4 %collective-permute-start.15 = (f32[8,128]{1,0:T(8,128)S(1)}, f32[8,128]{1,0:T(8,128)S(1)}, u32[]{:S(2)}, u32[]{:S(2)}) collective-permute-start(f32[8,128]{1,0:T(8,128)S(1)} %add_up.1), channel_id=1, source_target_pairs={{0,3},{1,2},{2,1},{3,0},{4,7},{5,6},{6,5},{7,4},{8,11},{9,10},{10,... | collective-permute-start | bytes 12296 | tf_op jit(solution)/shard_map/ppermute | solution.py:430
  51.0 3.3 %collective-permute-start.14 = (f32[8,128]{1,0:T(8,128)S(1)}, f32[8,128]{1,0:T(8,128)S(1)}, u32[]{:S(2)}, u32[]{:S(2)}) collective-permute-start(f32[8,128]{1,0:T(8,128)S(1)} %add_up.1), channel_id=1, source_target_pairs={{0,2},{1,3},{2,0},{3,1},{4,6},{5,7},{6,4},{7,5},{8,10},{9,11},{10,... | collective-permute-start | bytes 12296 | tf_op jit(solution)/shard_map/ppermute | solution.py:430
  51.0 3.3 %collective-permute-start.13 = (f32[8,128]{1,0:T(8,128)S(1)}, f32[8,128]{1,0:T(8,128)S(1)}, u32[]{:S(2)}, u32[]{:S(2)}) collective-permute-start(f32[8,128]{1,0:T(8,128)S(1)} %add_up.1), channel_id=1, source_target_pairs={{0,1},{1,0},{2,3},{3,2},{4,5},{5,4},{6,7},{7,6},{8,9},{9,8},{10,11... | collective-permute-start | bytes 12296 | tf_op jit(solution)/shard_map/ppermute | solution.py:430

commit v11 on v9

--- a/solution.py
+++ b/solution.py
@@ -332,19 +332,42 @@
     return outs[:groups], outs[groups]
 
 
-def second_base(xs, ys, rounded, same, mixing, channels):
-    groups = len(xs)
-    cells = xs[0].shape[0]
+def updated(field_mixed, base, x):
+    y_new = base - 0.2 * field_mixed
+    return jnp.clip(x + 0.5 * y_new, -1.0, 1.0), y_new
+
+
+def second_base(xs, ys, later, fields, first_base, first_x, rounded, same, mixing, channels):
+    groups = len(rounded)
+    cells = rounded[0].shape[0]
     width = groups * LANES
+    done, m = len(xs), len(later)
 
     def body(*refs):
-        x, y, r = [[ref[...] for ref in refs[k * groups : (k + 1) * groups]] for k in range(3)]
-        same_ref, mixing_ref = refs[3 * groups : 3 * groups + 2]
-        outs = refs[3 * groups + 2 :]
-        bases_into(outs[:groups], x, y, same_ref, 1, channels)
+        refs = list(refs)
+
+        def take(n):
+            taken = refs[:n]
+            del refs[:n]
+            return taken
+
+        x = [ref[...] for ref in take(done)]
+        y = [ref[...] for ref in take(done)]
+        held = [ref[...] for ref in take(groups)]
+        base_refs, x_refs = take(m), take(m)
+        r = [ref[...] for ref in take(groups)]
+        same_ref, mixing_ref = take(2)
+        for i, t in enumerate(later):
+            x_new, y_new = updated(
+                mixed_of(held, mixing_ref, t, channels), base_refs[i][...], x_refs[i][...]
+            )
+            x.append(x_new)
+            y.append(y_new)
+            refs[2 * groups + i][...] = x_new
+        bases_into(refs[:groups], x, y, same_ref, 1, channels)
         for g in range(groups):
             near = spanned(g, channels, width)
-            outs[groups + g][...] = lax.dot_general(
+            refs[groups + g][...] = lax.dot_general(
                 jnp.concatenate([r[n] for n in near], axis=1),
                 mixing_ref[lanes(g), span_lanes(near)],
                 (((1,), (1,)), ((), ())),
@@ -353,12 +376,12 @@
 
     outs = call(
         body,
-        vmem(*xs, *ys, *rounded, same, mixing),
-        [((cells, LANES), F32, pltpu.VMEM)] * (2 * groups),
+        vmem(*xs, *ys, *fields, *first_base, *first_x, *rounded, same, mixing),
+        [((cells, LANES), F32, pltpu.VMEM)] * (2 * groups + m),
         [],
         "second_base",
     )
-    return outs[:groups], outs[groups:]
+    return outs[:groups], outs[groups : 2 * groups], outs[2 * groups :]
 
 
 def finish(fields, xs, bases, mixing, channels):
@@ -480,13 +503,12 @@
     )
     fars.append(far_swap(sent[0]))
 
-    fields, new_x, new_y, rounded, new_fars = {}, {}, {}, {}, []
+    fields, new_x, new_y, rounded, new_fars = {}, [], [], {}, []
     for p, piece in enumerate(first_pieces):
-        todo = ready(piece, new_x)
+        last = p == len(first_pieces) - 1
+        todo = ready(piece, rounded)
         known = needed(todo, piece)
-        going = second_pieces[p]
-        assert going == todo
-        last = p == len(first_pieces) - 1
+        assert second_pieces[p] == todo
 
         def work(done, ins, outs, piece=piece, todo=todo, known=known, last=last):
             held = {n: ins[1 + i][...] for i, n in enumerate(known)}
@@ -494,16 +516,17 @@
             held.update(zip(piece, done))
             rest = ins[1 + len(known) :]
             for i, t in enumerate(todo):
-                y_new = rest[2 * i][...] - 0.2 * mixed_of(held, ins[0], t, channels)
-                x_new = jnp.clip(rest[2 * i + 1][...] + 0.5 * y_new, -1.0, 1.0)
+                x_new, y_new = updated(
+                    mixed_of(held, ins[0], t, channels), rest[2 * i][...], rest[2 * i + 1][...]
+                )
                 r_new = x_new.astype(BF16)
-                outs[3 * i][...] = x_new
-                outs[3 * i + 1][...] = y_new
-                outs[3 * i + 2][...] = r_new
-                outs[3 * len(todo)][:, lanes(i)] = r_new
-            if not last:
-                for i, field in enumerate(done):
-                    outs[3 * len(todo) + 1 + i][...] = field
+                outs[0][:, lanes(i)] = r_new
+                outs[1 + i][...] = r_new
+                if not last:
+                    outs[1 + len(todo) + len(piece) + 2 * i][...] = x_new
+                    outs[2 + len(todo) + len(piece) + 2 * i][...] = y_new
+            for i, field in enumerate(done):
+                outs[1 + len(todo) + i][...] = field
 
         results = far_fields(
             lists,
@@ -511,24 +534,38 @@
             [near[n] for n in piece],
             fars[p],
             [mixing] + [fields[n] for n in known] + [a for t in todo for a in (base[t], xs[t])],
-            [(wide, F32), (wide, F32), (wide, BF16)] * len(todo)
-            + [((cells, len(todo) * LANES), BF16)]
-            + ([] if last else [(wide, BF16)] * len(piece)),
+            [((cells, len(todo) * LANES), BF16)]
+            + [(wide, BF16)] * (len(todo) + len(piece))
+            + ([] if last else [(wide, F32)] * (2 * len(todo))),
             work,
             f"far_first_{p}",
         )
-        for i, t in enumerate(todo):
-            new_x[t], new_y[t], rounded[t] = results[3 * i : 3 * i + 3]
-        new_fars.append(far_swap(results[3 * len(todo)]))
-        fields.update(zip(piece, results[3 * len(todo) + 1 :]))
-
-    xs, ys, owns = [[of[g] for g in every] for of in (new_x, new_y, rounded)]
+        new_fars.append(far_swap(results[0]))
+        rounded.update(zip(todo, results[1:]))
+        fields.update(zip(piece, results[1 + len(todo) :]))
+        new_x += results[1 + len(todo) + len(piece) :: 2]
+        new_y += results[2 + len(todo) + len(piece) :: 2]
+
+    owns = [rounded[g] for g in every]
     others = [near_swap(r) for r in owns]
     (part,) = far_fields(
         lists, tile_values, [], new_fars[0], [], [(wide, F32)], keep, "far_second_0", NEAR_FLOPS
     )
     near, _ = near_fields(lists, tile_values, owns, others, part, [], [], 0, "near_second")
-    base, weights = second_base(xs, ys, owns, same, mixing, channels)
+    later = second_pieces[1]
+    base, weights, more_x = second_base(
+        new_x,
+        new_y,
+        later,
+        [fields[g] for g in every],
+        [base[t] for t in later],
+        [xs[t] for t in later],
+        owns,
+        same,
+        mixing,
+        channels,
+    )
+    xs = [*new_x, *more_x]
     piece = second_pieces[1]
 
     def last_work(done, ins, outs):

time: 54.2 us -> 54.4 us (level)
  transfers between devices with their start and end apart: 16 -> 16, of which waited for: 2 -> 4; matrix products, arithmetic and copies ran while one was open for 0% -> 0% of each run, Pallas kernels for 29% -> 29%
where the time goes in v11:
time: 54.4 us; the launch traced here: 53.6 us
  starting transfers between devices  28.1 us (52%)
  Pallas kernels  18 us (33%)
  waiting for transfers between devices  4.88 us (9%)
  between operations  1.57 us (3%)
    pallas_call x12, Pallas kernels, call(): pl.pallas_call(body, in_specs=[pl.BlockSpec(memory_space=pl.ANY if s is p...  18 us
    ppermute x6, starting transfers between devices, near_swap(): return lax.ppermute(mine, RING, on_chip)  10.6 us
    ppermute x4, starting transfers between devices, far_swap(): return lax.ppermute(mine, RING, off_chip)  10.1 us
    ppermute x6, starting transfers between devices, sum_over_ring(): lax.ppermute(value, RING, [(j, j ^ bit) for j in range(ring)])  7.41 us
    ppermute x4, waiting for transfers between devices, far_swap(): return lax.ppermute(mine, RING, off_chip)  2.88 us
    ppermute x6, waiting for transfers between devices, sum_over_ring(): lax.ppermute(value, RING, [(j, j ^ bit) for j in range(ring)])  1.89 us
  transfers between devices with their start and end apart: 16, of which 4 were waited for; matrix products, arithmetic and copies ran while one was open for 0% of the time, Pallas kernels for 29%

profile of v11, /device:TPU:0, one launch (start us, length us, event | category | flops | bytes accessed | tf_op | source)
XLA Modules:
  0.0 53.6 jit_solution(14189961043121648318)
XLA Ops:
  0.6 0.0 copy-start.2
  0.7 1.4 %load_first.1 = (f32[1024,128]{1,0:T(8,128)S(1)}, f32[1024,128]{1,0:T(8,128)S(1)}, bf16[1024,128]{1,0:T(8,128)(2,1)S(1)}, bf16[1024,128]{1,0:T(8,128)(2,1)S(1)}, bf16[1024,256]{1,0:T(8,128)(2,1)S(1)}) custom-call(f32[1024,384]{1,0:T(8,128)} %x_ref.3), custom_call_target="tpu_custom_call" | custom-call | flops 1000 | bytes 1000 | tf_op jit(solution)/shard_map/load_first/pallas_call | solution.py:21
  2.1 5.5 %collective-permute-start.4 = (bf16[1024,256]{1,0:T(8,128)(2,1)S(1)}, bf16[1024,256]{1,0:T(8,128)(2,1)S(1)}, u32[]{:S(2)}, u32[]{:S(2)}) collective-permute-start(bf16[1024,256]{1,0:T(8,128)(2,1)S(1)} %get-tuple-element.54._), channel_id=1, source_target_pairs={{0,15},{1,2},{2,1},{3,4},{4,3},{5,6},{6,5},{7,8},{8,7},{9,10},{10,... | collective-permute-start | bytes 1572872 | tf_op jit(solution)/shard_map/ppermute | solution.py:477
  7.6 0.5 collective-permute-start.1
  8.8 2.1 %make_lists.1 = (s32[214]{0:T(256)S(4)}, f32[1024,128]{1,0:T(8,128)S(1)}, bf16[1024,128]{1,0:T(8,128)(2,1)S(1)}) custom-call(s32[96]{0:T(128)S(1)} %copy-done.5, s32[96]{0:T(128)S(1)} %copy-done.6, s32[1]{0:T(128)S(6)} %copy.28.count_hbm, f32[1024,384]{1,0:T(8,128)} %x_ref.3, bf16[1024,256]{1,0:T(8,128)(2,1)S(1)} %get-tuple-element.54._), custom_call_target="tpu_custom_call" | custom-call | flops 1000 | bytes 1000 | tf_op jit(solution)/shard_map/make_lists/pallas_call | solution.py:21
  10.9 0.1 collective-permute-start.2
  11.0 1.4 %first_base.1 = (f32[1024,128]{1,0:T(8,128)S(1)}, f32[1024,128]{1,0:T(8,128)S(1)}, f32[1024,128]{1,0:T(8,128)S(1)}, bf16[384,384]{1,0:T(8,128)(2,1)S(1)}) custom-call(f32[1024,128]{1,0:T(8,128)S(1)} %get-tuple-element.59.refs_0_.refs_4_, f32[1024,128]{1,0:T(8,128)S(1)} %get-tuple-element.60.refs_1_.refs_5_.refs_7_, ...), custom_call_target="tpu_custom_call" | custom-call | flops 1000 | bytes 1000 | tf_op jit(solution)/shard_map/first_base/pallas_call | solution.py:21
  12.4 0.1 collective-permute-done.2.refs_5_
  12.5 0.4 copy-done
  12.9 2.2 %near_first.1 = (f32[1024,128]{1,0:T(8,128)S(1)}, f32[1024,128]{1,0:T(8,128)S(1)}, f32[1024,128]{1,0:T(8,128)S(1)}, bf16[1024,128]{1,0:T(8,128)(2,1)S(1)}) custom-call(s32[214]{0:T(256)S(4)} %get-tuple-element.55.list_ref, bf16[96,128,128]{2,1,0:T(8,128)(2,1)S(1)} %copy-done, bf16[1024,128]{1,0:T(8,128)(2,1)S(1)} %get-tuple-element.56.refs_0_, ...), custom_call_target="tpu_custom_call" | custom-call | flops 1000 | bytes 1000 | tf_op jit(solution)/shard_map/near_first/pallas_call | solution.py:21
  15.1 0.1 collective-permute-start.3
  15.2 1.3 %far_first_0.1 = (bf16[1024,128]{1,0:T(8,128)(2,1)S(1)}, bf16[1024,128]{1,0:T(8,128)(2,1)S(1)}, bf16[1024,128]{1,0:T(8,128)(2,1)S(1)}, bf16[1024,128]{1,0:T(8,12...) custom-call(s32[214]{0:T(256)S(4)} %get-tuple-element.55.list_ref, bf16[96,128,128]{2,1,0:T(8,128)(2,1)S(1)} %copy-done, ...), custom_call_target="tpu_custom_call" | custom-call | flops 1000 | bytes 1000 | tf_op jit(solution)/shard_map/far_first_0/pallas_call | solution.py:21
  16.5 4.4 %collective-permute-start.9 = (bf16[1024,128]{1,0:T(8,128)(2,1)S(1)}, bf16[1024,128]{1,0:T(8,128)(2,1)S(1)}, u32[]{:S(2)}, u32[]{:S(2)}) collective-permute-start(bf16[1024,128]{1,0:T(8,128)(2,1)S(1)} %get-tuple-element.76), channel_id=1, source_target_pairs={{0,15},{1,2},{2,1},{3,4},{4,3},{5,6},{6,5},{7,8},{8,7},{9,10},{10,... | collective-permute-start | bytes 786440 | tf_op jit(solution)/shard_map/ppermute | solution.py:477
  20.9 2.9 %collective-permute-done.3.far_ref = bf16[1024,128]{1,0:T(8,128)(2,1)S(1)} collective-permute-done((bf16[1024,128]{1,0:T(8,128)(2,1)S(1)}, bf16[1024,128]{1,0:T(8,128)(2,1)S(1)}, u32[]{:S(2)}, u32[]{:S(2)}) %collective-permute-start.3) | collective-permute-done | bytes 262176 | tf_op jit(solution)/shard_map/ppermute | solution.py:477
  23.8 1.3 %far_first_1.1 = (bf16[1024,256]{1,0:T(8,128)(2,1)S(1)}, bf16[1024,128]{1,0:T(8,128)(2,1)S(1)}, bf16[1024,128]{1,0:T(8,128)(2,1)S(1)}, bf16[1024,128]{1,0:T(8,128)(2,1)S(1)}) custom-call(s32[214]{0:T(256)S(4)} %get-tuple-element.55.list_ref, bf16[96,128,128]{2,1,0:T(8,128)(2,1)S(1)} %copy-done, bf16[1024,128]{1,0:T(8,128)(2,1)S(1)} %collective-permute-done.3.far_ref, ...), custom_call_target="tpu_custom_call" | custom-call | flops 1000 | bytes 1000 | tf_op jit(solution)/shard_map/far_first_1/pallas_call | solution.py:21
  25.1 0.1 collective-permute-start.5
  25.2 9.5 %collective-permute-start.6 = (bf16[1024,128]{1,0:T(8,128)(2,1)S(1)}, bf16[1024,128]{1,0:T(8,128)(2,1)S(1)}, u32[]{:S(2)}, u32[]{:S(2)}) collective-permute-start(bf16[1024,128]{1,0:T(8,128)(2,1)S(1)} %get-tuple-element.73.refs_0_.refs_9_), channel_id=1, source_target_pairs={{0,1},{1,0},{2,3},{3,2},{4,5},{5,4},{6,7},{7,6},{8,9},{9,8},{10,11... | collective-permute-start | bytes 786440 | tf_op jit(solution)/shard_map/ppermute | solution.py:480
  34.7 0.5 collective-permute-start.8
  35.2 2.0 %second_base.1 = (f32[1024,128]{1,0:T(8,128)S(1)}, f32[1024,128]{1,0:T(8,128)S(1)}, f32[1024,128]{1,0:T(8,128)S(1)}, f32[1024,128]{1,0:T(8,128)S(1)}, f32[1024,1...) custom-call(f32[1024,128]{1,0:T(8,128)S(1)} %get-tuple-element.79.refs_0_.refs_6_, ...), custom_call_target="tpu_custom_call" | custom-call | flops 1000 | bytes 1000 | tf_op jit(solution)/shard_map/second_base/pallas_call | solution.py:21
  37.2 0.8 %far_second_0.1.refs_6_ = f32[1024,128]{1,0:T(8,128)S(1)} custom-call(s32[214]{0:T(256)S(4)} %get-tuple-element.55.list_ref, bf16[96,128,128]{2,1,0:T(8,128)(2,1)S(1)} %copy-done, bf16[1024,128]{1,0:T(8,128)(2,1)S(1)} %collective-permute-done.9.far_ref), custom_call_target="tpu_custom_call" | custom-call | flops 4000000000 | bytes 1000 | tf_op jit(solution)/shard_map/far_second_0/pallas_call | solution.py:21
  38.1 2.1 %near_second.1 = (bf16[1024,128]{1,0:T(8,128)(2,1)S(1)}, f32[1024,128]{1,0:T(8,128)S(1)}, f32[1024,128]{1,0:T(8,128)S(1)}) custom-call(s32[214]{0:T(256)S(4)} %get-tuple-element.55.list_ref, bf16[96,128,128]{2,1,0:T(8,128)(2,1)S(1)} %copy-done, bf16[1024,128]{1,0:T(8,128)(2,1)S(1)} %get-tuple-element.73.refs_0_.refs_9_, ...), custom_call_target="tpu_custom_call" | custom-call | flops 1000 | bytes 1000 | tf_op jit(solution)/shard_map/near_second/pallas_call | solution.py:21
  40.2 1.3 %far_second_1.1 = (bf16[1024,128]{1,0:T(8,128)(2,1)S(1)}, bf16[1024,128]{1,0:T(8,128)(2,1)S(1)}, f32[8,128]{1,0:T(8,128)S(1)}, bf16[1024,128]{1,0:T(8,128)(2,1)S...) custom-call(s32[214]{0:T(256)S(4)} %get-tuple-element.55.list_ref, ...), custom_call_target="tpu_custom_call", output_to_operand_aliasing={{3}: (8, {}), {4}: (9, {}), {5}: (10, {}), {6}: (11, {}), {... | custom-call | flops 1000 | bytes 1000 | tf_op jit(solution)/shard_map/far_second_1/pallas_call | solution.py:21
  41.6 1.5 %collective-permute-start.12 = (f32[8,128]{1,0:T(8,128)S(1)}, f32[8,128]{1,0:T(8,128)S(1)}, u32[]{:S(2)}, u32[]{:S(2)}) collective-permute-start(f32[8,128]{1,0:T(8,128)S(1)} %get-tuple-element.103.refs_0_), channel_id=1, source_target_pairs={{0,12},{1,13},{2,14},{3,15},{4,8},{5,9},{6,10},{7,11},{8,4},{9,5},... | collective-permute-start | bytes 12296 | tf_op jit(solution)/shard_map/ppermute | solution.py:446
  43.1 1.7 %collective-permute-start.11 = (f32[8,128]{1,0:T(8,128)S(1)}, f32[8,128]{1,0:T(8,128)S(1)}, u32[]{:S(2)}, u32[]{:S(2)}) collective-permute-start(f32[8,128]{1,0:T(8,128)S(1)} %get-tuple-element.103.refs_0_), channel_id=1, source_target_pairs={{0,8},{1,9},{2,10},{3,11},{4,12},{5,13},{6,14},{7,15},{8,0},{9,1},... | collective-permute-start | bytes 12296 | tf_op jit(solution)/shard_map/ppermute | solution.py:446
  44.8 1.1 %collective-permute-start.10 = (f32[8,128]{1,0:T(8,128)S(1)}, f32[8,128]{1,0:T(8,128)S(1)}, u32[]{:S(2)}, u32[]{:S(2)}) collective-permute-start(f32[8,128]{1,0:T(8,128)S(1)} %get-tuple-element.103.refs_0_), channel_id=1, source_target_pairs={{0,4},{1,5},{2,6},{3,7},{4,0},{5,1},{6,2},{7,3},{8,12},{9,13},{10,... | collective-permute-start | bytes 12296 | tf_op jit(solution)/shard_map/ppermute | solution.py:446
  45.9 2.2 %finish.1 = (f32[1024,384]{1,0:T(8,128)}, f32[1024,384]{1,0:T(8,128)}, f32[8,128]{1,0:T(8,128)S(1)}) custom-call(bf16[1024,128]{1,0:T(8,128)(2,1)S(1)} %get-tuple-element.91.refs_0_, bf16[1024,128]{1,0:T(8,128)(2,1)S(1)} %get-tuple-element.92.refs_1_, bf16[1024,128]{1,0:T(8,128)(2,1)S(1)} %get-tuple-element.93.refs_2_, ...), custom_call_target="tpu_custom_call" | custom-call | flops 1000 | bytes 1000 | tf_op jit(solution)/shard_map/finish/pallas_call | solution.py:21
  48.1 0.3 collective-permute-done.10.refs_1_
  48.4 3.0 %collective-permute-start.14 = (f32[8,128]{1,0:T(8,128)S(1)}, f32[8,128]{1,0:T(8,128)S(1)}, u32[]{:S(2)}, u32[]{:S(2)}) collective-permute-start(f32[8,128]{1,0:T(8,128)S(1)} %add_up.1), channel_id=1, source_target_pairs={{0,2},{1,3},{2,0},{3,1},{4,6},{5,7},{6,4},{7,5},{8,10},{9,11},{10,... | collective-permute-start | bytes 12296 | tf_op jit(solution)/shard_map/ppermute | solution.py:446
  51.4 0.0 collective-permute-start.13
  51.4 0.0 collective-permute-done.15
  51.5 1.6 %collective-permute-done.14 = f32[8,128]{1,0:T(8,128)S(1)} collective-permute-done((f32[8,128]{1,0:T(8,128)S(1)}, f32[8,128]{1,0:T(8,128)S(1)}, u32[]{:S(2)}, u32[]{:S(2)}) %collective-permute-start.14) | collective-permute-done | bytes 4128 | tf_op jit(solution)/shard_map/ppermute | solution.py:446
  53.1 0.5 multiply_bitcast_fusion
  (28 shorter events, 0.1 us)
Async XLA Ops:
  0.6 10.4 %copy-start.2 = (bf16[384,384]{1,0:T(8,128)(2,1)S(1)}, bf16[384,384]{1,0:T(8,128)(2,1)}, u32[]{:S(2)}) copy-start(bf16[384,384]{1,0:T(8,128)(2,1)} %constant.7.clone.refs_4_.refs_12_) | copy-start | bytes 884740
  0.6 10.4 %copy-start.3 = (bf16[384,48]{1,0:T(8,128)(2,1)S(1)}, bf16[384,48]{1,0:T(8,128)(2,1)}, u32[]{:S(2)}) copy-start(bf16[384,48]{1,0:T(8,128)(2,1)} %constant.8.clone.refs_5_) | copy-start | bytes 110596
  0.7 8.1 %copy-start.6 = (s32[96]{0:T(128)S(1)}, s32[96]{0:T(128)}, u32[]{:S(2)}) copy-start(s32[96]{0:T(128)} %cols_hbm.1) | copy-start | bytes 1156
  0.7 8.1 %copy-start.5 = (s32[96]{0:T(128)S(1)}, s32[96]{0:T(128)}, u32[]{:S(2)}) copy-start(s32[96]{0:T(128)} %rows_hbm.1) | copy-start | bytes 1156
  0.7 10.3 %copy-start.4 = (bf16[48,48]{1,0:T(8,128)(2,1)S(1)}, bf16[48,48]{1,0:T(8,128)(2,1)}, u32[]{:S(2)}) copy-start(bf16[48,48]{1,0:T(8,128)(2,1)} %refs_6_.1) | copy-start | bytes 13828
  0.7 10.3 %copy-start.1 = (f32[1024,384]{1,0:T(8,128)S(1)}, f32[1024,384]{1,0:T(8,128)}, u32[]{:S(2)}) copy-start(f32[1024,384]{1,0:T(8,128)} %refs_3_.1) | copy-start | bytes 4718596
  2.1 13.1 %collective-permute-start.4 = (bf16[1024,256]{1,0:T(8,128)(2,1)S(1)}, bf16[1024,256]{1,0:T(8,128)(2,1)S(1)}, u32[]{:S(2)}, u32[]{:S(2)}) collective-permute-start(bf16[1024,256]{1,0:T(8,128)(2,1)S(1)} %get-tuple-element.54._), channel_id=1, source_target_pairs={{0,15},{1,2},{2,1},{3,4},{4,3},{5,6},{6,5},{7,8},{8,7},{9,10},{10,... | collective-permute-start | bytes 1572872 | tf_op jit(solution)/shard_map/ppermute | solution.py:477
  7.6 4.8 %collective-permute-start = (bf16[1024,128]{1,0:T(8,128)(2,1)S(1)}, bf16[1024,128]{1,0:T(8,128)(2,1)S(1)}, u32[]{:S(2)}, u32[]{:S(2)}) collective-permute-start(bf16[1024,128]{1,0:T(8,128)(2,1)S(1)} %get-tuple-element.56.refs_0_), channel_id=1, source_target_pairs={{0,1},{1,0},{2,3},{3,2},{4,5},{5,4},{6,7},{7,6},{8,9},{9,8},{10,11... | collective-permute-start | bytes 786440 | tf_op jit(solution)/shard_map/ppermute | solution.py:480
  7.6 4.8 %collective-permute-start.1 = (bf16[1024,128]{1,0:T(8,128)(2,1)S(1)}, bf16[1024,128]{1,0:T(8,128)(2,1)S(1)}, u32[]{:S(2)}, u32[]{:S(2)}) collective-permute-start(bf16[1024,128]{1,0:T(8,128)(2,1)S(1)} %get-tuple-element.57.refs_1_), channel_id=1, source_target_pairs={{0,1},{1,0},{2,3},{3,2},{4,5},{5,4},{6,7},{7,6},{8,9},{9,8},{10,11... | collective-permute-start | bytes 786440 | tf_op jit(solution)/shard_map/ppermute | solution.py:480
  10.9 1.6 %collective-permute-start.2 = (bf16[1024,128]{1,0:T(8,128)(2,1)S(1)}, bf16[1024,128]{1,0:T(8,128)(2,1)S(1)}, u32[]{:S(2)}, u32[]{:S(2)}) collective-permute-start(bf16[1024,128]{1,0:T(8,128)(2,1)S(1)} %get-tuple-element.58.refs_2_.refs_6_), channel_id=1, source_target_pairs={{0,1},{1,0},{2,3},{3,2},{4,5},{5,4},{6,7},{7,6},{8,9},{9,8},{10,11... | collective-permute-start | bytes 786440 | tf_op jit(solution)/shard_map/ppermute | solution.py:480
  11.0 1.9 %copy-start = (bf16[96,128,128]{2,1,0:T(8,128)(2,1)S(1)}, bf16[96,128,128]{2,1,0:T(8,128)(2,1)}, u32[]{:S(2)}) copy-start(bf16[96,128,128]{2,1,0:T(8,128)(2,1)} %tiles_ref.11) | copy-start | bytes 9437188
  15.1 8.7 %collective-permute-start.3 = (bf16[1024,128]{1,0:T(8,128)(2,1)S(1)}, bf16[1024,128]{1,0:T(8,128)(2,1)S(1)}, u32[]{:S(2)}, u32[]{:S(2)}) collective-permute-start(bf16[1024,128]{1,0:T(8,128)(2,1)S(1)} %get-tuple-element.63), channel_id=1, source_target_pairs={{0,15},{1,2},{2,1},{3,4},{4,3},{5,6},{6,5},{7,8},{8,7},{9,10},{10,... | collective-permute-start | bytes 786440 | tf_op jit(solution)/shard_map/ppermute | solution.py:477
  16.5 20.8 %collective-permute-start.9 = (bf16[1024,128]{1,0:T(8,128)(2,1)S(1)}, bf16[1024,128]{1,0:T(8,128)(2,1)S(1)}, u32[]{:S(2)}, u32[]{:S(2)}) collective-permute-start(bf16[1024,128]{1,0:T(8,128)(2,1)S(1)} %get-tuple-element.76), channel_id=1, source_target_pairs={{0,15},{1,2},{2,1},{3,4},{4,3},{5,6},{6,5},{7,8},{8,7},{9,10},{10,... | collective-permute-start | bytes 786440 | tf_op jit(solution)/shard_map/ppermute | solution.py:477
  25.1 15.2 %collective-permute-start.5 = (bf16[1024,256]{1,0:T(8,128)(2,1)S(1)}, bf16[1024,256]{1,0:T(8,128)(2,1)S(1)}, u32[]{:S(2)}, u32[]{:S(2)}) collective-permute-start(bf16[1024,256]{1,0:T(8,128)(2,1)S(1)} %get-tuple-element.72), channel_id=1, source_target_pairs={{0,15},{1,2},{2,1},{3,4},{4,3},{5,6},{6,5},{7,8},{8,7},{9,10},{10,... | collective-permute-start | bytes 1572872 | tf_op jit(solution)/shard_map/ppermute | solution.py:477
  25.2 12.9 %collective-permute-start.6 = (bf16[1024,128]{1,0:T(8,128)(2,1)S(1)}, bf16[1024,128]{1,0:T(8,128)(2,1)S(1)}, u32[]{:S(2)}, u32[]{:S(2)}) collective-permute-start(bf16[1024,128]{1,0:T(8,128)(2,1)S(1)} %get-tuple-element.73.refs_0_.refs_9_), channel_id=1, source_target_pairs={{0,1},{1,0},{2,3},{3,2},{4,5},{5,4},{6,7},{7,6},{8,9},{9,8},{10,11... | collective-permute-start | bytes 786440 | tf_op jit(solution)/shard_map/ppermute | solution.py:480
  34.7 3.4 %collective-permute-start.7 = (bf16[1024,128]{1,0:T(8,128)(2,1)S(1)}, bf16[1024,128]{1,0:T(8,128)(2,1)S(1)}, u32[]{:S(2)}, u32[]{:S(2)}) collective-permute-start(bf16[1024,128]{1,0:T(8,128)(2,1)S(1)} %get-tuple-element.74.refs_1_.refs_10_), channel_id=1, source_target_pairs={{0,1},{1,0},{2,3},{3,2},{4,5},{5,4},{6,7},{7,6},{8,9},{9,8},{10,11... | collective-permute-start | bytes 786440 | tf_op jit(solution)/shard_map/ppermute | solution.py:480
  34.7 3.4 %collective-permute-start.8 = (bf16[1024,128]{1,0:T(8,128)(2,1)S(1)}, bf16[1024,128]{1,0:T(8,128)(2,1)S(1)}, u32[]{:S(2)}, u32[]{:S(2)}) collective-permute-start(bf16[1024,128]{1,0:T(8,128)(2,1)S(1)} %get-tuple-element.75.refs_2_.refs_11_), channel_id=1, source_target_pairs={{0,1},{1,0},{2,3},{3,2},{4,5},{5,4},{6,7},{7,6},{8,9},{9,8},{10,11... | collective-permute-start | bytes 786440 | tf_op jit(solution)/shard_map/ppermute | solution.py:480
  41.6 6.6 %collective-permute-start.12 = (f32[8,128]{1,0:T(8,128)S(1)}, f32[8,128]{1,0:T(8,128)S(1)}, u32[]{:S(2)}, u32[]{:S(2)}) collective-permute-start(f32[8,128]{1,0:T(8,128)S(1)} %get-tuple-element.103.refs_0_), channel_id=1, source_target_pairs={{0,12},{1,13},{2,14},{3,15},{4,8},{5,9},{6,10},{7,11},{8,4},{9,5},... | collective-permute-start | bytes 12296 | tf_op jit(solution)/shard_map/ppermute | solution.py:446
  43.1 5.0 %collective-permute-start.11 = (f32[8,128]{1,0:T(8,128)S(1)}, f32[8,128]{1,0:T(8,128)S(1)}, u32[]{:S(2)}, u32[]{:S(2)}) collective-permute-start(f32[8,128]{1,0:T(8,128)S(1)} %get-tuple-element.103.refs_0_), channel_id=1, source_target_pairs={{0,8},{1,9},{2,10},{3,11},{4,12},{5,13},{6,14},{7,15},{8,0},{9,1},... | collective-permute-start | bytes 12296 | tf_op jit(solution)/shard_map/ppermute | solution.py:446
  44.8 3.6 %collective-permute-start.10 = (f32[8,128]{1,0:T(8,128)S(1)}, f32[8,128]{1,0:T(8,128)S(1)}, u32[]{:S(2)}, u32[]{:S(2)}) collective-permute-start(f32[8,128]{1,0:T(8,128)S(1)} %get-tuple-element.103.refs_0_), channel_id=1, source_target_pairs={{0,4},{1,5},{2,6},{3,7},{4,0},{5,1},{6,2},{7,3},{8,12},{9,13},{10,... | collective-permute-start | bytes 12296 | tf_op jit(solution)/shard_map/ppermute | solution.py:446
  48.4 3.0 %collective-permute-start.15 = (f32[8,128]{1,0:T(8,128)S(1)}, f32[8,128]{1,0:T(8,128)S(1)}, u32[]{:S(2)}, u32[]{:S(2)}) collective-permute-start(f32[8,128]{1,0:T(8,128)S(1)} %add_up.1), channel_id=1, source_target_pairs={{0,3},{1,2},{2,1},{3,0},{4,7},{5,6},{6,5},{7,4},{8,11},{9,10},{10,... | collective-permute-start | bytes 12296 | tf_op jit(solution)/shard_map/ppermute | solution.py:446
  48.4 4.6 %collective-permute-start.14 = (f32[8,128]{1,0:T(8,128)S(1)}, f32[8,128]{1,0:T(8,128)S(1)}, u32[]{:S(2)}, u32[]{:S(2)}) collective-permute-start(f32[8,128]{1,0:T(8,128)S(1)} %add_up.1), channel_id=1, source_target_pairs={{0,2},{1,3},{2,0},{3,1},{4,6},{5,7},{6,4},{7,5},{8,10},{9,11},{10,... | collective-permute-start | bytes 12296 | tf_op jit(solution)/shard_map/ppermute | solution.py:446
  51.4 1.6 %collective-permute-start.13 = (f32[8,128]{1,0:T(8,128)S(1)}, f32[8,128]{1,0:T(8,128)S(1)}, u32[]{:S(2)}, u32[]{:S(2)}) collective-permute-start(f32[8,128]{1,0:T(8,128)S(1)} %add_up.1), channel_id=1, source_target_pairs={{0,1},{1,0},{2,3},{3,2},{4,5},{5,4},{6,7},{7,6},{8,9},{9,8},{10,11... | collective-permute-start | bytes 12296 | tf_op jit(solution)/shard_map/ppermute | solution.py:446

commit v12 on v11

--- a/solution.py
+++ b/solution.py
@@ -9,7 +9,7 @@
 
 STEPS = 2
 LANES = 128
-LONG, SHORT = 16, 4
+LONG, SHORT = 24, 4
 VMEM_LIMIT = 14 * 1024 * 1024
 NEAR_FLOPS = 4 * 10**9
 F32 = jnp.float32
@@ -119,7 +119,7 @@
 
 
 def section(slots, per):
-    return -(-(slots + per) // (2 * SHORT)) * SHORT
+    return -(-(slots + per) // (2 * LONG)) * LONG
 
 
 def make_lists(rows, cols, count, positions, groups_of, after, slots, tile, ring_index):
@@ -174,16 +174,19 @@
                 list_ref[2 * (start + total)] = other
                 list_ref[2 * (start + total) + 1] = zero * 256 + k
                 total = total + (other >= 0).astype(jnp.int32)
-            short_turns = (total + SHORT - 1) // SHORT
+            rest = total % LONG
+            padded = rest > 2 * SHORT
+            long_turns = total // LONG + padded.astype(jnp.int32)
+            short_turns = jnp.where(padded, 0, (rest + SHORT - 1) // SHORT)
 
             def pad(pair, carry, start=start, zero=zero):
                 for e in range(2):
                     list_ref[2 * (start + pair) + e] = zero * 256 + per
                 return carry
 
-            lax.fori_loop(total, short_turns * SHORT, pad, 0)
-            list_ref[4 * pairs + 2 * part] = short_turns // (LONG // SHORT)
-            list_ref[4 * pairs + 2 * part + 1] = short_turns % (LONG // SHORT)
+            lax.fori_loop(total, long_turns * LONG + short_turns * SHORT, pad, 0)
+            list_ref[4 * pairs + 2 * part] = long_turns
+            list_ref[4 * pairs + 2 * part + 1] = short_turns
         for i, copy in enumerate(copies[3:]):
             copy.wait()
             r_outs[i][...] = x_outs[i][...].astype(BF16)

time: 54.4 us -> 54.2 us (level)
  Pallas kernels: 18 us -> 17.4 us
    pallas_call x12, Pallas kernels: 18 us -> 17.4 us  [call(): pl.pallas_call(body, in_specs=[pl.BlockSpec(memory_space=pl.ANY if s is p...]
  transfers between devices with their start and end apart: 16 -> 16, of which waited for: 4 -> 4; matrix products, arithmetic and copies ran while one was open for 0% -> 0% of each run, Pallas kernels for 29% -> 27%
where the time goes in v12:
time: 54.2 us; the launch traced here: 53.5 us
  starting transfers between devices  28.4 us (52%)
  Pallas kernels  17.4 us (32%)
  waiting for transfers between devices  5.16 us (10%)
  between operations  1.57 us (3%)
    pallas_call x12, Pallas kernels, call(): pl.pallas_call(body, in_specs=[pl.BlockSpec(memory_space=pl.ANY if s is p...  17.4 us
    ppermute x6, starting transfers between devices, near_swap(): return lax.ppermute(mine, RING, on_chip)  11.1 us
    ppermute x4, starting transfers between devices, far_swap(): return lax.ppermute(mine, RING, off_chip)  9.82 us
    ppermute x6, starting transfers between devices, sum_over_ring(): lax.ppermute(value, RING, [(j, j ^ bit) for j in range(ring)])  7.51 us
    ppermute x4, waiting for transfers between devices, far_swap(): return lax.ppermute(mine, RING, off_chip)  3.13 us
    ppermute x6, waiting for transfers between devices, sum_over_ring(): lax.ppermute(value, RING, [(j, j ^ bit) for j in range(ring)])  1.92 us
  transfers between devices with their start and end apart: 16, of which 4 were waited for; matrix products, arithmetic and copies ran while one was open for 0% of the time, Pallas kernels for 27%

profile of v12, /device:TPU:0, one launch (start us, length us, event | category | flops | bytes accessed | tf_op | source)
XLA Modules:
  0.0 53.5 jit_solution(3271999077683357922)
XLA Ops:
  0.6 0.0 copy-start.2
  0.6 0.0 copy-start.3
  0.7 1.4 %load_first.1 = (f32[1024,128]{1,0:T(8,128)S(1)}, f32[1024,128]{1,0:T(8,128)S(1)}, bf16[1024,128]{1,0:T(8,128)(2,1)S(1)}, bf16[1024,128]{1,0:T(8,128)(2,1)S(1)}, bf16[1024,256]{1,0:T(8,128)(2,1)S(1)}) custom-call(f32[1024,384]{1,0:T(8,128)} %x_ref.3), custom_call_target="tpu_custom_call" | custom-call | flops 1000 | bytes 1000 | tf_op jit(solution)/shard_map/load_first/pallas_call | solution.py:21
  2.1 5.5 %collective-permute-start.4 = (bf16[1024,256]{1,0:T(8,128)(2,1)S(1)}, bf16[1024,256]{1,0:T(8,128)(2,1)S(1)}, u32[]{:S(2)}, u32[]{:S(2)}) collective-permute-start(bf16[1024,256]{1,0:T(8,128)(2,1)S(1)} %get-tuple-element.54._), channel_id=1, source_target_pairs={{0,15},{1,2},{2,1},{3,4},{4,3},{5,6},{6,5},{7,8},{8,7},{9,10},{10,... | collective-permute-start | bytes 1572872 | tf_op jit(solution)/shard_map/ppermute | solution.py:480
  7.6 0.5 collective-permute-start.1
  8.8 2.1 %make_lists.1 = (s32[294]{0:T(512)S(4)}, f32[1024,128]{1,0:T(8,128)S(1)}, bf16[1024,128]{1,0:T(8,128)(2,1)S(1)}) custom-call(s32[96]{0:T(128)S(1)} %copy-done.5, s32[96]{0:T(128)S(1)} %copy-done.6, s32[1]{0:T(128)S(6)} %copy.28.count_hbm, f32[1024,384]{1,0:T(8,128)} %x_ref.3, bf16[1024,256]{1,0:T(8,128)(2,1)S(1)} %get-tuple-element.54._), custom_call_target="tpu_custom_call" | custom-call | flops 1000 | bytes 1000 | tf_op jit(solution)/shard_map/make_lists/pallas_call | solution.py:21
  10.9 0.1 collective-permute-start.2
  11.1 1.4 %first_base.1 = (f32[1024,128]{1,0:T(8,128)S(1)}, f32[1024,128]{1,0:T(8,128)S(1)}, f32[1024,128]{1,0:T(8,128)S(1)}, bf16[384,384]{1,0:T(8,128)(2,1)S(1)}) custom-call(f32[1024,128]{1,0:T(8,128)S(1)} %get-tuple-element.59.refs_0_.refs_4_, f32[1024,128]{1,0:T(8,128)S(1)} %get-tuple-element.60.refs_1_.refs_5_.refs_7_, ...), custom_call_target="tpu_custom_call" | custom-call | flops 1000 | bytes 1000 | tf_op jit(solution)/shard_map/first_base/pallas_call | solution.py:21
  12.4 0.1 collective-permute-done.2.refs_5_
  12.5 0.4 copy-done
  12.9 1.9 %near_first.1 = (f32[1024,128]{1,0:T(8,128)S(1)}, f32[1024,128]{1,0:T(8,128)S(1)}, f32[1024,128]{1,0:T(8,128)S(1)}, bf16[1024,128]{1,0:T(8,128)(2,1)S(1)}) custom-call(s32[294]{0:T(512)S(4)} %get-tuple-element.55.list_ref, bf16[96,128,128]{2,1,0:T(8,128)(2,1)S(1)} %copy-done, bf16[1024,128]{1,0:T(8,128)(2,1)S(1)} %get-tuple-element.56.refs_0_, ...), custom_call_target="tpu_custom_call" | custom-call | flops 1000 | bytes 1000 | tf_op jit(solution)/shard_map/near_first/pallas_call | solution.py:21
  14.8 0.1 collective-permute-start.3
  14.9 1.3 %far_first_0.1 = (bf16[1024,128]{1,0:T(8,128)(2,1)S(1)}, bf16[1024,128]{1,0:T(8,128)(2,1)S(1)}, bf16[1024,128]{1,0:T(8,128)(2,1)S(1)}, bf16[1024,128]{1,0:T(8,12...) custom-call(s32[294]{0:T(512)S(4)} %get-tuple-element.55.list_ref, bf16[96,128,128]{2,1,0:T(8,128)(2,1)S(1)} %copy-done, ...), custom_call_target="tpu_custom_call" | custom-call | flops 1000 | bytes 1000 | tf_op jit(solution)/shard_map/far_first_0/pallas_call | solution.py:21
  16.2 4.2 %collective-permute-start.9 = (bf16[1024,128]{1,0:T(8,128)(2,1)S(1)}, bf16[1024,128]{1,0:T(8,128)(2,1)S(1)}, u32[]{:S(2)}, u32[]{:S(2)}) collective-permute-start(bf16[1024,128]{1,0:T(8,128)(2,1)S(1)} %get-tuple-element.76), channel_id=1, source_target_pairs={{0,15},{1,2},{2,1},{3,4},{4,3},{5,6},{6,5},{7,8},{8,7},{9,10},{10,... | collective-permute-start | bytes 786440 | tf_op jit(solution)/shard_map/ppermute | solution.py:480
  20.4 3.1 %collective-permute-done.3.far_ref = bf16[1024,128]{1,0:T(8,128)(2,1)S(1)} collective-permute-done((bf16[1024,128]{1,0:T(8,128)(2,1)S(1)}, bf16[1024,128]{1,0:T(8,128)(2,1)S(1)}, u32[]{:S(2)}, u32[]{:S(2)}) %collective-permute-start.3) | collective-permute-done | bytes 262176 | tf_op jit(solution)/shard_map/ppermute | solution.py:480
  23.5 1.2 %far_first_1.1 = (bf16[1024,256]{1,0:T(8,128)(2,1)S(1)}, bf16[1024,128]{1,0:T(8,128)(2,1)S(1)}, bf16[1024,128]{1,0:T(8,128)(2,1)S(1)}, bf16[1024,128]{1,0:T(8,128)(2,1)S(1)}) custom-call(s32[294]{0:T(512)S(4)} %get-tuple-element.55.list_ref, bf16[96,128,128]{2,1,0:T(8,128)(2,1)S(1)} %copy-done, bf16[1024,128]{1,0:T(8,128)(2,1)S(1)} %collective-permute-done.3.far_ref, ...), custom_call_target="tpu_custom_call" | custom-call | flops 1000 | bytes 1000 | tf_op jit(solution)/shard_map/far_first_1/pallas_call | solution.py:21
  24.7 0.1 collective-permute-start.5
  24.8 10.0 %collective-permute-start.6 = (bf16[1024,128]{1,0:T(8,128)(2,1)S(1)}, bf16[1024,128]{1,0:T(8,128)(2,1)S(1)}, u32[]{:S(2)}, u32[]{:S(2)}) collective-permute-start(bf16[1024,128]{1,0:T(8,128)(2,1)S(1)} %get-tuple-element.73.refs_0_.refs_9_), channel_id=1, source_target_pairs={{0,1},{1,0},{2,3},{3,2},{4,5},{5,4},{6,7},{7,6},{8,9},{9,8},{10,11... | collective-permute-start | bytes 786440 | tf_op jit(solution)/shard_map/ppermute | solution.py:483
  34.8 0.5 collective-permute-start.8
  35.3 2.0 %second_base.1 = (f32[1024,128]{1,0:T(8,128)S(1)}, f32[1024,128]{1,0:T(8,128)S(1)}, f32[1024,128]{1,0:T(8,128)S(1)}, f32[1024,128]{1,0:T(8,128)S(1)}, f32[1024,1...) custom-call(f32[1024,128]{1,0:T(8,128)S(1)} %get-tuple-element.79.refs_0_.refs_6_, ...), custom_call_target="tpu_custom_call" | custom-call | flops 1000 | bytes 1000 | tf_op jit(solution)/shard_map/second_base/pallas_call | solution.py:21
  37.4 0.7 %far_second_0.1.refs_6_ = f32[1024,128]{1,0:T(8,128)S(1)} custom-call(s32[294]{0:T(512)S(4)} %get-tuple-element.55.list_ref, bf16[96,128,128]{2,1,0:T(8,128)(2,1)S(1)} %copy-done, bf16[1024,128]{1,0:T(8,128)(2,1)S(1)} %collective-permute-done.9.far_ref), custom_call_target="tpu_custom_call" | custom-call | flops 4000000000 | bytes 1000 | tf_op jit(solution)/shard_map/far_second_0/pallas_call | solution.py:21
  38.2 1.8 %near_second.1 = (bf16[1024,128]{1,0:T(8,128)(2,1)S(1)}, f32[1024,128]{1,0:T(8,128)S(1)}, f32[1024,128]{1,0:T(8,128)S(1)}) custom-call(s32[294]{0:T(512)S(4)} %get-tuple-element.55.list_ref, bf16[96,128,128]{2,1,0:T(8,128)(2,1)S(1)} %copy-done, bf16[1024,128]{1,0:T(8,128)(2,1)S(1)} %get-tuple-element.73.refs_0_.refs_9_, ...), custom_call_target="tpu_custom_call" | custom-call | flops 1000 | bytes 1000 | tf_op jit(solution)/shard_map/near_second/pallas_call | solution.py:21
  40.0 1.3 %far_second_1.1 = (bf16[1024,128]{1,0:T(8,128)(2,1)S(1)}, bf16[1024,128]{1,0:T(8,128)(2,1)S(1)}, f32[8,128]{1,0:T(8,128)S(1)}, bf16[1024,128]{1,0:T(8,128)(2,1)S...) custom-call(s32[294]{0:T(512)S(4)} %get-tuple-element.55.list_ref, ...), custom_call_target="tpu_custom_call", output_to_operand_aliasing={{3}: (8, {}), {4}: (9, {}), {5}: (10, {}), {6}: (11, {}), {... | custom-call | flops 1000 | bytes 1000 | tf_op jit(solution)/shard_map/far_second_1/pallas_call | solution.py:21
  41.4 1.6 %collective-permute-start.12 = (f32[8,128]{1,0:T(8,128)S(1)}, f32[8,128]{1,0:T(8,128)S(1)}, u32[]{:S(2)}, u32[]{:S(2)}) collective-permute-start(f32[8,128]{1,0:T(8,128)S(1)} %get-tuple-element.103.refs_0_), channel_id=1, source_target_pairs={{0,12},{1,13},{2,14},{3,15},{4,8},{5,9},{6,10},{7,11},{8,4},{9,5},... | collective-permute-start | bytes 12296 | tf_op jit(solution)/shard_map/ppermute | solution.py:449
  42.9 1.8 %collective-permute-start.11 = (f32[8,128]{1,0:T(8,128)S(1)}, f32[8,128]{1,0:T(8,128)S(1)}, u32[]{:S(2)}, u32[]{:S(2)}) collective-permute-start(f32[8,128]{1,0:T(8,128)S(1)} %get-tuple-element.103.refs_0_), channel_id=1, source_target_pairs={{0,8},{1,9},{2,10},{3,11},{4,12},{5,13},{6,14},{7,15},{8,0},{9,1},... | collective-permute-start | bytes 12296 | tf_op jit(solution)/shard_map/ppermute | solution.py:449
  44.7 1.0 %collective-permute-start.10 = (f32[8,128]{1,0:T(8,128)S(1)}, f32[8,128]{1,0:T(8,128)S(1)}, u32[]{:S(2)}, u32[]{:S(2)}) collective-permute-start(f32[8,128]{1,0:T(8,128)S(1)} %get-tuple-element.103.refs_0_), channel_id=1, source_target_pairs={{0,4},{1,5},{2,6},{3,7},{4,0},{5,1},{6,2},{7,3},{8,12},{9,13},{10,... | collective-permute-start | bytes 12296 | tf_op jit(solution)/shard_map/ppermute | solution.py:449
  45.8 2.2 %finish.1 = (f32[1024,384]{1,0:T(8,128)}, f32[1024,384]{1,0:T(8,128)}, f32[8,128]{1,0:T(8,128)S(1)}) custom-call(bf16[1024,128]{1,0:T(8,128)(2,1)S(1)} %get-tuple-element.91.refs_0_, bf16[1024,128]{1,0:T(8,128)(2,1)S(1)} %get-tuple-element.92.refs_1_, bf16[1024,128]{1,0:T(8,128)(2,1)S(1)} %get-tuple-element.93.refs_2_, ...), custom_call_target="tpu_custom_call" | custom-call | flops 1000 | bytes 1000 | tf_op jit(solution)/shard_map/finish/pallas_call | solution.py:21
  47.9 0.4 collective-permute-done.10.refs_1_
  48.3 3.1 %collective-permute-start.14 = (f32[8,128]{1,0:T(8,128)S(1)}, f32[8,128]{1,0:T(8,128)S(1)}, u32[]{:S(2)}, u32[]{:S(2)}) collective-permute-start(f32[8,128]{1,0:T(8,128)S(1)} %add_up.1), channel_id=1, source_target_pairs={{0,2},{1,3},{2,0},{3,1},{4,6},{5,7},{6,4},{7,5},{8,10},{9,11},{10,... | collective-permute-start | bytes 12296 | tf_op jit(solution)/shard_map/ppermute | solution.py:449
  51.4 0.0 collective-permute-start.13
  51.5 1.5 %collective-permute-done.14 = f32[8,128]{1,0:T(8,128)S(1)} collective-permute-done((f32[8,128]{1,0:T(8,128)S(1)}, f32[8,128]{1,0:T(8,128)S(1)}, u32[]{:S(2)}, u32[]{:S(2)}) %collective-permute-start.14) | collective-permute-done | bytes 4128 | tf_op jit(solution)/shard_map/ppermute | solution.py:449
  53.0 0.5 multiply_bitcast_fusion
  (28 shorter events, 0.1 us)
Async XLA Ops:
  0.6 10.4 %copy-start.2 = (bf16[384,384]{1,0:T(8,128)(2,1)S(1)}, bf16[384,384]{1,0:T(8,128)(2,1)}, u32[]{:S(2)}) copy-start(bf16[384,384]{1,0:T(8,128)(2,1)} %constant.7.clone.refs_4_.refs_12_) | copy-start | bytes 884740
  0.6 10.4 %copy-start.3 = (bf16[384,48]{1,0:T(8,128)(2,1)S(1)}, bf16[384,48]{1,0:T(8,128)(2,1)}, u32[]{:S(2)}) copy-start(bf16[384,48]{1,0:T(8,128)(2,1)} %constant.8.clone.refs_5_) | copy-start | bytes 110596
  0.7 8.1 %copy-start.6 = (s32[96]{0:T(128)S(1)}, s32[96]{0:T(128)}, u32[]{:S(2)}) copy-start(s32[96]{0:T(128)} %cols_hbm.1) | copy-start | bytes 1156
  0.7 8.1 %copy-start.5 = (s32[96]{0:T(128)S(1)}, s32[96]{0:T(128)}, u32[]{:S(2)}) copy-start(s32[96]{0:T(128)} %rows_hbm.1) | copy-start | bytes 1156
  0.7 10.4 %copy-start.4 = (bf16[48,48]{1,0:T(8,128)(2,1)S(1)}, bf16[48,48]{1,0:T(8,128)(2,1)}, u32[]{:S(2)}) copy-start(bf16[48,48]{1,0:T(8,128)(2,1)} %refs_6_.1) | copy-start | bytes 13828
  0.7 10.4 %copy-start.1 = (f32[1024,384]{1,0:T(8,128)S(1)}, f32[1024,384]{1,0:T(8,128)}, u32[]{:S(2)}) copy-start(f32[1024,384]{1,0:T(8,128)} %refs_3_.1) | copy-start | bytes 4718596
  2.1 12.8 %collective-permute-start.4 = (bf16[1024,256]{1,0:T(8,128)(2,1)S(1)}, bf16[1024,256]{1,0:T(8,128)(2,1)S(1)}, u32[]{:S(2)}, u32[]{:S(2)}) collective-permute-start(bf16[1024,256]{1,0:T(8,128)(2,1)S(1)} %get-tuple-element.54._), channel_id=1, source_target_pairs={{0,15},{1,2},{2,1},{3,4},{4,3},{5,6},{6,5},{7,8},{8,7},{9,10},{10,... | collective-permute-start | bytes 1572872 | tf_op jit(solution)/shard_map/ppermute | solution.py:480
  7.6 4.8 %collective-permute-start = (bf16[1024,128]{1,0:T(8,128)(2,1)S(1)}, bf16[1024,128]{1,0:T(8,128)(2,1)S(1)}, u32[]{:S(2)}, u32[]{:S(2)}) collective-permute-start(bf16[1024,128]{1,0:T(8,128)(2,1)S(1)} %get-tuple-element.56.refs_0_), channel_id=1, source_target_pairs={{0,1},{1,0},{2,3},{3,2},{4,5},{5,4},{6,7},{7,6},{8,9},{9,8},{10,11... | collective-permute-start | bytes 786440 | tf_op jit(solution)/shard_map/ppermute | solution.py:483
  7.6 4.8 %collective-permute-start.1 = (bf16[1024,128]{1,0:T(8,128)(2,1)S(1)}, bf16[1024,128]{1,0:T(8,128)(2,1)S(1)}, u32[]{:S(2)}, u32[]{:S(2)}) collective-permute-start(bf16[1024,128]{1,0:T(8,128)(2,1)S(1)} %get-tuple-element.57.refs_1_), channel_id=1, source_target_pairs={{0,1},{1,0},{2,3},{3,2},{4,5},{5,4},{6,7},{7,6},{8,9},{9,8},{10,11... | collective-permute-start | bytes 786440 | tf_op jit(solution)/shard_map/ppermute | solution.py:483
  10.9 1.6 %collective-permute-start.2 = (bf16[1024,128]{1,0:T(8,128)(2,1)S(1)}, bf16[1024,128]{1,0:T(8,128)(2,1)S(1)}, u32[]{:S(2)}, u32[]{:S(2)}) collective-permute-start(bf16[1024,128]{1,0:T(8,128)(2,1)S(1)} %get-tuple-element.58.refs_2_.refs_6_), channel_id=1, source_target_pairs={{0,1},{1,0},{2,3},{3,2},{4,5},{5,4},{6,7},{7,6},{8,9},{9,8},{10,11... | collective-permute-start | bytes 786440 | tf_op jit(solution)/shard_map/ppermute | solution.py:483
  11.1 1.9 %copy-start = (bf16[96,128,128]{2,1,0:T(8,128)(2,1)S(1)}, bf16[96,128,128]{2,1,0:T(8,128)(2,1)}, u32[]{:S(2)}) copy-start(bf16[96,128,128]{2,1,0:T(8,128)(2,1)} %tiles_ref.11) | copy-start | bytes 9437188
  14.8 8.7 %collective-permute-start.3 = (bf16[1024,128]{1,0:T(8,128)(2,1)S(1)}, bf16[1024,128]{1,0:T(8,128)(2,1)S(1)}, u32[]{:S(2)}, u32[]{:S(2)}) collective-permute-start(bf16[1024,128]{1,0:T(8,128)(2,1)S(1)} %get-tuple-element.63), channel_id=1, source_target_pairs={{0,15},{1,2},{2,1},{3,4},{4,3},{5,6},{6,5},{7,8},{8,7},{9,10},{10,... | collective-permute-start | bytes 786440 | tf_op jit(solution)/shard_map/ppermute | solution.py:480
  16.2 21.2 %collective-permute-start.9 = (bf16[1024,128]{1,0:T(8,128)(2,1)S(1)}, bf16[1024,128]{1,0:T(8,128)(2,1)S(1)}, u32[]{:S(2)}, u32[]{:S(2)}) collective-permute-start(bf16[1024,128]{1,0:T(8,128)(2,1)S(1)} %get-tuple-element.76), channel_id=1, source_target_pairs={{0,15},{1,2},{2,1},{3,4},{4,3},{5,6},{6,5},{7,8},{8,7},{9,10},{10,... | collective-permute-start | bytes 786440 | tf_op jit(solution)/shard_map/ppermute | solution.py:480
  24.7 15.3 %collective-permute-start.5 = (bf16[1024,256]{1,0:T(8,128)(2,1)S(1)}, bf16[1024,256]{1,0:T(8,128)(2,1)S(1)}, u32[]{:S(2)}, u32[]{:S(2)}) collective-permute-start(bf16[1024,256]{1,0:T(8,128)(2,1)S(1)} %get-tuple-element.72), channel_id=1, source_target_pairs={{0,15},{1,2},{2,1},{3,4},{4,3},{5,6},{6,5},{7,8},{8,7},{9,10},{10,... | collective-permute-start | bytes 1572872 | tf_op jit(solution)/shard_map/ppermute | solution.py:480
  24.8 13.3 %collective-permute-start.6 = (bf16[1024,128]{1,0:T(8,128)(2,1)S(1)}, bf16[1024,128]{1,0:T(8,128)(2,1)S(1)}, u32[]{:S(2)}, u32[]{:S(2)}) collective-permute-start(bf16[1024,128]{1,0:T(8,128)(2,1)S(1)} %get-tuple-element.73.refs_0_.refs_9_), channel_id=1, source_target_pairs={{0,1},{1,0},{2,3},{3,2},{4,5},{5,4},{6,7},{7,6},{8,9},{9,8},{10,11... | collective-permute-start | bytes 786440 | tf_op jit(solution)/shard_map/ppermute | solution.py:483
  34.8 3.3 %collective-permute-start.7 = (bf16[1024,128]{1,0:T(8,128)(2,1)S(1)}, bf16[1024,128]{1,0:T(8,128)(2,1)S(1)}, u32[]{:S(2)}, u32[]{:S(2)}) collective-permute-start(bf16[1024,128]{1,0:T(8,128)(2,1)S(1)} %get-tuple-element.74.refs_1_.refs_10_), channel_id=1, source_target_pairs={{0,1},{1,0},{2,3},{3,2},{4,5},{5,4},{6,7},{7,6},{8,9},{9,8},{10,11... | collective-permute-start | bytes 786440 | tf_op jit(solution)/shard_map/ppermute | solution.py:483
  34.8 3.3 %collective-permute-start.8 = (bf16[1024,128]{1,0:T(8,128)(2,1)S(1)}, bf16[1024,128]{1,0:T(8,128)(2,1)S(1)}, u32[]{:S(2)}, u32[]{:S(2)}) collective-permute-start(bf16[1024,128]{1,0:T(8,128)(2,1)S(1)} %get-tuple-element.75.refs_2_.refs_11_), channel_id=1, source_target_pairs={{0,1},{1,0},{2,3},{3,2},{4,5},{5,4},{6,7},{7,6},{8,9},{9,8},{10,11... | collective-permute-start | bytes 786440 | tf_op jit(solution)/shard_map/ppermute | solution.py:483
  41.4 6.6 %collective-permute-start.12 = (f32[8,128]{1,0:T(8,128)S(1)}, f32[8,128]{1,0:T(8,128)S(1)}, u32[]{:S(2)}, u32[]{:S(2)}) collective-permute-start(f32[8,128]{1,0:T(8,128)S(1)} %get-tuple-element.103.refs_0_), channel_id=1, source_target_pairs={{0,12},{1,13},{2,14},{3,15},{4,8},{5,9},{6,10},{7,11},{8,4},{9,5},... | collective-permute-start | bytes 12296 | tf_op jit(solution)/shard_map/ppermute | solution.py:449
  42.9 5.0 %collective-permute-start.11 = (f32[8,128]{1,0:T(8,128)S(1)}, f32[8,128]{1,0:T(8,128)S(1)}, u32[]{:S(2)}, u32[]{:S(2)}) collective-permute-start(f32[8,128]{1,0:T(8,128)S(1)} %get-tuple-element.103.refs_0_), channel_id=1, source_target_pairs={{0,8},{1,9},{2,10},{3,11},{4,12},{5,13},{6,14},{7,15},{8,0},{9,1},... | collective-permute-start | bytes 12296 | tf_op jit(solution)/shard_map/ppermute | solution.py:449
  44.7 3.6 %collective-permute-start.10 = (f32[8,128]{1,0:T(8,128)S(1)}, f32[8,128]{1,0:T(8,128)S(1)}, u32[]{:S(2)}, u32[]{:S(2)}) collective-permute-start(f32[8,128]{1,0:T(8,128)S(1)} %get-tuple-element.103.refs_0_), channel_id=1, source_target_pairs={{0,4},{1,5},{2,6},{3,7},{4,0},{5,1},{6,2},{7,3},{8,12},{9,13},{10,... | collective-permute-start | bytes 12296 | tf_op jit(solution)/shard_map/ppermute | solution.py:449
  48.3 3.1 %collective-permute-start.15 = (f32[8,128]{1,0:T(8,128)S(1)}, f32[8,128]{1,0:T(8,128)S(1)}, u32[]{:S(2)}, u32[]{:S(2)}) collective-permute-start(f32[8,128]{1,0:T(8,128)S(1)} %add_up.1), channel_id=1, source_target_pairs={{0,3},{1,2},{2,1},{3,0},{4,7},{5,6},{6,5},{7,4},{8,11},{9,10},{10,... | collective-permute-start | bytes 12296 | tf_op jit(solution)/shard_map/ppermute | solution.py:449
  48.3 4.7 %collective-permute-start.14 = (f32[8,128]{1,0:T(8,128)S(1)}, f32[8,128]{1,0:T(8,128)S(1)}, u32[]{:S(2)}, u32[]{:S(2)}) collective-permute-start(f32[8,128]{1,0:T(8,128)S(1)} %add_up.1), channel_id=1, source_target_pairs={{0,2},{1,3},{2,0},{3,1},{4,6},{5,7},{6,4},{7,5},{8,10},{9,11},{10,... | collective-permute-start | bytes 12296 | tf_op jit(solution)/shard_map/ppermute | solution.py:449
  51.4 1.6 %collective-permute-start.13 = (f32[8,128]{1,0:T(8,128)S(1)}, f32[8,128]{1,0:T(8,128)S(1)}, u32[]{:S(2)}, u32[]{:S(2)}) collective-permute-start(f32[8,128]{1,0:T(8,128)S(1)} %add_up.1), channel_id=1, source_target_pairs={{0,1},{1,0},{2,3},{3,2},{4,5},{5,4},{6,7},{7,6},{8,9},{9,8},{10,11... | collective-permute-start | bytes 12296 | tf_op jit(solution)/shard_map/ppermute | solution.py:449

commit v13 on v11

--- a/solution.py
+++ b/solution.py
@@ -228,14 +228,18 @@
     lax.fori_loop(0, list_ref[4 * pairs + 2 * part + 1], short, 0)
 
 
-def near_fields(lists, tiles, owns, others, far_part, sent, after, flops, name):
+def weighted(field, weight):
+    return jnp.sum(field.astype(F32) * weight[...], axis=0, keepdims=True)
+
+
+def near_fields(lists, tiles, owns, others, far_part, weight, sent, after, name):
     slots, tile, _ = tiles.shape
     cells = owns[0].shape[0]
     groups = len(owns)
     width = groups * LANES
     per = cells // tile
     pairs = section(slots, per)
-    start = [] if far_part is None else [far_part]
+    start = [] if far_part is None else [far_part, weight]
 
     def body(list_ref, tiles_ref, *refs):
         own_refs, other_refs, refs = refs[:groups], refs[groups : 2 * groups], refs[2 * groups :]
@@ -249,11 +253,13 @@
             window[per : 2 * per, :, lanes(g)] = other_refs[g][...].reshape(per, tile, LANES)
         window[2 * per] = jnp.zeros((tile, width), BF16)
         field[:per] = jnp.zeros((per, tile, width), F32)
-        for ref in start_refs:
-            field[:per, :, lanes(0)] = ref[...].reshape(per, tile, LANES)
+        if start:
+            field[:per, :, lanes(0)] = start_refs[0][...].reshape(per, tile, LANES)
         add_pairs(0, list_ref, tiles_ref, field, window, pairs)
         for g, out in enumerate(field_outs):
             out[...] = field[:per, :, lanes(g)].reshape(cells, LANES).astype(out.dtype)
+        if start:
+            sent_outs[len(sent)][...] = weighted(field_outs[0][...], start_refs[1])
 
     outs = call(
         body,
@@ -262,13 +268,13 @@
             ((cells, LANES), BF16 if start and g == 0 else F32, pltpu.VMEM)
             for g in range(groups)
         ]
-        + [(a.shape, BF16, pltpu.VMEM) for a in sent],
+        + [(a.shape, BF16, pltpu.VMEM) for a in sent]
+        + ([((1, LANES), F32, pltpu.VMEM)] if start else []),
         [
             pltpu.VMEM((per + 1, tile, width), F32),
             pltpu.VMEM((2 * per + 1, tile, width), BF16),
         ],
         name,
-        flops,
     )
     return outs[:groups], outs[groups:]
 
@@ -388,20 +394,24 @@
     groups = len(xs)
     cells = xs[0].shape[0]
     width = groups * LANES
+    blocks = 4 if cells % 64 == 0 else 1
+    size = cells // blocks
 
     def body(*refs):
         field_refs, x_refs, base_refs = [refs[k * groups : (k + 1) * groups] for k in range(3)]
         mixing_ref, x_out, y_out, token, x_buf, y_buf, sems = refs[3 * groups :]
-        held = [ref[...] for ref in field_refs]
         copies = []
-        for g in range(groups):
-            y_new = base_refs[g][...] - 0.2 * mixed_of(held, mixing_ref, g, channels)
-            y_buf[g] = y_new
-            x_buf[g] = jnp.clip(x_refs[g][...] + 0.5 * y_new, -1.0, 1.0)
+        for b in range(blocks):
+            rows = slice(b * size, (b + 1) * size)
+            held = [ref[rows, :] for ref in field_refs]
+            for g in range(groups):
+                x_new, y_new = updated(
+                    mixed_of(held, mixing_ref, g, channels), base_refs[g][rows, :], x_refs[g][rows, :]
+                )
+                x_buf[rows, lanes(g)] = x_new
+                y_buf[rows, lanes(g)] = y_new
             for k, (buf, out) in enumerate(((y_buf, y_out), (x_buf, x_out))):
-                copies.append(
-                    pltpu.make_async_copy(buf.at[g], out.at[:, lanes(g)], sems.at[g, k])
-                )
+                copies.append(pltpu.make_async_copy(buf.at[rows], out.at[rows], sems.at[b, k]))
                 copies[-1].start()
         token[...] = jnp.zeros_like(token)
         for copy in copies:
@@ -412,9 +422,9 @@
         vmem(*fields, *xs, *bases, mixing),
         [((cells, width), F32, pltpu.HBM)] * 2 + [((8, LANES), F32, pltpu.VMEM)],
         [
-            pltpu.VMEM((groups, cells, LANES), F32),
-            pltpu.VMEM((groups, cells, LANES), F32),
-            pltpu.SemaphoreType.DMA((groups, 2)),
+            pltpu.VMEM((cells, width), F32),
+            pltpu.VMEM((cells, width), F32),
+            pltpu.SemaphoreType.DMA((blocks, 2)),
         ],
         "finish",
     )
@@ -499,7 +509,7 @@
     others = [near_swap(r) for r in owns]
     base, mixing = first_base(xs, momenta, same, spread, channel_coupling, channels)
     near, sent = near_fields(
-        lists, tile_values, owns, others, None, more_own, [mixing], 0, "near_first"
+        lists, tile_values, owns, others, None, None, more_own, [mixing], "near_first"
     )
     fars.append(far_swap(sent[0]))
 
@@ -551,7 +561,6 @@
     (part,) = far_fields(
         lists, tile_values, [], new_fars[0], [], [(wide, F32)], keep, "far_second_0", NEAR_FLOPS
     )
-    near, _ = near_fields(lists, tile_values, owns, others, part, [], [], 0, "near_second")
     later = second_pieces[1]
     base, weights, more_x = second_base(
         new_x,
@@ -566,18 +575,17 @@
         channels,
     )
     xs = [*new_x, *more_x]
+    near, (share,) = near_fields(
+        lists, tile_values, owns, others, part, weights[0], [], [], "near_second"
+    )
     piece = second_pieces[1]
 
     def last_work(done, ins, outs):
-        held = [ins[groups][...]] + [field.astype(BF16) for field in done]
-        for out, field in zip(outs, held[1:]):
+        held = [field.astype(BF16) for field in done]
+        for out, field in zip(outs, held):
             out[...] = field
         row = jnp.concatenate(
-            [
-                jnp.sum(field.astype(F32) * ref[...], axis=0, keepdims=True)
-                for field, ref in zip(held, ins[:groups])
-            ],
-            axis=1,
+            [ins[0][...]] + [weighted(field, ref) for field, ref in zip(held, ins[1:])], axis=1
         )
         row = jnp.broadcast_to(row, (replicas, width))
         lane = lax.broadcasted_iota(jnp.int32, (replicas, width), 1)
@@ -594,7 +602,7 @@
         tile_values,
         near[1:],
         new_fars[1],
-        weights,
+        [share, *weights[1:]],
         [(wide, BF16)] * len(piece) + [((8, LANES), F32)],
         last_work,
         "far_second_1",

time: 54.4 us -> 57.4 us (1.055)
  starting transfers between devices: 28.1 us -> 31.6 us
  Pallas kernels: 18 us -> 15.6 us
  waiting for transfers between devices: 4.88 us -> 6.94 us
    ppermute x6, waiting for transfers between devices: 1.89 us -> 4.51 us  [sum_over_ring(): lax.ppermute(value, RING, [(j, j ^ bit) for j in range(ring)])]
    pallas_call x12, Pallas kernels: 18 us -> 15.6 us  [call(): pl.pallas_call(body, in_specs=[pl.BlockSpec(memory_space=pl.ANY if s is p...]
    ppermute x4, starting transfers between devices: 10.1 us -> 12.3 us  [far_swap(): return lax.ppermute(mine, RING, off_chip)]
    ppermute x6, starting transfers between devices: 7.41 us -> 8.31 us  [sum_over_ring(): lax.ppermute(value, RING, [(j, j ^ bit) for j in range(ring)])]
    ppermute x4, waiting for transfers between devices: 2.88 us -> 2.16 us  [far_swap(): return lax.ppermute(mine, RING, off_chip)]
  transfers between devices with their start and end apart: 16 -> 16, of which waited for: 4 -> 5; matrix products, arithmetic and copies ran while one was open for 0% -> 0% of each run, Pallas kernels for 29% -> 23%
where the time goes in v13:
time: 57.4 us; the launch traced here: 56.4 us
  starting transfers between devices  31.6 us (55%)
  Pallas kernels  15.6 us (27%)
  waiting for transfers between devices  6.94 us (12%)
  between operations  1.51 us (3%)
    pallas_call x12, Pallas kernels, call(): pl.pallas_call(body, in_specs=[pl.BlockSpec(memory_space=pl.ANY if s is p...  15.6 us
    ppermute x4, starting transfers between devices, far_swap(): return lax.ppermute(mine, RING, off_chip)  12.3 us
    ppermute x6, starting transfers between devices, near_swap(): return lax.ppermute(mine, RING, on_chip)  11 us
    ppermute x6, starting transfers between devices, sum_over_ring(): lax.ppermute(value, RING, [(j, j ^ bit) for j in range(ring)])  8.31 us
    ppermute x6, waiting for transfers between devices, sum_over_ring(): lax.ppermute(value, RING, [(j, j ^ bit) for j in range(ring)])  4.51 us
    ppermute x4, waiting for transfers between devices, far_swap(): return lax.ppermute(mine, RING, off_chip)  2.16 us
  transfers between devices with their start and end apart: 16, of which 5 were waited for; matrix products, arithmetic and copies ran while one was open for 0% of the time, Pallas kernels for 23%

profile of v13, /device:TPU:0, one launch (start us, length us, event | category | flops | bytes accessed | tf_op | source)
XLA Modules:
  0.0 56.4 jit_solution(16866631712522025689)
XLA Ops:
  0.7 1.4 %load_first.1 = (f32[1024,128]{1,0:T(8,128)S(1)}, f32[1024,128]{1,0:T(8,128)S(1)}, bf16[1024,128]{1,0:T(8,128)(2,1)S(1)}, bf16[1024,128]{1,0:T(8,128)(2,1)S(1)}, bf16[1024,256]{1,0:T(8,128)(2,1)S(1)}) custom-call(f32[1024,384]{1,0:T(8,128)} %x_ref.3), custom_call_target="tpu_custom_call" | custom-call | flops 1000 | bytes 1000 | tf_op jit(solution)/shard_map/load_first/pallas_call | solution.py:21
  2.1 5.5 %collective-permute-start.4 = (bf16[1024,256]{1,0:T(8,128)(2,1)S(1)}, bf16[1024,256]{1,0:T(8,128)(2,1)S(1)}, u32[]{:S(2)}, u32[]{:S(2)}) collective-permute-start(bf16[1024,256]{1,0:T(8,128)(2,1)S(1)} %get-tuple-element.55._), channel_id=1, source_target_pairs={{0,15},{1,2},{2,1},{3,4},{4,3},{5,6},{6,5},{7,8},{8,7},{9,10},{10,... | collective-permute-start | bytes 1572872 | tf_op jit(solution)/shard_map/ppermute | solution.py:487
  8.3 1.4 %make_lists.1 = (s32[214]{0:T(256)S(4)}, f32[1024,128]{1,0:T(8,128)S(1)}, bf16[1024,128]{1,0:T(8,128)(2,1)S(1)}) custom-call(s32[96]{0:T(128)S(1)} %copy-done.5, s32[96]{0:T(128)S(1)} %copy-done.6, s32[1]{0:T(128)S(6)} %copy.28.count_hbm, f32[1024,384]{1,0:T(8,128)} %x_ref.3, bf16[1024,256]{1,0:T(8,128)(2,1)S(1)} %get-tuple-element.55._), custom_call_target="tpu_custom_call" | custom-call | flops 1000 | bytes 1000 | tf_op jit(solution)/shard_map/make_lists/pallas_call | solution.py:21
  9.8 0.5 collective-permute-start
  10.3 0.1 collective-permute-start.1
  10.4 1.4 %first_base.1 = (f32[1024,128]{1,0:T(8,128)S(1)}, f32[1024,128]{1,0:T(8,128)S(1)}, f32[1024,128]{1,0:T(8,128)S(1)}, bf16[384,384]{1,0:T(8,128)(2,1)S(1)}) custom-call(f32[1024,128]{1,0:T(8,128)S(1)} %get-tuple-element.60.refs_0_.refs_4_, f32[1024,128]{1,0:T(8,128)S(1)} %get-tuple-element.61.refs_1_.refs_5_.refs_7_, ...), custom_call_target="tpu_custom_call" | custom-call | flops 1000 | bytes 1000 | tf_op jit(solution)/shard_map/first_base/pallas_call | solution.py:21
  11.8 0.3 collective-permute-done.1.refs_4_
  12.1 0.2 copy-done
  12.3 1.3 %near_first.1 = (f32[1024,128]{1,0:T(8,128)S(1)}, f32[1024,128]{1,0:T(8,128)S(1)}, f32[1024,128]{1,0:T(8,128)S(1)}, bf16[1024,128]{1,0:T(8,128)(2,1)S(1)}) custom-call(s32[214]{0:T(256)S(4)} %get-tuple-element.56.list_ref, bf16[96,128,128]{2,1,0:T(8,128)(2,1)S(1)} %copy-done, bf16[1024,128]{1,0:T(8,128)(2,1)S(1)} %get-tuple-element.57.refs_0_, ...), custom_call_target="tpu_custom_call" | custom-call | flops 1000 | bytes 1000 | tf_op jit(solution)/shard_map/near_first/pallas_call | solution.py:21
  13.6 1.7 %collective-permute-start.3 = (bf16[1024,128]{1,0:T(8,128)(2,1)S(1)}, bf16[1024,128]{1,0:T(8,128)(2,1)S(1)}, u32[]{:S(2)}, u32[]{:S(2)}) collective-permute-start(bf16[1024,128]{1,0:T(8,128)(2,1)S(1)} %get-tuple-element.64), channel_id=1, source_target_pairs={{0,15},{1,2},{2,1},{3,4},{4,3},{5,6},{6,5},{7,8},{8,7},{9,10},{10,... | collective-permute-start | bytes 786440 | tf_op jit(solution)/shard_map/ppermute | solution.py:487
  15.3 1.2 %far_first_0.1 = (bf16[1024,128]{1,0:T(8,128)(2,1)S(1)}, bf16[1024,128]{1,0:T(8,128)(2,1)S(1)}, bf16[1024,128]{1,0:T(8,128)(2,1)S(1)}, bf16[1024,128]{1,0:T(8,12...) custom-call(s32[214]{0:T(256)S(4)} %get-tuple-element.56.list_ref, bf16[96,128,128]{2,1,0:T(8,128)(2,1)S(1)} %copy-done, ...), custom_call_target="tpu_custom_call" | custom-call | flops 1000 | bytes 1000 | tf_op jit(solution)/shard_map/far_first_0/pallas_call | solution.py:21
  16.5 3.6 %collective-permute-start.9 = (bf16[1024,128]{1,0:T(8,128)(2,1)S(1)}, bf16[1024,128]{1,0:T(8,128)(2,1)S(1)}, u32[]{:S(2)}, u32[]{:S(2)}) collective-permute-start(bf16[1024,128]{1,0:T(8,128)(2,1)S(1)} %get-tuple-element.77), channel_id=1, source_target_pairs={{0,15},{1,2},{2,1},{3,4},{4,3},{5,6},{6,5},{7,8},{8,7},{9,10},{10,... | collective-permute-start | bytes 786440 | tf_op jit(solution)/shard_map/ppermute | solution.py:487
  20.1 2.2 %collective-permute-done.3.far_ref = bf16[1024,128]{1,0:T(8,128)(2,1)S(1)} collective-permute-done((bf16[1024,128]{1,0:T(8,128)(2,1)S(1)}, bf16[1024,128]{1,0:T(8,128)(2,1)S(1)}, u32[]{:S(2)}, u32[]{:S(2)}) %collective-permute-start.3) | collective-permute-done | bytes 262176 | tf_op jit(solution)/shard_map/ppermute | solution.py:487
  22.2 1.3 %far_first_1.1 = (bf16[1024,256]{1,0:T(8,128)(2,1)S(1)}, bf16[1024,128]{1,0:T(8,128)(2,1)S(1)}, bf16[1024,128]{1,0:T(8,128)(2,1)S(1)}, bf16[1024,128]{1,0:T(8,128)(2,1)S(1)}) custom-call(s32[214]{0:T(256)S(4)} %get-tuple-element.56.list_ref, bf16[96,128,128]{2,1,0:T(8,128)(2,1)S(1)} %copy-done, bf16[1024,128]{1,0:T(8,128)(2,1)S(1)} %collective-permute-done.3.far_ref, ...), custom_call_target="tpu_custom_call" | custom-call | flops 1000 | bytes 1000 | tf_op jit(solution)/shard_map/far_first_1/pallas_call | solution.py:21
  23.6 1.5 %collective-permute-start.5 = (bf16[1024,256]{1,0:T(8,128)(2,1)S(1)}, bf16[1024,256]{1,0:T(8,128)(2,1)S(1)}, u32[]{:S(2)}, u32[]{:S(2)}) collective-permute-start(bf16[1024,256]{1,0:T(8,128)(2,1)S(1)} %get-tuple-element.73), channel_id=1, source_target_pairs={{0,15},{1,2},{2,1},{3,4},{4,3},{5,6},{6,5},{7,8},{8,7},{9,10},{10,... | collective-permute-start | bytes 1572872 | tf_op jit(solution)/shard_map/ppermute | solution.py:487
  25.0 9.9 %collective-permute-start.7 = (bf16[1024,128]{1,0:T(8,128)(2,1)S(1)}, bf16[1024,128]{1,0:T(8,128)(2,1)S(1)}, u32[]{:S(2)}, u32[]{:S(2)}) collective-permute-start(bf16[1024,128]{1,0:T(8,128)(2,1)S(1)} %get-tuple-element.75.refs_10_.refs_1_), channel_id=1, source_target_pairs={{0,1},{1,0},{2,3},{3,2},{4,5},{5,4},{6,7},{7,6},{8,9},{9,8},{10,11... | collective-permute-start | bytes 786440 | tf_op jit(solution)/shard_map/ppermute | solution.py:490
  34.9 0.5 collective-permute-start.6
  35.4 2.1 %second_base.1 = (f32[1024,128]{1,0:T(8,128)S(1)}, f32[1024,128]{1,0:T(8,128)S(1)}, f32[1024,128]{1,0:T(8,128)S(1)}, f32[1024,128]{1,0:T(8,128)S(1)}, f32[1024,1...) custom-call(f32[1024,128]{1,0:T(8,128)S(1)} %get-tuple-element.78.refs_0_.refs_6_, ...), custom_call_target="tpu_custom_call" | custom-call | flops 1000 | bytes 1000 | tf_op jit(solution)/shard_map/second_base/pallas_call | solution.py:21
  37.5 0.8 %far_second_0.1.refs_6_ = f32[1024,128]{1,0:T(8,128)S(1)} custom-call(s32[214]{0:T(256)S(4)} %get-tuple-element.56.list_ref, bf16[96,128,128]{2,1,0:T(8,128)(2,1)S(1)} %copy-done, bf16[1024,128]{1,0:T(8,128)(2,1)S(1)} %collective-permute-done.9.far_ref), custom_call_target="tpu_custom_call" | custom-call | flops 4000000000 | bytes 1000 | tf_op jit(solution)/shard_map/far_second_0/pallas_call | solution.py:21
  38.4 1.4 %near_second.1 = (bf16[1024,128]{1,0:T(8,128)(2,1)S(1)}, f32[1024,128]{1,0:T(8,128)S(1)}, f32[1024,128]{1,0:T(8,128)S(1)}, f32[1,128]{1,0:T(1,128)S(1)}) custom-call(s32[214]{0:T(256)S(4)} %get-tuple-element.56.list_ref, bf16[96,128,128]{2,1,0:T(8,128)(2,1)S(1)} %copy-done, bf16[1024,128]{1,0:T(8,128)(2,1)S(1)} %get-tuple-element.74.refs_9_.refs_0_, ...), custom_call_target="tpu_custom_call" | custom-call | flops 1000 | bytes 1000 | tf_op jit(solution)/shard_map/near_second/pallas_call | solution.py:21
  39.8 1.3 %far_second_1.1 = (bf16[1024,128]{1,0:T(8,128)(2,1)S(1)}, bf16[1024,128]{1,0:T(8,128)(2,1)S(1)}, f32[8,128]{1,0:T(8,128)S(1)}, bf16[1024,128]{1,0:T(8,128)(2,1)S...) custom-call(s32[214]{0:T(256)S(4)} %get-tuple-element.56.list_ref, ...), custom_call_target="tpu_custom_call", output_to_operand_aliasing={{3}: (8, {}), {4}: (9, {}), {5}: (10, {}), {6}: (11, {}), {... | custom-call | flops 1000 | bytes 1000 | tf_op jit(solution)/shard_map/far_second_1/pallas_call | solution.py:21
  41.0 2.2 %collective-permute-start.10 = (f32[8,128]{1,0:T(8,128)S(1)}, f32[8,128]{1,0:T(8,128)S(1)}, u32[]{:S(2)}, u32[]{:S(2)}) collective-permute-start(f32[8,128]{1,0:T(8,128)S(1)} %get-tuple-element.105.refs_0_), channel_id=1, source_target_pairs={{0,4},{1,5},{2,6},{3,7},{4,0},{5,1},{6,2},{7,3},{8,12},{9,13},{10,... | collective-permute-start | bytes 12296 | tf_op jit(solution)/shard_map/ppermute | solution.py:456
  43.2 0.6 %collective-permute-start.11 = (f32[8,128]{1,0:T(8,128)S(1)}, f32[8,128]{1,0:T(8,128)S(1)}, u32[]{:S(2)}, u32[]{:S(2)}) collective-permute-start(f32[8,128]{1,0:T(8,128)S(1)} %get-tuple-element.105.refs_0_), channel_id=1, source_target_pairs={{0,8},{1,9},{2,10},{3,11},{4,12},{5,13},{6,14},{7,15},{8,0},{9,1},... | collective-permute-start | bytes 12296 | tf_op jit(solution)/shard_map/ppermute | solution.py:456
  43.8 1.8 %collective-permute-start.12 = (f32[8,128]{1,0:T(8,128)S(1)}, f32[8,128]{1,0:T(8,128)S(1)}, u32[]{:S(2)}, u32[]{:S(2)}) collective-permute-start(f32[8,128]{1,0:T(8,128)S(1)} %get-tuple-element.105.refs_0_), channel_id=1, source_target_pairs={{0,12},{1,13},{2,14},{3,15},{4,8},{5,9},{6,10},{7,11},{8,4},{9,5},... | collective-permute-start | bytes 12296 | tf_op jit(solution)/shard_map/ppermute | solution.py:456
  45.6 2.1 %finish.1 = (f32[1024,384]{1,0:T(8,128)}, f32[1024,384]{1,0:T(8,128)}, f32[8,128]{1,0:T(8,128)S(1)}) custom-call(bf16[1024,128]{1,0:T(8,128)(2,1)S(1)} %get-tuple-element.93.refs_0_, bf16[1024,128]{1,0:T(8,128)(2,1)S(1)} %get-tuple-element.94.refs_1_, bf16[1024,128]{1,0:T(8,128)(2,1)S(1)} %get-tuple-element.95.refs_2_, ...), custom_call_target="tpu_custom_call" | custom-call | flops 1000 | bytes 1000 | tf_op jit(solution)/shard_map/finish/pallas_call | solution.py:21
  47.7 1.5 %collective-permute-done.12.refs_3_ = f32[8,128]{1,0:T(8,128)S(1)} collective-permute-done((f32[8,128]{1,0:T(8,128)S(1)}, f32[8,128]{1,0:T(8,128)S(1)}, u32[]{:S(2)}, u32[]{:S(2)}) %collective-permute-start.12) | collective-permute-done | bytes 4128 | tf_op jit(solution)/shard_map/ppermute | solution.py:456
  49.2 2.2 %collective-permute-start.13 = (f32[8,128]{1,0:T(8,128)S(1)}, f32[8,128]{1,0:T(8,128)S(1)}, u32[]{:S(2)}, u32[]{:S(2)}) collective-permute-start(f32[8,128]{1,0:T(8,128)S(1)} %add_up.1), channel_id=1, source_target_pairs={{0,1},{1,0},{2,3},{3,2},{4,5},{5,4},{6,7},{7,6},{8,9},{9,8},{10,11... | collective-permute-start | bytes 12296 | tf_op jit(solution)/shard_map/ppermute | solution.py:456
  51.5 1.4 %collective-permute-start.14 = (f32[8,128]{1,0:T(8,128)S(1)}, f32[8,128]{1,0:T(8,128)S(1)}, u32[]{:S(2)}, u32[]{:S(2)}) collective-permute-start(f32[8,128]{1,0:T(8,128)S(1)} %add_up.1), channel_id=1, source_target_pairs={{0,2},{1,3},{2,0},{3,1},{4,6},{5,7},{6,4},{7,5},{8,10},{9,11},{10,... | collective-permute-start | bytes 12296 | tf_op jit(solution)/shard_map/ppermute | solution.py:456
  52.9 0.1 collective-permute-start.15
  53.0 2.1 %collective-permute-done.14 = f32[8,128]{1,0:T(8,128)S(1)} collective-permute-done((f32[8,128]{1,0:T(8,128)S(1)}, f32[8,128]{1,0:T(8,128)S(1)}, u32[]{:S(2)}, u32[]{:S(2)}) %collective-permute-start.14) | collective-permute-done | bytes 4128 | tf_op jit(solution)/shard_map/ppermute | solution.py:456
  55.1 0.9 %collective-permute-done.15 = f32[8,128]{1,0:T(8,128)S(1)} collective-permute-done((f32[8,128]{1,0:T(8,128)S(1)}, f32[8,128]{1,0:T(8,128)S(1)}, u32[]{:S(2)}, u32[]{:S(2)}) %collective-permute-start.15) | collective-permute-done | bytes 4128 | tf_op jit(solution)/shard_map/ppermute | solution.py:456
  55.9 0.5 multiply_bitcast_fusion
  (28 shorter events, 0.2 us)
Async XLA Ops:
  0.6 9.7 %copy-start.2 = (bf16[384,384]{1,0:T(8,128)(2,1)S(1)}, bf16[384,384]{1,0:T(8,128)(2,1)}, u32[]{:S(2)}) copy-start(bf16[384,384]{1,0:T(8,128)(2,1)} %constant.7.clone.refs_4_.refs_12_) | copy-start | bytes 884740
  0.6 9.7 %copy-start.3 = (bf16[384,48]{1,0:T(8,128)(2,1)S(1)}, bf16[384,48]{1,0:T(8,128)(2,1)}, u32[]{:S(2)}) copy-start(bf16[384,48]{1,0:T(8,128)(2,1)} %constant.8.clone.refs_5_) | copy-start | bytes 110596
  0.7 7.6 %copy-start.5 = (s32[96]{0:T(128)S(1)}, s32[96]{0:T(128)}, u32[]{:S(2)}) copy-start(s32[96]{0:T(128)} %rows_hbm.1) | copy-start | bytes 1156
  0.7 7.6 %copy-start.6 = (s32[96]{0:T(128)S(1)}, s32[96]{0:T(128)}, u32[]{:S(2)}) copy-start(s32[96]{0:T(128)} %cols_hbm.1) | copy-start | bytes 1156
  0.7 9.7 %copy-start.1 = (f32[1024,384]{1,0:T(8,128)S(1)}, f32[1024,384]{1,0:T(8,128)}, u32[]{:S(2)}) copy-start(f32[1024,384]{1,0:T(8,128)} %refs_3_.1) | copy-start | bytes 4718596
  0.7 9.7 %copy-start.4 = (bf16[48,48]{1,0:T(8,128)(2,1)S(1)}, bf16[48,48]{1,0:T(8,128)(2,1)}, u32[]{:S(2)}) copy-start(bf16[48,48]{1,0:T(8,128)(2,1)} %refs_6_.1) | copy-start | bytes 13828
  2.1 13.2 %collective-permute-start.4 = (bf16[1024,256]{1,0:T(8,128)(2,1)S(1)}, bf16[1024,256]{1,0:T(8,128)(2,1)S(1)}, u32[]{:S(2)}, u32[]{:S(2)}) collective-permute-start(bf16[1024,256]{1,0:T(8,128)(2,1)S(1)} %get-tuple-element.55._), channel_id=1, source_target_pairs={{0,15},{1,2},{2,1},{3,4},{4,3},{5,6},{6,5},{7,8},{8,7},{9,10},{10,... | collective-permute-start | bytes 1572872 | tf_op jit(solution)/shard_map/ppermute | solution.py:487
  9.7 2.1 %collective-permute-start.2 = (bf16[1024,128]{1,0:T(8,128)(2,1)S(1)}, bf16[1024,128]{1,0:T(8,128)(2,1)S(1)}, u32[]{:S(2)}, u32[]{:S(2)}) collective-permute-start(bf16[1024,128]{1,0:T(8,128)(2,1)S(1)} %get-tuple-element.59.refs_2_.refs_6_), channel_id=1, source_target_pairs={{0,1},{1,0},{2,3},{3,2},{4,5},{5,4},{6,7},{7,6},{8,9},{9,8},{10,11... | collective-permute-start | bytes 786440 | tf_op jit(solution)/shard_map/ppermute | solution.py:490
  9.8 2.0 %collective-permute-start = (bf16[1024,128]{1,0:T(8,128)(2,1)S(1)}, bf16[1024,128]{1,0:T(8,128)(2,1)S(1)}, u32[]{:S(2)}, u32[]{:S(2)}) collective-permute-start(bf16[1024,128]{1,0:T(8,128)(2,1)S(1)} %get-tuple-element.57.refs_0_), channel_id=1, source_target_pairs={{0,1},{1,0},{2,3},{3,2},{4,5},{5,4},{6,7},{7,6},{8,9},{9,8},{10,11... | collective-permute-start | bytes 786440 | tf_op jit(solution)/shard_map/ppermute | solution.py:490
  10.3 1.8 %collective-permute-start.1 = (bf16[1024,128]{1,0:T(8,128)(2,1)S(1)}, bf16[1024,128]{1,0:T(8,128)(2,1)S(1)}, u32[]{:S(2)}, u32[]{:S(2)}) collective-permute-start(bf16[1024,128]{1,0:T(8,128)(2,1)S(1)} %get-tuple-element.58.refs_1_), channel_id=1, source_target_pairs={{0,1},{1,0},{2,3},{3,2},{4,5},{5,4},{6,7},{7,6},{8,9},{9,8},{10,11... | collective-permute-start | bytes 786440 | tf_op jit(solution)/shard_map/ppermute | solution.py:490
  10.4 1.9 %copy-start = (bf16[96,128,128]{2,1,0:T(8,128)(2,1)S(1)}, bf16[96,128,128]{2,1,0:T(8,128)(2,1)}, u32[]{:S(2)}) copy-start(bf16[96,128,128]{2,1,0:T(8,128)(2,1)} %tiles_ref.11) | copy-start | bytes 9437188
  13.6 8.7 %collective-permute-start.3 = (bf16[1024,128]{1,0:T(8,128)(2,1)S(1)}, bf16[1024,128]{1,0:T(8,128)(2,1)S(1)}, u32[]{:S(2)}, u32[]{:S(2)}) collective-permute-start(bf16[1024,128]{1,0:T(8,128)(2,1)S(1)} %get-tuple-element.64), channel_id=1, source_target_pairs={{0,15},{1,2},{2,1},{3,4},{4,3},{5,6},{6,5},{7,8},{8,7},{9,10},{10,... | collective-permute-start | bytes 786440 | tf_op jit(solution)/shard_map/ppermute | solution.py:487
  16.5 21.0 %collective-permute-start.9 = (bf16[1024,128]{1,0:T(8,128)(2,1)S(1)}, bf16[1024,128]{1,0:T(8,128)(2,1)S(1)}, u32[]{:S(2)}, u32[]{:S(2)}) collective-permute-start(bf16[1024,128]{1,0:T(8,128)(2,1)S(1)} %get-tuple-element.77), channel_id=1, source_target_pairs={{0,15},{1,2},{2,1},{3,4},{4,3},{5,6},{6,5},{7,8},{8,7},{9,10},{10,... | collective-permute-start | bytes 786440 | tf_op jit(solution)/shard_map/ppermute | solution.py:487
  23.6 16.2 %collective-permute-start.5 = (bf16[1024,256]{1,0:T(8,128)(2,1)S(1)}, bf16[1024,256]{1,0:T(8,128)(2,1)S(1)}, u32[]{:S(2)}, u32[]{:S(2)}) collective-permute-start(bf16[1024,256]{1,0:T(8,128)(2,1)S(1)} %get-tuple-element.73), channel_id=1, source_target_pairs={{0,15},{1,2},{2,1},{3,4},{4,3},{5,6},{6,5},{7,8},{8,7},{9,10},{10,... | collective-permute-start | bytes 1572872 | tf_op jit(solution)/shard_map/ppermute | solution.py:487
  25.0 13.3 %collective-permute-start.7 = (bf16[1024,128]{1,0:T(8,128)(2,1)S(1)}, bf16[1024,128]{1,0:T(8,128)(2,1)S(1)}, u32[]{:S(2)}, u32[]{:S(2)}) collective-permute-start(bf16[1024,128]{1,0:T(8,128)(2,1)S(1)} %get-tuple-element.75.refs_10_.refs_1_), channel_id=1, source_target_pairs={{0,1},{1,0},{2,3},{3,2},{4,5},{5,4},{6,7},{7,6},{8,9},{9,8},{10,11... | collective-permute-start | bytes 786440 | tf_op jit(solution)/shard_map/ppermute | solution.py:490
  34.9 3.4 %collective-permute-start.8 = (bf16[1024,128]{1,0:T(8,128)(2,1)S(1)}, bf16[1024,128]{1,0:T(8,128)(2,1)S(1)}, u32[]{:S(2)}, u32[]{:S(2)}) collective-permute-start(bf16[1024,128]{1,0:T(8,128)(2,1)S(1)} %get-tuple-element.76.refs_11_.refs_2_), channel_id=1, source_target_pairs={{0,1},{1,0},{2,3},{3,2},{4,5},{5,4},{6,7},{7,6},{8,9},{9,8},{10,11... | collective-permute-start | bytes 786440 | tf_op jit(solution)/shard_map/ppermute | solution.py:490
  34.9 3.4 %collective-permute-start.6 = (bf16[1024,128]{1,0:T(8,128)(2,1)S(1)}, bf16[1024,128]{1,0:T(8,128)(2,1)S(1)}, u32[]{:S(2)}, u32[]{:S(2)}) collective-permute-start(bf16[1024,128]{1,0:T(8,128)(2,1)S(1)} %get-tuple-element.74.refs_9_.refs_0_), channel_id=1, source_target_pairs={{0,1},{1,0},{2,3},{3,2},{4,5},{5,4},{6,7},{7,6},{8,9},{9,8},{10,11... | collective-permute-start | bytes 786440 | tf_op jit(solution)/shard_map/ppermute | solution.py:490
  41.0 6.6 %collective-permute-start.10 = (f32[8,128]{1,0:T(8,128)S(1)}, f32[8,128]{1,0:T(8,128)S(1)}, u32[]{:S(2)}, u32[]{:S(2)}) collective-permute-start(f32[8,128]{1,0:T(8,128)S(1)} %get-tuple-element.105.refs_0_), channel_id=1, source_target_pairs={{0,4},{1,5},{2,6},{3,7},{4,0},{5,1},{6,2},{7,3},{8,12},{9,13},{10,... | collective-permute-start | bytes 12296 | tf_op jit(solution)/shard_map/ppermute | solution.py:456
  43.2 4.5 %collective-permute-start.11 = (f32[8,128]{1,0:T(8,128)S(1)}, f32[8,128]{1,0:T(8,128)S(1)}, u32[]{:S(2)}, u32[]{:S(2)}) collective-permute-start(f32[8,128]{1,0:T(8,128)S(1)} %get-tuple-element.105.refs_0_), channel_id=1, source_target_pairs={{0,8},{1,9},{2,10},{3,11},{4,12},{5,13},{6,14},{7,15},{8,0},{9,1},... | collective-permute-start | bytes 12296 | tf_op jit(solution)/shard_map/ppermute | solution.py:456
  43.8 5.4 %collective-permute-start.12 = (f32[8,128]{1,0:T(8,128)S(1)}, f32[8,128]{1,0:T(8,128)S(1)}, u32[]{:S(2)}, u32[]{:S(2)}) collective-permute-start(f32[8,128]{1,0:T(8,128)S(1)} %get-tuple-element.105.refs_0_), channel_id=1, source_target_pairs={{0,12},{1,13},{2,14},{3,15},{4,8},{5,9},{6,10},{7,11},{8,4},{9,5},... | collective-permute-start | bytes 12296 | tf_op jit(solution)/shard_map/ppermute | solution.py:456
  49.2 3.7 %collective-permute-start.13 = (f32[8,128]{1,0:T(8,128)S(1)}, f32[8,128]{1,0:T(8,128)S(1)}, u32[]{:S(2)}, u32[]{:S(2)}) collective-permute-start(f32[8,128]{1,0:T(8,128)S(1)} %add_up.1), channel_id=1, source_target_pairs={{0,1},{1,0},{2,3},{3,2},{4,5},{5,4},{6,7},{7,6},{8,9},{9,8},{10,11... | collective-permute-start | bytes 12296 | tf_op jit(solution)/shard_map/ppermute | solution.py:456
  51.5 3.6 %collective-permute-start.14 = (f32[8,128]{1,0:T(8,128)S(1)}, f32[8,128]{1,0:T(8,128)S(1)}, u32[]{:S(2)}, u32[]{:S(2)}) collective-permute-start(f32[8,128]{1,0:T(8,128)S(1)} %add_up.1), channel_id=1, source_target_pairs={{0,2},{1,3},{2,0},{3,1},{4,6},{5,7},{6,4},{7,5},{8,10},{9,11},{10,... | collective-permute-start | bytes 12296 | tf_op jit(solution)/shard_map/ppermute | solution.py:456
  52.9 3.0 %collective-permute-start.15 = (f32[8,128]{1,0:T(8,128)S(1)}, f32[8,128]{1,0:T(8,128)S(1)}, u32[]{:S(2)}, u32[]{:S(2)}) collective-permute-start(f32[8,128]{1,0:T(8,128)S(1)} %add_up.1), channel_id=1, source_target_pairs={{0,3},{1,2},{2,1},{3,0},{4,7},{5,6},{6,5},{7,4},{8,11},{9,10},{10,... | collective-permute-start | bytes 12296 | tf_op jit(solution)/shard_map/ppermute | solution.py:456

commit v14 on v11

--- a/solution.py
+++ b/solution.py
@@ -420,33 +420,48 @@
     )
 
 
-def add_up(arrays, token):
+def copies_of(rows):
+    return [((rows * n, LANES), F32) for n in (1, 2, 3)]
+
+
+def spread_out(outs, value):
+    for out in outs:
+        out[...] = jnp.concatenate([value] * (out.shape[0] // value.shape[0]), axis=0)
+
+
+def add_up(arrays, token, name):
+    rows = arrays[0].shape[0]
+
     def body(*refs):
-        refs[-1][...] = sum(ref[...] for ref in refs[:-2])
+        total = refs[0][...]
+        for ref in refs[1 : len(arrays)]:
+            total = total + ref[:rows, :]
+        spread_out(refs[len(arrays) + len(token) :], total)
 
     return call(
         body,
-        vmem(*arrays, token),
-        [(arrays[0].shape, F32, pltpu.VMEM)],
+        vmem(*arrays, *token),
+        [(*size, pltpu.VMEM) for size in copies_of(rows)],
         [],
-        "add_up",
-    )[0]
-
-
-def sum_over_ring(value, ring, token):
+        name,
+    )
+
+
+def sum_over_ring(values, ring, token):
     if ring & (ring - 1):
-        return lax.psum(value, RING)
+        return lax.psum(values[0], RING)
     rounds, size = [], 1
     while size < ring:
         digits = (1, 2, 3) if 4 * size <= ring else (1,)
         rounds.append([size * d for d in digits])
         size *= len(digits) + 1
     for i, bits in enumerate(reversed(rounds)):
-        parts = [value] + [
-            lax.ppermute(value, RING, [(j, j ^ bit) for j in range(ring)]) for bit in bits
+        received = [
+            lax.ppermute(value, RING, [(j, j ^ bit) for j in range(ring)])
+            for value, bit in zip(values, bits)
         ]
-        value = add_up(parts, token) if i == 0 else sum(parts)
-    return value
+        values = add_up([values[0], *received], [token] if i == 0 else [], f"add_up_{i}")
+    return values[0]
 
 
 def local(positions, momenta, tile_values, tile_rows, tile_cols, tile_count, channel_coupling):
@@ -587,7 +602,7 @@
         place = lax.broadcasted_iota(jnp.int32, (replicas, LANES), 1)
         which = lax.broadcasted_iota(jnp.int32, (replicas, LANES), 0)
         flat = jnp.sum(jnp.where(place == which, total, 0.0), axis=0, keepdims=True)
-        outs[len(piece)][...] = jnp.broadcast_to(flat, (8, LANES))
+        spread_out(outs[len(piece) :], jnp.broadcast_to(flat, (8, LANES)))
 
     results = far_fields(
         lists,
@@ -595,18 +610,19 @@
         near[1:],
         new_fars[1],
         weights,
-        [(wide, BF16)] * len(piece) + [((8, LANES), F32)],
+        [(wide, BF16)] * len(piece) + copies_of(8),
         last_work,
         "far_second_1",
         through=[near[0], *xs, *base, mixing],
     )
-    fields, partial, kept = results[: len(piece)], results[len(piece)], results[len(piece) + 1 :]
+    sent = len(piece) + len(copies_of(8))
+    fields, partials, kept = results[: len(piece)], results[len(piece) : sent], results[sent:]
     fields, kept = [kept[0], *fields], kept[1:]
 
     x_new, y_new, token = finish(
         fields, kept[:groups], kept[groups : 2 * groups], kept[2 * groups], channels
     )
-    total = sum_over_ring(partial, ring, token)
+    total = sum_over_ring(partials, ring, token)
     energy = total[0, :replicas] / jnp.sqrt(jnp.float32(cells * ring * channels))
     return (x_new, y_new, energy)
 

time: 54.4 us -> 54.9 us (level)
  Pallas kernels: 18 us -> 19 us
    ppermute x6, starting transfers between devices: 10.6 us -> 9.54 us  [near_swap(): return lax.ppermute(mine, RING, on_chip)]
    pallas_call x12 -> x13, Pallas kernels: 18 us -> 19 us  [call(): pl.pallas_call(body, in_specs=[pl.BlockSpec(memory_space=pl.ANY if s is p...]
    ppermute x4, starting transfers between devices: 10.1 us -> 10.9 us  [far_swap(): return lax.ppermute(mine, RING, off_chip)]
where the time goes in v14:
time: 54.9 us; the launch traced here: 54.3 us
  starting transfers between devices  28 us (51%)
  Pallas kernels  19 us (35%)
  waiting for transfers between devices  4.71 us (9%)
  between operations  1.57 us (3%)
    pallas_call x13, Pallas kernels, call(): pl.pallas_call(body, in_specs=[pl.BlockSpec(memory_space=pl.ANY if s is p...  19 us
    ppermute x4, starting transfers between devices, far_swap(): return lax.ppermute(mine, RING, off_chip)  10.9 us
    ppermute x6, starting transfers between devices, near_swap(): return lax.ppermute(mine, RING, on_chip)  9.54 us
    ppermute x6, starting transfers between devices, sum_over_ring(): lax.ppermute(value, RING, [(j, j ^ bit) for j in range(ring)])  7.61 us
    ppermute x4, waiting for transfers between devices, far_swap(): return lax.ppermute(mine, RING, off_chip)  2.95 us
    ppermute x6, waiting for transfers between devices, sum_over_ring(): lax.ppermute(value, RING, [(j, j ^ bit) for j in range(ring)])  1.65 us
  transfers between devices with their start and end apart: 16, of which 4 were waited for; matrix products, arithmetic and copies ran while one was open for 0% of the time, Pallas kernels for 29%

profile of v14, /device:TPU:0, one launch (start us, length us, event | category | flops | bytes accessed | tf_op | source)
XLA Modules:
  0.0 54.3 jit_solution(1791218248476103528)
XLA Ops:
  0.7 1.4 %load_first.1 = (f32[1024,128]{1,0:T(8,128)S(1)}, f32[1024,128]{1,0:T(8,128)S(1)}, bf16[1024,128]{1,0:T(8,128)(2,1)S(1)}, bf16[1024,128]{1,0:T(8,128)(2,1)S(1)}, bf16[1024,256]{1,0:T(8,128)(2,1)S(1)}) custom-call(f32[1024,384]{1,0:T(8,128)} %x_ref.3), custom_call_target="tpu_custom_call" | custom-call | flops 1000 | bytes 1000 | tf_op jit(solution)/shard_map/load_first/pallas_call | solution.py:21
  2.1 5.5 %collective-permute-start.4 = (bf16[1024,256]{1,0:T(8,128)(2,1)S(1)}, bf16[1024,256]{1,0:T(8,128)(2,1)S(1)}, u32[]{:S(2)}, u32[]{:S(2)}) collective-permute-start(bf16[1024,256]{1,0:T(8,128)(2,1)S(1)} %get-tuple-element.60._), channel_id=1, source_target_pairs={{0,15},{1,2},{2,1},{3,4},{4,3},{5,6},{6,5},{7,8},{8,7},{9,10},{10,... | collective-permute-start | bytes 1572872 | tf_op jit(solution)/shard_map/ppermute | solution.py:492
  7.6 0.5 collective-permute-start.1
  8.8 2.2 %make_lists.1 = (s32[214]{0:T(256)S(4)}, f32[1024,128]{1,0:T(8,128)S(1)}, bf16[1024,128]{1,0:T(8,128)(2,1)S(1)}) custom-call(s32[96]{0:T(128)S(1)} %copy-done.5, s32[96]{0:T(128)S(1)} %copy-done.6, s32[1]{0:T(128)S(6)} %copy.28.count_hbm, f32[1024,384]{1,0:T(8,128)} %x_ref.3, bf16[1024,256]{1,0:T(8,128)(2,1)S(1)} %get-tuple-element.60._), custom_call_target="tpu_custom_call" | custom-call | flops 1000 | bytes 1000 | tf_op jit(solution)/shard_map/make_lists/pallas_call | solution.py:21
  11.0 0.1 collective-permute-start.2
  11.1 1.3 %first_base.1 = (f32[1024,128]{1,0:T(8,128)S(1)}, f32[1024,128]{1,0:T(8,128)S(1)}, f32[1024,128]{1,0:T(8,128)S(1)}, bf16[384,384]{1,0:T(8,128)(2,1)S(1)}) custom-call(f32[1024,128]{1,0:T(8,128)S(1)} %get-tuple-element.65.refs_0_.refs_4_, f32[1024,128]{1,0:T(8,128)S(1)} %get-tuple-element.66.refs_1_.refs_5_.refs_7_, ...), custom_call_target="tpu_custom_call" | custom-call | flops 1000 | bytes 1000 | tf_op jit(solution)/shard_map/first_base/pallas_call | solution.py:21
  12.5 0.1 collective-permute-done.2.refs_5_
  12.6 0.4 copy-done
  13.0 2.3 %near_first.1 = (f32[1024,128]{1,0:T(8,128)S(1)}, f32[1024,128]{1,0:T(8,128)S(1)}, f32[1024,128]{1,0:T(8,128)S(1)}, bf16[1024,128]{1,0:T(8,128)(2,1)S(1)}) custom-call(s32[214]{0:T(256)S(4)} %get-tuple-element.61.list_ref, bf16[96,128,128]{2,1,0:T(8,128)(2,1)S(1)} %copy-done, bf16[1024,128]{1,0:T(8,128)(2,1)S(1)} %get-tuple-element.62.refs_0_, ...), custom_call_target="tpu_custom_call" | custom-call | flops 1000 | bytes 1000 | tf_op jit(solution)/shard_map/near_first/pallas_call | solution.py:21
  15.3 1.1 %collective-permute-start.3 = (bf16[1024,128]{1,0:T(8,128)(2,1)S(1)}, bf16[1024,128]{1,0:T(8,128)(2,1)S(1)}, u32[]{:S(2)}, u32[]{:S(2)}) collective-permute-start(bf16[1024,128]{1,0:T(8,128)(2,1)S(1)} %get-tuple-element.69), channel_id=1, source_target_pairs={{0,15},{1,2},{2,1},{3,4},{4,3},{5,6},{6,5},{7,8},{8,7},{9,10},{10,... | collective-permute-start | bytes 786440 | tf_op jit(solution)/shard_map/ppermute | solution.py:492
  16.5 1.2 %far_first_0.1 = (bf16[1024,128]{1,0:T(8,128)(2,1)S(1)}, bf16[1024,128]{1,0:T(8,128)(2,1)S(1)}, bf16[1024,128]{1,0:T(8,128)(2,1)S(1)}, bf16[1024,128]{1,0:T(8,12...) custom-call(s32[214]{0:T(256)S(4)} %get-tuple-element.61.list_ref, bf16[96,128,128]{2,1,0:T(8,128)(2,1)S(1)} %copy-done, ...), custom_call_target="tpu_custom_call" | custom-call | flops 1000 | bytes 1000 | tf_op jit(solution)/shard_map/far_first_0/pallas_call | solution.py:21
  17.7 3.2 %collective-permute-start.9 = (bf16[1024,128]{1,0:T(8,128)(2,1)S(1)}, bf16[1024,128]{1,0:T(8,128)(2,1)S(1)}, u32[]{:S(2)}, u32[]{:S(2)}) collective-permute-start(bf16[1024,128]{1,0:T(8,128)(2,1)S(1)} %get-tuple-element.82), channel_id=1, source_target_pairs={{0,15},{1,2},{2,1},{3,4},{4,3},{5,6},{6,5},{7,8},{8,7},{9,10},{10,... | collective-permute-start | bytes 786440 | tf_op jit(solution)/shard_map/ppermute | solution.py:492
  21.0 2.9 %collective-permute-done.3.far_ref = bf16[1024,128]{1,0:T(8,128)(2,1)S(1)} collective-permute-done((bf16[1024,128]{1,0:T(8,128)(2,1)S(1)}, bf16[1024,128]{1,0:T(8,128)(2,1)S(1)}, u32[]{:S(2)}, u32[]{:S(2)}) %collective-permute-start.3) | collective-permute-done | bytes 262176 | tf_op jit(solution)/shard_map/ppermute | solution.py:492
  23.9 1.3 %far_first_1.1 = (bf16[1024,256]{1,0:T(8,128)(2,1)S(1)}, bf16[1024,128]{1,0:T(8,128)(2,1)S(1)}, bf16[1024,128]{1,0:T(8,128)(2,1)S(1)}, bf16[1024,128]{1,0:T(8,128)(2,1)S(1)}) custom-call(s32[214]{0:T(256)S(4)} %get-tuple-element.61.list_ref, bf16[96,128,128]{2,1,0:T(8,128)(2,1)S(1)} %copy-done, bf16[1024,128]{1,0:T(8,128)(2,1)S(1)} %collective-permute-done.3.far_ref, ...), custom_call_target="tpu_custom_call" | custom-call | flops 1000 | bytes 1000 | tf_op jit(solution)/shard_map/far_first_1/pallas_call | solution.py:21
  25.2 1.0 %collective-permute-start.5 = (bf16[1024,256]{1,0:T(8,128)(2,1)S(1)}, bf16[1024,256]{1,0:T(8,128)(2,1)S(1)}, u32[]{:S(2)}, u32[]{:S(2)}) collective-permute-start(bf16[1024,256]{1,0:T(8,128)(2,1)S(1)} %get-tuple-element.78), channel_id=1, source_target_pairs={{0,15},{1,2},{2,1},{3,4},{4,3},{5,6},{6,5},{7,8},{8,7},{9,10},{10,... | collective-permute-start | bytes 1572872 | tf_op jit(solution)/shard_map/ppermute | solution.py:492
  26.2 8.4 %collective-permute-start.6 = (bf16[1024,128]{1,0:T(8,128)(2,1)S(1)}, bf16[1024,128]{1,0:T(8,128)(2,1)S(1)}, u32[]{:S(2)}, u32[]{:S(2)}) collective-permute-start(bf16[1024,128]{1,0:T(8,128)(2,1)S(1)} %get-tuple-element.79.refs_0_.refs_9_), channel_id=1, source_target_pairs={{0,1},{1,0},{2,3},{3,2},{4,5},{5,4},{6,7},{7,6},{8,9},{9,8},{10,11... | collective-permute-start | bytes 786440 | tf_op jit(solution)/shard_map/ppermute | solution.py:495
  34.7 0.5 collective-permute-start.8
  35.2 2.0 %second_base.1 = (f32[1024,128]{1,0:T(8,128)S(1)}, f32[1024,128]{1,0:T(8,128)S(1)}, f32[1024,128]{1,0:T(8,128)S(1)}, f32[1024,128]{1,0:T(8,128)S(1)}, f32[1024,1...) custom-call(f32[1024,128]{1,0:T(8,128)S(1)} %get-tuple-element.85.refs_0_.refs_6_, ...), custom_call_target="tpu_custom_call" | custom-call | flops 1000 | bytes 1000 | tf_op jit(solution)/shard_map/second_base/pallas_call | solution.py:21
  37.3 0.8 %far_second_0.1.refs_6_ = f32[1024,128]{1,0:T(8,128)S(1)} custom-call(s32[214]{0:T(256)S(4)} %get-tuple-element.61.list_ref, bf16[96,128,128]{2,1,0:T(8,128)(2,1)S(1)} %copy-done, bf16[1024,128]{1,0:T(8,128)(2,1)S(1)} %collective-permute-done.9.far_ref), custom_call_target="tpu_custom_call" | custom-call | flops 4000000000 | bytes 1000 | tf_op jit(solution)/shard_map/far_second_0/pallas_call | solution.py:21
  38.1 2.3 %near_second.1 = (bf16[1024,128]{1,0:T(8,128)(2,1)S(1)}, f32[1024,128]{1,0:T(8,128)S(1)}, f32[1024,128]{1,0:T(8,128)S(1)}) custom-call(s32[214]{0:T(256)S(4)} %get-tuple-element.61.list_ref, bf16[96,128,128]{2,1,0:T(8,128)(2,1)S(1)} %copy-done, bf16[1024,128]{1,0:T(8,128)(2,1)S(1)} %get-tuple-element.79.refs_0_.refs_9_, ...), custom_call_target="tpu_custom_call" | custom-call | flops 1000 | bytes 1000 | tf_op jit(solution)/shard_map/near_second/pallas_call | solution.py:21
  40.4 1.3 %far_second_1.1 = (bf16[1024,128]{1,0:T(8,128)(2,1)S(1)}, bf16[1024,128]{1,0:T(8,128)(2,1)S(1)}, f32[8,128]{1,0:T(8,128)S(1)}, f32[16,128]{1,0:T(8,128)S(1)}, f3...) custom-call(s32[214]{0:T(256)S(4)} %get-tuple-element.61.list_ref, ...), custom_call_target="tpu_custom_call", output_to_operand_aliasing={{5}: (8, {}), {6}: (9, {}), {7}: (10, {}), {8}: (11, {}), {... | custom-call | flops 1000 | bytes 1000 | tf_op jit(solution)/shard_map/far_second_1/pallas_call | solution.py:21
  41.7 1.8 %collective-permute-start.12 = (f32[24,128]{1,0:T(8,128)S(1)}, f32[24,128]{1,0:T(8,128)S(1)}, u32[]{:S(2)}, u32[]{:S(2)}) collective-permute-start(f32[24,128]{1,0:T(8,128)S(1)} %get-tuple-element.111), channel_id=1, source_target_pairs={{0,12},{1,13},{2,14},{3,15},{4,8},{5,9},{6,10},{7,11},{8,4},{9,5},... | collective-permute-start | bytes 36872 | tf_op jit(solution)/shard_map/ppermute | solution.py:460
  43.5 0.1 collective-permute-start.11
  43.6 2.6 %collective-permute-start.10 = (f32[8,128]{1,0:T(8,128)S(1)}, f32[8,128]{1,0:T(8,128)S(1)}, u32[]{:S(2)}, u32[]{:S(2)}) collective-permute-start(f32[8,128]{1,0:T(8,128)S(1)} %get-tuple-element.109.refs_0_), channel_id=1, source_target_pairs={{0,4},{1,5},{2,6},{3,7},{4,0},{5,1},{6,2},{7,3},{8,12},{9,13},{10,... | collective-permute-start | bytes 12296 | tf_op jit(solution)/shard_map/ppermute | solution.py:460
  46.1 2.2 %finish.1 = (f32[1024,384]{1,0:T(8,128)}, f32[1024,384]{1,0:T(8,128)}, f32[8,128]{1,0:T(8,128)S(1)}) custom-call(bf16[1024,128]{1,0:T(8,128)(2,1)S(1)} %get-tuple-element.97.refs_0_, bf16[1024,128]{1,0:T(8,128)(2,1)S(1)} %get-tuple-element.98.refs_1_, bf16[1024,128]{1,0:T(8,128)(2,1)S(1)} %get-tuple-element.99.refs_2_, ...), custom_call_target="tpu_custom_call" | custom-call | flops 1000 | bytes 1000 | tf_op jit(solution)/shard_map/finish/pallas_call | solution.py:21
  48.3 0.1 collective-permute-start.15
  48.4 3.1 %collective-permute-start.14 = (f32[16,128]{1,0:T(8,128)S(1)}, f32[16,128]{1,0:T(8,128)S(1)}, u32[]{:S(2)}, u32[]{:S(2)}) collective-permute-start(f32[16,128]{1,0:T(8,128)S(1)} %get-tuple-element.114), channel_id=1, source_target_pairs={{0,2},{1,3},{2,0},{3,1},{4,6},{5,7},{6,4},{7,5},{8,10},{9,11},{10,... | collective-permute-start | bytes 24584 | tf_op jit(solution)/shard_map/ppermute | solution.py:460
  51.5 0.0 collective-permute-start.13
  51.5 1.1 %collective-permute-done.13.refs_1_ = f32[8,128]{1,0:T(8,128)S(1)} collective-permute-done((f32[8,128]{1,0:T(8,128)S(1)}, f32[8,128]{1,0:T(8,128)S(1)}, u32[]{:S(2)}, u32[]{:S(2)}) %collective-permute-start.13) | collective-permute-done | bytes 4128 | tf_op jit(solution)/shard_map/ppermute | solution.py:460
  52.7 0.5 collective-permute-done.14.refs_2_
  53.2 0.6 %add_up_1.1 = (f32[8,128]{1,0:T(8,128)S(1)}, f32[16,128]{1,0:T(8,128)}, f32[24,128]{1,0:T(8,128)}) custom-call(f32[8,128]{1,0:T(8,128)S(1)} %get-tuple-element.113.refs_0_, f32[8,128]{1,0:T(8,128)S(1)} %collective-permute-done.13.refs_1_, f32[16,128]{1,0:T(8,128)S(1)} %collective-permute-done.14.refs_2_, f32[24,128]{1,0:T(8,128)S(1)} %collective-permute-done.15.refs_3_), custom_call_target="tpu_custom_call" | custom-call | flops 1000 | bytes 1000 | tf_op jit(solution)/shard_map/add_up_1/pallas_call | solution.py:21
  53.8 0.5 multiply_bitcast_fusion
  (28 shorter events, 0.1 us)
Async XLA Ops:
  0.6 10.4 %copy-start.2 = (bf16[384,384]{1,0:T(8,128)(2,1)S(1)}, bf16[384,384]{1,0:T(8,128)(2,1)}, u32[]{:S(2)}) copy-start(bf16[384,384]{1,0:T(8,128)(2,1)} %constant.7.clone.refs_4_.refs_12_) | copy-start | bytes 884740
  0.6 10.4 %copy-start.3 = (bf16[384,48]{1,0:T(8,128)(2,1)S(1)}, bf16[384,48]{1,0:T(8,128)(2,1)}, u32[]{:S(2)}) copy-start(bf16[384,48]{1,0:T(8,128)(2,1)} %constant.8.clone.refs_5_) | copy-start | bytes 110596
  0.7 8.1 %copy-start.6 = (s32[96]{0:T(128)S(1)}, s32[96]{0:T(128)}, u32[]{:S(2)}) copy-start(s32[96]{0:T(128)} %cols_hbm.1) | copy-start | bytes 1156
  0.7 8.1 %copy-start.5 = (s32[96]{0:T(128)S(1)}, s32[96]{0:T(128)}, u32[]{:S(2)}) copy-start(s32[96]{0:T(128)} %rows_hbm.1) | copy-start | bytes 1156
  0.7 10.4 %copy-start.4 = (bf16[48,48]{1,0:T(8,128)(2,1)S(1)}, bf16[48,48]{1,0:T(8,128)(2,1)}, u32[]{:S(2)}) copy-start(bf16[48,48]{1,0:T(8,128)(2,1)} %refs_6_.1) | copy-start | bytes 13828
  0.7 10.4 %copy-start.1 = (f32[1024,384]{1,0:T(8,128)S(1)}, f32[1024,384]{1,0:T(8,128)}, u32[]{:S(2)}) copy-start(f32[1024,384]{1,0:T(8,128)} %refs_3_.1) | copy-start | bytes 4718596
  2.1 14.4 %collective-permute-start.4 = (bf16[1024,256]{1,0:T(8,128)(2,1)S(1)}, bf16[1024,256]{1,0:T(8,128)(2,1)S(1)}, u32[]{:S(2)}, u32[]{:S(2)}) collective-permute-start(bf16[1024,256]{1,0:T(8,128)(2,1)S(1)} %get-tuple-element.60._), channel_id=1, source_target_pairs={{0,15},{1,2},{2,1},{3,4},{4,3},{5,6},{6,5},{7,8},{8,7},{9,10},{10,... | collective-permute-start | bytes 1572872 | tf_op jit(solution)/shard_map/ppermute | solution.py:492
  7.6 4.8 %collective-permute-start = (bf16[1024,128]{1,0:T(8,128)(2,1)S(1)}, bf16[1024,128]{1,0:T(8,128)(2,1)S(1)}, u32[]{:S(2)}, u32[]{:S(2)}) collective-permute-start(bf16[1024,128]{1,0:T(8,128)(2,1)S(1)} %get-tuple-element.62.refs_0_), channel_id=1, source_target_pairs={{0,1},{1,0},{2,3},{3,2},{4,5},{5,4},{6,7},{7,6},{8,9},{9,8},{10,11... | collective-permute-start | bytes 786440 | tf_op jit(solution)/shard_map/ppermute | solution.py:495
  7.6 4.8 %collective-permute-start.1 = (bf16[1024,128]{1,0:T(8,128)(2,1)S(1)}, bf16[1024,128]{1,0:T(8,128)(2,1)S(1)}, u32[]{:S(2)}, u32[]{:S(2)}) collective-permute-start(bf16[1024,128]{1,0:T(8,128)(2,1)S(1)} %get-tuple-element.63.refs_1_), channel_id=1, source_target_pairs={{0,1},{1,0},{2,3},{3,2},{4,5},{5,4},{6,7},{7,6},{8,9},{9,8},{10,11... | collective-permute-start | bytes 786440 | tf_op jit(solution)/shard_map/ppermute | solution.py:495
  11.0 1.6 %collective-permute-start.2 = (bf16[1024,128]{1,0:T(8,128)(2,1)S(1)}, bf16[1024,128]{1,0:T(8,128)(2,1)S(1)}, u32[]{:S(2)}, u32[]{:S(2)}) collective-permute-start(bf16[1024,128]{1,0:T(8,128)(2,1)S(1)} %get-tuple-element.64.refs_2_.refs_6_), channel_id=1, source_target_pairs={{0,1},{1,0},{2,3},{3,2},{4,5},{5,4},{6,7},{7,6},{8,9},{9,8},{10,11... | collective-permute-start | bytes 786440 | tf_op jit(solution)/shard_map/ppermute | solution.py:495
  11.1 1.9 %copy-start = (bf16[96,128,128]{2,1,0:T(8,128)(2,1)S(1)}, bf16[96,128,128]{2,1,0:T(8,128)(2,1)}, u32[]{:S(2)}) copy-start(bf16[96,128,128]{2,1,0:T(8,128)(2,1)} %tiles_ref.11) | copy-start | bytes 9437188
  15.3 8.6 %collective-permute-start.3 = (bf16[1024,128]{1,0:T(8,128)(2,1)S(1)}, bf16[1024,128]{1,0:T(8,128)(2,1)S(1)}, u32[]{:S(2)}, u32[]{:S(2)}) collective-permute-start(bf16[1024,128]{1,0:T(8,128)(2,1)S(1)} %get-tuple-element.69), channel_id=1, source_target_pairs={{0,15},{1,2},{2,1},{3,4},{4,3},{5,6},{6,5},{7,8},{8,7},{9,10},{10,... | collective-permute-start | bytes 786440 | tf_op jit(solution)/shard_map/ppermute | solution.py:492
  17.7 19.5 %collective-permute-start.9 = (bf16[1024,128]{1,0:T(8,128)(2,1)S(1)}, bf16[1024,128]{1,0:T(8,128)(2,1)S(1)}, u32[]{:S(2)}, u32[]{:S(2)}) collective-permute-start(bf16[1024,128]{1,0:T(8,128)(2,1)S(1)} %get-tuple-element.82), channel_id=1, source_target_pairs={{0,15},{1,2},{2,1},{3,4},{4,3},{5,6},{6,5},{7,8},{8,7},{9,10},{10,... | collective-permute-start | bytes 786440 | tf_op jit(solution)/shard_map/ppermute | solution.py:492
  25.2 15.2 %collective-permute-start.5 = (bf16[1024,256]{1,0:T(8,128)(2,1)S(1)}, bf16[1024,256]{1,0:T(8,128)(2,1)S(1)}, u32[]{:S(2)}, u32[]{:S(2)}) collective-permute-start(bf16[1024,256]{1,0:T(8,128)(2,1)S(1)} %get-tuple-element.78), channel_id=1, source_target_pairs={{0,15},{1,2},{2,1},{3,4},{4,3},{5,6},{6,5},{7,8},{8,7},{9,10},{10,... | collective-permute-start | bytes 1572872 | tf_op jit(solution)/shard_map/ppermute | solution.py:492
  26.2 11.8 %collective-permute-start.6 = (bf16[1024,128]{1,0:T(8,128)(2,1)S(1)}, bf16[1024,128]{1,0:T(8,128)(2,1)S(1)}, u32[]{:S(2)}, u32[]{:S(2)}) collective-permute-start(bf16[1024,128]{1,0:T(8,128)(2,1)S(1)} %get-tuple-element.79.refs_0_.refs_9_), channel_id=1, source_target_pairs={{0,1},{1,0},{2,3},{3,2},{4,5},{5,4},{6,7},{7,6},{8,9},{9,8},{10,11... | collective-permute-start | bytes 786440 | tf_op jit(solution)/shard_map/ppermute | solution.py:495
  34.7 3.4 %collective-permute-start.7 = (bf16[1024,128]{1,0:T(8,128)(2,1)S(1)}, bf16[1024,128]{1,0:T(8,128)(2,1)S(1)}, u32[]{:S(2)}, u32[]{:S(2)}) collective-permute-start(bf16[1024,128]{1,0:T(8,128)(2,1)S(1)} %get-tuple-element.80.refs_1_.refs_10_), channel_id=1, source_target_pairs={{0,1},{1,0},{2,3},{3,2},{4,5},{5,4},{6,7},{7,6},{8,9},{9,8},{10,11... | collective-permute-start | bytes 786440 | tf_op jit(solution)/shard_map/ppermute | solution.py:495
  34.7 3.4 %collective-permute-start.8 = (bf16[1024,128]{1,0:T(8,128)(2,1)S(1)}, bf16[1024,128]{1,0:T(8,128)(2,1)S(1)}, u32[]{:S(2)}, u32[]{:S(2)}) collective-permute-start(bf16[1024,128]{1,0:T(8,128)(2,1)S(1)} %get-tuple-element.81.refs_2_.refs_11_), channel_id=1, source_target_pairs={{0,1},{1,0},{2,3},{3,2},{4,5},{5,4},{6,7},{7,6},{8,9},{9,8},{10,11... | collective-permute-start | bytes 786440 | tf_op jit(solution)/shard_map/ppermute | solution.py:495
  41.7 6.6 %collective-permute-start.12 = (f32[24,128]{1,0:T(8,128)S(1)}, f32[24,128]{1,0:T(8,128)S(1)}, u32[]{:S(2)}, u32[]{:S(2)}) collective-permute-start(f32[24,128]{1,0:T(8,128)S(1)} %get-tuple-element.111), channel_id=1, source_target_pairs={{0,12},{1,13},{2,14},{3,15},{4,8},{5,9},{6,10},{7,11},{8,4},{9,5},... | collective-permute-start | bytes 36872 | tf_op jit(solution)/shard_map/ppermute | solution.py:460
  43.5 4.8 %collective-permute-start.11 = (f32[16,128]{1,0:T(8,128)S(1)}, f32[16,128]{1,0:T(8,128)S(1)}, u32[]{:S(2)}, u32[]{:S(2)}) collective-permute-start(f32[16,128]{1,0:T(8,128)S(1)} %get-tuple-element.110), channel_id=1, source_target_pairs={{0,8},{1,9},{2,10},{3,11},{4,12},{5,13},{6,14},{7,15},{8,0},{9,1},... | collective-permute-start | bytes 24584 | tf_op jit(solution)/shard_map/ppermute | solution.py:460
  43.6 4.7 %collective-permute-start.10 = (f32[8,128]{1,0:T(8,128)S(1)}, f32[8,128]{1,0:T(8,128)S(1)}, u32[]{:S(2)}, u32[]{:S(2)}) collective-permute-start(f32[8,128]{1,0:T(8,128)S(1)} %get-tuple-element.109.refs_0_), channel_id=1, source_target_pairs={{0,4},{1,5},{2,6},{3,7},{4,0},{5,1},{6,2},{7,3},{8,12},{9,13},{10,... | collective-permute-start | bytes 12296 | tf_op jit(solution)/shard_map/ppermute | solution.py:460
  48.3 4.9 %collective-permute-start.15 = (f32[24,128]{1,0:T(8,128)S(1)}, f32[24,128]{1,0:T(8,128)S(1)}, u32[]{:S(2)}, u32[]{:S(2)}) collective-permute-start(f32[24,128]{1,0:T(8,128)S(1)} %get-tuple-element.115), channel_id=1, source_target_pairs={{0,3},{1,2},{2,1},{3,0},{4,7},{5,6},{6,5},{7,4},{8,11},{9,10},{10,... | collective-permute-start | bytes 36872 | tf_op jit(solution)/shard_map/ppermute | solution.py:460
  48.4 4.8 %collective-permute-start.14 = (f32[16,128]{1,0:T(8,128)S(1)}, f32[16,128]{1,0:T(8,128)S(1)}, u32[]{:S(2)}, u32[]{:S(2)}) collective-permute-start(f32[16,128]{1,0:T(8,128)S(1)} %get-tuple-element.114), channel_id=1, source_target_pairs={{0,2},{1,3},{2,0},{3,1},{4,6},{5,7},{6,4},{7,5},{8,10},{9,11},{10,... | collective-permute-start | bytes 24584 | tf_op jit(solution)/shard_map/ppermute | solution.py:460
  51.5 1.2 %collective-permute-start.13 = (f32[8,128]{1,0:T(8,128)S(1)}, f32[8,128]{1,0:T(8,128)S(1)}, u32[]{:S(2)}, u32[]{:S(2)}) collective-permute-start(f32[8,128]{1,0:T(8,128)S(1)} %get-tuple-element.113.refs_0_), channel_id=1, source_target_pairs={{0,1},{1,0},{2,3},{3,2},{4,5},{5,4},{6,7},{7,6},{8,9},{9,8},{10,11... | collective-permute-start | bytes 12296 | tf_op jit(solution)/shard_map/ppermute | solution.py:460

commit v15 on v14

--- a/solution.py
+++ b/solution.py
@@ -460,6 +460,9 @@
             lax.ppermute(value, RING, [(j, j ^ bit) for j in range(ring)])
             for value, bit in zip(values, bits)
         ]
+        if i == len(rounds) - 1:
+            rows = values[0].shape[0]
+            return values[0] + sum(part[:rows] for part in received)
         values = add_up([values[0], *received], [token] if i == 0 else [], f"add_up_{i}")
     return values[0]
 

time: 54.9 us -> 54.8 us (level)
  starting transfers between devices: 28 us -> 31.5 us
  Pallas kernels: 19 us -> 16.4 us
    pallas_call x13 -> x12, Pallas kernels: 19 us -> 16.4 us  [call(): pl.pallas_call(body, in_specs=[pl.BlockSpec(memory_space=pl.ANY if s is p...]
    ppermute x6, starting transfers between devices: 7.61 us -> 9.14 us  [sum_over_ring(): lax.ppermute(value, RING, [(j, j ^ bit) for j in range(ring)])]
    ppermute x4, starting transfers between devices: 10.9 us -> 11.9 us  [far_swap(): return lax.ppermute(mine, RING, off_chip)]
    ppermute x6, starting transfers between devices: 9.54 us -> 10.4 us  [near_swap(): return lax.ppermute(mine, RING, on_chip)]
  transfers between devices with their start and end apart: 16 -> 16, of which waited for: 4 -> 3; matrix products, arithmetic and copies ran while one was open for 0% -> 0% of each run, Pallas kernels for 29% -> 25%
where the time goes in v15:
time: 54.8 us; the launch traced here: 54.7 us
  starting transfers between devices  31.5 us (57%)
  Pallas kernels  16.4 us (30%)
  waiting for transfers between devices  4.26 us (8%)
  between operations  1.54 us (3%)
    pallas_call x12, Pallas kernels, call(): pl.pallas_call(body, in_specs=[pl.BlockSpec(memory_space=pl.ANY if s is p...  16.4 us
    ppermute x4, starting transfers between devices, far_swap(): return lax.ppermute(mine, RING, off_chip)  11.9 us
    ppermute x6, starting transfers between devices, near_swap(): return lax.ppermute(mine, RING, on_chip)  10.4 us
    ppermute x6, starting transfers between devices, sum_over_ring(): lax.ppermute(value, RING, [(j, j ^ bit) for j in range(ring)])  9.14 us
    ppermute x4, waiting for transfers between devices, far_swap(): return lax.ppermute(mine, RING, off_chip)  2.59 us
    ppermute x6, waiting for transfers between devices, sum_over_ring(): lax.ppermute(value, RING, [(j, j ^ bit) for j in range(ring)])  1.65 us
  transfers between devices with their start and end apart: 16, of which 3 were waited for; matrix products, arithmetic and copies ran while one was open for 0% of the time, Pallas kernels for 25%

profile of v15, /device:TPU:0, one launch (start us, length us, event | category | flops | bytes accessed | tf_op | source)
XLA Modules:
  0.0 54.7 jit_solution(6270017146975344248)
XLA Ops:
  0.6 0.0 copy-start.2
  0.6 0.0 copy-start.3
  0.7 1.4 %load_first.1 = (f32[1024,128]{1,0:T(8,128)S(1)}, f32[1024,128]{1,0:T(8,128)S(1)}, bf16[1024,128]{1,0:T(8,128)(2,1)S(1)}, bf16[1024,128]{1,0:T(8,128)(2,1)S(1)}, bf16[1024,256]{1,0:T(8,128)(2,1)S(1)}) custom-call(f32[1024,384]{1,0:T(8,128)} %x_ref.3), custom_call_target="tpu_custom_call" | custom-call | flops 1000 | bytes 1000 | tf_op jit(solution)/shard_map/load_first/pallas_call | solution.py:21
  2.1 5.5 %collective-permute-start.4 = (bf16[1024,256]{1,0:T(8,128)(2,1)S(1)}, bf16[1024,256]{1,0:T(8,128)(2,1)S(1)}, u32[]{:S(2)}, u32[]{:S(2)}) collective-permute-start(bf16[1024,256]{1,0:T(8,128)(2,1)S(1)} %get-tuple-element.59._), channel_id=1, source_target_pairs={{0,15},{1,2},{2,1},{3,4},{4,3},{5,6},{6,5},{7,8},{8,7},{9,10},{10,... | collective-permute-start | bytes 1572872 | tf_op jit(solution)/shard_map/ppermute | solution.py:495
  7.6 0.5 collective-permute-start.1
  8.8 1.7 %make_lists.1 = (s32[214]{0:T(256)S(4)}, f32[1024,128]{1,0:T(8,128)S(1)}, bf16[1024,128]{1,0:T(8,128)(2,1)S(1)}) custom-call(s32[96]{0:T(128)S(1)} %copy-done.5, s32[96]{0:T(128)S(1)} %copy-done.6, s32[1]{0:T(128)S(6)} %copy.28.count_hbm, f32[1024,384]{1,0:T(8,128)} %x_ref.3, bf16[1024,256]{1,0:T(8,128)(2,1)S(1)} %get-tuple-element.59._), custom_call_target="tpu_custom_call" | custom-call | flops 1000 | bytes 1000 | tf_op jit(solution)/shard_map/make_lists/pallas_call | solution.py:21
  10.5 0.4 collective-permute-start.2
  10.9 1.3 %first_base.1 = (f32[1024,128]{1,0:T(8,128)S(1)}, f32[1024,128]{1,0:T(8,128)S(1)}, f32[1024,128]{1,0:T(8,128)S(1)}, bf16[384,384]{1,0:T(8,128)(2,1)S(1)}) custom-call(f32[1024,128]{1,0:T(8,128)S(1)} %get-tuple-element.64.refs_0_.refs_4_, f32[1024,128]{1,0:T(8,128)S(1)} %get-tuple-element.65.refs_1_.refs_5_.refs_7_, ...), custom_call_target="tpu_custom_call" | custom-call | flops 1000 | bytes 1000 | tf_op jit(solution)/shard_map/first_base/pallas_call | solution.py:21
  12.3 0.5 copy-done
  12.8 1.6 %near_first.1 = (f32[1024,128]{1,0:T(8,128)S(1)}, f32[1024,128]{1,0:T(8,128)S(1)}, f32[1024,128]{1,0:T(8,128)S(1)}, bf16[1024,128]{1,0:T(8,128)(2,1)S(1)}) custom-call(s32[214]{0:T(256)S(4)} %get-tuple-element.60.list_ref, bf16[96,128,128]{2,1,0:T(8,128)(2,1)S(1)} %copy-done, bf16[1024,128]{1,0:T(8,128)(2,1)S(1)} %get-tuple-element.61.refs_0_, ...), custom_call_target="tpu_custom_call" | custom-call | flops 1000 | bytes 1000 | tf_op jit(solution)/shard_map/near_first/pallas_call | solution.py:21
  14.3 1.6 %collective-permute-start.3 = (bf16[1024,128]{1,0:T(8,128)(2,1)S(1)}, bf16[1024,128]{1,0:T(8,128)(2,1)S(1)}, u32[]{:S(2)}, u32[]{:S(2)}) collective-permute-start(bf16[1024,128]{1,0:T(8,128)(2,1)S(1)} %get-tuple-element.68), channel_id=1, source_target_pairs={{0,15},{1,2},{2,1},{3,4},{4,3},{5,6},{6,5},{7,8},{8,7},{9,10},{10,... | collective-permute-start | bytes 786440 | tf_op jit(solution)/shard_map/ppermute | solution.py:495
  15.9 1.2 %far_first_0.1 = (bf16[1024,128]{1,0:T(8,128)(2,1)S(1)}, bf16[1024,128]{1,0:T(8,128)(2,1)S(1)}, bf16[1024,128]{1,0:T(8,128)(2,1)S(1)}, bf16[1024,128]{1,0:T(8,12...) custom-call(s32[214]{0:T(256)S(4)} %get-tuple-element.60.list_ref, bf16[96,128,128]{2,1,0:T(8,128)(2,1)S(1)} %copy-done, ...), custom_call_target="tpu_custom_call" | custom-call | flops 1000 | bytes 1000 | tf_op jit(solution)/shard_map/far_first_0/pallas_call | solution.py:21
  17.2 3.3 %collective-permute-start.9 = (bf16[1024,128]{1,0:T(8,128)(2,1)S(1)}, bf16[1024,128]{1,0:T(8,128)(2,1)S(1)}, u32[]{:S(2)}, u32[]{:S(2)}) collective-permute-start(bf16[1024,128]{1,0:T(8,128)(2,1)S(1)} %get-tuple-element.81), channel_id=1, source_target_pairs={{0,15},{1,2},{2,1},{3,4},{4,3},{5,6},{6,5},{7,8},{8,7},{9,10},{10,... | collective-permute-start | bytes 786440 | tf_op jit(solution)/shard_map/ppermute | solution.py:495
  20.4 2.6 %collective-permute-done.3.far_ref = bf16[1024,128]{1,0:T(8,128)(2,1)S(1)} collective-permute-done((bf16[1024,128]{1,0:T(8,128)(2,1)S(1)}, bf16[1024,128]{1,0:T(8,128)(2,1)S(1)}, u32[]{:S(2)}, u32[]{:S(2)}) %collective-permute-start.3) | collective-permute-done | bytes 262176 | tf_op jit(solution)/shard_map/ppermute | solution.py:495
  23.0 1.3 %far_first_1.1 = (bf16[1024,256]{1,0:T(8,128)(2,1)S(1)}, bf16[1024,128]{1,0:T(8,128)(2,1)S(1)}, bf16[1024,128]{1,0:T(8,128)(2,1)S(1)}, bf16[1024,128]{1,0:T(8,128)(2,1)S(1)}) custom-call(s32[214]{0:T(256)S(4)} %get-tuple-element.60.list_ref, bf16[96,128,128]{2,1,0:T(8,128)(2,1)S(1)} %copy-done, bf16[1024,128]{1,0:T(8,128)(2,1)S(1)} %collective-permute-done.3.far_ref, ...), custom_call_target="tpu_custom_call" | custom-call | flops 1000 | bytes 1000 | tf_op jit(solution)/shard_map/far_first_1/pallas_call | solution.py:21
  24.3 1.6 %collective-permute-start.5 = (bf16[1024,256]{1,0:T(8,128)(2,1)S(1)}, bf16[1024,256]{1,0:T(8,128)(2,1)S(1)}, u32[]{:S(2)}, u32[]{:S(2)}) collective-permute-start(bf16[1024,256]{1,0:T(8,128)(2,1)S(1)} %get-tuple-element.77), channel_id=1, source_target_pairs={{0,15},{1,2},{2,1},{3,4},{4,3},{5,6},{6,5},{7,8},{8,7},{9,10},{10,... | collective-permute-start | bytes 1572872 | tf_op jit(solution)/shard_map/ppermute | solution.py:495
  25.9 9.0 %collective-permute-start.6 = (bf16[1024,128]{1,0:T(8,128)(2,1)S(1)}, bf16[1024,128]{1,0:T(8,128)(2,1)S(1)}, u32[]{:S(2)}, u32[]{:S(2)}) collective-permute-start(bf16[1024,128]{1,0:T(8,128)(2,1)S(1)} %get-tuple-element.78.refs_0_.refs_9_), channel_id=1, source_target_pairs={{0,1},{1,0},{2,3},{3,2},{4,5},{5,4},{6,7},{7,6},{8,9},{9,8},{10,11... | collective-permute-start | bytes 786440 | tf_op jit(solution)/shard_map/ppermute | solution.py:498
  34.9 0.5 collective-permute-start.8
  35.4 2.0 %second_base.1 = (f32[1024,128]{1,0:T(8,128)S(1)}, f32[1024,128]{1,0:T(8,128)S(1)}, f32[1024,128]{1,0:T(8,128)S(1)}, f32[1024,128]{1,0:T(8,128)S(1)}, f32[1024,1...) custom-call(f32[1024,128]{1,0:T(8,128)S(1)} %get-tuple-element.84.refs_0_.refs_6_, ...), custom_call_target="tpu_custom_call" | custom-call | flops 1000 | bytes 1000 | tf_op jit(solution)/shard_map/second_base/pallas_call | solution.py:21
  37.5 0.8 %far_second_0.1.refs_6_ = f32[1024,128]{1,0:T(8,128)S(1)} custom-call(s32[214]{0:T(256)S(4)} %get-tuple-element.60.list_ref, bf16[96,128,128]{2,1,0:T(8,128)(2,1)S(1)} %copy-done, bf16[1024,128]{1,0:T(8,128)(2,1)S(1)} %collective-permute-done.9.far_ref), custom_call_target="tpu_custom_call" | custom-call | flops 4000000000 | bytes 1000 | tf_op jit(solution)/shard_map/far_second_0/pallas_call | solution.py:21
  38.3 1.5 %near_second.1 = (bf16[1024,128]{1,0:T(8,128)(2,1)S(1)}, f32[1024,128]{1,0:T(8,128)S(1)}, f32[1024,128]{1,0:T(8,128)S(1)}) custom-call(s32[214]{0:T(256)S(4)} %get-tuple-element.60.list_ref, bf16[96,128,128]{2,1,0:T(8,128)(2,1)S(1)} %copy-done, bf16[1024,128]{1,0:T(8,128)(2,1)S(1)} %get-tuple-element.78.refs_0_.refs_9_, ...), custom_call_target="tpu_custom_call" | custom-call | flops 1000 | bytes 1000 | tf_op jit(solution)/shard_map/near_second/pallas_call | solution.py:21
  39.9 1.3 %far_second_1.1 = (bf16[1024,128]{1,0:T(8,128)(2,1)S(1)}, bf16[1024,128]{1,0:T(8,128)(2,1)S(1)}, f32[8,128]{1,0:T(8,128)S(1)}, f32[16,128]{1,0:T(8,128)S(1)}, f3...) custom-call(s32[214]{0:T(256)S(4)} %get-tuple-element.60.list_ref, ...), custom_call_target="tpu_custom_call", output_to_operand_aliasing={{5}: (8, {}), {6}: (9, {}), {7}: (10, {}), {8}: (11, {}), {... | custom-call | flops 1000 | bytes 1000 | tf_op jit(solution)/shard_map/far_second_1/pallas_call | solution.py:21
  41.2 0.9 %collective-permute-start.12 = (f32[24,128]{1,0:T(8,128)S(1)}, f32[24,128]{1,0:T(8,128)S(1)}, u32[]{:S(2)}, u32[]{:S(2)}) collective-permute-start(f32[24,128]{1,0:T(8,128)S(1)} %get-tuple-element.110), channel_id=1, source_target_pairs={{0,12},{1,13},{2,14},{3,15},{4,8},{5,9},{6,10},{7,11},{8,4},{9,5},... | collective-permute-start | bytes 36872 | tf_op jit(solution)/shard_map/ppermute | solution.py:460
  42.1 1.9 %collective-permute-start.11 = (f32[16,128]{1,0:T(8,128)S(1)}, f32[16,128]{1,0:T(8,128)S(1)}, u32[]{:S(2)}, u32[]{:S(2)}) collective-permute-start(f32[16,128]{1,0:T(8,128)S(1)} %get-tuple-element.109), channel_id=1, source_target_pairs={{0,8},{1,9},{2,10},{3,11},{4,12},{5,13},{6,14},{7,15},{8,0},{9,1},... | collective-permute-start | bytes 24584 | tf_op jit(solution)/shard_map/ppermute | solution.py:460
  44.0 1.6 %collective-permute-start.10 = (f32[8,128]{1,0:T(8,128)S(1)}, f32[8,128]{1,0:T(8,128)S(1)}, u32[]{:S(2)}, u32[]{:S(2)}) collective-permute-start(f32[8,128]{1,0:T(8,128)S(1)} %get-tuple-element.108.refs_0_), channel_id=1, source_target_pairs={{0,4},{1,5},{2,6},{3,7},{4,0},{5,1},{6,2},{7,3},{8,12},{9,13},{10,... | collective-permute-start | bytes 12296 | tf_op jit(solution)/shard_map/ppermute | solution.py:460
  45.6 2.2 %finish.1 = (f32[1024,384]{1,0:T(8,128)}, f32[1024,384]{1,0:T(8,128)}, f32[8,128]{1,0:T(8,128)S(1)}) custom-call(bf16[1024,128]{1,0:T(8,128)(2,1)S(1)} %get-tuple-element.96.refs_0_, bf16[1024,128]{1,0:T(8,128)(2,1)S(1)} %get-tuple-element.97.refs_1_, bf16[1024,128]{1,0:T(8,128)(2,1)S(1)} %get-tuple-element.98.refs_2_, ...), custom_call_target="tpu_custom_call" | custom-call | flops 1000 | bytes 1000 | tf_op jit(solution)/shard_map/finish/pallas_call | solution.py:21
  47.8 0.8 %collective-permute-start.15 = (f32[24,128]{1,0:T(8,128)S(1)}, f32[24,128]{1,0:T(8,128)S(1)}, u32[]{:S(2)}, u32[]{:S(2)}) collective-permute-start(f32[24,128]{1,0:T(8,128)S(1)} %get-tuple-element.114), channel_id=1, source_target_pairs={{0,3},{1,2},{2,1},{3,0},{4,7},{5,6},{6,5},{7,4},{8,11},{9,10},{10,... | collective-permute-start | bytes 36872 | tf_op jit(solution)/shard_map/ppermute | solution.py:460
  48.6 3.9 %collective-permute-start.14 = (f32[16,128]{1,0:T(8,128)S(1)}, f32[16,128]{1,0:T(8,128)S(1)}, u32[]{:S(2)}, u32[]{:S(2)}) collective-permute-start(f32[16,128]{1,0:T(8,128)S(1)} %get-tuple-element.113), channel_id=1, source_target_pairs={{0,2},{1,3},{2,0},{3,1},{4,6},{5,7},{6,4},{7,5},{8,10},{9,11},{10,... | collective-permute-start | bytes 24584 | tf_op jit(solution)/shard_map/ppermute | solution.py:460
  52.5 0.0 collective-permute-start.13
  52.5 1.1 %collective-permute-done.13 = f32[8,128]{1,0:T(8,128)S(1)} collective-permute-done((f32[8,128]{1,0:T(8,128)S(1)}, f32[8,128]{1,0:T(8,128)S(1)}, u32[]{:S(2)}, u32[]{:S(2)}) %collective-permute-start.13) | collective-permute-done | bytes 4128 | tf_op jit(solution)/shard_map/ppermute | solution.py:460
  53.7 0.5 collective-permute-done.14
  54.2 0.5 multiply_bitcast_fusion
  (28 shorter events, 0.1 us)
Async XLA Ops:
  0.6 10.2 %copy-start.2 = (bf16[384,384]{1,0:T(8,128)(2,1)S(1)}, bf16[384,384]{1,0:T(8,128)(2,1)}, u32[]{:S(2)}) copy-start(bf16[384,384]{1,0:T(8,128)(2,1)} %constant.7.clone.refs_4_.refs_12_) | copy-start | bytes 884740
  0.6 10.2 %copy-start.3 = (bf16[384,48]{1,0:T(8,128)(2,1)S(1)}, bf16[384,48]{1,0:T(8,128)(2,1)}, u32[]{:S(2)}) copy-start(bf16[384,48]{1,0:T(8,128)(2,1)} %constant.8.clone.refs_5_) | copy-start | bytes 110596
  0.7 8.1 %copy-start.6 = (s32[96]{0:T(128)S(1)}, s32[96]{0:T(128)}, u32[]{:S(2)}) copy-start(s32[96]{0:T(128)} %cols_hbm.1) | copy-start | bytes 1156
  0.7 8.1 %copy-start.5 = (s32[96]{0:T(128)S(1)}, s32[96]{0:T(128)}, u32[]{:S(2)}) copy-start(s32[96]{0:T(128)} %rows_hbm.1) | copy-start | bytes 1156
  0.7 10.2 %copy-start.4 = (bf16[48,48]{1,0:T(8,128)(2,1)S(1)}, bf16[48,48]{1,0:T(8,128)(2,1)}, u32[]{:S(2)}) copy-start(bf16[48,48]{1,0:T(8,128)(2,1)} %refs_6_.1) | copy-start | bytes 13828
  0.7 10.2 %copy-start.1 = (f32[1024,384]{1,0:T(8,128)S(1)}, f32[1024,384]{1,0:T(8,128)}, u32[]{:S(2)}) copy-start(f32[1024,384]{1,0:T(8,128)} %refs_3_.1) | copy-start | bytes 4718596
  2.1 13.8 %collective-permute-start.4 = (bf16[1024,256]{1,0:T(8,128)(2,1)S(1)}, bf16[1024,256]{1,0:T(8,128)(2,1)S(1)}, u32[]{:S(2)}, u32[]{:S(2)}) collective-permute-start(bf16[1024,256]{1,0:T(8,128)(2,1)S(1)} %get-tuple-element.59._), channel_id=1, source_target_pairs={{0,15},{1,2},{2,1},{3,4},{4,3},{5,6},{6,5},{7,8},{8,7},{9,10},{10,... | collective-permute-start | bytes 1572872 | tf_op jit(solution)/shard_map/ppermute | solution.py:495
  7.6 4.6 %collective-permute-start = (bf16[1024,128]{1,0:T(8,128)(2,1)S(1)}, bf16[1024,128]{1,0:T(8,128)(2,1)S(1)}, u32[]{:S(2)}, u32[]{:S(2)}) collective-permute-start(bf16[1024,128]{1,0:T(8,128)(2,1)S(1)} %get-tuple-element.61.refs_0_), channel_id=1, source_target_pairs={{0,1},{1,0},{2,3},{3,2},{4,5},{5,4},{6,7},{7,6},{8,9},{9,8},{10,11... | collective-permute-start | bytes 786440 | tf_op jit(solution)/shard_map/ppermute | solution.py:498
  7.6 4.6 %collective-permute-start.1 = (bf16[1024,128]{1,0:T(8,128)(2,1)S(1)}, bf16[1024,128]{1,0:T(8,128)(2,1)S(1)}, u32[]{:S(2)}, u32[]{:S(2)}) collective-permute-start(bf16[1024,128]{1,0:T(8,128)(2,1)S(1)} %get-tuple-element.62.refs_1_), channel_id=1, source_target_pairs={{0,1},{1,0},{2,3},{3,2},{4,5},{5,4},{6,7},{7,6},{8,9},{9,8},{10,11... | collective-permute-start | bytes 786440 | tf_op jit(solution)/shard_map/ppermute | solution.py:498
  10.5 1.8 %collective-permute-start.2 = (bf16[1024,128]{1,0:T(8,128)(2,1)S(1)}, bf16[1024,128]{1,0:T(8,128)(2,1)S(1)}, u32[]{:S(2)}, u32[]{:S(2)}) collective-permute-start(bf16[1024,128]{1,0:T(8,128)(2,1)S(1)} %get-tuple-element.63.refs_2_.refs_6_), channel_id=1, source_target_pairs={{0,1},{1,0},{2,3},{3,2},{4,5},{5,4},{6,7},{7,6},{8,9},{9,8},{10,11... | collective-permute-start | bytes 786440 | tf_op jit(solution)/shard_map/ppermute | solution.py:498
  10.9 1.9 %copy-start = (bf16[96,128,128]{2,1,0:T(8,128)(2,1)S(1)}, bf16[96,128,128]{2,1,0:T(8,128)(2,1)}, u32[]{:S(2)}) copy-start(bf16[96,128,128]{2,1,0:T(8,128)(2,1)} %tiles_ref.11) | copy-start | bytes 9437188
  14.3 8.7 %collective-permute-start.3 = (bf16[1024,128]{1,0:T(8,128)(2,1)S(1)}, bf16[1024,128]{1,0:T(8,128)(2,1)S(1)}, u32[]{:S(2)}, u32[]{:S(2)}) collective-permute-start(bf16[1024,128]{1,0:T(8,128)(2,1)S(1)} %get-tuple-element.68), channel_id=1, source_target_pairs={{0,15},{1,2},{2,1},{3,4},{4,3},{5,6},{6,5},{7,8},{8,7},{9,10},{10,... | collective-permute-start | bytes 786440 | tf_op jit(solution)/shard_map/ppermute | solution.py:495
  17.2 20.3 %collective-permute-start.9 = (bf16[1024,128]{1,0:T(8,128)(2,1)S(1)}, bf16[1024,128]{1,0:T(8,128)(2,1)S(1)}, u32[]{:S(2)}, u32[]{:S(2)}) collective-permute-start(bf16[1024,128]{1,0:T(8,128)(2,1)S(1)} %get-tuple-element.81), channel_id=1, source_target_pairs={{0,15},{1,2},{2,1},{3,4},{4,3},{5,6},{6,5},{7,8},{8,7},{9,10},{10,... | collective-permute-start | bytes 786440 | tf_op jit(solution)/shard_map/ppermute | solution.py:495
  24.3 15.6 %collective-permute-start.5 = (bf16[1024,256]{1,0:T(8,128)(2,1)S(1)}, bf16[1024,256]{1,0:T(8,128)(2,1)S(1)}, u32[]{:S(2)}, u32[]{:S(2)}) collective-permute-start(bf16[1024,256]{1,0:T(8,128)(2,1)S(1)} %get-tuple-element.77), channel_id=1, source_target_pairs={{0,15},{1,2},{2,1},{3,4},{4,3},{5,6},{6,5},{7,8},{8,7},{9,10},{10,... | collective-permute-start | bytes 1572872 | tf_op jit(solution)/shard_map/ppermute | solution.py:495
  25.9 12.4 %collective-permute-start.6 = (bf16[1024,128]{1,0:T(8,128)(2,1)S(1)}, bf16[1024,128]{1,0:T(8,128)(2,1)S(1)}, u32[]{:S(2)}, u32[]{:S(2)}) collective-permute-start(bf16[1024,128]{1,0:T(8,128)(2,1)S(1)} %get-tuple-element.78.refs_0_.refs_9_), channel_id=1, source_target_pairs={{0,1},{1,0},{2,3},{3,2},{4,5},{5,4},{6,7},{7,6},{8,9},{9,8},{10,11... | collective-permute-start | bytes 786440 | tf_op jit(solution)/shard_map/ppermute | solution.py:498
  34.9 3.4 %collective-permute-start.7 = (bf16[1024,128]{1,0:T(8,128)(2,1)S(1)}, bf16[1024,128]{1,0:T(8,128)(2,1)S(1)}, u32[]{:S(2)}, u32[]{:S(2)}) collective-permute-start(bf16[1024,128]{1,0:T(8,128)(2,1)S(1)} %get-tuple-element.79.refs_1_.refs_10_), channel_id=1, source_target_pairs={{0,1},{1,0},{2,3},{3,2},{4,5},{5,4},{6,7},{7,6},{8,9},{9,8},{10,11... | collective-permute-start | bytes 786440 | tf_op jit(solution)/shard_map/ppermute | solution.py:498
  34.9 3.4 %collective-permute-start.8 = (bf16[1024,128]{1,0:T(8,128)(2,1)S(1)}, bf16[1024,128]{1,0:T(8,128)(2,1)S(1)}, u32[]{:S(2)}, u32[]{:S(2)}) collective-permute-start(bf16[1024,128]{1,0:T(8,128)(2,1)S(1)} %get-tuple-element.80.refs_2_.refs_11_), channel_id=1, source_target_pairs={{0,1},{1,0},{2,3},{3,2},{4,5},{5,4},{6,7},{7,6},{8,9},{9,8},{10,11... | collective-permute-start | bytes 786440 | tf_op jit(solution)/shard_map/ppermute | solution.py:498
  41.2 6.6 %collective-permute-start.12 = (f32[24,128]{1,0:T(8,128)S(1)}, f32[24,128]{1,0:T(8,128)S(1)}, u32[]{:S(2)}, u32[]{:S(2)}) collective-permute-start(f32[24,128]{1,0:T(8,128)S(1)} %get-tuple-element.110), channel_id=1, source_target_pairs={{0,12},{1,13},{2,14},{3,15},{4,8},{5,9},{6,10},{7,11},{8,4},{9,5},... | collective-permute-start | bytes 36872 | tf_op jit(solution)/shard_map/ppermute | solution.py:460
  42.1 5.7 %collective-permute-start.11 = (f32[16,128]{1,0:T(8,128)S(1)}, f32[16,128]{1,0:T(8,128)S(1)}, u32[]{:S(2)}, u32[]{:S(2)}) collective-permute-start(f32[16,128]{1,0:T(8,128)S(1)} %get-tuple-element.109), channel_id=1, source_target_pairs={{0,8},{1,9},{2,10},{3,11},{4,12},{5,13},{6,14},{7,15},{8,0},{9,1},... | collective-permute-start | bytes 24584 | tf_op jit(solution)/shard_map/ppermute | solution.py:460
  44.0 3.7 %collective-permute-start.10 = (f32[8,128]{1,0:T(8,128)S(1)}, f32[8,128]{1,0:T(8,128)S(1)}, u32[]{:S(2)}, u32[]{:S(2)}) collective-permute-start(f32[8,128]{1,0:T(8,128)S(1)} %get-tuple-element.108.refs_0_), channel_id=1, source_target_pairs={{0,4},{1,5},{2,6},{3,7},{4,0},{5,1},{6,2},{7,3},{8,12},{9,13},{10,... | collective-permute-start | bytes 12296 | tf_op jit(solution)/shard_map/ppermute | solution.py:460
  47.8 6.4 %collective-permute-start.15 = (f32[24,128]{1,0:T(8,128)S(1)}, f32[24,128]{1,0:T(8,128)S(1)}, u32[]{:S(2)}, u32[]{:S(2)}) collective-permute-start(f32[24,128]{1,0:T(8,128)S(1)} %get-tuple-element.114), channel_id=1, source_target_pairs={{0,3},{1,2},{2,1},{3,0},{4,7},{5,6},{6,5},{7,4},{8,11},{9,10},{10,... | collective-permute-start | bytes 36872 | tf_op jit(solution)/shard_map/ppermute | solution.py:460
  48.6 5.6 %collective-permute-start.14 = (f32[16,128]{1,0:T(8,128)S(1)}, f32[16,128]{1,0:T(8,128)S(1)}, u32[]{:S(2)}, u32[]{:S(2)}) collective-permute-start(f32[16,128]{1,0:T(8,128)S(1)} %get-tuple-element.113), channel_id=1, source_target_pairs={{0,2},{1,3},{2,0},{3,1},{4,6},{5,7},{6,4},{7,5},{8,10},{9,11},{10,... | collective-permute-start | bytes 24584 | tf_op jit(solution)/shard_map/ppermute | solution.py:460
  52.5 1.2 %collective-permute-start.13 = (f32[8,128]{1,0:T(8,128)S(1)}, f32[8,128]{1,0:T(8,128)S(1)}, u32[]{:S(2)}, u32[]{:S(2)}) collective-permute-start(f32[8,128]{1,0:T(8,128)S(1)} %get-tuple-element.112), channel_id=1, source_target_pairs={{0,1},{1,0},{2,3},{3,2},{4,5},{5,4},{6,7},{7,6},{8,9},{9,8},{10,11... | collective-permute-start | bytes 12296 | tf_op jit(solution)/shard_map/ppermute | solution.py:460

commit v16 on v15

--- a/solution.py
+++ b/solution.py
@@ -384,39 +384,49 @@
     return outs[:groups], outs[groups : 2 * groups], outs[2 * groups :]
 
 
-def finish(fields, xs, bases, mixing, channels):
+def finish(here, fields, xs, bases, mixing, channels, outputs, name):
     groups = len(xs)
     cells = xs[0].shape[0]
     width = groups * LANES
 
     def body(*refs):
         field_refs, x_refs, base_refs = [refs[k * groups : (k + 1) * groups] for k in range(3)]
-        mixing_ref, x_out, y_out, token, x_buf, y_buf, sems = refs[3 * groups :]
-        held = [ref[...] for ref in field_refs]
-        copies = []
-        for g in range(groups):
-            y_new = base_refs[g][...] - 0.2 * mixed_of(held, mixing_ref, g, channels)
-            y_buf[g] = y_new
-            x_buf[g] = jnp.clip(x_refs[g][...] + 0.5 * y_new, -1.0, 1.0)
-            for k, (buf, out) in enumerate(((y_buf, y_out), (x_buf, x_out))):
-                copies.append(
-                    pltpu.make_async_copy(buf.at[g], out.at[:, lanes(g)], sems.at[g, k])
+        mixing_ref = refs[3 * groups]
+        x_buf, y_buf, sems = refs[-3:]
+        x_out, y_out = refs[-5:-3] if outputs else refs[-6:-4]
+        if not outputs:
+            refs[-4][...] = jnp.zeros_like(refs[-4])
+
+        @pl.when(here())
+        def _():
+            held = [ref[...] for ref in field_refs]
+            copies = []
+            for g in range(groups):
+                x_buf[g], y_buf[g] = updated(
+                    mixed_of(held, mixing_ref, g, channels), base_refs[g][...], x_refs[g][...]
                 )
-                copies[-1].start()
-        token[...] = jnp.zeros_like(token)
-        for copy in copies:
-            copy.wait()
-
+                for k, (buf, out) in enumerate(((y_buf, y_out), (x_buf, x_out))):
+                    copies.append(
+                        pltpu.make_async_copy(buf.at[g], out.at[:, lanes(g)], sems.at[g, k])
+                    )
+                    copies[-1].start()
+            for copy in copies:
+                copy.wait()
+
+    ins = vmem(*fields, *xs, *bases, mixing)
     return call(
         body,
-        vmem(*fields, *xs, *bases, mixing),
-        [((cells, width), F32, pltpu.HBM)] * 2 + [((8, LANES), F32, pltpu.VMEM)],
+        ins + [(a, pltpu.HBM) for a in outputs],
+        [((cells, width), F32, pltpu.HBM)] * 2
+        + ([] if outputs else [((8, LANES), F32, pltpu.VMEM)]),
         [
             pltpu.VMEM((groups, cells, LANES), F32),
             pltpu.VMEM((groups, cells, LANES), F32),
             pltpu.SemaphoreType.DMA((groups, 2)),
         ],
-        "finish",
+        name,
+        0,
+        [(len(ins) + i, i) for i in range(len(outputs))],
     )
 
 
@@ -622,11 +632,17 @@
     fields, partials, kept = results[: len(piece)], results[len(piece) : sent], results[sent:]
     fields, kept = [kept[0], *fields], kept[1:]
 
-    x_new, y_new, token = finish(
-        fields, kept[:groups], kept[groups : 2 * groups], kept[2 * groups], channels
-    )
+    def early():
+        return ((ring_index() + 1) // 2) % 2 == 0
+
+    def late():
+        return ((ring_index() + 1) // 2) % 2 == 1
+
+    rest = (fields, kept[:groups], kept[groups : 2 * groups], kept[2 * groups], channels)
+    *outputs, token = finish(early, *rest, [], "finish_early")
     total = sum_over_ring(partials, ring, token)
     energy = total[0, :replicas] / jnp.sqrt(jnp.float32(cells * ring * channels))
+    x_new, y_new = finish(late, *rest, outputs, "finish_late")
     return (x_new, y_new, energy)
 
 

time: 54.8 us -> 54.5 us (level); the launches traced: 54.7 us -> 53.8 us
  starting transfers between devices: 31.5 us -> 29.2 us
  Pallas kernels: 16.4 us -> 17.1 us
  waiting for transfers between devices: 4.26 us -> 4.91 us
    ppermute x4, starting transfers between devices: 11.9 us -> 10.1 us  [far_swap(): return lax.ppermute(mine, RING, off_chip)]
    ppermute x6, starting transfers between devices: 9.14 us -> 7.98 us  [sum_over_ring(): lax.ppermute(value, RING, [(j, j ^ bit) for j in range(ring)])]
    ppermute x6, starting transfers between devices: 10.4 us -> 11.1 us  [near_swap(): return lax.ppermute(mine, RING, on_chip)]
    pallas_call x12 -> x13, Pallas kernels: 16.4 us -> 17.1 us  [call(): pl.pallas_call(body, in_specs=[pl.BlockSpec(memory_space=pl.ANY if s is p...]
  transfers between devices with their start and end apart: 16 -> 16, of which waited for: 3 -> 4; matrix products, arithmetic and copies ran while one was open for 0% -> 0% of each run, Pallas kernels for 25% -> 27%
where the time goes in v16:
time: 54.5 us; the launch traced here: 53.8 us
  starting transfers between devices  29.2 us (54%)
  Pallas kernels  17.1 us (31%)
  waiting for transfers between devices  4.91 us (9%)
  between operations  1.55 us (3%)
    pallas_call x13, Pallas kernels, call(): pl.pallas_call(body, in_specs=[pl.BlockSpec(memory_space=pl.ANY if s is p...  17.1 us
    ppermute x6, starting transfers between devices, near_swap(): return lax.ppermute(mine, RING, on_chip)  11.1 us
    ppermute x4, starting transfers between devices, far_swap(): return lax.ppermute(mine, RING, off_chip)  10.1 us
    ppermute x6, starting transfers between devices, sum_over_ring(): lax.ppermute(value, RING, [(j, j ^ bit) for j in range(ring)])  7.98 us
    ppermute x4, waiting for transfers between devices, far_swap(): return lax.ppermute(mine, RING, off_chip)  2.85 us
    ppermute x6, waiting for transfers between devices, sum_over_ring(): lax.ppermute(value, RING, [(j, j ^ bit) for j in range(ring)])  2.04 us
  transfers between devices with their start and end apart: 16, of which 4 were waited for; matrix products, arithmetic and copies ran while one was open for 0% of the time, Pallas kernels for 27%

profile of v16, /device:TPU:0, one launch (start us, length us, event | category | flops | bytes accessed | tf_op | source)
XLA Modules:
  0.0 53.8 jit_solution(2592731446389497628)
XLA Ops:
  0.6 0.0 copy-start.2
  0.7 1.4 %load_first.1 = (f32[1024,128]{1,0:T(8,128)S(1)}, f32[1024,128]{1,0:T(8,128)S(1)}, bf16[1024,128]{1,0:T(8,128)(2,1)S(1)}, bf16[1024,128]{1,0:T(8,128)(2,1)S(1)}, bf16[1024,256]{1,0:T(8,128)(2,1)S(1)}) custom-call(f32[1024,384]{1,0:T(8,128)} %x_ref.3), custom_call_target="tpu_custom_call" | custom-call | flops 1000 | bytes 1000 | tf_op jit(solution)/shard_map/load_first/pallas_call | solution.py:21
  2.1 5.5 %collective-permute-start.4 = (bf16[1024,256]{1,0:T(8,128)(2,1)S(1)}, bf16[1024,256]{1,0:T(8,128)(2,1)S(1)}, u32[]{:S(2)}, u32[]{:S(2)}) collective-permute-start(bf16[1024,256]{1,0:T(8,128)(2,1)S(1)} %get-tuple-element.61._), channel_id=1, source_target_pairs={{0,15},{1,2},{2,1},{3,4},{4,3},{5,6},{6,5},{7,8},{8,7},{9,10},{10,... | collective-permute-start | bytes 1572872 | tf_op jit(solution)/shard_map/ppermute | solution.py:505
  7.6 0.5 collective-permute-start.1
  8.8 1.7 %make_lists.1 = (s32[214]{0:T(256)S(4)}, f32[1024,128]{1,0:T(8,128)S(1)}, bf16[1024,128]{1,0:T(8,128)(2,1)S(1)}) custom-call(s32[96]{0:T(128)S(1)} %copy-done.5, s32[96]{0:T(128)S(1)} %copy-done.6, s32[1]{0:T(128)S(6)} %copy.32.count_hbm, f32[1024,384]{1,0:T(8,128)} %x_ref.3, bf16[1024,256]{1,0:T(8,128)(2,1)S(1)} %get-tuple-element.61._), custom_call_target="tpu_custom_call" | custom-call | flops 1000 | bytes 1000 | tf_op jit(solution)/shard_map/make_lists/pallas_call | solution.py:21
  10.5 0.5 collective-permute-start.2
  11.0 1.4 %first_base.1 = (f32[1024,128]{1,0:T(8,128)S(1)}, f32[1024,128]{1,0:T(8,128)S(1)}, f32[1024,128]{1,0:T(8,128)S(1)}, bf16[384,384]{1,0:T(8,128)(2,1)S(1)}) custom-call(f32[1024,128]{1,0:T(8,128)S(1)} %get-tuple-element.66.refs_0_.refs_4_, f32[1024,128]{1,0:T(8,128)S(1)} %get-tuple-element.67.refs_1_.refs_5_.refs_7_, ...), custom_call_target="tpu_custom_call" | custom-call | flops 1000 | bytes 1000 | tf_op jit(solution)/shard_map/first_base/pallas_call | solution.py:21
  12.4 0.5 copy-done
  12.9 1.9 %near_first.1 = (f32[1024,128]{1,0:T(8,128)S(1)}, f32[1024,128]{1,0:T(8,128)S(1)}, f32[1024,128]{1,0:T(8,128)S(1)}, bf16[1024,128]{1,0:T(8,128)(2,1)S(1)}) custom-call(s32[214]{0:T(256)S(4)} %get-tuple-element.62.list_ref, bf16[96,128,128]{2,1,0:T(8,128)(2,1)S(1)} %copy-done, bf16[1024,128]{1,0:T(8,128)(2,1)S(1)} %get-tuple-element.63.refs_0_, ...), custom_call_target="tpu_custom_call" | custom-call | flops 1000 | bytes 1000 | tf_op jit(solution)/shard_map/near_first/pallas_call | solution.py:21
  14.8 0.1 collective-permute-start.3
  14.9 1.2 %far_first_0.1 = (bf16[1024,128]{1,0:T(8,128)(2,1)S(1)}, bf16[1024,128]{1,0:T(8,128)(2,1)S(1)}, bf16[1024,128]{1,0:T(8,128)(2,1)S(1)}, bf16[1024,128]{1,0:T(8,12...) custom-call(s32[214]{0:T(256)S(4)} %get-tuple-element.62.list_ref, bf16[96,128,128]{2,1,0:T(8,128)(2,1)S(1)} %copy-done, ...), custom_call_target="tpu_custom_call" | custom-call | flops 1000 | bytes 1000 | tf_op jit(solution)/shard_map/far_first_0/pallas_call | solution.py:21
  16.1 4.5 %collective-permute-start.9 = (bf16[1024,128]{1,0:T(8,128)(2,1)S(1)}, bf16[1024,128]{1,0:T(8,128)(2,1)S(1)}, u32[]{:S(2)}, u32[]{:S(2)}) collective-permute-start(bf16[1024,128]{1,0:T(8,128)(2,1)S(1)} %get-tuple-element.83), channel_id=1, source_target_pairs={{0,15},{1,2},{2,1},{3,4},{4,3},{5,6},{6,5},{7,8},{8,7},{9,10},{10,... | collective-permute-start | bytes 786440 | tf_op jit(solution)/shard_map/ppermute | solution.py:505
  20.6 2.8 %collective-permute-done.3.far_ref = bf16[1024,128]{1,0:T(8,128)(2,1)S(1)} collective-permute-done((bf16[1024,128]{1,0:T(8,128)(2,1)S(1)}, bf16[1024,128]{1,0:T(8,128)(2,1)S(1)}, u32[]{:S(2)}, u32[]{:S(2)}) %collective-permute-start.3) | collective-permute-done | bytes 262176 | tf_op jit(solution)/shard_map/ppermute | solution.py:505
  23.4 1.3 %far_first_1.1 = (bf16[1024,256]{1,0:T(8,128)(2,1)S(1)}, bf16[1024,128]{1,0:T(8,128)(2,1)S(1)}, bf16[1024,128]{1,0:T(8,128)(2,1)S(1)}, bf16[1024,128]{1,0:T(8,128)(2,1)S(1)}) custom-call(s32[214]{0:T(256)S(4)} %get-tuple-element.62.list_ref, bf16[96,128,128]{2,1,0:T(8,128)(2,1)S(1)} %copy-done, bf16[1024,128]{1,0:T(8,128)(2,1)S(1)} %collective-permute-done.3.far_ref, ...), custom_call_target="tpu_custom_call" | custom-call | flops 1000 | bytes 1000 | tf_op jit(solution)/shard_map/far_first_1/pallas_call | solution.py:21
  24.8 0.1 collective-permute-start.5
  24.8 9.6 %collective-permute-start.6 = (bf16[1024,128]{1,0:T(8,128)(2,1)S(1)}, bf16[1024,128]{1,0:T(8,128)(2,1)S(1)}, u32[]{:S(2)}, u32[]{:S(2)}) collective-permute-start(bf16[1024,128]{1,0:T(8,128)(2,1)S(1)} %get-tuple-element.80.refs_0_.refs_9_), channel_id=1, source_target_pairs={{0,1},{1,0},{2,3},{3,2},{4,5},{5,4},{6,7},{7,6},{8,9},{9,8},{10,11... | collective-permute-start | bytes 786440 | tf_op jit(solution)/shard_map/ppermute | solution.py:508
  34.5 0.5 collective-permute-start.8
  35.0 2.1 %second_base.1 = (f32[1024,128]{1,0:T(8,128)S(1)}, f32[1024,128]{1,0:T(8,128)S(1)}, f32[1024,128]{1,0:T(8,128)S(1)}, f32[1024,128]{1,0:T(8,128)S(1)}, f32[1024,1...) custom-call(f32[1024,128]{1,0:T(8,128)S(1)} %get-tuple-element.86.refs_0_.refs_6_, ...), custom_call_target="tpu_custom_call" | custom-call | flops 1000 | bytes 1000 | tf_op jit(solution)/shard_map/second_base/pallas_call | solution.py:21
  37.0 0.8 %far_second_0.1.refs_6_ = f32[1024,128]{1,0:T(8,128)S(1)} custom-call(s32[214]{0:T(256)S(4)} %get-tuple-element.62.list_ref, bf16[96,128,128]{2,1,0:T(8,128)(2,1)S(1)} %copy-done, bf16[1024,128]{1,0:T(8,128)(2,1)S(1)} %collective-permute-done.9.far_ref), custom_call_target="tpu_custom_call" | custom-call | flops 4000000000 | bytes 1000 | tf_op jit(solution)/shard_map/far_second_0/pallas_call | solution.py:21
  37.9 1.8 %near_second.1 = (bf16[1024,128]{1,0:T(8,128)(2,1)S(1)}, f32[1024,128]{1,0:T(8,128)S(1)}, f32[1024,128]{1,0:T(8,128)S(1)}) custom-call(s32[214]{0:T(256)S(4)} %get-tuple-element.62.list_ref, bf16[96,128,128]{2,1,0:T(8,128)(2,1)S(1)} %copy-done, bf16[1024,128]{1,0:T(8,128)(2,1)S(1)} %get-tuple-element.80.refs_0_.refs_9_, ...), custom_call_target="tpu_custom_call" | custom-call | flops 1000 | bytes 1000 | tf_op jit(solution)/shard_map/near_second/pallas_call | solution.py:21
  39.7 1.3 %far_second_1.1 = (bf16[1024,128]{1,0:T(8,128)(2,1)S(1)}, bf16[1024,128]{1,0:T(8,128)(2,1)S(1)}, f32[8,128]{1,0:T(8,128)S(1)}, f32[16,128]{1,0:T(8,128)S(1)}, f3...) custom-call(s32[214]{0:T(256)S(4)} %get-tuple-element.62.list_ref, ...), custom_call_target="tpu_custom_call", output_to_operand_aliasing={{5}: (8, {}), {6}: (9, {}), {7}: (10, {}), {8}: (11, {}), {... | custom-call | flops 1000 | bytes 1000 | tf_op jit(solution)/shard_map/far_second_1/pallas_call | solution.py:21
  41.0 2.2 %collective-permute-start.12 = (f32[24,128]{1,0:T(8,128)S(1)}, f32[24,128]{1,0:T(8,128)S(1)}, u32[]{:S(2)}, u32[]{:S(2)}) collective-permute-start(f32[24,128]{1,0:T(8,128)S(1)} %get-tuple-element.114), channel_id=1, source_target_pairs={{0,12},{1,13},{2,14},{3,15},{4,8},{5,9},{6,10},{7,11},{8,4},{9,5},... | collective-permute-start | bytes 36872 | tf_op jit(solution)/shard_map/ppermute | solution.py:470
  43.3 1.1 %collective-permute-start.11 = (f32[16,128]{1,0:T(8,128)S(1)}, f32[16,128]{1,0:T(8,128)S(1)}, u32[]{:S(2)}, u32[]{:S(2)}) collective-permute-start(f32[16,128]{1,0:T(8,128)S(1)} %get-tuple-element.113), channel_id=1, source_target_pairs={{0,8},{1,9},{2,10},{3,11},{4,12},{5,13},{6,14},{7,15},{8,0},{9,1},... | collective-permute-start | bytes 24584 | tf_op jit(solution)/shard_map/ppermute | solution.py:470
  44.3 1.1 %collective-permute-start.10 = (f32[8,128]{1,0:T(8,128)S(1)}, f32[8,128]{1,0:T(8,128)S(1)}, u32[]{:S(2)}, u32[]{:S(2)}) collective-permute-start(f32[8,128]{1,0:T(8,128)S(1)} %get-tuple-element.112.refs_0_), channel_id=1, source_target_pairs={{0,4},{1,5},{2,6},{3,7},{4,0},{5,1},{6,2},{7,3},{8,12},{9,13},{10,... | collective-permute-start | bytes 12296 | tf_op jit(solution)/shard_map/ppermute | solution.py:470
  45.4 2.2 %finish_early.1 = (f32[1024,384]{1,0:T(8,128)}, f32[1024,384]{1,0:T(8,128)}, f32[8,128]{1,0:T(8,128)S(1)}) custom-call(bf16[1024,128]{1,0:T(8,128)(2,1)S(1)} %get-tuple-element.98.refs_0_, bf16[1024,128]{1,0:T(8,128)(2,1)S(1)} %get-tuple-element.99.refs_1_, bf16[1024,128]{1,0:T(8,128)(2,1)S(1)} %get-tuple-element.100.refs_2_, ...), custom_call_target="tpu_custom_call" | custom-call | flops 1000 | bytes 1000 | tf_op jit(solution)/shard_map/finish_early/pallas_call | solution.py:21
  47.6 0.3 collective-permute-done.10.refs_1_
  47.9 0.1 collective-permute-start.15
  48.0 3.5 %collective-permute-start.14 = (f32[16,128]{1,0:T(8,128)S(1)}, f32[16,128]{1,0:T(8,128)S(1)}, u32[]{:S(2)}, u32[]{:S(2)}) collective-permute-start(f32[16,128]{1,0:T(8,128)S(1)} %get-tuple-element.117), channel_id=1, source_target_pairs={{0,2},{1,3},{2,0},{3,1},{4,6},{5,7},{6,4},{7,5},{8,10},{9,11},{10,... | collective-permute-start | bytes 24584 | tf_op jit(solution)/shard_map/ppermute | solution.py:470
  51.5 0.1 finish_late.1
  51.6 1.1 %collective-permute-done.13 = f32[8,128]{1,0:T(8,128)S(1)} collective-permute-done((f32[8,128]{1,0:T(8,128)S(1)}, f32[8,128]{1,0:T(8,128)S(1)}, u32[]{:S(2)}, u32[]{:S(2)}) %collective-permute-start.13) | collective-permute-done | bytes 4128 | tf_op jit(solution)/shard_map/ppermute | solution.py:470
  52.7 0.6 %collective-permute-done.14 = f32[16,128]{1,0:T(8,128)S(1)} collective-permute-done((f32[16,128]{1,0:T(8,128)S(1)}, f32[16,128]{1,0:T(8,128)S(1)}, u32[]{:S(2)}, u32[]{:S(2)}) %collective-permute-start.14) | collective-permute-done | bytes 8224 | tf_op jit(solution)/shard_map/ppermute | solution.py:470
  53.3 0.5 multiply_bitcast_fusion
  (29 shorter events, 0.1 us)
Async XLA Ops:
  0.6 10.4 %copy-start.2 = (bf16[384,384]{1,0:T(8,128)(2,1)S(1)}, bf16[384,384]{1,0:T(8,128)(2,1)}, u32[]{:S(2)}) copy-start(bf16[384,384]{1,0:T(8,128)(2,1)} %constant.7.clone.refs_4_.refs_12_) | copy-start | bytes 884740
  0.6 10.4 %copy-start.3 = (bf16[384,48]{1,0:T(8,128)(2,1)S(1)}, bf16[384,48]{1,0:T(8,128)(2,1)}, u32[]{:S(2)}) copy-start(bf16[384,48]{1,0:T(8,128)(2,1)} %constant.8.clone.refs_5_) | copy-start | bytes 110596
  0.7 8.1 %copy-start.6 = (s32[96]{0:T(128)S(1)}, s32[96]{0:T(128)}, u32[]{:S(2)}) copy-start(s32[96]{0:T(128)} %cols_hbm.1) | copy-start | bytes 1156
  0.7 8.1 %copy-start.5 = (s32[96]{0:T(128)S(1)}, s32[96]{0:T(128)}, u32[]{:S(2)}) copy-start(s32[96]{0:T(128)} %rows_hbm.1) | copy-start | bytes 1156
  0.7 10.3 %copy-start.4 = (bf16[48,48]{1,0:T(8,128)(2,1)S(1)}, bf16[48,48]{1,0:T(8,128)(2,1)}, u32[]{:S(2)}) copy-start(bf16[48,48]{1,0:T(8,128)(2,1)} %refs_6_.1) | copy-start | bytes 13828
  0.7 10.3 %copy-start.1 = (f32[1024,384]{1,0:T(8,128)S(1)}, f32[1024,384]{1,0:T(8,128)}, u32[]{:S(2)}) copy-start(f32[1024,384]{1,0:T(8,128)} %refs_3_.1) | copy-start | bytes 4718596
  2.1 12.7 %collective-permute-start.4 = (bf16[1024,256]{1,0:T(8,128)(2,1)S(1)}, bf16[1024,256]{1,0:T(8,128)(2,1)S(1)}, u32[]{:S(2)}, u32[]{:S(2)}) collective-permute-start(bf16[1024,256]{1,0:T(8,128)(2,1)S(1)} %get-tuple-element.61._), channel_id=1, source_target_pairs={{0,15},{1,2},{2,1},{3,4},{4,3},{5,6},{6,5},{7,8},{8,7},{9,10},{10,... | collective-permute-start | bytes 1572872 | tf_op jit(solution)/shard_map/ppermute | solution.py:505
  7.6 4.8 %collective-permute-start = (bf16[1024,128]{1,0:T(8,128)(2,1)S(1)}, bf16[1024,128]{1,0:T(8,128)(2,1)S(1)}, u32[]{:S(2)}, u32[]{:S(2)}) collective-permute-start(bf16[1024,128]{1,0:T(8,128)(2,1)S(1)} %get-tuple-element.63.refs_0_), channel_id=1, source_target_pairs={{0,1},{1,0},{2,3},{3,2},{4,5},{5,4},{6,7},{7,6},{8,9},{9,8},{10,11... | collective-permute-start | bytes 786440 | tf_op jit(solution)/shard_map/ppermute | solution.py:508
  7.6 4.8 %collective-permute-start.1 = (bf16[1024,128]{1,0:T(8,128)(2,1)S(1)}, bf16[1024,128]{1,0:T(8,128)(2,1)S(1)}, u32[]{:S(2)}, u32[]{:S(2)}) collective-permute-start(bf16[1024,128]{1,0:T(8,128)(2,1)S(1)} %get-tuple-element.64.refs_1_), channel_id=1, source_target_pairs={{0,1},{1,0},{2,3},{3,2},{4,5},{5,4},{6,7},{7,6},{8,9},{9,8},{10,11... | collective-permute-start | bytes 786440 | tf_op jit(solution)/shard_map/ppermute | solution.py:508
  10.5 1.9 %collective-permute-start.2 = (bf16[1024,128]{1,0:T(8,128)(2,1)S(1)}, bf16[1024,128]{1,0:T(8,128)(2,1)S(1)}, u32[]{:S(2)}, u32[]{:S(2)}) collective-permute-start(bf16[1024,128]{1,0:T(8,128)(2,1)S(1)} %get-tuple-element.65.refs_2_.refs_6_), channel_id=1, source_target_pairs={{0,1},{1,0},{2,3},{3,2},{4,5},{5,4},{6,7},{7,6},{8,9},{9,8},{10,11... | collective-permute-start | bytes 786440 | tf_op jit(solution)/shard_map/ppermute | solution.py:508
  11.0 1.9 %copy-start = (bf16[96,128,128]{2,1,0:T(8,128)(2,1)S(1)}, bf16[96,128,128]{2,1,0:T(8,128)(2,1)}, u32[]{:S(2)}) copy-start(bf16[96,128,128]{2,1,0:T(8,128)(2,1)} %tiles_ref.11) | copy-start | bytes 9437188
  14.8 8.7 %collective-permute-start.3 = (bf16[1024,128]{1,0:T(8,128)(2,1)S(1)}, bf16[1024,128]{1,0:T(8,128)(2,1)S(1)}, u32[]{:S(2)}, u32[]{:S(2)}) collective-permute-start(bf16[1024,128]{1,0:T(8,128)(2,1)S(1)} %get-tuple-element.70), channel_id=1, source_target_pairs={{0,15},{1,2},{2,1},{3,4},{4,3},{5,6},{6,5},{7,8},{8,7},{9,10},{10,... | collective-permute-start | bytes 786440 | tf_op jit(solution)/shard_map/ppermute | solution.py:505
  16.1 20.9 %collective-permute-start.9 = (bf16[1024,128]{1,0:T(8,128)(2,1)S(1)}, bf16[1024,128]{1,0:T(8,128)(2,1)S(1)}, u32[]{:S(2)}, u32[]{:S(2)}) collective-permute-start(bf16[1024,128]{1,0:T(8,128)(2,1)S(1)} %get-tuple-element.83), channel_id=1, source_target_pairs={{0,15},{1,2},{2,1},{3,4},{4,3},{5,6},{6,5},{7,8},{8,7},{9,10},{10,... | collective-permute-start | bytes 786440 | tf_op jit(solution)/shard_map/ppermute | solution.py:505
  24.8 15.0 %collective-permute-start.5 = (bf16[1024,256]{1,0:T(8,128)(2,1)S(1)}, bf16[1024,256]{1,0:T(8,128)(2,1)S(1)}, u32[]{:S(2)}, u32[]{:S(2)}) collective-permute-start(bf16[1024,256]{1,0:T(8,128)(2,1)S(1)} %get-tuple-element.79), channel_id=1, source_target_pairs={{0,15},{1,2},{2,1},{3,4},{4,3},{5,6},{6,5},{7,8},{8,7},{9,10},{10,... | collective-permute-start | bytes 1572872 | tf_op jit(solution)/shard_map/ppermute | solution.py:505
  24.8 13.0 %collective-permute-start.6 = (bf16[1024,128]{1,0:T(8,128)(2,1)S(1)}, bf16[1024,128]{1,0:T(8,128)(2,1)S(1)}, u32[]{:S(2)}, u32[]{:S(2)}) collective-permute-start(bf16[1024,128]{1,0:T(8,128)(2,1)S(1)} %get-tuple-element.80.refs_0_.refs_9_), channel_id=1, source_target_pairs={{0,1},{1,0},{2,3},{3,2},{4,5},{5,4},{6,7},{7,6},{8,9},{9,8},{10,11... | collective-permute-start | bytes 786440 | tf_op jit(solution)/shard_map/ppermute | solution.py:508
  34.4 3.4 %collective-permute-start.7 = (bf16[1024,128]{1,0:T(8,128)(2,1)S(1)}, bf16[1024,128]{1,0:T(8,128)(2,1)S(1)}, u32[]{:S(2)}, u32[]{:S(2)}) collective-permute-start(bf16[1024,128]{1,0:T(8,128)(2,1)S(1)} %get-tuple-element.81.refs_1_.refs_10_), channel_id=1, source_target_pairs={{0,1},{1,0},{2,3},{3,2},{4,5},{5,4},{6,7},{7,6},{8,9},{9,8},{10,11... | collective-permute-start | bytes 786440 | tf_op jit(solution)/shard_map/ppermute | solution.py:508
  34.5 3.4 %collective-permute-start.8 = (bf16[1024,128]{1,0:T(8,128)(2,1)S(1)}, bf16[1024,128]{1,0:T(8,128)(2,1)S(1)}, u32[]{:S(2)}, u32[]{:S(2)}) collective-permute-start(bf16[1024,128]{1,0:T(8,128)(2,1)S(1)} %get-tuple-element.82.refs_2_.refs_11_), channel_id=1, source_target_pairs={{0,1},{1,0},{2,3},{3,2},{4,5},{5,4},{6,7},{7,6},{8,9},{9,8},{10,11... | collective-permute-start | bytes 786440 | tf_op jit(solution)/shard_map/ppermute | solution.py:508
  41.0 6.9 %collective-permute-start.12 = (f32[24,128]{1,0:T(8,128)S(1)}, f32[24,128]{1,0:T(8,128)S(1)}, u32[]{:S(2)}, u32[]{:S(2)}) collective-permute-start(f32[24,128]{1,0:T(8,128)S(1)} %get-tuple-element.114), channel_id=1, source_target_pairs={{0,12},{1,13},{2,14},{3,15},{4,8},{5,9},{6,10},{7,11},{8,4},{9,5},... | collective-permute-start | bytes 36872 | tf_op jit(solution)/shard_map/ppermute | solution.py:470
  43.3 4.7 %collective-permute-start.11 = (f32[16,128]{1,0:T(8,128)S(1)}, f32[16,128]{1,0:T(8,128)S(1)}, u32[]{:S(2)}, u32[]{:S(2)}) collective-permute-start(f32[16,128]{1,0:T(8,128)S(1)} %get-tuple-element.113), channel_id=1, source_target_pairs={{0,8},{1,9},{2,10},{3,11},{4,12},{5,13},{6,14},{7,15},{8,0},{9,1},... | collective-permute-start | bytes 24584 | tf_op jit(solution)/shard_map/ppermute | solution.py:470
  44.3 3.6 %collective-permute-start.10 = (f32[8,128]{1,0:T(8,128)S(1)}, f32[8,128]{1,0:T(8,128)S(1)}, u32[]{:S(2)}, u32[]{:S(2)}) collective-permute-start(f32[8,128]{1,0:T(8,128)S(1)} %get-tuple-element.112.refs_0_), channel_id=1, source_target_pairs={{0,4},{1,5},{2,6},{3,7},{4,0},{5,1},{6,2},{7,3},{8,12},{9,13},{10,... | collective-permute-start | bytes 12296 | tf_op jit(solution)/shard_map/ppermute | solution.py:470
  47.9 5.4 %collective-permute-start.15 = (f32[24,128]{1,0:T(8,128)S(1)}, f32[24,128]{1,0:T(8,128)S(1)}, u32[]{:S(2)}, u32[]{:S(2)}) collective-permute-start(f32[24,128]{1,0:T(8,128)S(1)} %get-tuple-element.118), channel_id=1, source_target_pairs={{0,3},{1,2},{2,1},{3,0},{4,7},{5,6},{6,5},{7,4},{8,11},{9,10},{10,... | collective-permute-start | bytes 36872 | tf_op jit(solution)/shard_map/ppermute | solution.py:470
  48.0 5.3 %collective-permute-start.14 = (f32[16,128]{1,0:T(8,128)S(1)}, f32[16,128]{1,0:T(8,128)S(1)}, u32[]{:S(2)}, u32[]{:S(2)}) collective-permute-start(f32[16,128]{1,0:T(8,128)S(1)} %get-tuple-element.117), channel_id=1, source_target_pairs={{0,2},{1,3},{2,0},{3,1},{4,6},{5,7},{6,4},{7,5},{8,10},{9,11},{10,... | collective-permute-start | bytes 24584 | tf_op jit(solution)/shard_map/ppermute | solution.py:470
  51.5 1.2 %collective-permute-start.13 = (f32[8,128]{1,0:T(8,128)S(1)}, f32[8,128]{1,0:T(8,128)S(1)}, u32[]{:S(2)}, u32[]{:S(2)}) collective-permute-start(f32[8,128]{1,0:T(8,128)S(1)} %get-tuple-element.116), channel_id=1, source_target_pairs={{0,1},{1,0},{2,3},{3,2},{4,5},{5,4},{6,7},{7,6},{8,9},{9,8},{10,11... | collective-permute-start | bytes 12296 | tf_op jit(solution)/shard_map/ppermute | solution.py:470

commit v17 on v15

--- a/solution.py
+++ b/solution.py
@@ -9,7 +9,7 @@
 
 STEPS = 2
 LANES = 128
-LONG, SHORT = 16, 4
+LONG, SHORT = 20, 4
 VMEM_LIMIT = 14 * 1024 * 1024
 NEAR_FLOPS = 4 * 10**9
 F32 = jnp.float32
@@ -119,7 +119,7 @@
 
 
 def section(slots, per):
-    return -(-(slots + per) // (2 * SHORT)) * SHORT
+    return -(-(slots + per) // (2 * LONG)) * LONG
 
 
 def make_lists(rows, cols, count, positions, groups_of, after, slots, tile, ring_index):
@@ -174,16 +174,19 @@
                 list_ref[2 * (start + total)] = other
                 list_ref[2 * (start + total) + 1] = zero * 256 + k
                 total = total + (other >= 0).astype(jnp.int32)
-            short_turns = (total + SHORT - 1) // SHORT
+            rest = total % LONG
+            padded = rest > 2 * SHORT
+            long_turns = total // LONG + padded.astype(jnp.int32)
+            short_turns = jnp.where(padded, 0, (rest + SHORT - 1) // SHORT)
 
             def pad(pair, carry, start=start, zero=zero):
                 for e in range(2):
                     list_ref[2 * (start + pair) + e] = zero * 256 + per
                 return carry
 
-            lax.fori_loop(total, short_turns * SHORT, pad, 0)
-            list_ref[4 * pairs + 2 * part] = short_turns // (LONG // SHORT)
-            list_ref[4 * pairs + 2 * part + 1] = short_turns % (LONG // SHORT)
+            lax.fori_loop(total, long_turns * LONG + short_turns * SHORT, pad, 0)
+            list_ref[4 * pairs + 2 * part] = long_turns
+            list_ref[4 * pairs + 2 * part + 1] = short_turns
         for i, copy in enumerate(copies[3:]):
             copy.wait()
             r_outs[i][...] = x_outs[i][...].astype(BF16)

time: 54.8 us -> 54.8 us (level); the launches traced: 54.7 us -> 54 us
  starting transfers between devices: 31.5 us -> 28.6 us
  Pallas kernels: 16.4 us -> 18.1 us
  waiting for transfers between devices: 4.26 us -> 4.86 us
    pallas_call x12, Pallas kernels: 16.4 us -> 18.1 us  [call(): pl.pallas_call(body, in_specs=[pl.BlockSpec(memory_space=pl.ANY if s is p...]
    ppermute x6, starting transfers between devices: 9.14 us -> 7.92 us  [sum_over_ring(): lax.ppermute(value, RING, [(j, j ^ bit) for j in range(ring)])]
    ppermute x4, starting transfers between devices: 11.9 us -> 10.9 us  [far_swap(): return lax.ppermute(mine, RING, off_chip)]
    ppermute x6, starting transfers between devices: 10.4 us -> 9.79 us  [near_swap(): return lax.ppermute(mine, RING, on_chip)]
  transfers between devices with their start and end apart: 16 -> 16, of which waited for: 3 -> 5; matrix products, arithmetic and copies ran while one was open for 0% -> 0% of each run, Pallas kernels for 25% -> 29%
where the time goes in v17:
time: 54.8 us; the launch traced here: 54 us
  starting transfers between devices  28.6 us (52%)
  Pallas kernels  18.1 us (33%)
  waiting for transfers between devices  4.86 us (9%)
  between operations  1.54 us (3%)
    pallas_call x12, Pallas kernels, call(): pl.pallas_call(body, in_specs=[pl.BlockSpec(memory_space=pl.ANY if s is p...  18.1 us
    ppermute x4, starting transfers between devices, far_swap(): return lax.ppermute(mine, RING, off_chip)  10.9 us
    ppermute x6, starting transfers between devices, near_swap(): return lax.ppermute(mine, RING, on_chip)  9.79 us
    ppermute x6, starting transfers between devices, sum_over_ring(): lax.ppermute(value, RING, [(j, j ^ bit) for j in range(ring)])  7.92 us
    ppermute x4, waiting for transfers between devices, far_swap(): return lax.ppermute(mine, RING, off_chip)  2.84 us
    ppermute x6, waiting for transfers between devices, sum_over_ring(): lax.ppermute(value, RING, [(j, j ^ bit) for j in range(ring)])  1.91 us
  transfers between devices with their start and end apart: 16, of which 5 were waited for; matrix products, arithmetic and copies ran while one was open for 0% of the time, Pallas kernels for 29%

profile of v17, /device:TPU:0, one launch (start us, length us, event | category | flops | bytes accessed | tf_op | source)
XLA Modules:
  0.0 54.0 jit_solution(8855567104778789083)
XLA Ops:
  0.6 0.0 copy-start.2
  0.7 1.4 %load_first.1 = (f32[1024,128]{1,0:T(8,128)S(1)}, f32[1024,128]{1,0:T(8,128)S(1)}, bf16[1024,128]{1,0:T(8,128)(2,1)S(1)}, bf16[1024,128]{1,0:T(8,128)(2,1)S(1)}, bf16[1024,256]{1,0:T(8,128)(2,1)S(1)}) custom-call(f32[1024,384]{1,0:T(8,128)} %x_ref.3), custom_call_target="tpu_custom_call" | custom-call | flops 1000 | bytes 1000 | tf_op jit(solution)/shard_map/load_first/pallas_call | solution.py:21
  2.1 5.5 %collective-permute-start.4 = (bf16[1024,256]{1,0:T(8,128)(2,1)S(1)}, bf16[1024,256]{1,0:T(8,128)(2,1)S(1)}, u32[]{:S(2)}, u32[]{:S(2)}) collective-permute-start(bf16[1024,256]{1,0:T(8,128)(2,1)S(1)} %get-tuple-element.59._), channel_id=1, source_target_pairs={{0,15},{1,2},{2,1},{3,4},{4,3},{5,6},{6,5},{7,8},{8,7},{9,10},{10,... | collective-permute-start | bytes 1572872 | tf_op jit(solution)/shard_map/ppermute | solution.py:498
  7.6 0.5 collective-permute-start.1
  8.8 2.3 %make_lists.1 = (s32[246]{0:T(256)S(4)}, f32[1024,128]{1,0:T(8,128)S(1)}, bf16[1024,128]{1,0:T(8,128)(2,1)S(1)}) custom-call(s32[96]{0:T(128)S(1)} %copy-done.5, s32[96]{0:T(128)S(1)} %copy-done.6, s32[1]{0:T(128)S(6)} %copy.28.count_hbm, f32[1024,384]{1,0:T(8,128)} %x_ref.3, bf16[1024,256]{1,0:T(8,128)(2,1)S(1)} %get-tuple-element.59._), custom_call_target="tpu_custom_call" | custom-call | flops 1000 | bytes 1000 | tf_op jit(solution)/shard_map/make_lists/pallas_call | solution.py:21
  11.1 0.1 collective-permute-start.2
  11.2 1.3 %first_base.1 = (f32[1024,128]{1,0:T(8,128)S(1)}, f32[1024,128]{1,0:T(8,128)S(1)}, f32[1024,128]{1,0:T(8,128)S(1)}, bf16[384,384]{1,0:T(8,128)(2,1)S(1)}) custom-call(f32[1024,128]{1,0:T(8,128)S(1)} %get-tuple-element.64.refs_0_.refs_4_, f32[1024,128]{1,0:T(8,128)S(1)} %get-tuple-element.65.refs_1_.refs_5_.refs_7_, ...), custom_call_target="tpu_custom_call" | custom-call | flops 1000 | bytes 1000 | tf_op jit(solution)/shard_map/first_base/pallas_call | solution.py:21
  12.6 0.1 collective-permute-done.2.refs_5_
  12.7 0.4 copy-done
  13.1 2.4 %near_first.1 = (f32[1024,128]{1,0:T(8,128)S(1)}, f32[1024,128]{1,0:T(8,128)S(1)}, f32[1024,128]{1,0:T(8,128)S(1)}, bf16[1024,128]{1,0:T(8,128)(2,1)S(1)}) custom-call(s32[246]{0:T(256)S(4)} %get-tuple-element.60.list_ref, bf16[96,128,128]{2,1,0:T(8,128)(2,1)S(1)} %copy-done, bf16[1024,128]{1,0:T(8,128)(2,1)S(1)} %get-tuple-element.61.refs_0_, ...), custom_call_target="tpu_custom_call" | custom-call | flops 1000 | bytes 1000 | tf_op jit(solution)/shard_map/near_first/pallas_call | solution.py:21
  15.5 0.7 %collective-permute-start.3 = (bf16[1024,128]{1,0:T(8,128)(2,1)S(1)}, bf16[1024,128]{1,0:T(8,128)(2,1)S(1)}, u32[]{:S(2)}, u32[]{:S(2)}) collective-permute-start(bf16[1024,128]{1,0:T(8,128)(2,1)S(1)} %get-tuple-element.68), channel_id=1, source_target_pairs={{0,15},{1,2},{2,1},{3,4},{4,3},{5,6},{6,5},{7,8},{8,7},{9,10},{10,... | collective-permute-start | bytes 786440 | tf_op jit(solution)/shard_map/ppermute | solution.py:498
  16.2 1.1 %far_first_0.1 = (bf16[1024,128]{1,0:T(8,128)(2,1)S(1)}, bf16[1024,128]{1,0:T(8,128)(2,1)S(1)}, bf16[1024,128]{1,0:T(8,128)(2,1)S(1)}, bf16[1024,128]{1,0:T(8,12...) custom-call(s32[246]{0:T(256)S(4)} %get-tuple-element.60.list_ref, bf16[96,128,128]{2,1,0:T(8,128)(2,1)S(1)} %copy-done, ...), custom_call_target="tpu_custom_call" | custom-call | flops 1000 | bytes 1000 | tf_op jit(solution)/shard_map/far_first_0/pallas_call | solution.py:21
  17.3 3.9 %collective-permute-start.9 = (bf16[1024,128]{1,0:T(8,128)(2,1)S(1)}, bf16[1024,128]{1,0:T(8,128)(2,1)S(1)}, u32[]{:S(2)}, u32[]{:S(2)}) collective-permute-start(bf16[1024,128]{1,0:T(8,128)(2,1)S(1)} %get-tuple-element.81), channel_id=1, source_target_pairs={{0,15},{1,2},{2,1},{3,4},{4,3},{5,6},{6,5},{7,8},{8,7},{9,10},{10,... | collective-permute-start | bytes 786440 | tf_op jit(solution)/shard_map/ppermute | solution.py:498
  21.2 2.8 %collective-permute-done.3.far_ref = bf16[1024,128]{1,0:T(8,128)(2,1)S(1)} collective-permute-done((bf16[1024,128]{1,0:T(8,128)(2,1)S(1)}, bf16[1024,128]{1,0:T(8,128)(2,1)S(1)}, u32[]{:S(2)}, u32[]{:S(2)}) %collective-permute-start.3) | collective-permute-done | bytes 262176 | tf_op jit(solution)/shard_map/ppermute | solution.py:498
  24.0 1.2 %far_first_1.1 = (bf16[1024,256]{1,0:T(8,128)(2,1)S(1)}, bf16[1024,128]{1,0:T(8,128)(2,1)S(1)}, bf16[1024,128]{1,0:T(8,128)(2,1)S(1)}, bf16[1024,128]{1,0:T(8,128)(2,1)S(1)}) custom-call(s32[246]{0:T(256)S(4)} %get-tuple-element.60.list_ref, bf16[96,128,128]{2,1,0:T(8,128)(2,1)S(1)} %copy-done, bf16[1024,128]{1,0:T(8,128)(2,1)S(1)} %collective-permute-done.3.far_ref, ...), custom_call_target="tpu_custom_call" | custom-call | flops 1000 | bytes 1000 | tf_op jit(solution)/shard_map/far_first_1/pallas_call | solution.py:21
  25.2 0.8 %collective-permute-start.5 = (bf16[1024,256]{1,0:T(8,128)(2,1)S(1)}, bf16[1024,256]{1,0:T(8,128)(2,1)S(1)}, u32[]{:S(2)}, u32[]{:S(2)}) collective-permute-start(bf16[1024,256]{1,0:T(8,128)(2,1)S(1)} %get-tuple-element.77), channel_id=1, source_target_pairs={{0,15},{1,2},{2,1},{3,4},{4,3},{5,6},{6,5},{7,8},{8,7},{9,10},{10,... | collective-permute-start | bytes 1572872 | tf_op jit(solution)/shard_map/ppermute | solution.py:498
  26.0 8.7 %collective-permute-start.6 = (bf16[1024,128]{1,0:T(8,128)(2,1)S(1)}, bf16[1024,128]{1,0:T(8,128)(2,1)S(1)}, u32[]{:S(2)}, u32[]{:S(2)}) collective-permute-start(bf16[1024,128]{1,0:T(8,128)(2,1)S(1)} %get-tuple-element.78.refs_0_.refs_9_), channel_id=1, source_target_pairs={{0,1},{1,0},{2,3},{3,2},{4,5},{5,4},{6,7},{7,6},{8,9},{9,8},{10,11... | collective-permute-start | bytes 786440 | tf_op jit(solution)/shard_map/ppermute | solution.py:501
  34.7 0.5 collective-permute-start.8
  35.2 2.0 %second_base.1 = (f32[1024,128]{1,0:T(8,128)S(1)}, f32[1024,128]{1,0:T(8,128)S(1)}, f32[1024,128]{1,0:T(8,128)S(1)}, f32[1024,128]{1,0:T(8,128)S(1)}, f32[1024,1...) custom-call(f32[1024,128]{1,0:T(8,128)S(1)} %get-tuple-element.84.refs_0_.refs_6_, ...), custom_call_target="tpu_custom_call" | custom-call | flops 1000 | bytes 1000 | tf_op jit(solution)/shard_map/second_base/pallas_call | solution.py:21
  37.3 0.6 %far_second_0.1.refs_6_ = f32[1024,128]{1,0:T(8,128)S(1)} custom-call(s32[246]{0:T(256)S(4)} %get-tuple-element.60.list_ref, bf16[96,128,128]{2,1,0:T(8,128)(2,1)S(1)} %copy-done, bf16[1024,128]{1,0:T(8,128)(2,1)S(1)} %collective-permute-done.9.far_ref), custom_call_target="tpu_custom_call" | custom-call | flops 4000000000 | bytes 1000 | tf_op jit(solution)/shard_map/far_second_0/pallas_call | solution.py:21
  37.9 2.3 %near_second.1 = (bf16[1024,128]{1,0:T(8,128)(2,1)S(1)}, f32[1024,128]{1,0:T(8,128)S(1)}, f32[1024,128]{1,0:T(8,128)S(1)}) custom-call(s32[246]{0:T(256)S(4)} %get-tuple-element.60.list_ref, bf16[96,128,128]{2,1,0:T(8,128)(2,1)S(1)} %copy-done, bf16[1024,128]{1,0:T(8,128)(2,1)S(1)} %get-tuple-element.78.refs_0_.refs_9_, ...), custom_call_target="tpu_custom_call" | custom-call | flops 1000 | bytes 1000 | tf_op jit(solution)/shard_map/near_second/pallas_call | solution.py:21
  40.3 1.2 %far_second_1.1 = (bf16[1024,128]{1,0:T(8,128)(2,1)S(1)}, bf16[1024,128]{1,0:T(8,128)(2,1)S(1)}, f32[8,128]{1,0:T(8,128)S(1)}, f32[16,128]{1,0:T(8,128)S(1)}, f3...) custom-call(s32[246]{0:T(256)S(4)} %get-tuple-element.60.list_ref, ...), custom_call_target="tpu_custom_call", output_to_operand_aliasing={{5}: (8, {}), {6}: (9, {}), {7}: (10, {}), {8}: (11, {}), {... | custom-call | flops 1000 | bytes 1000 | tf_op jit(solution)/shard_map/far_second_1/pallas_call | solution.py:21
  41.5 1.1 %collective-permute-start.12 = (f32[24,128]{1,0:T(8,128)S(1)}, f32[24,128]{1,0:T(8,128)S(1)}, u32[]{:S(2)}, u32[]{:S(2)}) collective-permute-start(f32[24,128]{1,0:T(8,128)S(1)} %get-tuple-element.110), channel_id=1, source_target_pairs={{0,12},{1,13},{2,14},{3,15},{4,8},{5,9},{6,10},{7,11},{8,4},{9,5},... | collective-permute-start | bytes 36872 | tf_op jit(solution)/shard_map/ppermute | solution.py:463
  42.6 2.0 %collective-permute-start.11 = (f32[16,128]{1,0:T(8,128)S(1)}, f32[16,128]{1,0:T(8,128)S(1)}, u32[]{:S(2)}, u32[]{:S(2)}) collective-permute-start(f32[16,128]{1,0:T(8,128)S(1)} %get-tuple-element.109), channel_id=1, source_target_pairs={{0,8},{1,9},{2,10},{3,11},{4,12},{5,13},{6,14},{7,15},{8,0},{9,1},... | collective-permute-start | bytes 24584 | tf_op jit(solution)/shard_map/ppermute | solution.py:463
  44.6 1.3 %collective-permute-start.10 = (f32[8,128]{1,0:T(8,128)S(1)}, f32[8,128]{1,0:T(8,128)S(1)}, u32[]{:S(2)}, u32[]{:S(2)}) collective-permute-start(f32[8,128]{1,0:T(8,128)S(1)} %get-tuple-element.108.refs_0_), channel_id=1, source_target_pairs={{0,4},{1,5},{2,6},{3,7},{4,0},{5,1},{6,2},{7,3},{8,12},{9,13},{10,... | collective-permute-start | bytes 12296 | tf_op jit(solution)/shard_map/ppermute | solution.py:463
  45.9 2.2 %finish.1 = (f32[1024,384]{1,0:T(8,128)}, f32[1024,384]{1,0:T(8,128)}, f32[8,128]{1,0:T(8,128)S(1)}) custom-call(bf16[1024,128]{1,0:T(8,128)(2,1)S(1)} %get-tuple-element.96.refs_0_, bf16[1024,128]{1,0:T(8,128)(2,1)S(1)} %get-tuple-element.97.refs_1_, bf16[1024,128]{1,0:T(8,128)(2,1)S(1)} %get-tuple-element.98.refs_2_, ...), custom_call_target="tpu_custom_call" | custom-call | flops 1000 | bytes 1000 | tf_op jit(solution)/shard_map/finish/pallas_call | solution.py:21
  48.1 0.2 collective-permute-done.10.refs_1_
  48.2 0.5 collective-permute-start.15
  48.7 3.1 %collective-permute-start.14 = (f32[16,128]{1,0:T(8,128)S(1)}, f32[16,128]{1,0:T(8,128)S(1)}, u32[]{:S(2)}, u32[]{:S(2)}) collective-permute-start(f32[16,128]{1,0:T(8,128)S(1)} %get-tuple-element.113), channel_id=1, source_target_pairs={{0,2},{1,3},{2,0},{3,1},{4,6},{5,7},{6,4},{7,5},{8,10},{9,11},{10,... | collective-permute-start | bytes 24584 | tf_op jit(solution)/shard_map/ppermute | solution.py:463
  51.8 1.2 %collective-permute-done.13 = f32[8,128]{1,0:T(8,128)S(1)} collective-permute-done((f32[8,128]{1,0:T(8,128)S(1)}, f32[8,128]{1,0:T(8,128)S(1)}, u32[]{:S(2)}, u32[]{:S(2)}) %collective-permute-start.13) | collective-permute-done | bytes 4128 | tf_op jit(solution)/shard_map/ppermute | solution.py:463
  52.9 0.6 %collective-permute-done.14 = f32[16,128]{1,0:T(8,128)S(1)} collective-permute-done((f32[16,128]{1,0:T(8,128)S(1)}, f32[16,128]{1,0:T(8,128)S(1)}, u32[]{:S(2)}, u32[]{:S(2)}) %collective-permute-start.14) | collective-permute-done | bytes 8224 | tf_op jit(solution)/shard_map/ppermute | solution.py:463
  53.5 0.5 multiply_bitcast_fusion
  (28 shorter events, 0.1 us)
Async XLA Ops:
  0.6 10.6 %copy-start.2 = (bf16[384,384]{1,0:T(8,128)(2,1)S(1)}, bf16[384,384]{1,0:T(8,128)(2,1)}, u32[]{:S(2)}) copy-start(bf16[384,384]{1,0:T(8,128)(2,1)} %constant.7.clone.refs_4_.refs_12_) | copy-start | bytes 884740
  0.6 10.6 %copy-start.3 = (bf16[384,48]{1,0:T(8,128)(2,1)S(1)}, bf16[384,48]{1,0:T(8,128)(2,1)}, u32[]{:S(2)}) copy-start(bf16[384,48]{1,0:T(8,128)(2,1)} %constant.8.clone.refs_5_) | copy-start | bytes 110596
  0.7 8.1 %copy-start.6 = (s32[96]{0:T(128)S(1)}, s32[96]{0:T(128)}, u32[]{:S(2)}) copy-start(s32[96]{0:T(128)} %cols_hbm.1) | copy-start | bytes 1156
  0.7 8.1 %copy-start.5 = (s32[96]{0:T(128)S(1)}, s32[96]{0:T(128)}, u32[]{:S(2)}) copy-start(s32[96]{0:T(128)} %rows_hbm.1) | copy-start | bytes 1156
  0.7 10.5 %copy-start.4 = (bf16[48,48]{1,0:T(8,128)(2,1)S(1)}, bf16[48,48]{1,0:T(8,128)(2,1)}, u32[]{:S(2)}) copy-start(bf16[48,48]{1,0:T(8,128)(2,1)} %refs_6_.1) | copy-start | bytes 13828
  0.7 10.5 %copy-start.1 = (f32[1024,384]{1,0:T(8,128)S(1)}, f32[1024,384]{1,0:T(8,128)}, u32[]{:S(2)}) copy-start(f32[1024,384]{1,0:T(8,128)} %refs_3_.1) | copy-start | bytes 4718596
  2.1 14.1 %collective-permute-start.4 = (bf16[1024,256]{1,0:T(8,128)(2,1)S(1)}, bf16[1024,256]{1,0:T(8,128)(2,1)S(1)}, u32[]{:S(2)}, u32[]{:S(2)}) collective-permute-start(bf16[1024,256]{1,0:T(8,128)(2,1)S(1)} %get-tuple-element.59._), channel_id=1, source_target_pairs={{0,15},{1,2},{2,1},{3,4},{4,3},{5,6},{6,5},{7,8},{8,7},{9,10},{10,... | collective-permute-start | bytes 1572872 | tf_op jit(solution)/shard_map/ppermute | solution.py:498
  7.6 5.0 %collective-permute-start = (bf16[1024,128]{1,0:T(8,128)(2,1)S(1)}, bf16[1024,128]{1,0:T(8,128)(2,1)S(1)}, u32[]{:S(2)}, u32[]{:S(2)}) collective-permute-start(bf16[1024,128]{1,0:T(8,128)(2,1)S(1)} %get-tuple-element.61.refs_0_), channel_id=1, source_target_pairs={{0,1},{1,0},{2,3},{3,2},{4,5},{5,4},{6,7},{7,6},{8,9},{9,8},{10,11... | collective-permute-start | bytes 786440 | tf_op jit(solution)/shard_map/ppermute | solution.py:501
  7.6 5.0 %collective-permute-start.1 = (bf16[1024,128]{1,0:T(8,128)(2,1)S(1)}, bf16[1024,128]{1,0:T(8,128)(2,1)S(1)}, u32[]{:S(2)}, u32[]{:S(2)}) collective-permute-start(bf16[1024,128]{1,0:T(8,128)(2,1)S(1)} %get-tuple-element.62.refs_1_), channel_id=1, source_target_pairs={{0,1},{1,0},{2,3},{3,2},{4,5},{5,4},{6,7},{7,6},{8,9},{9,8},{10,11... | collective-permute-start | bytes 786440 | tf_op jit(solution)/shard_map/ppermute | solution.py:501
  11.1 1.6 %collective-permute-start.2 = (bf16[1024,128]{1,0:T(8,128)(2,1)S(1)}, bf16[1024,128]{1,0:T(8,128)(2,1)S(1)}, u32[]{:S(2)}, u32[]{:S(2)}) collective-permute-start(bf16[1024,128]{1,0:T(8,128)(2,1)S(1)} %get-tuple-element.63.refs_2_.refs_6_), channel_id=1, source_target_pairs={{0,1},{1,0},{2,3},{3,2},{4,5},{5,4},{6,7},{7,6},{8,9},{9,8},{10,11... | collective-permute-start | bytes 786440 | tf_op jit(solution)/shard_map/ppermute | solution.py:501
  11.2 1.9 %copy-start = (bf16[96,128,128]{2,1,0:T(8,128)(2,1)S(1)}, bf16[96,128,128]{2,1,0:T(8,128)(2,1)}, u32[]{:S(2)}) copy-start(bf16[96,128,128]{2,1,0:T(8,128)(2,1)} %tiles_ref.11) | copy-start | bytes 9437188
  15.5 8.6 %collective-permute-start.3 = (bf16[1024,128]{1,0:T(8,128)(2,1)S(1)}, bf16[1024,128]{1,0:T(8,128)(2,1)S(1)}, u32[]{:S(2)}, u32[]{:S(2)}) collective-permute-start(bf16[1024,128]{1,0:T(8,128)(2,1)S(1)} %get-tuple-element.68), channel_id=1, source_target_pairs={{0,15},{1,2},{2,1},{3,4},{4,3},{5,6},{6,5},{7,8},{8,7},{9,10},{10,... | collective-permute-start | bytes 786440 | tf_op jit(solution)/shard_map/ppermute | solution.py:498
  17.3 19.9 %collective-permute-start.9 = (bf16[1024,128]{1,0:T(8,128)(2,1)S(1)}, bf16[1024,128]{1,0:T(8,128)(2,1)S(1)}, u32[]{:S(2)}, u32[]{:S(2)}) collective-permute-start(bf16[1024,128]{1,0:T(8,128)(2,1)S(1)} %get-tuple-element.81), channel_id=1, source_target_pairs={{0,15},{1,2},{2,1},{3,4},{4,3},{5,6},{6,5},{7,8},{8,7},{9,10},{10,... | collective-permute-start | bytes 786440 | tf_op jit(solution)/shard_map/ppermute | solution.py:498
  25.2 15.1 %collective-permute-start.5 = (bf16[1024,256]{1,0:T(8,128)(2,1)S(1)}, bf16[1024,256]{1,0:T(8,128)(2,1)S(1)}, u32[]{:S(2)}, u32[]{:S(2)}) collective-permute-start(bf16[1024,256]{1,0:T(8,128)(2,1)S(1)} %get-tuple-element.77), channel_id=1, source_target_pairs={{0,15},{1,2},{2,1},{3,4},{4,3},{5,6},{6,5},{7,8},{8,7},{9,10},{10,... | collective-permute-start | bytes 1572872 | tf_op jit(solution)/shard_map/ppermute | solution.py:498
  26.0 11.9 %collective-permute-start.6 = (bf16[1024,128]{1,0:T(8,128)(2,1)S(1)}, bf16[1024,128]{1,0:T(8,128)(2,1)S(1)}, u32[]{:S(2)}, u32[]{:S(2)}) collective-permute-start(bf16[1024,128]{1,0:T(8,128)(2,1)S(1)} %get-tuple-element.78.refs_0_.refs_9_), channel_id=1, source_target_pairs={{0,1},{1,0},{2,3},{3,2},{4,5},{5,4},{6,7},{7,6},{8,9},{9,8},{10,11... | collective-permute-start | bytes 786440 | tf_op jit(solution)/shard_map/ppermute | solution.py:501
  34.7 3.2 %collective-permute-start.7 = (bf16[1024,128]{1,0:T(8,128)(2,1)S(1)}, bf16[1024,128]{1,0:T(8,128)(2,1)S(1)}, u32[]{:S(2)}, u32[]{:S(2)}) collective-permute-start(bf16[1024,128]{1,0:T(8,128)(2,1)S(1)} %get-tuple-element.79.refs_1_.refs_10_), channel_id=1, source_target_pairs={{0,1},{1,0},{2,3},{3,2},{4,5},{5,4},{6,7},{7,6},{8,9},{9,8},{10,11... | collective-permute-start | bytes 786440 | tf_op jit(solution)/shard_map/ppermute | solution.py:501
  34.7 3.2 %collective-permute-start.8 = (bf16[1024,128]{1,0:T(8,128)(2,1)S(1)}, bf16[1024,128]{1,0:T(8,128)(2,1)S(1)}, u32[]{:S(2)}, u32[]{:S(2)}) collective-permute-start(bf16[1024,128]{1,0:T(8,128)(2,1)S(1)} %get-tuple-element.80.refs_2_.refs_11_), channel_id=1, source_target_pairs={{0,1},{1,0},{2,3},{3,2},{4,5},{5,4},{6,7},{7,6},{8,9},{9,8},{10,11... | collective-permute-start | bytes 786440 | tf_op jit(solution)/shard_map/ppermute | solution.py:501
  41.5 6.7 %collective-permute-start.12 = (f32[24,128]{1,0:T(8,128)S(1)}, f32[24,128]{1,0:T(8,128)S(1)}, u32[]{:S(2)}, u32[]{:S(2)}) collective-permute-start(f32[24,128]{1,0:T(8,128)S(1)} %get-tuple-element.110), channel_id=1, source_target_pairs={{0,12},{1,13},{2,14},{3,15},{4,8},{5,9},{6,10},{7,11},{8,4},{9,5},... | collective-permute-start | bytes 36872 | tf_op jit(solution)/shard_map/ppermute | solution.py:463
  42.6 5.6 %collective-permute-start.11 = (f32[16,128]{1,0:T(8,128)S(1)}, f32[16,128]{1,0:T(8,128)S(1)}, u32[]{:S(2)}, u32[]{:S(2)}) collective-permute-start(f32[16,128]{1,0:T(8,128)S(1)} %get-tuple-element.109), channel_id=1, source_target_pairs={{0,8},{1,9},{2,10},{3,11},{4,12},{5,13},{6,14},{7,15},{8,0},{9,1},... | collective-permute-start | bytes 24584 | tf_op jit(solution)/shard_map/ppermute | solution.py:463
  44.6 3.6 %collective-permute-start.10 = (f32[8,128]{1,0:T(8,128)S(1)}, f32[8,128]{1,0:T(8,128)S(1)}, u32[]{:S(2)}, u32[]{:S(2)}) collective-permute-start(f32[8,128]{1,0:T(8,128)S(1)} %get-tuple-element.108.refs_0_), channel_id=1, source_target_pairs={{0,4},{1,5},{2,6},{3,7},{4,0},{5,1},{6,2},{7,3},{8,12},{9,13},{10,... | collective-permute-start | bytes 12296 | tf_op jit(solution)/shard_map/ppermute | solution.py:463
  48.2 5.3 %collective-permute-start.15 = (f32[24,128]{1,0:T(8,128)S(1)}, f32[24,128]{1,0:T(8,128)S(1)}, u32[]{:S(2)}, u32[]{:S(2)}) collective-permute-start(f32[24,128]{1,0:T(8,128)S(1)} %get-tuple-element.114), channel_id=1, source_target_pairs={{0,3},{1,2},{2,1},{3,0},{4,7},{5,6},{6,5},{7,4},{8,11},{9,10},{10,... | collective-permute-start | bytes 36872 | tf_op jit(solution)/shard_map/ppermute | solution.py:463
  48.7 4.8 %collective-permute-start.14 = (f32[16,128]{1,0:T(8,128)S(1)}, f32[16,128]{1,0:T(8,128)S(1)}, u32[]{:S(2)}, u32[]{:S(2)}) collective-permute-start(f32[16,128]{1,0:T(8,128)S(1)} %get-tuple-element.113), channel_id=1, source_target_pairs={{0,2},{1,3},{2,0},{3,1},{4,6},{5,7},{6,4},{7,5},{8,10},{9,11},{10,... | collective-permute-start | bytes 24584 | tf_op jit(solution)/shard_map/ppermute | solution.py:463
  51.8 1.2 %collective-permute-start.13 = (f32[8,128]{1,0:T(8,128)S(1)}, f32[8,128]{1,0:T(8,128)S(1)}, u32[]{:S(2)}, u32[]{:S(2)}) collective-permute-start(f32[8,128]{1,0:T(8,128)S(1)} %get-tuple-element.112), channel_id=1, source_target_pairs={{0,1},{1,0},{2,3},{3,2},{4,5},{5,4},{6,7},{7,6},{8,9},{9,8},{10,11... | collective-permute-start | bytes 12296 | tf_op jit(solution)/shard_map/ppermute | solution.py:463

commit v18 on v17

--- a/solution.py
+++ b/solution.py
@@ -93,7 +93,7 @@
     n = len(groups_of)
 
     def body(x_ref, *refs):
-        x_outs, r_outs, sent, sems = refs[:n], refs[n : 2 * n], refs[2 * n], refs[-1]
+        x_outs, sent, sems = refs[:n], refs[n], refs[-1]
         copies = [
             pltpu.make_async_copy(x_ref.at[:, lanes(g)], x_outs[i], sems.at[i])
             for i, g in enumerate(groups_of)
@@ -102,35 +102,31 @@
             copy.start()
         for i, copy in enumerate(copies):
             copy.wait()
-            rounded = x_outs[i][...].astype(BF16)
-            r_outs[i][...] = rounded
-            sent[:, lanes(i)] = rounded
+            sent[:, lanes(i)] = x_outs[i][...].astype(BF16)
 
     outs = call(
         body,
         [(positions, pltpu.HBM)],
-        [((cells, LANES), F32, pltpu.VMEM)] * n
-        + [((cells, LANES), BF16, pltpu.VMEM)] * n
-        + [((cells, n * LANES), BF16, pltpu.VMEM)],
+        [((cells, LANES), F32, pltpu.VMEM)] * n + [((cells, n * LANES), BF16, pltpu.VMEM)],
         [pltpu.SemaphoreType.DMA((n,))],
         "load_first",
     )
-    return outs[:n], outs[n : 2 * n], outs[2 * n]
+    return outs[:n], outs[n]
 
 
 def section(slots, per):
     return -(-(slots + per) // (2 * LONG)) * LONG
 
 
-def make_lists(rows, cols, count, positions, groups_of, after, slots, tile, ring_index):
+def make_lists(rows, cols, count, positions, groups_of, sent, slots, tile, ring_index):
     cells = positions.shape[0]
     per = cells // tile
     pairs = section(slots, per)
-    n = len(groups_of)
-
-    def body(rows_hbm, cols_hbm, count_hbm, x_ref, _, list_ref, *refs):
-        x_outs, r_outs = refs[:n], refs[n : 2 * n]
-        rows_ref, cols_ref, count_ref, held, sems = refs[2 * n :]
+    n, early = len(groups_of), sent.shape[1] // LANES
+
+    def body(rows_hbm, cols_hbm, count_hbm, x_ref, sent_ref, list_ref, *refs):
+        x_outs, r_outs, cut_outs = refs[:n], refs[n : 2 * n], refs[2 * n : 2 * n + early]
+        rows_ref, cols_ref, count_ref, held, sems = refs[2 * n + early :]
         copies = [
             pltpu.make_async_copy(*ends, sems.at[k])
             for k, ends in enumerate(
@@ -140,6 +136,8 @@
         ]
         for copy in copies:
             copy.start()
+        for i, out in enumerate(cut_outs):
+            out[...] = sent_ref[:, lanes(i)]
         for k in range(2 * per):
             held[k] = -1
         far_third = jnp.where(lax.rem(ring_index(), 2) == 1, 2, 0)
@@ -193,10 +191,10 @@
 
     outs = call(
         body,
-        [(a, pl.ANY) for a in (rows, cols, count)] + [(positions, pltpu.HBM)] + vmem(after),
+        [(a, pl.ANY) for a in (rows, cols, count)] + [(positions, pltpu.HBM)] + vmem(sent),
         [((4 * pairs + 4 + 2,), jnp.int32, pltpu.SMEM)]
         + [((cells, LANES), F32, pltpu.VMEM)] * n
-        + [((cells, LANES), BF16, pltpu.VMEM)] * n,
+        + [((cells, LANES), BF16, pltpu.VMEM)] * (n + early),
         [
             pltpu.SMEM(rows.shape, jnp.int32),
             pltpu.SMEM(cols.shape, jnp.int32),
@@ -206,7 +204,7 @@
         ],
         "make_lists",
     )
-    return outs[0], outs[1 : 1 + n], outs[1 + n :]
+    return outs[0], outs[1 : 1 + n], outs[1 + n : 1 + 2 * n], outs[1 + 2 * n :]
 
 
 def add_pairs(part, list_ref, tiles, field, window, pairs):
@@ -511,9 +509,9 @@
     def needed(todo, piece):
         return sorted({n for t in todo for n in spanned(t, channels, width)} - set(piece))
 
-    xs, owns, sent = load_first(positions, first_pieces[0])
+    xs, sent = load_first(positions, first_pieces[0])
     fars = [far_swap(sent)]
-    lists, more_x, more_own = make_lists(
+    lists, more_x, more_own, owns = make_lists(
         tile_rows, tile_cols, tile_count, positions, first_pieces[1], sent, slots, tile, ring_index
     )
     xs, owns = [*xs, *more_x], [*owns, *more_own]
@@ -536,10 +534,14 @@
             done = [field.astype(BF16) for field in done]
             held.update(zip(piece, done))
             rest = ins[1 + len(known) :]
+            near = sorted(held)
+            mixed = jnp.dot(
+                jnp.concatenate([held[n] for n in near], axis=1),
+                ins[0][span_lanes(near), span_lanes(todo)],
+                preferred_element_type=F32,
+            )
             for i, t in enumerate(todo):
-                x_new, y_new = updated(
-                    mixed_of(held, ins[0], t, channels), rest[2 * i][...], rest[2 * i + 1][...]
-                )
+                x_new, y_new = updated(mixed[:, lanes(i)], rest[2 * i][...], rest[2 * i + 1][...])
                 r_new = x_new.astype(BF16)
                 outs[0][:, lanes(i)] = r_new
                 outs[1 + i][...] = r_new

time: 54.8 us -> 54.1 us (0.987)
  Pallas kernels: 18.1 us -> 14.6 us
  starting transfers between devices: 28.6 us -> 31.9 us
    pallas_call x12, Pallas kernels: 18.1 us -> 14.6 us  [call(): pl.pallas_call(body, in_specs=[pl.BlockSpec(memory_space=pl.ANY if s is p...]
    ppermute x4, starting transfers between devices: 10.9 us -> 12.8 us  [far_swap(): return lax.ppermute(mine, RING, off_chip)]
    ppermute x6, starting transfers between devices: 9.79 us -> 10.8 us  [near_swap(): return lax.ppermute(mine, RING, on_chip)]
    ppermute x4, waiting for transfers between devices: 2.84 us -> 2.18 us  [far_swap(): return lax.ppermute(mine, RING, off_chip)]
  transfers between devices with their start and end apart: 16 -> 16, of which waited for: 5 -> 5; matrix products, arithmetic and copies ran while one was open for 0% -> 0% of each run, Pallas kernels for 29% -> 23%
where the time goes in v18:
time: 54.1 us; the launch traced here: 53.6 us
  starting transfers between devices  31.9 us (59%)
  Pallas kernels  14.6 us (27%)
  waiting for transfers between devices  4.7 us (9%)
  between operations  1.52 us (3%)
    pallas_call x12, Pallas kernels, call(): pl.pallas_call(body, in_specs=[pl.BlockSpec(memory_space=pl.ANY if s is p...  14.6 us
    ppermute x4, starting transfers between devices, far_swap(): return lax.ppermute(mine, RING, off_chip)  12.8 us
    ppermute x6, starting transfers between devices, near_swap(): return lax.ppermute(mine, RING, on_chip)  10.8 us
    ppermute x6, starting transfers between devices, sum_over_ring(): lax.ppermute(value, RING, [(j, j ^ bit) for j in range(ring)])  8.37 us
    ppermute x6, waiting for transfers between devices, sum_over_ring(): lax.ppermute(value, RING, [(j, j ^ bit) for j in range(ring)])  2.21 us
    ppermute x4, waiting for transfers between devices, far_swap(): return lax.ppermute(mine, RING, off_chip)  2.18 us
  transfers between devices with their start and end apart: 16, of which 5 were waited for; matrix products, arithmetic and copies ran while one was open for 0% of the time, Pallas kernels for 23%

profile of v18, /device:TPU:0, one launch (start us, length us, event | category | flops | bytes accessed | tf_op | source)
XLA Modules:
  0.0 53.6 jit_solution(5941225567306857714)
XLA Ops:
  0.7 1.4 %load_first.1 = (f32[1024,128]{1,0:T(8,128)S(1)}, f32[1024,128]{1,0:T(8,128)S(1)}, bf16[1024,256]{1,0:T(8,128)(2,1)S(1)}) custom-call(f32[1024,384]{1,0:T(8,128)} %x_ref.3), custom_call_target="tpu_custom_call" | custom-call | flops 1000 | bytes 1000 | tf_op jit(solution)/shard_map/load_first/pallas_call | solution.py:21
  2.1 5.5 %collective-permute-start.4 = (bf16[1024,256]{1,0:T(8,128)(2,1)S(1)}, bf16[1024,256]{1,0:T(8,128)(2,1)S(1)}, u32[]{:S(2)}, u32[]{:S(2)}) collective-permute-start(bf16[1024,256]{1,0:T(8,128)(2,1)S(1)} %get-tuple-element.59.sent_ref), channel_id=1, source_target_pairs={{0,15},{1,2},{2,1},{3,4},{4,3},{5,6},{6,5},{7,8},{8,7},{9,10},{10,... | collective-permute-start | bytes 1572872 | tf_op jit(solution)/shard_map/ppermute | solution.py:496
  8.3 1.3 %make_lists.1 = (s32[246]{0:T(256)S(4)}, f32[1024,128]{1,0:T(8,128)S(1)}, bf16[1024,128]{1,0:T(8,128)(2,1)S(1)}, bf16[1024,128]{1,0:T(8,128)(2,1)S(1)}, bf16[1024,128]{1,0:T(8,128)(2,1)S(1)}) custom-call(s32[96]{0:T(128)S(1)} %copy-done.5, s32[96]{0:T(128)S(1)} %copy-done.6, s32[1]{0:T(128)S(6)} %copy.28.count_hbm, f32[1024,384]{1,0:T(8,128)} %x_ref.3, ...), custom_call_target="tpu_custom_call" | custom-call | flops 1000 | bytes 1000 | tf_op jit(solution)/shard_map/make_lists/pallas_call | solution.py:21
  9.6 0.1 collective-permute-start
  9.7 0.5 collective-permute-start.1
  10.2 0.1 collective-permute-start.2
  10.3 1.3 %first_base.1 = (f32[1024,128]{1,0:T(8,128)S(1)}, f32[1024,128]{1,0:T(8,128)S(1)}, f32[1024,128]{1,0:T(8,128)S(1)}, bf16[384,384]{1,0:T(8,128)(2,1)S(1)}) custom-call(f32[1024,128]{1,0:T(8,128)S(1)} %get-tuple-element.64.refs_0_.refs_4_, f32[1024,128]{1,0:T(8,128)S(1)} %get-tuple-element.65.refs_1_.refs_5_.refs_7_, ...), custom_call_target="tpu_custom_call" | custom-call | flops 1000 | bytes 1000 | tf_op jit(solution)/shard_map/first_base/pallas_call | solution.py:21
  11.6 0.3 collective-permute-done.2.refs_5_
  11.9 0.2 copy-done
  12.2 1.4 %near_first.1 = (f32[1024,128]{1,0:T(8,128)S(1)}, f32[1024,128]{1,0:T(8,128)S(1)}, f32[1024,128]{1,0:T(8,128)S(1)}, bf16[1024,128]{1,0:T(8,128)(2,1)S(1)}) custom-call(s32[246]{0:T(256)S(4)} %get-tuple-element.60.list_ref, bf16[96,128,128]{2,1,0:T(8,128)(2,1)S(1)} %copy-done, bf16[1024,128]{1,0:T(8,128)(2,1)S(1)} %get-tuple-element.61.refs_0_, ...), custom_call_target="tpu_custom_call" | custom-call | flops 1000 | bytes 1000 | tf_op jit(solution)/shard_map/near_first/pallas_call | solution.py:21
  13.6 1.7 %collective-permute-start.3 = (bf16[1024,128]{1,0:T(8,128)(2,1)S(1)}, bf16[1024,128]{1,0:T(8,128)(2,1)S(1)}, u32[]{:S(2)}, u32[]{:S(2)}) collective-permute-start(bf16[1024,128]{1,0:T(8,128)(2,1)S(1)} %get-tuple-element.68), channel_id=1, source_target_pairs={{0,15},{1,2},{2,1},{3,4},{4,3},{5,6},{6,5},{7,8},{8,7},{9,10},{10,... | collective-permute-start | bytes 786440 | tf_op jit(solution)/shard_map/ppermute | solution.py:496
  15.3 1.0 %far_first_0.1 = (bf16[1024,128]{1,0:T(8,128)(2,1)S(1)}, bf16[1024,128]{1,0:T(8,128)(2,1)S(1)}, bf16[1024,128]{1,0:T(8,128)(2,1)S(1)}, bf16[1024,128]{1,0:T(8,12...) custom-call(s32[246]{0:T(256)S(4)} %get-tuple-element.60.list_ref, bf16[96,128,128]{2,1,0:T(8,128)(2,1)S(1)} %copy-done, ...), custom_call_target="tpu_custom_call" | custom-call | flops 1000 | bytes 1000 | tf_op jit(solution)/shard_map/far_first_0/pallas_call | solution.py:21
  16.3 3.7 %collective-permute-start.9 = (bf16[1024,128]{1,0:T(8,128)(2,1)S(1)}, bf16[1024,128]{1,0:T(8,128)(2,1)S(1)}, u32[]{:S(2)}, u32[]{:S(2)}) collective-permute-start(bf16[1024,128]{1,0:T(8,128)(2,1)S(1)} %get-tuple-element.81), channel_id=1, source_target_pairs={{0,15},{1,2},{2,1},{3,4},{4,3},{5,6},{6,5},{7,8},{8,7},{9,10},{10,... | collective-permute-start | bytes 786440 | tf_op jit(solution)/shard_map/ppermute | solution.py:496
  20.1 2.2 %collective-permute-done.3.far_ref = bf16[1024,128]{1,0:T(8,128)(2,1)S(1)} collective-permute-done((bf16[1024,128]{1,0:T(8,128)(2,1)S(1)}, bf16[1024,128]{1,0:T(8,128)(2,1)S(1)}, u32[]{:S(2)}, u32[]{:S(2)}) %collective-permute-start.3) | collective-permute-done | bytes 262176 | tf_op jit(solution)/shard_map/ppermute | solution.py:496
  22.2 1.0 %far_first_1.1 = (bf16[1024,256]{1,0:T(8,128)(2,1)S(1)}, bf16[1024,128]{1,0:T(8,128)(2,1)S(1)}, bf16[1024,128]{1,0:T(8,128)(2,1)S(1)}, bf16[1024,128]{1,0:T(8,128)(2,1)S(1)}) custom-call(s32[246]{0:T(256)S(4)} %get-tuple-element.60.list_ref, bf16[96,128,128]{2,1,0:T(8,128)(2,1)S(1)} %copy-done, bf16[1024,128]{1,0:T(8,128)(2,1)S(1)} %collective-permute-done.3.far_ref, ...), custom_call_target="tpu_custom_call" | custom-call | flops 1000 | bytes 1000 | tf_op jit(solution)/shard_map/far_first_1/pallas_call | solution.py:21
  23.2 1.8 %collective-permute-start.5 = (bf16[1024,256]{1,0:T(8,128)(2,1)S(1)}, bf16[1024,256]{1,0:T(8,128)(2,1)S(1)}, u32[]{:S(2)}, u32[]{:S(2)}) collective-permute-start(bf16[1024,256]{1,0:T(8,128)(2,1)S(1)} %get-tuple-element.77), channel_id=1, source_target_pairs={{0,15},{1,2},{2,1},{3,4},{4,3},{5,6},{6,5},{7,8},{8,7},{9,10},{10,... | collective-permute-start | bytes 1572872 | tf_op jit(solution)/shard_map/ppermute | solution.py:496
  25.0 9.6 %collective-permute-start.6 = (bf16[1024,128]{1,0:T(8,128)(2,1)S(1)}, bf16[1024,128]{1,0:T(8,128)(2,1)S(1)}, u32[]{:S(2)}, u32[]{:S(2)}) collective-permute-start(bf16[1024,128]{1,0:T(8,128)(2,1)S(1)} %get-tuple-element.78.refs_0_.refs_9_), channel_id=1, source_target_pairs={{0,1},{1,0},{2,3},{3,2},{4,5},{5,4},{6,7},{7,6},{8,9},{9,8},{10,11... | collective-permute-start | bytes 786440 | tf_op jit(solution)/shard_map/ppermute | solution.py:499
  34.6 0.5 collective-permute-start.8
  35.1 2.0 %second_base.1 = (f32[1024,128]{1,0:T(8,128)S(1)}, f32[1024,128]{1,0:T(8,128)S(1)}, f32[1024,128]{1,0:T(8,128)S(1)}, f32[1024,128]{1,0:T(8,128)S(1)}, f32[1024,1...) custom-call(f32[1024,128]{1,0:T(8,128)S(1)} %get-tuple-element.84.refs_0_.refs_6_, ...), custom_call_target="tpu_custom_call" | custom-call | flops 1000 | bytes 1000 | tf_op jit(solution)/shard_map/second_base/pallas_call | solution.py:21
  37.2 0.6 %far_second_0.1.refs_6_ = f32[1024,128]{1,0:T(8,128)S(1)} custom-call(s32[246]{0:T(256)S(4)} %get-tuple-element.60.list_ref, bf16[96,128,128]{2,1,0:T(8,128)(2,1)S(1)} %copy-done, bf16[1024,128]{1,0:T(8,128)(2,1)S(1)} %collective-permute-done.9.far_ref), custom_call_target="tpu_custom_call" | custom-call | flops 4000000000 | bytes 1000 | tf_op jit(solution)/shard_map/far_second_0/pallas_call | solution.py:21
  37.8 1.4 %near_second.1 = (bf16[1024,128]{1,0:T(8,128)(2,1)S(1)}, f32[1024,128]{1,0:T(8,128)S(1)}, f32[1024,128]{1,0:T(8,128)S(1)}) custom-call(s32[246]{0:T(256)S(4)} %get-tuple-element.60.list_ref, bf16[96,128,128]{2,1,0:T(8,128)(2,1)S(1)} %copy-done, bf16[1024,128]{1,0:T(8,128)(2,1)S(1)} %get-tuple-element.78.refs_0_.refs_9_, ...), custom_call_target="tpu_custom_call" | custom-call | flops 1000 | bytes 1000 | tf_op jit(solution)/shard_map/near_second/pallas_call | solution.py:21
  39.2 1.0 %far_second_1.1 = (bf16[1024,128]{1,0:T(8,128)(2,1)S(1)}, bf16[1024,128]{1,0:T(8,128)(2,1)S(1)}, f32[8,128]{1,0:T(8,128)S(1)}, f32[16,128]{1,0:T(8,128)S(1)}, f3...) custom-call(s32[246]{0:T(256)S(4)} %get-tuple-element.60.list_ref, ...), custom_call_target="tpu_custom_call", output_to_operand_aliasing={{5}: (8, {}), {6}: (9, {}), {7}: (10, {}), {8}: (11, {}), {... | custom-call | flops 1000 | bytes 1000 | tf_op jit(solution)/shard_map/far_second_1/pallas_call | solution.py:21
  40.3 1.9 %collective-permute-start.12 = (f32[24,128]{1,0:T(8,128)S(1)}, f32[24,128]{1,0:T(8,128)S(1)}, u32[]{:S(2)}, u32[]{:S(2)}) collective-permute-start(f32[24,128]{1,0:T(8,128)S(1)} %get-tuple-element.110), channel_id=1, source_target_pairs={{0,12},{1,13},{2,14},{3,15},{4,8},{5,9},{6,10},{7,11},{8,4},{9,5},... | collective-permute-start | bytes 36872 | tf_op jit(solution)/shard_map/ppermute | solution.py:461
  42.2 1.5 %collective-permute-start.11 = (f32[16,128]{1,0:T(8,128)S(1)}, f32[16,128]{1,0:T(8,128)S(1)}, u32[]{:S(2)}, u32[]{:S(2)}) collective-permute-start(f32[16,128]{1,0:T(8,128)S(1)} %get-tuple-element.109), channel_id=1, source_target_pairs={{0,8},{1,9},{2,10},{3,11},{4,12},{5,13},{6,14},{7,15},{8,0},{9,1},... | collective-permute-start | bytes 24584 | tf_op jit(solution)/shard_map/ppermute | solution.py:461
  43.7 1.0 %collective-permute-start.10 = (f32[8,128]{1,0:T(8,128)S(1)}, f32[8,128]{1,0:T(8,128)S(1)}, u32[]{:S(2)}, u32[]{:S(2)}) collective-permute-start(f32[8,128]{1,0:T(8,128)S(1)} %get-tuple-element.108.refs_0_), channel_id=1, source_target_pairs={{0,4},{1,5},{2,6},{3,7},{4,0},{5,1},{6,2},{7,3},{8,12},{9,13},{10,... | collective-permute-start | bytes 12296 | tf_op jit(solution)/shard_map/ppermute | solution.py:461
  44.7 2.2 %finish.1 = (f32[1024,384]{1,0:T(8,128)}, f32[1024,384]{1,0:T(8,128)}, f32[8,128]{1,0:T(8,128)S(1)}) custom-call(bf16[1024,128]{1,0:T(8,128)(2,1)S(1)} %get-tuple-element.96.refs_0_, bf16[1024,128]{1,0:T(8,128)(2,1)S(1)} %get-tuple-element.97.refs_1_, bf16[1024,128]{1,0:T(8,128)(2,1)S(1)} %get-tuple-element.98.refs_2_, ...), custom_call_target="tpu_custom_call" | custom-call | flops 1000 | bytes 1000 | tf_op jit(solution)/shard_map/finish/pallas_call | solution.py:21
  46.8 0.6 %collective-permute-done.10.refs_1_ = f32[8,128]{1,0:T(8,128)S(1)} collective-permute-done((f32[8,128]{1,0:T(8,128)S(1)}, f32[8,128]{1,0:T(8,128)S(1)}, u32[]{:S(2)}, u32[]{:S(2)}) %collective-permute-start.10) | collective-permute-done | bytes 4128 | tf_op jit(solution)/shard_map/ppermute | solution.py:461
  47.4 0.1 collective-permute-start.15
  47.5 3.9 %collective-permute-start.14 = (f32[16,128]{1,0:T(8,128)S(1)}, f32[16,128]{1,0:T(8,128)S(1)}, u32[]{:S(2)}, u32[]{:S(2)}) collective-permute-start(f32[16,128]{1,0:T(8,128)S(1)} %get-tuple-element.113), channel_id=1, source_target_pairs={{0,2},{1,3},{2,0},{3,1},{4,6},{5,7},{6,4},{7,5},{8,10},{9,11},{10,... | collective-permute-start | bytes 24584 | tf_op jit(solution)/shard_map/ppermute | solution.py:461
  51.4 1.1 %collective-permute-done.13 = f32[8,128]{1,0:T(8,128)S(1)} collective-permute-done((f32[8,128]{1,0:T(8,128)S(1)}, f32[8,128]{1,0:T(8,128)S(1)}, u32[]{:S(2)}, u32[]{:S(2)}) %collective-permute-start.13) | collective-permute-done | bytes 4128 | tf_op jit(solution)/shard_map/ppermute | solution.py:461
  52.5 0.5 collective-permute-done.14
  53.0 0.5 multiply_bitcast_fusion
  (28 shorter events, 0.1 us)
Async XLA Ops:
  0.6 9.6 %copy-start.2 = (bf16[384,384]{1,0:T(8,128)(2,1)S(1)}, bf16[384,384]{1,0:T(8,128)(2,1)}, u32[]{:S(2)}) copy-start(bf16[384,384]{1,0:T(8,128)(2,1)} %constant.7.clone.refs_4_.refs_12_) | copy-start | bytes 884740
  0.6 9.6 %copy-start.3 = (bf16[384,48]{1,0:T(8,128)(2,1)S(1)}, bf16[384,48]{1,0:T(8,128)(2,1)}, u32[]{:S(2)}) copy-start(bf16[384,48]{1,0:T(8,128)(2,1)} %constant.8.clone.refs_5_) | copy-start | bytes 110596
  0.7 7.6 %copy-start.6 = (s32[96]{0:T(128)S(1)}, s32[96]{0:T(128)}, u32[]{:S(2)}) copy-start(s32[96]{0:T(128)} %cols_hbm.1) | copy-start | bytes 1156
  0.7 7.6 %copy-start.5 = (s32[96]{0:T(128)S(1)}, s32[96]{0:T(128)}, u32[]{:S(2)}) copy-start(s32[96]{0:T(128)} %rows_hbm.1) | copy-start | bytes 1156
  0.7 9.6 %copy-start.4 = (bf16[48,48]{1,0:T(8,128)(2,1)S(1)}, bf16[48,48]{1,0:T(8,128)(2,1)}, u32[]{:S(2)}) copy-start(bf16[48,48]{1,0:T(8,128)(2,1)} %refs_6_.1) | copy-start | bytes 13828
  0.7 9.6 %copy-start.1 = (f32[1024,384]{1,0:T(8,128)S(1)}, f32[1024,384]{1,0:T(8,128)}, u32[]{:S(2)}) copy-start(f32[1024,384]{1,0:T(8,128)} %refs_3_.1) | copy-start | bytes 4718596
  2.1 13.2 %collective-permute-start.4 = (bf16[1024,256]{1,0:T(8,128)(2,1)S(1)}, bf16[1024,256]{1,0:T(8,128)(2,1)S(1)}, u32[]{:S(2)}, u32[]{:S(2)}) collective-permute-start(bf16[1024,256]{1,0:T(8,128)(2,1)S(1)} %get-tuple-element.59.sent_ref), channel_id=1, source_target_pairs={{0,15},{1,2},{2,1},{3,4},{4,3},{5,6},{6,5},{7,8},{8,7},{9,10},{10,... | collective-permute-start | bytes 1572872 | tf_op jit(solution)/shard_map/ppermute | solution.py:496
  9.6 2.0 %collective-permute-start = (bf16[1024,128]{1,0:T(8,128)(2,1)S(1)}, bf16[1024,128]{1,0:T(8,128)(2,1)S(1)}, u32[]{:S(2)}, u32[]{:S(2)}) collective-permute-start(bf16[1024,128]{1,0:T(8,128)(2,1)S(1)} %get-tuple-element.61.refs_0_), channel_id=1, source_target_pairs={{0,1},{1,0},{2,3},{3,2},{4,5},{5,4},{6,7},{7,6},{8,9},{9,8},{10,11... | collective-permute-start | bytes 786440 | tf_op jit(solution)/shard_map/ppermute | solution.py:499
  9.7 2.0 %collective-permute-start.1 = (bf16[1024,128]{1,0:T(8,128)(2,1)S(1)}, bf16[1024,128]{1,0:T(8,128)(2,1)S(1)}, u32[]{:S(2)}, u32[]{:S(2)}) collective-permute-start(bf16[1024,128]{1,0:T(8,128)(2,1)S(1)} %get-tuple-element.62.refs_1_), channel_id=1, source_target_pairs={{0,1},{1,0},{2,3},{3,2},{4,5},{5,4},{6,7},{7,6},{8,9},{9,8},{10,11... | collective-permute-start | bytes 786440 | tf_op jit(solution)/shard_map/ppermute | solution.py:499
  10.2 1.8 %collective-permute-start.2 = (bf16[1024,128]{1,0:T(8,128)(2,1)S(1)}, bf16[1024,128]{1,0:T(8,128)(2,1)S(1)}, u32[]{:S(2)}, u32[]{:S(2)}) collective-permute-start(bf16[1024,128]{1,0:T(8,128)(2,1)S(1)} %get-tuple-element.63.refs_2_.refs_6_), channel_id=1, source_target_pairs={{0,1},{1,0},{2,3},{3,2},{4,5},{5,4},{6,7},{7,6},{8,9},{9,8},{10,11... | collective-permute-start | bytes 786440 | tf_op jit(solution)/shard_map/ppermute | solution.py:499
  10.3 1.9 %copy-start = (bf16[96,128,128]{2,1,0:T(8,128)(2,1)S(1)}, bf16[96,128,128]{2,1,0:T(8,128)(2,1)}, u32[]{:S(2)}) copy-start(bf16[96,128,128]{2,1,0:T(8,128)(2,1)} %tiles_ref.11) | copy-start | bytes 9437188
  13.6 8.7 %collective-permute-start.3 = (bf16[1024,128]{1,0:T(8,128)(2,1)S(1)}, bf16[1024,128]{1,0:T(8,128)(2,1)S(1)}, u32[]{:S(2)}, u32[]{:S(2)}) collective-permute-start(bf16[1024,128]{1,0:T(8,128)(2,1)S(1)} %get-tuple-element.68), channel_id=1, source_target_pairs={{0,15},{1,2},{2,1},{3,4},{4,3},{5,6},{6,5},{7,8},{8,7},{9,10},{10,... | collective-permute-start | bytes 786440 | tf_op jit(solution)/shard_map/ppermute | solution.py:496
  16.3 20.9 %collective-permute-start.9 = (bf16[1024,128]{1,0:T(8,128)(2,1)S(1)}, bf16[1024,128]{1,0:T(8,128)(2,1)S(1)}, u32[]{:S(2)}, u32[]{:S(2)}) collective-permute-start(bf16[1024,128]{1,0:T(8,128)(2,1)S(1)} %get-tuple-element.81), channel_id=1, source_target_pairs={{0,15},{1,2},{2,1},{3,4},{4,3},{5,6},{6,5},{7,8},{8,7},{9,10},{10,... | collective-permute-start | bytes 786440 | tf_op jit(solution)/shard_map/ppermute | solution.py:496
  23.2 16.0 %collective-permute-start.5 = (bf16[1024,256]{1,0:T(8,128)(2,1)S(1)}, bf16[1024,256]{1,0:T(8,128)(2,1)S(1)}, u32[]{:S(2)}, u32[]{:S(2)}) collective-permute-start(bf16[1024,256]{1,0:T(8,128)(2,1)S(1)} %get-tuple-element.77), channel_id=1, source_target_pairs={{0,15},{1,2},{2,1},{3,4},{4,3},{5,6},{6,5},{7,8},{8,7},{9,10},{10,... | collective-permute-start | bytes 1572872 | tf_op jit(solution)/shard_map/ppermute | solution.py:496
  25.0 12.8 %collective-permute-start.6 = (bf16[1024,128]{1,0:T(8,128)(2,1)S(1)}, bf16[1024,128]{1,0:T(8,128)(2,1)S(1)}, u32[]{:S(2)}, u32[]{:S(2)}) collective-permute-start(bf16[1024,128]{1,0:T(8,128)(2,1)S(1)} %get-tuple-element.78.refs_0_.refs_9_), channel_id=1, source_target_pairs={{0,1},{1,0},{2,3},{3,2},{4,5},{5,4},{6,7},{7,6},{8,9},{9,8},{10,11... | collective-permute-start | bytes 786440 | tf_op jit(solution)/shard_map/ppermute | solution.py:499
  34.6 3.2 %collective-permute-start.7 = (bf16[1024,128]{1,0:T(8,128)(2,1)S(1)}, bf16[1024,128]{1,0:T(8,128)(2,1)S(1)}, u32[]{:S(2)}, u32[]{:S(2)}) collective-permute-start(bf16[1024,128]{1,0:T(8,128)(2,1)S(1)} %get-tuple-element.79.refs_1_.refs_10_), channel_id=1, source_target_pairs={{0,1},{1,0},{2,3},{3,2},{4,5},{5,4},{6,7},{7,6},{8,9},{9,8},{10,11... | collective-permute-start | bytes 786440 | tf_op jit(solution)/shard_map/ppermute | solution.py:499
  34.6 3.2 %collective-permute-start.8 = (bf16[1024,128]{1,0:T(8,128)(2,1)S(1)}, bf16[1024,128]{1,0:T(8,128)(2,1)S(1)}, u32[]{:S(2)}, u32[]{:S(2)}) collective-permute-start(bf16[1024,128]{1,0:T(8,128)(2,1)S(1)} %get-tuple-element.80.refs_2_.refs_11_), channel_id=1, source_target_pairs={{0,1},{1,0},{2,3},{3,2},{4,5},{5,4},{6,7},{7,6},{8,9},{9,8},{10,11... | collective-permute-start | bytes 786440 | tf_op jit(solution)/shard_map/ppermute | solution.py:499
  40.3 7.1 %collective-permute-start.12 = (f32[24,128]{1,0:T(8,128)S(1)}, f32[24,128]{1,0:T(8,128)S(1)}, u32[]{:S(2)}, u32[]{:S(2)}) collective-permute-start(f32[24,128]{1,0:T(8,128)S(1)} %get-tuple-element.110), channel_id=1, source_target_pairs={{0,12},{1,13},{2,14},{3,15},{4,8},{5,9},{6,10},{7,11},{8,4},{9,5},... | collective-permute-start | bytes 36872 | tf_op jit(solution)/shard_map/ppermute | solution.py:461
  42.2 5.2 %collective-permute-start.11 = (f32[16,128]{1,0:T(8,128)S(1)}, f32[16,128]{1,0:T(8,128)S(1)}, u32[]{:S(2)}, u32[]{:S(2)}) collective-permute-start(f32[16,128]{1,0:T(8,128)S(1)} %get-tuple-element.109), channel_id=1, source_target_pairs={{0,8},{1,9},{2,10},{3,11},{4,12},{5,13},{6,14},{7,15},{8,0},{9,1},... | collective-permute-start | bytes 24584 | tf_op jit(solution)/shard_map/ppermute | solution.py:461
  43.7 3.7 %collective-permute-start.10 = (f32[8,128]{1,0:T(8,128)S(1)}, f32[8,128]{1,0:T(8,128)S(1)}, u32[]{:S(2)}, u32[]{:S(2)}) collective-permute-start(f32[8,128]{1,0:T(8,128)S(1)} %get-tuple-element.108.refs_0_), channel_id=1, source_target_pairs={{0,4},{1,5},{2,6},{3,7},{4,0},{5,1},{6,2},{7,3},{8,12},{9,13},{10,... | collective-permute-start | bytes 12296 | tf_op jit(solution)/shard_map/ppermute | solution.py:461
  47.4 5.6 %collective-permute-start.15 = (f32[24,128]{1,0:T(8,128)S(1)}, f32[24,128]{1,0:T(8,128)S(1)}, u32[]{:S(2)}, u32[]{:S(2)}) collective-permute-start(f32[24,128]{1,0:T(8,128)S(1)} %get-tuple-element.114), channel_id=1, source_target_pairs={{0,3},{1,2},{2,1},{3,0},{4,7},{5,6},{6,5},{7,4},{8,11},{9,10},{10,... | collective-permute-start | bytes 36872 | tf_op jit(solution)/shard_map/ppermute | solution.py:461
  47.5 5.6 %collective-permute-start.14 = (f32[16,128]{1,0:T(8,128)S(1)}, f32[16,128]{1,0:T(8,128)S(1)}, u32[]{:S(2)}, u32[]{:S(2)}) collective-permute-start(f32[16,128]{1,0:T(8,128)S(1)} %get-tuple-element.113), channel_id=1, source_target_pairs={{0,2},{1,3},{2,0},{3,1},{4,6},{5,7},{6,4},{7,5},{8,10},{9,11},{10,... | collective-permute-start | bytes 24584 | tf_op jit(solution)/shard_map/ppermute | solution.py:461
  51.3 1.2 %collective-permute-start.13 = (f32[8,128]{1,0:T(8,128)S(1)}, f32[8,128]{1,0:T(8,128)S(1)}, u32[]{:S(2)}, u32[]{:S(2)}) collective-permute-start(f32[8,128]{1,0:T(8,128)S(1)} %get-tuple-element.112), channel_id=1, source_target_pairs={{0,1},{1,0},{2,3},{3,2},{4,5},{5,4},{6,7},{7,6},{8,9},{9,8},{10,11... | collective-permute-start | bytes 12296 | tf_op jit(solution)/shard_map/ppermute | solution.py:461

commit v19 on v17

--- a/solution.py
+++ b/solution.py
@@ -536,10 +536,14 @@
             done = [field.astype(BF16) for field in done]
             held.update(zip(piece, done))
             rest = ins[1 + len(known) :]
+            near = sorted(held)
+            mixed = jnp.dot(
+                jnp.concatenate([held[n] for n in near], axis=1),
+                ins[0][span_lanes(near), span_lanes(todo)],
+                preferred_element_type=F32,
+            )
             for i, t in enumerate(todo):
-                x_new, y_new = updated(
-                    mixed_of(held, ins[0], t, channels), rest[2 * i][...], rest[2 * i + 1][...]
-                )
+                x_new, y_new = updated(mixed[:, lanes(i)], rest[2 * i][...], rest[2 * i + 1][...])
                 r_new = x_new.astype(BF16)
                 outs[0][:, lanes(i)] = r_new
                 outs[1 + i][...] = r_new

time: 54.8 us -> 54.6 us (level); the launches traced: 54 us -> 54.6 us
  Pallas kernels: 18.1 us -> 14.6 us
  starting transfers between devices: 28.6 us -> 31.7 us
  waiting for transfers between devices: 4.86 us -> 5.76 us
    pallas_call x12, Pallas kernels: 18.1 us -> 14.6 us  [call(): pl.pallas_call(body, in_specs=[pl.BlockSpec(memory_space=pl.ANY if s is p...]
    ppermute x6, starting transfers between devices: 9.79 us -> 11.7 us  [near_swap(): return lax.ppermute(mine, RING, on_chip)]
    ppermute x6, waiting for transfers between devices: 1.91 us -> 3.4 us  [sum_over_ring(): lax.ppermute(value, RING, [(j, j ^ bit) for j in range(ring)])]
    ppermute x4, starting transfers between devices: 10.9 us -> 11.8 us  [far_swap(): return lax.ppermute(mine, RING, off_chip)]
    ppermute x4, waiting for transfers between devices: 2.84 us -> 2.25 us  [far_swap(): return lax.ppermute(mine, RING, off_chip)]
  transfers between devices with their start and end apart: 16 -> 16, of which waited for: 5 -> 7; matrix products, arithmetic and copies ran while one was open for 0% -> 0% of each run, Pallas kernels for 29% -> 22%
where the time goes in v19:
time: 54.6 us
  starting transfers between devices  31.7 us (58%)
  Pallas kernels  14.6 us (27%)
  waiting for transfers between devices  5.76 us (11%)
  between operations  1.54 us (3%)
    pallas_call x12, Pallas kernels, call(): pl.pallas_call(body, in_specs=[pl.BlockSpec(memory_space=pl.ANY if s is p...  14.6 us
    ppermute x4, starting transfers between devices, far_swap(): return lax.ppermute(mine, RING, off_chip)  11.8 us
    ppermute x6, starting transfers between devices, near_swap(): return lax.ppermute(mine, RING, on_chip)  11.7 us
    ppermute x6, starting transfers between devices, sum_over_ring(): lax.ppermute(value, RING, [(j, j ^ bit) for j in range(ring)])  8.22 us
    ppermute x6, waiting for transfers between devices, sum_over_ring(): lax.ppermute(value, RING, [(j, j ^ bit) for j in range(ring)])  3.4 us
    ppermute x4, waiting for transfers between devices, far_swap(): return lax.ppermute(mine, RING, off_chip)  2.25 us
  transfers between devices with their start and end apart: 16, of which 7 were waited for; matrix products, arithmetic and copies ran while one was open for 0% of the time, Pallas kernels for 22%

profile of v19, /device:TPU:0, one launch (start us, length us, event | category | flops | bytes accessed | tf_op | source)
XLA Modules:
  0.0 54.6 jit_solution(17218593489878086502)
XLA Ops:
  0.7 1.4 %load_first.1 = (f32[1024,128]{1,0:T(8,128)S(1)}, f32[1024,128]{1,0:T(8,128)S(1)}, bf16[1024,128]{1,0:T(8,128)(2,1)S(1)}, bf16[1024,128]{1,0:T(8,128)(2,1)S(1)}, bf16[1024,256]{1,0:T(8,128)(2,1)S(1)}) custom-call(f32[1024,384]{1,0:T(8,128)} %x_ref.3), custom_call_target="tpu_custom_call" | custom-call | flops 1000 | bytes 1000 | tf_op jit(solution)/shard_map/load_first/pallas_call | solution.py:21
  2.1 5.5 %collective-permute-start.4 = (bf16[1024,256]{1,0:T(8,128)(2,1)S(1)}, bf16[1024,256]{1,0:T(8,128)(2,1)S(1)}, u32[]{:S(2)}, u32[]{:S(2)}) collective-permute-start(bf16[1024,256]{1,0:T(8,128)(2,1)S(1)} %get-tuple-element.59._), channel_id=1, source_target_pairs={{0,15},{1,2},{2,1},{3,4},{4,3},{5,6},{6,5},{7,8},{8,7},{9,10},{10,... | collective-permute-start | bytes 1572872 | tf_op jit(solution)/shard_map/ppermute | solution.py:498
  7.6 0.5 collective-permute-start.1
  8.8 1.3 %make_lists.1 = (s32[246]{0:T(256)S(4)}, f32[1024,128]{1,0:T(8,128)S(1)}, bf16[1024,128]{1,0:T(8,128)(2,1)S(1)}) custom-call(s32[96]{0:T(128)S(1)} %copy-done.5, s32[96]{0:T(128)S(1)} %copy-done.6, s32[1]{0:T(128)S(6)} %copy.28.count_hbm, f32[1024,384]{1,0:T(8,128)} %x_ref.3, bf16[1024,256]{1,0:T(8,128)(2,1)S(1)} %get-tuple-element.59._), custom_call_target="tpu_custom_call" | custom-call | flops 1000 | bytes 1000 | tf_op jit(solution)/shard_map/make_lists/pallas_call | solution.py:21
  10.1 0.1 collective-permute-start.2
  10.2 1.3 %first_base.1 = (f32[1024,128]{1,0:T(8,128)S(1)}, f32[1024,128]{1,0:T(8,128)S(1)}, f32[1024,128]{1,0:T(8,128)S(1)}, bf16[384,384]{1,0:T(8,128)(2,1)S(1)}) custom-call(f32[1024,128]{1,0:T(8,128)S(1)} %get-tuple-element.64.refs_0_.refs_4_, f32[1024,128]{1,0:T(8,128)S(1)} %get-tuple-element.65.refs_1_.refs_5_.refs_7_, ...), custom_call_target="tpu_custom_call" | custom-call | flops 1000 | bytes 1000 | tf_op jit(solution)/shard_map/first_base/pallas_call | solution.py:21
  11.6 0.1 collective-permute-done.2.refs_5_
  11.7 0.4 copy-done
  12.1 1.4 %near_first.1 = (f32[1024,128]{1,0:T(8,128)S(1)}, f32[1024,128]{1,0:T(8,128)S(1)}, f32[1024,128]{1,0:T(8,128)S(1)}, bf16[1024,128]{1,0:T(8,128)(2,1)S(1)}) custom-call(s32[246]{0:T(256)S(4)} %get-tuple-element.60.list_ref, bf16[96,128,128]{2,1,0:T(8,128)(2,1)S(1)} %copy-done, bf16[1024,128]{1,0:T(8,128)(2,1)S(1)} %get-tuple-element.61.refs_0_, ...), custom_call_target="tpu_custom_call" | custom-call | flops 1000 | bytes 1000 | tf_op jit(solution)/shard_map/near_first/pallas_call | solution.py:21
  13.5 0.8 %collective-permute-start.3 = (bf16[1024,128]{1,0:T(8,128)(2,1)S(1)}, bf16[1024,128]{1,0:T(8,128)(2,1)S(1)}, u32[]{:S(2)}, u32[]{:S(2)}) collective-permute-start(bf16[1024,128]{1,0:T(8,128)(2,1)S(1)} %get-tuple-element.68), channel_id=1, source_target_pairs={{0,15},{1,2},{2,1},{3,4},{4,3},{5,6},{6,5},{7,8},{8,7},{9,10},{10,... | collective-permute-start | bytes 786440 | tf_op jit(solution)/shard_map/ppermute | solution.py:498
  14.3 0.3 collective-permute-done.4.far_ref
  14.6 1.0 %far_first_0.1 = (bf16[1024,128]{1,0:T(8,128)(2,1)S(1)}, bf16[1024,128]{1,0:T(8,128)(2,1)S(1)}, bf16[1024,128]{1,0:T(8,128)(2,1)S(1)}, bf16[1024,128]{1,0:T(8,12...) custom-call(s32[246]{0:T(256)S(4)} %get-tuple-element.60.list_ref, bf16[96,128,128]{2,1,0:T(8,128)(2,1)S(1)} %copy-done, ...), custom_call_target="tpu_custom_call" | custom-call | flops 1000 | bytes 1000 | tf_op jit(solution)/shard_map/far_first_0/pallas_call | solution.py:21
  15.6 4.7 %collective-permute-start.9 = (bf16[1024,128]{1,0:T(8,128)(2,1)S(1)}, bf16[1024,128]{1,0:T(8,128)(2,1)S(1)}, u32[]{:S(2)}, u32[]{:S(2)}) collective-permute-start(bf16[1024,128]{1,0:T(8,128)(2,1)S(1)} %get-tuple-element.81), channel_id=1, source_target_pairs={{0,15},{1,2},{2,1},{3,4},{4,3},{5,6},{6,5},{7,8},{8,7},{9,10},{10,... | collective-permute-start | bytes 786440 | tf_op jit(solution)/shard_map/ppermute | solution.py:498
  20.3 1.9 %collective-permute-done.3.far_ref = bf16[1024,128]{1,0:T(8,128)(2,1)S(1)} collective-permute-done((bf16[1024,128]{1,0:T(8,128)(2,1)S(1)}, bf16[1024,128]{1,0:T(8,128)(2,1)S(1)}, u32[]{:S(2)}, u32[]{:S(2)}) %collective-permute-start.3) | collective-permute-done | bytes 262176 | tf_op jit(solution)/shard_map/ppermute | solution.py:498
  22.2 1.0 %far_first_1.1 = (bf16[1024,256]{1,0:T(8,128)(2,1)S(1)}, bf16[1024,128]{1,0:T(8,128)(2,1)S(1)}, bf16[1024,128]{1,0:T(8,128)(2,1)S(1)}, bf16[1024,128]{1,0:T(8,128)(2,1)S(1)}) custom-call(s32[246]{0:T(256)S(4)} %get-tuple-element.60.list_ref, bf16[96,128,128]{2,1,0:T(8,128)(2,1)S(1)} %copy-done, bf16[1024,128]{1,0:T(8,128)(2,1)S(1)} %collective-permute-done.3.far_ref, ...), custom_call_target="tpu_custom_call" | custom-call | flops 1000 | bytes 1000 | tf_op jit(solution)/shard_map/far_first_1/pallas_call | solution.py:21
  23.2 0.8 %collective-permute-start.5 = (bf16[1024,256]{1,0:T(8,128)(2,1)S(1)}, bf16[1024,256]{1,0:T(8,128)(2,1)S(1)}, u32[]{:S(2)}, u32[]{:S(2)}) collective-permute-start(bf16[1024,256]{1,0:T(8,128)(2,1)S(1)} %get-tuple-element.77), channel_id=1, source_target_pairs={{0,15},{1,2},{2,1},{3,4},{4,3},{5,6},{6,5},{7,8},{8,7},{9,10},{10,... | collective-permute-start | bytes 1572872 | tf_op jit(solution)/shard_map/ppermute | solution.py:498
  24.0 10.6 %collective-permute-start.6 = (bf16[1024,128]{1,0:T(8,128)(2,1)S(1)}, bf16[1024,128]{1,0:T(8,128)(2,1)S(1)}, u32[]{:S(2)}, u32[]{:S(2)}) collective-permute-start(bf16[1024,128]{1,0:T(8,128)(2,1)S(1)} %get-tuple-element.78.refs_0_.refs_9_), channel_id=1, source_target_pairs={{0,1},{1,0},{2,3},{3,2},{4,5},{5,4},{6,7},{7,6},{8,9},{9,8},{10,11... | collective-permute-start | bytes 786440 | tf_op jit(solution)/shard_map/ppermute | solution.py:501
  34.7 0.5 collective-permute-start.8
  35.2 2.0 %second_base.1 = (f32[1024,128]{1,0:T(8,128)S(1)}, f32[1024,128]{1,0:T(8,128)S(1)}, f32[1024,128]{1,0:T(8,128)S(1)}, f32[1024,128]{1,0:T(8,128)S(1)}, f32[1024,1...) custom-call(f32[1024,128]{1,0:T(8,128)S(1)} %get-tuple-element.84.refs_0_.refs_6_, ...), custom_call_target="tpu_custom_call" | custom-call | flops 1000 | bytes 1000 | tf_op jit(solution)/shard_map/second_base/pallas_call | solution.py:21
  37.2 0.6 %far_second_0.1.refs_6_ = f32[1024,128]{1,0:T(8,128)S(1)} custom-call(s32[246]{0:T(256)S(4)} %get-tuple-element.60.list_ref, bf16[96,128,128]{2,1,0:T(8,128)(2,1)S(1)} %copy-done, bf16[1024,128]{1,0:T(8,128)(2,1)S(1)} %collective-permute-done.9.far_ref), custom_call_target="tpu_custom_call" | custom-call | flops 4000000000 | bytes 1000 | tf_op jit(solution)/shard_map/far_second_0/pallas_call | solution.py:21
  37.8 1.4 %near_second.1 = (bf16[1024,128]{1,0:T(8,128)(2,1)S(1)}, f32[1024,128]{1,0:T(8,128)S(1)}, f32[1024,128]{1,0:T(8,128)S(1)}) custom-call(s32[246]{0:T(256)S(4)} %get-tuple-element.60.list_ref, bf16[96,128,128]{2,1,0:T(8,128)(2,1)S(1)} %copy-done, bf16[1024,128]{1,0:T(8,128)(2,1)S(1)} %get-tuple-element.78.refs_0_.refs_9_, ...), custom_call_target="tpu_custom_call" | custom-call | flops 1000 | bytes 1000 | tf_op jit(solution)/shard_map/near_second/pallas_call | solution.py:21
  39.3 1.0 %far_second_1.1 = (bf16[1024,128]{1,0:T(8,128)(2,1)S(1)}, bf16[1024,128]{1,0:T(8,128)(2,1)S(1)}, f32[8,128]{1,0:T(8,128)S(1)}, f32[16,128]{1,0:T(8,128)S(1)}, f3...) custom-call(s32[246]{0:T(256)S(4)} %get-tuple-element.60.list_ref, ...), custom_call_target="tpu_custom_call", output_to_operand_aliasing={{5}: (8, {}), {6}: (9, {}), {7}: (10, {}), {8}: (11, {}), {... | custom-call | flops 1000 | bytes 1000 | tf_op jit(solution)/shard_map/far_second_1/pallas_call | solution.py:21
  40.3 4.1 %collective-permute-start.12 = (f32[24,128]{1,0:T(8,128)S(1)}, f32[24,128]{1,0:T(8,128)S(1)}, u32[]{:S(2)}, u32[]{:S(2)}) collective-permute-start(f32[24,128]{1,0:T(8,128)S(1)} %get-tuple-element.110), channel_id=1, source_target_pairs={{0,12},{1,13},{2,14},{3,15},{4,8},{5,9},{6,10},{7,11},{8,4},{9,5},... | collective-permute-start | bytes 36872 | tf_op jit(solution)/shard_map/ppermute | solution.py:463
  44.4 0.6 %collective-permute-start.10 = (f32[8,128]{1,0:T(8,128)S(1)}, f32[8,128]{1,0:T(8,128)S(1)}, u32[]{:S(2)}, u32[]{:S(2)}) collective-permute-start(f32[8,128]{1,0:T(8,128)S(1)} %get-tuple-element.108.refs_0_), channel_id=1, source_target_pairs={{0,4},{1,5},{2,6},{3,7},{4,0},{5,1},{6,2},{7,3},{8,12},{9,13},{10,... | collective-permute-start | bytes 12296 | tf_op jit(solution)/shard_map/ppermute | solution.py:463
  45.0 2.2 %finish.1 = (f32[1024,384]{1,0:T(8,128)}, f32[1024,384]{1,0:T(8,128)}, f32[8,128]{1,0:T(8,128)S(1)}) custom-call(bf16[1024,128]{1,0:T(8,128)(2,1)S(1)} %get-tuple-element.96.refs_0_, bf16[1024,128]{1,0:T(8,128)(2,1)S(1)} %get-tuple-element.97.refs_1_, bf16[1024,128]{1,0:T(8,128)(2,1)S(1)} %get-tuple-element.98.refs_2_, ...), custom_call_target="tpu_custom_call" | custom-call | flops 1000 | bytes 1000 | tf_op jit(solution)/shard_map/finish/pallas_call | solution.py:21
  47.2 0.8 %collective-permute-done.10.refs_1_ = f32[8,128]{1,0:T(8,128)S(1)} collective-permute-done((f32[8,128]{1,0:T(8,128)S(1)}, f32[8,128]{1,0:T(8,128)S(1)}, u32[]{:S(2)}, u32[]{:S(2)}) %collective-permute-start.10) | collective-permute-done | bytes 4128 | tf_op jit(solution)/shard_map/ppermute | solution.py:463
  48.0 0.9 %collective-permute-done.11.refs_2_ = f32[16,128]{1,0:T(8,128)S(1)} collective-permute-done((f32[16,128]{1,0:T(8,128)S(1)}, f32[16,128]{1,0:T(8,128)S(1)}, u32[]{:S(2)}, u32[]{:S(2)}) %collective-permute-start.11) | collective-permute-done | bytes 8224 | tf_op jit(solution)/shard_map/ppermute | solution.py:463
  48.9 0.1 collective-permute-start.15
  49.0 3.4 %collective-permute-start.14 = (f32[16,128]{1,0:T(8,128)S(1)}, f32[16,128]{1,0:T(8,128)S(1)}, u32[]{:S(2)}, u32[]{:S(2)}) collective-permute-start(f32[16,128]{1,0:T(8,128)S(1)} %get-tuple-element.113), channel_id=1, source_target_pairs={{0,2},{1,3},{2,0},{3,1},{4,6},{5,7},{6,4},{7,5},{8,10},{9,11},{10,... | collective-permute-start | bytes 24584 | tf_op jit(solution)/shard_map/ppermute | solution.py:463
  52.4 1.1 %collective-permute-done.13 = f32[8,128]{1,0:T(8,128)S(1)} collective-permute-done((f32[8,128]{1,0:T(8,128)S(1)}, f32[8,128]{1,0:T(8,128)S(1)}, u32[]{:S(2)}, u32[]{:S(2)}) %collective-permute-start.13) | collective-permute-done | bytes 4128 | tf_op jit(solution)/shard_map/ppermute | solution.py:463
  53.6 0.5 collective-permute-done.14
  54.1 0.5 multiply_bitcast_fusion
  (28 shorter events, 0.1 us)
Async XLA Ops:
  0.6 9.5 %copy-start.2 = (bf16[384,384]{1,0:T(8,128)(2,1)S(1)}, bf16[384,384]{1,0:T(8,128)(2,1)}, u32[]{:S(2)}) copy-start(bf16[384,384]{1,0:T(8,128)(2,1)} %constant.7.clone.refs_4_.refs_12_) | copy-start | bytes 884740
  0.6 9.5 %copy-start.3 = (bf16[384,48]{1,0:T(8,128)(2,1)S(1)}, bf16[384,48]{1,0:T(8,128)(2,1)}, u32[]{:S(2)}) copy-start(bf16[384,48]{1,0:T(8,128)(2,1)} %constant.8.clone.refs_5_) | copy-start | bytes 110596
  0.7 8.1 %copy-start.6 = (s32[96]{0:T(128)S(1)}, s32[96]{0:T(128)}, u32[]{:S(2)}) copy-start(s32[96]{0:T(128)} %cols_hbm.1) | copy-start | bytes 1156
  0.7 8.1 %copy-start.5 = (s32[96]{0:T(128)S(1)}, s32[96]{0:T(128)}, u32[]{:S(2)}) copy-start(s32[96]{0:T(128)} %rows_hbm.1) | copy-start | bytes 1156
  0.7 9.5 %copy-start.4 = (bf16[48,48]{1,0:T(8,128)(2,1)S(1)}, bf16[48,48]{1,0:T(8,128)(2,1)}, u32[]{:S(2)}) copy-start(bf16[48,48]{1,0:T(8,128)(2,1)} %refs_6_.1) | copy-start | bytes 13828
  0.7 9.5 %copy-start.1 = (f32[1024,384]{1,0:T(8,128)S(1)}, f32[1024,384]{1,0:T(8,128)}, u32[]{:S(2)}) copy-start(f32[1024,384]{1,0:T(8,128)} %refs_3_.1) | copy-start | bytes 4718596
  2.1 12.5 %collective-permute-start.4 = (bf16[1024,256]{1,0:T(8,128)(2,1)S(1)}, bf16[1024,256]{1,0:T(8,128)(2,1)S(1)}, u32[]{:S(2)}, u32[]{:S(2)}) collective-permute-start(bf16[1024,256]{1,0:T(8,128)(2,1)S(1)} %get-tuple-element.59._), channel_id=1, source_target_pairs={{0,15},{1,2},{2,1},{3,4},{4,3},{5,6},{6,5},{7,8},{8,7},{9,10},{10,... | collective-permute-start | bytes 1572872 | tf_op jit(solution)/shard_map/ppermute | solution.py:498
  7.6 4.0 %collective-permute-start = (bf16[1024,128]{1,0:T(8,128)(2,1)S(1)}, bf16[1024,128]{1,0:T(8,128)(2,1)S(1)}, u32[]{:S(2)}, u32[]{:S(2)}) collective-permute-start(bf16[1024,128]{1,0:T(8,128)(2,1)S(1)} %get-tuple-element.61.refs_0_), channel_id=1, source_target_pairs={{0,1},{1,0},{2,3},{3,2},{4,5},{5,4},{6,7},{7,6},{8,9},{9,8},{10,11... | collective-permute-start | bytes 786440 | tf_op jit(solution)/shard_map/ppermute | solution.py:501
  7.6 4.0 %collective-permute-start.1 = (bf16[1024,128]{1,0:T(8,128)(2,1)S(1)}, bf16[1024,128]{1,0:T(8,128)(2,1)S(1)}, u32[]{:S(2)}, u32[]{:S(2)}) collective-permute-start(bf16[1024,128]{1,0:T(8,128)(2,1)S(1)} %get-tuple-element.62.refs_1_), channel_id=1, source_target_pairs={{0,1},{1,0},{2,3},{3,2},{4,5},{5,4},{6,7},{7,6},{8,9},{9,8},{10,11... | collective-permute-start | bytes 786440 | tf_op jit(solution)/shard_map/ppermute | solution.py:501
  10.1 1.6 %collective-permute-start.2 = (bf16[1024,128]{1,0:T(8,128)(2,1)S(1)}, bf16[1024,128]{1,0:T(8,128)(2,1)S(1)}, u32[]{:S(2)}, u32[]{:S(2)}) collective-permute-start(bf16[1024,128]{1,0:T(8,128)(2,1)S(1)} %get-tuple-element.63.refs_2_.refs_6_), channel_id=1, source_target_pairs={{0,1},{1,0},{2,3},{3,2},{4,5},{5,4},{6,7},{7,6},{8,9},{9,8},{10,11... | collective-permute-start | bytes 786440 | tf_op jit(solution)/shard_map/ppermute | solution.py:501
  10.2 1.9 %copy-start = (bf16[96,128,128]{2,1,0:T(8,128)(2,1)S(1)}, bf16[96,128,128]{2,1,0:T(8,128)(2,1)}, u32[]{:S(2)}) copy-start(bf16[96,128,128]{2,1,0:T(8,128)(2,1)} %tiles_ref.11) | copy-start | bytes 9437188
  13.5 8.7 %collective-permute-start.3 = (bf16[1024,128]{1,0:T(8,128)(2,1)S(1)}, bf16[1024,128]{1,0:T(8,128)(2,1)S(1)}, u32[]{:S(2)}, u32[]{:S(2)}) collective-permute-start(bf16[1024,128]{1,0:T(8,128)(2,1)S(1)} %get-tuple-element.68), channel_id=1, source_target_pairs={{0,15},{1,2},{2,1},{3,4},{4,3},{5,6},{6,5},{7,8},{8,7},{9,10},{10,... | collective-permute-start | bytes 786440 | tf_op jit(solution)/shard_map/ppermute | solution.py:498
  15.6 21.7 %collective-permute-start.9 = (bf16[1024,128]{1,0:T(8,128)(2,1)S(1)}, bf16[1024,128]{1,0:T(8,128)(2,1)S(1)}, u32[]{:S(2)}, u32[]{:S(2)}) collective-permute-start(bf16[1024,128]{1,0:T(8,128)(2,1)S(1)} %get-tuple-element.81), channel_id=1, source_target_pairs={{0,15},{1,2},{2,1},{3,4},{4,3},{5,6},{6,5},{7,8},{8,7},{9,10},{10,... | collective-permute-start | bytes 786440 | tf_op jit(solution)/shard_map/ppermute | solution.py:498
  23.2 16.1 %collective-permute-start.5 = (bf16[1024,256]{1,0:T(8,128)(2,1)S(1)}, bf16[1024,256]{1,0:T(8,128)(2,1)S(1)}, u32[]{:S(2)}, u32[]{:S(2)}) collective-permute-start(bf16[1024,256]{1,0:T(8,128)(2,1)S(1)} %get-tuple-element.77), channel_id=1, source_target_pairs={{0,15},{1,2},{2,1},{3,4},{4,3},{5,6},{6,5},{7,8},{8,7},{9,10},{10,... | collective-permute-start | bytes 1572872 | tf_op jit(solution)/shard_map/ppermute | solution.py:498
  24.0 13.8 %collective-permute-start.6 = (bf16[1024,128]{1,0:T(8,128)(2,1)S(1)}, bf16[1024,128]{1,0:T(8,128)(2,1)S(1)}, u32[]{:S(2)}, u32[]{:S(2)}) collective-permute-start(bf16[1024,128]{1,0:T(8,128)(2,1)S(1)} %get-tuple-element.78.refs_0_.refs_9_), channel_id=1, source_target_pairs={{0,1},{1,0},{2,3},{3,2},{4,5},{5,4},{6,7},{7,6},{8,9},{9,8},{10,11... | collective-permute-start | bytes 786440 | tf_op jit(solution)/shard_map/ppermute | solution.py:501
  34.7 3.2 %collective-permute-start.7 = (bf16[1024,128]{1,0:T(8,128)(2,1)S(1)}, bf16[1024,128]{1,0:T(8,128)(2,1)S(1)}, u32[]{:S(2)}, u32[]{:S(2)}) collective-permute-start(bf16[1024,128]{1,0:T(8,128)(2,1)S(1)} %get-tuple-element.79.refs_1_.refs_10_), channel_id=1, source_target_pairs={{0,1},{1,0},{2,3},{3,2},{4,5},{5,4},{6,7},{7,6},{8,9},{9,8},{10,11... | collective-permute-start | bytes 786440 | tf_op jit(solution)/shard_map/ppermute | solution.py:501
  34.7 3.2 %collective-permute-start.8 = (bf16[1024,128]{1,0:T(8,128)(2,1)S(1)}, bf16[1024,128]{1,0:T(8,128)(2,1)S(1)}, u32[]{:S(2)}, u32[]{:S(2)}) collective-permute-start(bf16[1024,128]{1,0:T(8,128)(2,1)S(1)} %get-tuple-element.80.refs_2_.refs_11_), channel_id=1, source_target_pairs={{0,1},{1,0},{2,3},{3,2},{4,5},{5,4},{6,7},{7,6},{8,9},{9,8},{10,11... | collective-permute-start | bytes 786440 | tf_op jit(solution)/shard_map/ppermute | solution.py:501
  40.3 8.6 %collective-permute-start.12 = (f32[24,128]{1,0:T(8,128)S(1)}, f32[24,128]{1,0:T(8,128)S(1)}, u32[]{:S(2)}, u32[]{:S(2)}) collective-permute-start(f32[24,128]{1,0:T(8,128)S(1)} %get-tuple-element.110), channel_id=1, source_target_pairs={{0,12},{1,13},{2,14},{3,15},{4,8},{5,9},{6,10},{7,11},{8,4},{9,5},... | collective-permute-start | bytes 36872 | tf_op jit(solution)/shard_map/ppermute | solution.py:463
  44.4 4.5 %collective-permute-start.11 = (f32[16,128]{1,0:T(8,128)S(1)}, f32[16,128]{1,0:T(8,128)S(1)}, u32[]{:S(2)}, u32[]{:S(2)}) collective-permute-start(f32[16,128]{1,0:T(8,128)S(1)} %get-tuple-element.109), channel_id=1, source_target_pairs={{0,8},{1,9},{2,10},{3,11},{4,12},{5,13},{6,14},{7,15},{8,0},{9,1},... | collective-permute-start | bytes 24584 | tf_op jit(solution)/shard_map/ppermute | solution.py:463
  44.4 3.6 %collective-permute-start.10 = (f32[8,128]{1,0:T(8,128)S(1)}, f32[8,128]{1,0:T(8,128)S(1)}, u32[]{:S(2)}, u32[]{:S(2)}) collective-permute-start(f32[8,128]{1,0:T(8,128)S(1)} %get-tuple-element.108.refs_0_), channel_id=1, source_target_pairs={{0,4},{1,5},{2,6},{3,7},{4,0},{5,1},{6,2},{7,3},{8,12},{9,13},{10,... | collective-permute-start | bytes 12296 | tf_op jit(solution)/shard_map/ppermute | solution.py:463
  48.9 5.2 %collective-permute-start.15 = (f32[24,128]{1,0:T(8,128)S(1)}, f32[24,128]{1,0:T(8,128)S(1)}, u32[]{:S(2)}, u32[]{:S(2)}) collective-permute-start(f32[24,128]{1,0:T(8,128)S(1)} %get-tuple-element.114), channel_id=1, source_target_pairs={{0,3},{1,2},{2,1},{3,0},{4,7},{5,6},{6,5},{7,4},{8,11},{9,10},{10,... | collective-permute-start | bytes 36872 | tf_op jit(solution)/shard_map/ppermute | solution.py:463
  49.0 5.1 %collective-permute-start.14 = (f32[16,128]{1,0:T(8,128)S(1)}, f32[16,128]{1,0:T(8,128)S(1)}, u32[]{:S(2)}, u32[]{:S(2)}) collective-permute-start(f32[16,128]{1,0:T(8,128)S(1)} %get-tuple-element.113), channel_id=1, source_target_pairs={{0,2},{1,3},{2,0},{3,1},{4,6},{5,7},{6,4},{7,5},{8,10},{9,11},{10,... | collective-permute-start | bytes 24584 | tf_op jit(solution)/shard_map/ppermute | solution.py:463
  52.4 1.2 %collective-permute-start.13 = (f32[8,128]{1,0:T(8,128)S(1)}, f32[8,128]{1,0:T(8,128)S(1)}, u32[]{:S(2)}, u32[]{:S(2)}) collective-permute-start(f32[8,128]{1,0:T(8,128)S(1)} %get-tuple-element.112), channel_id=1, source_target_pairs={{0,1},{1,0},{2,3},{3,2},{4,5},{5,4},{6,7},{7,6},{8,9},{9,8},{10,11... | collective-permute-start | bytes 12296 | tf_op jit(solution)/shard_map/ppermute | solution.py:463
